TPU v7x, 32 devices: a whole 2x2x4 slice. The times are simulated.
32 devices in a mesh: fsdp: 4 (over y, x), tp: 8 (over z, core).
Axes of the slice: x: 2, y: 2, z: 4, core: 2. Of those that a mesh axis runs over, the one named last changes fastest.
Arguments:
- inputs: bfloat16 [16384, 2048], P(('fsdp', 'tp')), may hold values from -6 to 6
- att_proj: bfloat16 [2048, 3, 2048], P('fsdp', None, 'tp'), may hold values from -0.1875 to 0.1875
- attn_out: bfloat16 [2048, 2048], P('tp', 'fsdp'), may hold values from -0.75 to 0.75
- ff_proj: bfloat16 [2048, 2, 8192], P('fsdp', None, 'tp'), may hold values from -0.125 to 0.125
- ff_out: bfloat16 [8192, 2048], P('tp', 'fsdp'), may hold values from -0.0625 to 0.0625
- segments: int32 [16384], P('fsdp'), may hold values from 0 to 2, as said below
- pad_mask: int32 [16384], P('fsdp'), may hold values from 0 to 1, as said below
- positions: int32 [16384], P('fsdp'), may hold values from 0 to 6143, as said below
- cotangent: bfloat16 [16384, 2048], P(('fsdp', 'tp')), may hold values from -6 to 6
Outputs:
- output: bfloat16 [16384, 2048], P(('fsdp', 'tp'))
- grad_input: bfloat16 [16384, 2048], P(('fsdp', 'tp'))
- grad_att_proj: float32 [2048, 3, 2048], P('fsdp', None, 'tp')
- grad_attn_out: float32 [2048, 2048], P('tp', 'fsdp')
- grad_ff_proj: float32 [2048, 2, 8192], P('fsdp', None, 'tp')
- grad_ff_out: float32 [8192, 2048], P('tp', 'fsdp')
Inputs may be any that keep to these rules, and one draw needn't show every extreme that they name: `segments`: within each packed sequence of 2048 tokens the ids never fall. `pad_mask`: in each packed sequence the padding is one run at its end, of one token or more. `positions`: within a document the position rises by one from token to token.
All inputs are finite; a program needn't handle non-finite values.
Results may differ from a plain program's by a relative error of at most 0.023.
Values may be sent and summed in bfloat16 or wider, within the bound.
A program may use at most 320 MiB of HBM per device.

v0:
```python
import math

import jax
import jax.numpy as jnp
from jax import lax
from jax.sharding import PartitionSpec as P

HD = 128
WINDOW = 1024
SEQ_LEN = 2048


EPSILON = 1e-05
NEGATIVE = -1e30
ROPE_BASE = 10000.0
BLOCK_ROWS = 512


def layer_norm(values):
    average = jnp.mean(values, axis=-1, keepdims=True)
    centered = values - average
    variance = jnp.mean(centered * centered, axis=-1, keepdims=True)
    return centered * lax.rsqrt(variance + EPSILON)


def rope_tables(positions, size):
    half_size = size // 2
    frequency = ROPE_BASE ** (-(jnp.arange(half_size, dtype=jnp.float32) * 2.0 / size))
    angles = positions.astype(jnp.float32)[:, None] * frequency[None, :]
    cosine = jnp.concatenate([jnp.cos(angles), jnp.cos(angles)], axis=-1)
    sine_part = jnp.concatenate([jnp.sin(angles), jnp.sin(angles)], axis=-1)
    return (cosine[:, None, :], sine_part[:, None, :])


def rotate(values, cosine, sine_part):
    half_size = values.shape[-1] // 2
    turned = jnp.concatenate([-values[..., half_size:], values[..., :half_size]], axis=-1)
    return values * cosine + turned * sine_part


def visible(query_place, key_place, query_doc, key_doc, key_live, window):
    distance = query_place[:, None] - key_place[None, :]
    same_doc = query_doc[:, None] == key_doc[None, :]
    live_key = (key_live[None, :] == 1) | (distance == 0)
    return (distance >= 0) & (distance < window) & same_doc & live_key


def dot_last(left, right):
    return lax.dot_general(
        left, right, (((1,), (1,)), ((), ())), preferred_element_type=jnp.float32
    )


def dot_first(left, right):
    return lax.dot_general(
        left, right, (((0,), (0,)), ((), ())), preferred_element_type=jnp.float32
    )


def block_mask(first, block, window, segment, segment_pad, padding_pad):
    query_place = first + jnp.arange(block, dtype=jnp.int32)
    key_place = first - window + jnp.arange(block + window, dtype=jnp.int32)
    return visible(
        query_place,
        key_place,
        segment[first : first + block],
        segment_pad[first : first + block + window],
        padding_pad[first : first + block + window],
        window,
    )


def block_scores(rows_query, rows_key, allowed, scaling):
    scores = (
        jnp.einsum("qhd,khd->hqk", rows_query, rows_key, preferred_element_type=jnp.float32)
        * scaling
    )
    return jnp.where(allowed[None], scores, NEGATIVE)


def attend_forward(pieces, window, block, scaling):
    query_low, key_low, value_low, segment, padding = pieces
    length = query_low.shape[0]
    keys_pad = jnp.pad(key_low, ((window, 0), (0, 0), (0, 0)))
    values_pad = jnp.pad(value_low, ((window, 0), (0, 0), (0, 0)))
    segment_pad = jnp.pad(segment, (window, 0), constant_values=-1)
    padding_pad = jnp.pad(padding, (window, 0))
    outputs = []
    totals = []
    for first in range(0, length, block):
        allowed = block_mask(first, block, window, segment, segment_pad, padding_pad)
        scores = block_scores(
            query_low[first : first + block],
            keys_pad[first : first + block + window],
            allowed,
            scaling,
        )
        row_max = jnp.max(scores, axis=-1, keepdims=True)
        weights = jnp.exp(scores - row_max)
        total = jnp.sum(weights, axis=-1, keepdims=True)
        probability = (weights / total).astype(jnp.bfloat16)
        outputs.append(
            jnp.einsum(
                "hqk,khd->qhd",
                probability,
                values_pad[first : first + block + window],
                preferred_element_type=jnp.float32,
            )
        )
        totals.append(row_max + jnp.log(total))
    return (jnp.concatenate(outputs, axis=0), jnp.concatenate(totals, axis=1))


def attend_backward(pieces, window, block, scaling):
    query_low, key_low, value_low, out_grad, log_total, segment, padding = pieces
    length, heads_here, size = query_low.shape
    keys_pad = jnp.pad(key_low, ((window, 0), (0, 0), (0, 0)))
    values_pad = jnp.pad(value_low, ((window, 0), (0, 0), (0, 0)))
    segment_pad = jnp.pad(segment, (window, 0), constant_values=-1)
    padding_pad = jnp.pad(padding, (window, 0))
    grad_keys = jnp.zeros((length + window, heads_here, size), jnp.float32)
    grad_values = jnp.zeros((length + window, heads_here, size), jnp.float32)
    grad_queries = []
    for first in range(0, length, block):
        allowed = block_mask(first, block, window, segment, segment_pad, padding_pad)
        rows_query = query_low[first : first + block]
        rows_key = keys_pad[first : first + block + window]
        rows_value = values_pad[first : first + block + window]
        rows_grad = out_grad[first : first + block]
        scores = block_scores(rows_query, rows_key, allowed, scaling)
        probability = jnp.exp(scores - log_total[:, first : first + block])
        grad_prob = jnp.einsum(
            "qhd,khd->hqk", rows_grad, rows_value, preferred_element_type=jnp.float32
        )
        inner = jnp.sum(probability * grad_prob, axis=-1, keepdims=True)
        grad_raw = (probability * (grad_prob - inner) * scaling).astype(jnp.bfloat16)
        grad_queries.append(
            jnp.einsum("hqk,khd->qhd", grad_raw, rows_key, preferred_element_type=jnp.float32)
        )
        grad_keys = grad_keys.at[first : first + block + window].add(
            jnp.einsum("hqk,qhd->khd", grad_raw, rows_query, preferred_element_type=jnp.float32)
        )
        grad_values = grad_values.at[first : first + block + window].add(
            jnp.einsum(
                "hqk,qhd->khd",
                probability.astype(jnp.bfloat16),
                rows_grad,
                preferred_element_type=jnp.float32,
            )
        )
    return (jnp.concatenate(grad_queries, axis=0), grad_keys[window:], grad_values[window:])


def local(inputs, att_proj, attn_out, ff_proj, ff_out, segments, pad_mask, positions, cotangent):
    w_attn, w_heads, w_ffn, w_down = (
        lax.all_gather(att_proj, "fsdp", axis=0, tiled=True),
        lax.all_gather(attn_out, "fsdp", axis=1, tiled=True),
        lax.all_gather(ff_proj, "fsdp", axis=0, tiled=True),
        lax.all_gather(ff_out, "fsdp", axis=1, tiled=True),
    )
    model = w_attn.shape[0]
    local_width = w_attn.shape[2]
    ffn_width = w_ffn.shape[2]
    size = HD
    heads_here = local_width // size
    length = SEQ_LEN
    window = WINDOW
    group = segments.shape[0]
    seq_count = group // length
    block = min(BLOCK_ROWS, length)
    scaling = 1.0 / math.sqrt(size)
    attn_matrix = w_attn.reshape(model, 3 * local_width)
    ffn_matrix = w_ffn.reshape(model, 2 * ffn_width)

    def split_seq(values):
        return values.reshape((seq_count, length) + values.shape[1:])

    x_float = inputs.astype(jnp.float32)
    normed, norm_pull = jax.vjp(layer_norm, x_float)
    normed_all = lax.all_gather(normed.astype(jnp.bfloat16), "tp", axis=0, tiled=True)
    project = jnp.dot(normed_all, attn_matrix, preferred_element_type=jnp.float32)
    project = project.reshape(group, 3, heads_here, size)
    cosine, sine_part = rope_tables(positions, size)

    def rope_both(query_pre, key_pre):
        return (rotate(query_pre, cosine, sine_part), rotate(key_pre, cosine, sine_part))

    (query_rot, key_rot), rope_pull = jax.vjp(rope_both, project[:, 0], project[:, 1])
    query_low = query_rot.astype(jnp.bfloat16)
    key_low = key_rot.astype(jnp.bfloat16)
    value_low = project[:, 2].astype(jnp.bfloat16)

    def forward_piece(pieces):
        return attend_forward(pieces, window, block, scaling)

    head_out, log_total = lax.map(
        forward_piece,
        (
            split_seq(query_low),
            split_seq(key_low),
            split_seq(value_low),
            split_seq(segments),
            split_seq(pad_mask),
        ),
    )
    heads_low = head_out.reshape(group, local_width).astype(jnp.bfloat16)
    heads_rows = lax.all_to_all(heads_low, "tp", split_axis=0, concat_axis=1, tiled=True)
    w_heads_all = lax.all_gather(w_heads, "tp", axis=0, tiled=True)
    attn_branch = jnp.dot(heads_rows, w_heads_all, preferred_element_type=jnp.float32)
    resid = x_float + attn_branch
    normed_two, norm_two_pull = jax.vjp(layer_norm, resid)
    normed_two_all = lax.all_gather(normed_two.astype(jnp.bfloat16), "tp", axis=0, tiled=True)
    projected = jnp.dot(normed_two_all, ffn_matrix, preferred_element_type=jnp.float32)
    projected = projected.reshape(group, 2, ffn_width)

    def swiglu(up_value, gate_value):
        return jax.nn.silu(gate_value) * up_value

    hidden_float, swiglu_pull = jax.vjp(swiglu, projected[:, 0], projected[:, 1])
    hidden_low = hidden_float.astype(jnp.bfloat16)
    ffn_branch = lax.psum_scatter(
        jnp.dot(hidden_low, w_down, preferred_element_type=jnp.float32).astype(jnp.bfloat16),
        "tp",
        scatter_dimension=0,
        tiled=True,
    ).astype(jnp.float32)
    output = (resid + ffn_branch).astype(jnp.bfloat16)
    out_grad_all = lax.all_gather(cotangent, "tp", axis=0, tiled=True)
    grad_hidden = dot_last(out_grad_all, w_down)
    grad_down = dot_first(hidden_low, out_grad_all)
    grad_up, grad_gate = swiglu_pull(grad_hidden)
    grad_ffn_low = (
        jnp.stack([grad_up, grad_gate], axis=1).astype(jnp.bfloat16).reshape(group, 2 * ffn_width)
    )
    grad_ffn = dot_first(normed_two_all, grad_ffn_low).reshape(model, 2, ffn_width)
    grad_normed_two = lax.psum_scatter(
        dot_last(grad_ffn_low, ffn_matrix).astype(jnp.bfloat16),
        "tp",
        scatter_dimension=0,
        tiled=True,
    ).astype(jnp.float32)
    grad_resid = cotangent.astype(jnp.float32) + norm_two_pull(grad_normed_two)[0]
    resid_grad_low = grad_resid.astype(jnp.bfloat16)
    resid_grad_all = lax.all_gather(resid_grad_low, "tp", axis=0, tiled=True)
    grad_heads_weight = dot_first(heads_low, resid_grad_all)
    rows_head_grad = dot_last(resid_grad_low, w_heads_all).astype(jnp.bfloat16)
    head_grad = lax.all_to_all(rows_head_grad, "tp", split_axis=1, concat_axis=0, tiled=True)
    head_grad = head_grad.reshape(group, heads_here, size)

    def backward_piece(pieces):
        return attend_backward(pieces, window, block, scaling)

    grad_query_rot, grad_key_rot, grad_value = lax.map(
        backward_piece,
        (
            split_seq(query_low),
            split_seq(key_low),
            split_seq(value_low),
            split_seq(head_grad),
            log_total,
            split_seq(segments),
            split_seq(pad_mask),
        ),
    )
    grad_query, grad_key = rope_pull(
        (
            grad_query_rot.reshape(group, heads_here, size),
            grad_key_rot.reshape(group, heads_here, size),
        )
    )
    grad_project_low = jnp.stack(
        [grad_query, grad_key, grad_value.reshape(group, heads_here, size)], axis=1
    )
    grad_project_low = grad_project_low.astype(jnp.bfloat16).reshape(group, 3 * local_width)
    grad_attn = dot_first(normed_all, grad_project_low).reshape(model, 3, local_width)
    grad_normed = lax.psum_scatter(
        dot_last(grad_project_low, attn_matrix).astype(jnp.bfloat16),
        "tp",
        scatter_dimension=0,
        tiled=True,
    ).astype(jnp.float32)
    grad_input = (grad_resid + norm_pull(grad_normed)[0]).astype(jnp.bfloat16)
    summed = (
        lax.psum_scatter(
            grad_attn.astype(jnp.bfloat16), "fsdp", scatter_dimension=0, tiled=True
        ).astype(jnp.float32),
        lax.psum_scatter(
            grad_heads_weight.astype(jnp.bfloat16), "fsdp", scatter_dimension=1, tiled=True
        ).astype(jnp.float32),
        lax.psum_scatter(
            grad_ffn.astype(jnp.bfloat16), "fsdp", scatter_dimension=0, tiled=True
        ).astype(jnp.float32),
        lax.psum_scatter(
            grad_down.astype(jnp.bfloat16), "fsdp", scatter_dimension=1, tiled=True
        ).astype(jnp.float32),
    )
    return (output, grad_input, summed[0], summed[1], summed[2], summed[3])


def solution(mesh):
    placed = (
        P(("fsdp", "tp"), None),
        P("fsdp", None, "tp"),
        P("tp", "fsdp"),
        P("fsdp", None, "tp"),
        P("tp", "fsdp"),
        P("fsdp"),
        P("fsdp"),
        P("fsdp"),
        P(("fsdp", "tp"), None),
    )
    return jax.shard_map(
        local,
        mesh=mesh,
        in_specs=placed,
        out_specs=(
            P(("fsdp", "tp"), None),
            P(("fsdp", "tp"), None),
            P("fsdp", None, "tp"),
            P("tp", "fsdp"),
            P("fsdp", None, "tp"),
            P("tp", "fsdp"),
        ),
        check_vma=False,
    )
```

profile of v0, /device:TPU:0, one launch (start us, length us, event | category | flops | bytes accessed | tf_op | source)
XLA Modules:
  0.0 2101.9 jit_solution(2029531507865927149)
XLA Ops:
  16.1 22.9 %all-gather.14.cloned.1.call-done = bf16[256,2048]{1,0:T(8,128)(2,1)} async-done(((bf16[256,512]{1,0:T(8,128)(2,1)}), bf16[256,2048]{1,0:T(8,128)(2,1)}) %all-gather.14.cloned.1.call-update) | async-done | bytes 1048592 | tf_op jit(solution)/shard_map/all_gather | solution.py:157
  42.9 7.3 multiply_cosine_fusion.1
  53.4 32.0 %all-gather.12.cloned.1.call-done = bf16[2048,3,256]{0,2,1:T(8,128)(2,1)} async-done(((bf16[512,3,256]{0,2,1:T(8,128)(2,1)}), bf16[2048,3,256]{0,2,1:T(8,128)(2,1)}) %all-gather.12.cloned.1.call-update) | async-done | bytes 3145744 | tf_op jit(solution)/shard_map/all_gather | solution.py:156
  85.3 153.3 %all-gather.10.cloned.1.call-done = bf16[4096,2048]{1,0:T(8,128)(2,1)} async-done(((bf16[512,2048]{1,0:T(8,128)(2,1)}), bf16[4096,2048]{1,0:T(8,128)(2,1)}) %all-gather.10.cloned.1.call-update) | async-done | bytes 16777232 | tf_op jit(solution)/shard_map/all_gather | solution.py:180
  238.7 20.5 fusion.252
  259.2 8.8 fusion.294
  335.9 10.7 fusion.277
  346.6 70.2 %while.39 = (s32[]{:T(128)}, bf16[2,2048,2,128]{1,3,2,0:T(8,128)(2,1)}, f32[2,2,2048,1]{2,1,3,0:T(2,128)S(1)}, bf16[2,2048,2,128]{1,3,2,0:T(8,128)(2,1)}, s32[2,...) while((s32[]{:T(128)}, ...), condition=%wide.region_11.12_spmd, body=%wide.region_2.11_spmd.sunk | while | flops 3329249280 | bytes 112574208 | solution.py:196
  427.6 53.6 %all_to_all.32 = bf16[8,512,256]{2,1,0:T(8,128)(2,1)} all-to-all(bf16[8,512,256]{2,1,0:T(8,128)(2,1)} %convert_element_type.212), channel_id=1, replica_groups=mesh['fsdp'=4,'tp'=8] {'tp'}, dimensions={0} | all-to-all | bytes 4194304 | tf_op jit(solution)/shard_map/all_to_all | solution.py:207
  485.1 7.8 fusion.297
  498.9 12.2 copy.98
  511.1 136.3 %all-gather.18.cloned.1.call-done = bf16[4096,2048]{1,0:T(8,128)(2,1)} async-done(((bf16[512,2048]{1,0:T(8,128)(2,1)}), bf16[4096,2048]{1,0:T(8,128)(2,1)}) %all-gather.18.cloned.1.call-update) | async-done | bytes 16777232 | tf_op jit(solution)/shard_map/all_gather | solution.py:212
  647.4 43.7 %fusion.257 = f32[4096,2,1024]{0,2,1:T(8,128)} fusion(bf16[4096,2048]{1,0:T(8,128)(2,1)} %all-gather.18.cloned.1.call-done, bf16[2048,2,1024]{0,2,1:T(8,128)(2,1)} %copy.98), kind=kOutput, calls=%fused_computation.318 | convolution fusion | flops 34359738368 | bytes 58720256 | tf_op jit(solution)/shard_map/dot_general | solution.py:213
  691.1 9.0 all-gather.22.cloned.1.call-done
  700.0 152.7 %all-gather.24.cloned.1.call-done = bf16[4096,2048]{1,0:T(8,128)(2,1)} async-done(((bf16[512,2048]{1,0:T(8,128)(2,1)}), bf16[4096,2048]{1,0:T(8,128)(2,1)}) %all-gather.24.cloned.1.call-update) | async-done | bytes 16777232 | tf_op jit(solution)/shard_map/all_gather | solution.py:228
  852.8 34.1 %multiply_bitcast_fusion = (bf16[4096,1,1024]{0,2,1:T(8,128)(2,1)}, bf16[4096,1,1024]{0,2,1:T(8,128)(2,1)}) fusion(f32[4096,2,1024]{0,2,1:T(8,128)} %fusion.257, bf16[4096,2048]{1,0:T(8,128)(2,1)} %all-gather.24.cloned.1.call-done, bf16[1024,2048]{1,0:T(8,128)(2,1)} %all-gather.22.cloned.1.call-done), kind=kOutput, calls=%fused_computation.320 | convolution fusion | flops 17238589440 | bytes 71303168 | tf_op jit(solution)/shard_map/dot_general | solution.py:49
  886.9 40.2 %bitcast_convert_fusion = bf16[4096,2048]{1,0:T(8,128)(2,1)} fusion(bf16[2048,2,1024]{2,0,1:T(8,128)(2,1)S(1)} %copy-done.33, bf16[4096,1,1024]{0,2,1:T(8,128)(2,1)} %get-tuple-element.558, bf16[4096,1,1024]{0,2,1:T(8,128)(2,1)} %get-tuple-element.557), kind=kOutput, calls=%fused_computation.304 | convolution fusion | flops 34376515584 | bytes 41943040 | tf_op jit(solution)/shard_map/dot_general | solution.py:49
  927.2 16.8 multiply_convert_fusion.4
  944.0 23.8 %convolution_convert_fusion.1 = bf16[4096,2048]{1,0:T(8,128)(2,1)} fusion(bf16[4096,1024]{0,1:T(8,128)(2,1)} %multiply_convert_fusion.4, bf16[1024,2048]{1,0:T(8,128)(2,1)S(1)} %copy-done.63), kind=kOutput, calls=%fused_computation.325 | convolution fusion | flops 17188257792 | bytes 29360128 | tf_op jit(solution)/shard_map/dot_general | solution.py:222
  967.9 125.8 %reduce-scatter.10.cloned.1.call-done = bf16[512,2048]{1,0:T(8,128)(2,1)} async-done(((bf16[4096,2048]{1,0:T(8,128)(2,1)}), bf16[512,2048]{1,0:T(8,128)(2,1)}) %reduce-scatter.10.cloned.1.call-update) | async-done | bytes 2097168 | tf_op jit(solution)/shard_map/reduce_scatter | solution.py:236
  1097.3 165.3 %reduce-scatter.8.cloned.1.call-done = bf16[512,2048]{1,0:T(8,128)(2,1)} async-done(((bf16[4096,2048]{1,0:T(8,128)(2,1)}), bf16[512,2048]{1,0:T(8,128)(2,1)}) %reduce-scatter.8.cloned.1.call-update) | async-done | bytes 2097168 | tf_op jit(solution)/shard_map/reduce_scatter | solution.py:221
  1271.8 24.0 %convolution_convert_fusion.2 = bf16[1024,2048]{1,0:T(8,128)(2,1)} fusion(bf16[4096,1024]{0,1:T(8,128)(2,1)} %multiply_convert_fusion.4, bf16[4096,2048]{1,0:T(8,128)(2,1)} %all-gather.24.cloned.1.call-done), kind=kOutput, calls=%fused_computation.367 | convolution fusion | flops 17181966336 | bytes 29360128 | tf_op jit(solution)/shard_map/dot_general | solution.py:55
  1312.3 8.6 convolution_convert_fusion.3
  1326.8 43.1 %fusion.265 = bf16[2048,2,1024]{2,0,1:T(8,128)(2,1)} fusion(bf16[4096,2048]{1,0:T(8,128)(2,1)} %all-gather.18.cloned.1.call-done, bf16[4096,1,1024]{0,2,1:T(8,128)(2,1)} %get-tuple-element.558, bf16[4096,1,1024]{0,2,1:T(8,128)(2,1)} %get-tuple-element.557), kind=kOutput, calls=%fused_computation.337 | convolution fusion | flops 34397487104 | bytes 41943040 | tf_op jit(solution)/shard_map/dot_general | solution.py:55
  1370.0 60.9 %all-to-all-done.1 = bf16[512,8,256]{2,0,1:T(8,128)(2,1)} async-done(((bf16[512,8,256]{2,0,1:T(8,128)(2,1)}), bf16[512,8,256]{2,0,1:T(8,128)(2,1)}, u32[]{:S(2)}, u32[]{:S(2)}) %all-to-all-start.1) | async-done | bytes 2097184 | tf_op jit(solution)/shard_map/all_to_all | solution.py:247
  1435.0 353.7 %while.40 = (s32[]{:T(128)}, f32[2,2048,2,128]{3,1,0,2:T(8,128)}, f32[2,2048,2,128]{3,1,0,2:T(8,128)}, bf16[2,2048,2,128]{3,1,0,2:T(8,128)(2,1)}, bf16[2,2048,2,...) while((s32[]{:T(128)}, f32[2,2048,2,128]{3,1,0,2:T(8,128)}, ...), condition=%wide.region_23.24_spmd, body=%wide.region_18.23_spmd.sunk | while | flops 8173420544 | bytes 495752608 | solution.py:253
  1471.3 10.6 fusion.408
  1494.2 11.9 fusion.409
  1520.4 10.1 fusion.410
  1541.1 10.7 fusion.411
  1556.8 11.5 fusion.404
  1568.3 11.2 fusion.407
  1579.5 11.4 fusion.400
  1590.9 11.6 fusion.398
  1636.2 10.3 fusion.408
  1658.9 11.9 fusion.409
  1685.1 10.1 fusion.410
  1705.7 10.0 fusion.411
  1720.6 11.1 fusion.404
  1731.7 11.2 fusion.407
  1742.9 10.9 fusion.400
  1753.8 10.8 fusion.398
  1813.3 8.7 copy.106
  1822.0 20.0 fusion.282
  1843.6 9.8 convolution_convert_fusion.4
  1853.5 20.2 convolution_convert_fusion
  1886.8 28.7 %reduce-scatter.16.cloned.1.call-done = bf16[256,512]{1,0:T(8,128)(2,1)} async-done(((bf16[256,2048]{1,0:T(8,128)(2,1)}), bf16[256,512]{1,0:T(8,128)(2,1)}) %reduce-scatter.16.cloned.1.call-update) | async-done | bytes 262160 | tf_op jit(solution)/shard_map/reduce_scatter | solution.py:287
  1917.3 168.8 %reduce-scatter.12.cloned.1.call-done = bf16[512,2048]{1,0:T(8,128)(2,1)} async-done(((bf16[4096,2048]{1,0:T(8,128)(2,1)}), bf16[512,2048]{1,0:T(8,128)(2,1)}) %reduce-scatter.12.cloned.1.call-update) | async-done | bytes 2097168 | tf_op jit(solution)/shard_map/reduce_scatter | solution.py:276
  (450 shorter events, 413.7 us)
Async XLA Ops:
  7.2 31.9 %all-gather.14.cloned.1.call-start = ((), (), s32[]{:S(2)}) async-start(), calls=%async_computation.11 | async-start | bytes 1310720 | tf_op jit(solution)/shard_map/all_gather | solution.py:157
  7.9 77.4 %all-gather.12.cloned.1.call-start = ((), (), s32[]{:S(2)}) async-start(), calls=%async_computation.10 | async-start | bytes 3932160 | tf_op jit(solution)/shard_map/all_gather | solution.py:156
  10.3 228.4 %all-gather.10.cloned.1.call-start = ((), (), s32[]{:S(2)}) async-start(), calls=%async_computation.9 | async-start | bytes 18874368 | tf_op jit(solution)/shard_map/all_gather | solution.py:180
  16.0 26.7 %copy-start.58 = (s32[4096]{0:T(1024)S(1)}, s32[4096]{0:T(1024)}, u32[]{:S(2)}) copy-start(s32[4096]{0:T(1024)} %param.36) | copy-start | bytes 49156
  16.1 26.8 %copy-start.59 = (s32[4096]{0:T(1024)S(1)}, s32[4096]{0:T(1024)}, u32[]{:S(2)}) copy-start(s32[4096]{0:T(1024)} %param.34) | copy-start | bytes 49156
  16.1 26.8 %copy-start.60 = (s32[4096]{0:T(1024)S(1)}, s32[4096]{0:T(1024)}, u32[]{:S(2)}) copy-start(s32[4096]{0:T(1024)} %param.35) | copy-start | bytes 49156
  16.1 469.0 %all-gather.16.cloned.1.call-start = ((), (), s32[]{:S(2)}) async-start(), calls=%async_computation.12 | async-start | bytes 9437184 | tf_op jit(solution)/shard_map/all_gather | solution.py:208
  39.1 459.8 %all-gather.20.cloned.1.call-start = ((), (), s32[]{:S(2)}) async-start(), calls=%async_computation.14 | async-start | bytes 10485760 | tf_op jit(solution)/shard_map/all_gather | solution.py:158
  42.7 604.7 %all-gather.18.cloned.1.call-start = ((), (), s32[]{:S(2)}) async-start(), calls=%async_computation.13 | async-start | bytes 18874368 | tf_op jit(solution)/shard_map/all_gather | solution.py:212
  416.8 10.8 copy-start.35
  416.8 10.8 copy-start.37
  416.8 10.8 copy-start.40
  427.6 57.5 %copy-start.5 = (bf16[512,2048]{1,0:T(8,128)(2,1)S(1)}, bf16[512,2048]{1,0:T(8,128)(2,1)}, u32[]{:S(2)}) copy-start(bf16[512,2048]{1,0:T(8,128)(2,1)} %param.29) | copy-start | bytes 6291460
  497.3 202.7 %all-gather.22.cloned.1.call-start = ((), (), s32[]{:S(2)}) async-start(), calls=%async_computation.15 | async-start | bytes 5242880 | tf_op jit(solution)/shard_map/all_gather | solution.py:159
  498.1 354.7 %all-gather.24.cloned.1.call-start = ((), (), s32[]{:S(2)}) async-start(), calls=%async_computation.17 | async-start | bytes 18874368 | tf_op jit(solution)/shard_map/all_gather | solution.py:228
  498.8 594.9 %reduce-scatter.10.cloned.1.call-start = ((), (), s32[]{:S(2)}) async-start(), calls=%async_computation.18 | async-start | bytes 18874368 | tf_op jit(solution)/shard_map/reduce_scatter | solution.py:236
  852.8 34.1 %copy-start.33 = (bf16[2048,2,1024]{2,0,1:T(8,128)(2,1)S(1)}, bf16[2048,2,1024]{2,0,1:T(8,128)(2,1)}, u32[]{:S(2)}) copy-start(bf16[2048,2,1024]{2,0,1:T(8,128)(2,1)} %all-gather.20.cloned.1.call-done) | copy-start | bytes 25165828
  927.1 335.5 %reduce-scatter.8.cloned.1.call-start = ((), (), s32[]{:S(2)}) async-start(), calls=%async_computation.16 | async-start | bytes 18874368 | tf_op jit(solution)/shard_map/reduce_scatter | solution.py:221
  927.1 16.8 copy-start.63
  967.8 125.9 %copy-start.47 = (f32[512]{0:T(512)S(1)}, f32[512]{0:T(512)}, u32[]{:S(2)}) copy-start(f32[512]{0:T(512)} %copy-done.46) | copy-start | bytes 6148
  967.8 129.4 %copy-start.51 = (f32[512]{0:T(512)S(1)}, f32[512]{0:T(512)}, u32[]{:S(2)}) copy-start(f32[512]{0:T(512)} %copy-done.50) | copy-start | bytes 6148
  967.8 294.7 %copy-start.55 = (f32[512]{0:T(512)S(1)}, f32[512]{0:T(512)}, u32[]{:S(2)}) copy-start(f32[512]{0:T(512)} %copy-done.54) | copy-start | bytes 6148
  967.9 874.3 %all-gather.26.cloned.1.call-start = ((), (), s32[]{:S(2)}) async-start(), calls=%async_computation.21 | async-start | bytes 18874368 | tf_op jit(solution)/shard_map/all_gather | solution.py:244
  1097.3 172.5 %copy-start.23 = (bf16[512,2048]{1,0:T(8,128)(2,1)S(1)}, bf16[512,2048]{1,0:T(8,128)(2,1)}, u32[]{:S(2)}) copy-start(bf16[512,2048]{1,0:T(8,128)(2,1)} %param.37) | copy-start | bytes 6291460
  1271.8 601.9 %reduce-scatter.20.cloned.1.call-start = ((), (), s32[]{:S(2)}) async-start(), calls=%async_computation.24 | async-start | bytes 5242880 | tf_op jit(solution)/shard_map/reduce_scatter | solution.py:293
  1322.4 108.5 %all-to-all-start.1 = ((bf16[512,8,256]{2,0,1:T(8,128)(2,1)}), bf16[512,8,256]{2,0,1:T(8,128)(2,1)}, u32[]{:S(2)}, u32[]{:S(2)}) async-start(bf16[512,8,256]{2,0,1:T(8,128)(2,1)} %bitcast.477), calls=%async_computation.3 | async-start | bytes 4194304 | tf_op jit(solution)/shard_map/all_to_all | solution.py:247
  1326.7 549.8 %reduce-scatter.18.cloned.1.call-start = ((), (), s32[]{:S(2)}) async-start(), calls=%async_computation.23 | async-start | bytes 10485760 | tf_op jit(solution)/shard_map/reduce_scatter | solution.py:290
  1369.9 65.1 %copy-start.36 = (s32[2,2048]{1,0:T(2,128)S(1)}, s32[2,2048]{1,0:T(2,128)}, u32[]{:S(2)}) copy-start(s32[2,2048]{1,0:T(2,128)} %copy-done.35) | copy-start | bytes 49156
  1369.9 65.1 %copy-start.38 = (s32[2,2048]{1,0:T(2,128)S(1)}, s32[2,2048]{1,0:T(2,128)}, u32[]{:S(2)}) copy-start(s32[2,2048]{1,0:T(2,128)} %copy-done.37) | copy-start | bytes 49156
  1369.9 65.1 %copy-start.41 = (f32[2,2,2048,1]{2,1,3,0:T(2,128)S(1)}, f32[2,2,2048,1]{2,1,3,0:T(2,128)}, u32[]{:S(2)}) copy-start(f32[2,2,2048,1]{2,1,3,0:T(2,128)} %copy-done.40) | copy-start | bytes 98308
  1369.9 514.5 %reduce-scatter.14.cloned.1.call-start = ((), (), s32[]{:S(2)}) async-start(), calls=%async_computation.20 | async-start | bytes 3932160 | tf_op jit(solution)/shard_map/reduce_scatter | solution.py:284
  1467.7 14.2 copy-start.13
  1467.7 22.8 %copy-start.11 = (bf16[1,512,2,128]{3,2,1,0:T(2,128)(2,1)}, bf16[1,512,2,128]{3,2,1,0:T(2,128)(2,1)S(1)}, u32[]{:S(2)}) copy-start(bf16[1,512,2,128]{3,2,1,0:T(2,128)(2,1)S(1)} %get-tuple-element.800) | copy-start | bytes 786436 | tf_op jit(solution)/shard_map/while
  1568.3 11.2 copy-start.8
  1590.9 11.6 copy-start.31
  1590.9 11.6 copy-start.32
  1632.6 13.9 copy-start.13
  1632.6 22.5 %copy-start.11 = (bf16[1,512,2,128]{3,2,1,0:T(2,128)(2,1)}, bf16[1,512,2,128]{3,2,1,0:T(2,128)(2,1)S(1)}, u32[]{:S(2)}) copy-start(bf16[1,512,2,128]{3,2,1,0:T(2,128)(2,1)S(1)} %get-tuple-element.800) | copy-start | bytes 786436 | tf_op jit(solution)/shard_map/while
  1731.7 11.2 copy-start.8
  1753.8 10.8 copy-start.31
  1753.8 10.8 copy-start.32
  1842.0 73.5 %reduce-scatter.16.cloned.1.call-start = ((), (), s32[]{:S(2)}) async-start(), calls=%async_computation.22 | async-start | bytes 1310720 | tf_op jit(solution)/shard_map/reduce_scatter | solution.py:287
  1853.4 232.7 %reduce-scatter.12.cloned.1.call-start = ((), (), s32[]{:S(2)}) async-start(), calls=%async_computation.19 | async-start | bytes 18874368 | tf_op jit(solution)/shard_map/reduce_scatter | solution.py:276
  1876.5 209.6 %copy-start.6 = (bf16[512,2048]{1,0:T(8,128)(2,1)S(1)}, bf16[512,2048]{1,0:T(8,128)(2,1)}, u32[]{:S(2)}) copy-start(bf16[512,2048]{1,0:T(8,128)(2,1)} %param.29) | copy-start | bytes 6291460
  1876.5 209.6 %copy-start.45 = (f32[512]{0:T(512)S(1)}, f32[512]{0:T(512)}, u32[]{:S(2)}) copy-start(f32[512]{0:T(512)} %copy-done.44) | copy-start | bytes 6148
  1882.5 206.2 %copy-start.57 = (f32[512]{0:T(512)S(1)}, f32[512]{0:T(512)}, u32[]{:S(2)}) copy-start(f32[512]{0:T(512)} %copy-done.56) | copy-start | bytes 6148
  1882.5 206.3 %copy-start.49 = (f32[512]{0:T(512)S(1)}, f32[512]{0:T(512)}, u32[]{:S(2)}) copy-start(f32[512]{0:T(512)} %copy-done.48) | copy-start | bytes 6148
  1917.3 174.7 %copy-start.53 = (f32[512]{0:T(512)S(1)}, f32[512]{0:T(512)}, u32[]{:S(2)}) copy-start(f32[512]{0:T(512)} %copy-done.52) | copy-start | bytes 6148
  (62 other events, 245.0 us)
Sparse Core Ops, SparseCore 0:
  9.8 29.1 all-gather.13
  41.5 43.8 all-gather.11
  87.5 151.1 all-gather.9
  240.1 80.2 all-gather.15
  322.7 86.1 all-gather.19
  497.4 149.9 all-gather.17
  649.2 50.7 all-gather.21
  701.6 151.1 all-gather.23
  927.2 166.4 reduce-scatter.9
  1095.9 166.5 reduce-scatter.7
  1271.9 194.1 all-gather.25
  1468.9 50.8 reduce-scatter.19
  1523.1 86.4 reduce-scatter.17
  1842.2 42.2 reduce-scatter.13
  1887.7 27.7 reduce-scatter.15
  1917.8 168.2 reduce-scatter.11
where the time goes:
time: 2110 us; the launch traced here: 2100 us
  waiting for transfers between devices  1060 us (50%)
  matrix products  600 us (28%)
  local copies, waits for them, and re-layouts  185 us (9%)
  other arithmetic  155 us (7%)
  blocking collectives  53.6 us (3%)
  loops' own time  28.3 us (1%)
    reduce_scatter x1, waiting for transfers between devices, local(): lax.psum_scatter(dot_last(grad_project_low, attn_matrix).astype(jnp.bfloa...  169 us
    reduce_scatter x1, waiting for transfers between devices, local(): lax.psum_scatter(jnp.dot(hidden_low, w_down, preferred_element_type=jnp.f...  165 us
    all_gather x1, waiting for transfers between devices, local(): lax.all_gather(normed.astype(jnp.bfloat16), 'tp', axis=0, tiled=True)  153 us
    all_gather x1, waiting for transfers between devices, local(): out_grad_all = lax.all_gather(cotangent, 'tp', axis=0, tiled=True)  153 us
    all_gather x1, waiting for transfers between devices, local(): lax.all_gather(normed_two.astype(jnp.bfloat16), 'tp', axis=0, tiled=True)  136 us
    reduce_scatter x1, waiting for transfers between devices, local(): lax.psum_scatter(dot_last(grad_ffn_low, ffn_matrix).astype(jnp.bfloat16),...  126 us
    dot_general x4, matrix products, dot_last(): lax.dot_general(left, right, (((1,), (1,)), ((), ())), preferred_element_...  103 us
    dot_general x4, matrix products, dot_first(): lax.dot_general(left, right, (((0,), (0,)), ((), ())), preferred_element_...  96.9 us
  transfers between devices with their start and end apart: 17, of which 12 were waited for; matrix products, arithmetic and copies ran while one was open for 40% of the time, Pallas kernels for 0%

commit v1 on v0

v1 whole, which is shorter than its diff:
```python
import functools
import math

import jax
import jax.numpy as jnp
from jax import lax
from jax.experimental import pallas as pl
from jax.experimental.pallas import tpu as pltpu
from jax.sharding import PartitionSpec as P

HD = 128
WINDOW = 1024
SEQ_LEN = 2048
EPSILON = 1e-05
NEGATIVE = -1e30
ROPE_BASE = 10000.0
LOG2E = math.log2(math.e)
VMEM_LIMIT = 56 * 1024 * 1024
F32 = jnp.float32
BF16 = jnp.bfloat16


def dot_nn(left, right):
    return lax.dot_general(left, right, (((1,), (0,)), ((), ())), preferred_element_type=F32)


def dot_nt(left, right):
    return lax.dot_general(left, right, (((1,), (1,)), ((), ())), preferred_element_type=F32)


def dot_tn(left, right):
    return lax.dot_general(left, right, (((0,), (0,)), ((), ())), preferred_element_type=F32)


def layer_norm(values):
    average = jnp.mean(values, axis=-1, keepdims=True)
    centered = values - average
    variance = jnp.mean(centered * centered, axis=-1, keepdims=True)
    return centered * lax.rsqrt(variance + EPSILON)


def layer_norm_back(values, grad):
    average = jnp.mean(values, axis=-1, keepdims=True)
    centered = values - average
    variance = jnp.mean(centered * centered, axis=-1, keepdims=True)
    root = lax.rsqrt(variance + EPSILON)
    normed = centered * root
    inner = jnp.mean(normed * grad, axis=-1, keepdims=True)
    return root * (grad - jnp.mean(grad, axis=-1, keepdims=True) - normed * inner)


def rope_tables(positions):
    half = HD // 2
    frequency = ROPE_BASE ** (-(jnp.arange(half, dtype=F32) * 2.0 / HD))
    angles = positions.astype(F32)[:, None] * frequency[None, :]
    cosine, sine = jnp.cos(angles), jnp.sin(angles)
    return jnp.concatenate([cosine, cosine], axis=-1), jnp.concatenate([-sine, sine], axis=-1)


def project_kernel(x_ref, w_ref, cos_ref, sin_ref, out_ref):
    product = dot_nn(x_ref[...], w_ref[...])
    width = product.shape[1] // 3
    for column in range(0, 3 * width, HD):
        part = product[:, column : column + HD]
        if column < 2 * width:
            part = part * cos_ref[...] + pltpu.roll(part, HD // 2, 1) * sin_ref[...]
        out_ref[:, column : column + HD] = part.astype(BF16)


def project(x, w, cosine, sine):
    tokens, model = x.shape
    width = w.shape[1]
    block = min(512, tokens)
    return pl.pallas_call(
        project_kernel,
        grid=(tokens // block,),
        in_specs=[
            pl.BlockSpec((block, model), lambda i: (i, 0)),
            pl.BlockSpec((model, width), lambda i: (0, 0)),
            pl.BlockSpec((block, HD), lambda i: (i, 0)),
            pl.BlockSpec((block, HD), lambda i: (i, 0)),
        ],
        out_specs=pl.BlockSpec((block, width), lambda i: (i, 0)),
        out_shape=jax.ShapeDtypeStruct((tokens, width), BF16),
        compiler_params=pltpu.CompilerParams(vmem_limit_bytes=VMEM_LIMIT),
        cost_estimate=pl.CostEstimate(
            flops=2 * tokens * model * width, bytes_accessed=2 * (tokens * model + model * width + tokens * width), transcendentals=0
        ),
        name="project",
    )(x, w, cosine, sine)


def forward_kernel(block, reach, g_ref, q_ref, k_ref, v_ref, seg_ref, key_ref, out_ref, lse_ref):
    i = pl.program_id(1)
    g = g_ref[0]
    scale = LOG2E / math.sqrt(HD)

    def run(count):
        q = q_ref[...]
        row = lax.broadcasted_iota(jnp.int32, (block, block), 0)
        column = lax.broadcasted_iota(jnp.int32, (block, block), 1)
        scores, rows = [], []
        for back in range(count):
            b = i - back
            rows.append(pl.ds(pl.multiple_of((b ^ g) * block, block), block))
            keep = seg_ref[0] == key_ref[b]
            if back == 0:
                keep = (keep & (row > column)) | (row == column)
            if back == reach:
                keep = keep & (row < column)
            scores.append(jnp.where(keep, dot_nt(q, k_ref[rows[-1], :]) * scale, NEGATIVE))
        top = functools.reduce(jnp.maximum, [jnp.max(s, axis=1, keepdims=True) for s in scores])
        weights = [jnp.exp2(s - top) for s in scores]
        total = sum(jnp.sum(w, axis=1, keepdims=True) for w in weights)
        out = sum(dot_nn(w.astype(BF16), v_ref[r, :]) for w, r in zip(weights, rows))
        out_ref[...] = (out / total).astype(BF16)
        lse = top + jnp.log2(total)
        lse_ref[0, 0] = jnp.transpose(jnp.broadcast_to(lse, (block, HD)))[0:1, :]

    for i_here in range(reach):
        pl.when(i == i_here)(functools.partial(run, i_here + 1))
    pl.when(i >= reach)(functools.partial(run, reach + 1))


def attend_forward(qkv, place, segment, key_code, block):
    tokens, width = qkv.shape
    heads = width // 3 // HD
    count = tokens // block
    reach = WINDOW // block
    pairs = sum(min(i, reach) + 1 for i in range(count)) * block * block * heads
    return pl.pallas_call(
        functools.partial(forward_kernel, block, reach),
        grid_spec=pltpu.PrefetchScalarGridSpec(
            num_scalar_prefetch=1,
            grid=(heads, count),
            in_specs=[
                pl.BlockSpec((block, HD), lambda h, i, g: (i ^ g[0], h)),
                pl.BlockSpec((tokens, HD), lambda h, i, g: (0, heads + h)),
                pl.BlockSpec((tokens, HD), lambda h, i, g: (0, 2 * heads + h)),
                pl.BlockSpec((1, block, 1), lambda h, i, g: (i, 0, 0)),
                pl.BlockSpec((count, 1, block), lambda h, i, g: (0, 0, 0)),
            ],
            out_specs=[
                pl.BlockSpec((block, HD), lambda h, i, g: (i ^ g[0], h)),
                pl.BlockSpec((1, 1, 1, block), lambda h, i, g: (h, i, 0, 0)),
            ],
        ),
        out_shape=[
            jax.ShapeDtypeStruct((tokens, heads * HD), BF16),
            jax.ShapeDtypeStruct((heads, count, 1, block), F32),
        ],
        compiler_params=pltpu.CompilerParams(vmem_limit_bytes=VMEM_LIMIT),
        cost_estimate=pl.CostEstimate(flops=8 * pairs * HD, bytes_accessed=8 * tokens * heads * HD, transcendentals=pairs),
        name="attend_forward",
    )(place, qkv, qkv, qkv, segment.reshape(count, block, 1), key_code.reshape(count, 1, block))


def backward_kernel(
    block, reach, heads, g_ref, q_ref, k_ref, v_ref, grad_ref, out_ref, lse_ref, seg_ref, key_ref, cos_ref, sin_ref, result_ref, dq_ref, dk_ref, dv_ref, inner_ref
):
    h = pl.program_id(0)
    g = g_ref[0]
    count = q_ref.shape[0] // block
    scale = 1.0 / math.sqrt(HD)

    def rows_of(b):
        return pl.ds(pl.multiple_of((b ^ g) * block, block), block)

    dq_ref[...] = jnp.zeros_like(dq_ref)
    dk_ref[...] = jnp.zeros_like(dk_ref)
    dv_ref[...] = jnp.zeros_like(dv_ref)

    def inner_block(i, carry):
        rows = rows_of(i)
        product = grad_ref[rows, :].astype(F32) * out_ref[rows, :].astype(F32)
        inner_ref[i] = jnp.sum(jnp.transpose(product), axis=0, keepdims=True)
        return carry

    lax.fori_loop(0, count, inner_block, 0)
    for back in range(reach + 1):

        def pair(i, carry, back=back):
            b = i - back
            query_rows, key_rows = rows_of(i), rows_of(b)
            q, k = q_ref[query_rows, :], k_ref[key_rows, :]
            v, grad = v_ref[key_rows, :], grad_ref[query_rows, :]
            keep = key_ref[b] == seg_ref[i]
            if back == 0 or back == reach:
                key = lax.broadcasted_iota(jnp.int32, (block, block), 0)
                query = lax.broadcasted_iota(jnp.int32, (block, block), 1)
                if back == 0:
                    keep = (keep & (query > key)) | (query == key)
                else:
                    keep = keep & (query < key)
            scores = dot_nt(k, q) * (scale * LOG2E)
            weights = jnp.where(keep, jnp.exp2(scores - lse_ref[0, i]), 0.0)
            grad_weights = dot_nt(v, grad)
            grad_scores = (weights * (grad_weights - inner_ref[i]) * scale).astype(BF16)
            dv_ref[key_rows, :] += dot_nn(weights.astype(BF16), grad)
            dk_ref[key_rows, :] += dot_nn(grad_scores, q)
            dq_ref[query_rows, :] += dot_tn(grad_scores, k)
            return carry

        lax.fori_loop(back, count, pair, 0)

    column = pl.multiple_of(h * HD, HD)

    def store(i, carry):
        rows = pl.ds(pl.multiple_of(i * block, block), block)
        cosine, sine = cos_ref[rows, :], sin_ref[rows, :]
        for part, ref in enumerate((dq_ref, dk_ref)):
            value = ref[rows, :]
            turned = value * cosine - pltpu.roll(value, HD // 2, 1) * sine
            result_ref[rows, pl.ds(part * heads * HD + column, HD)] = turned.astype(BF16)
        result_ref[rows, pl.ds(2 * heads * HD + column, HD)] = dv_ref[rows, :].astype(BF16)
        return carry

    lax.fori_loop(0, count, store, 0)


def attend_backward(qkv, grad, out, lse, place, segment, key_code, cosine, sine, block):
    tokens, width = qkv.shape
    heads = width // 3 // HD
    count = tokens // block
    reach = WINDOW // block
    pairs = sum(min(i, reach) + 1 for i in range(count)) * block * block * heads
    return pl.pallas_call(
        functools.partial(backward_kernel, block, reach, heads),
        grid_spec=pltpu.PrefetchScalarGridSpec(
            num_scalar_prefetch=1,
            grid=(heads,),
            in_specs=[
                pl.BlockSpec((tokens, HD), lambda h, g: (0, h)),
                pl.BlockSpec((tokens, HD), lambda h, g: (0, heads + h)),
                pl.BlockSpec((tokens, HD), lambda h, g: (0, 2 * heads + h)),
                pl.BlockSpec((tokens, HD), lambda h, g: (0, h)),
                pl.BlockSpec((tokens, HD), lambda h, g: (0, h)),
                pl.BlockSpec((1, count, 1, block), lambda h, g: (h, 0, 0, 0)),
                pl.BlockSpec((count, 1, block), lambda h, g: (0, 0, 0)),
                pl.BlockSpec((count, block, 1), lambda h, g: (0, 0, 0)),
                pl.BlockSpec((tokens, HD), lambda h, g: (0, 0)),
                pl.BlockSpec((tokens, HD), lambda h, g: (0, 0)),
            ],
            out_specs=pl.BlockSpec((tokens, width), lambda h, g: (0, 0)),
            scratch_shapes=[
                pltpu.VMEM((tokens, HD), F32),
                pltpu.VMEM((tokens, HD), F32),
                pltpu.VMEM((tokens, HD), F32),
                pltpu.VMEM((count, 1, block), F32),
            ],
        ),
        out_shape=jax.ShapeDtypeStruct((tokens, width), BF16),
        compiler_params=pltpu.CompilerParams(vmem_limit_bytes=VMEM_LIMIT),
        cost_estimate=pl.CostEstimate(flops=20 * pairs * HD, bytes_accessed=16 * tokens * heads * HD, transcendentals=pairs),
        name="attend_backward",
    )(
        place, qkv, qkv, qkv, grad, out, lse,
        segment.reshape(count, 1, block), key_code.reshape(count, block, 1), cosine, sine,
    )


def local(inputs, att_proj, attn_out, ff_proj, ff_out, segments, pad_mask, positions, cotangent):
    tp_size = lax.axis_size("tp")
    rows, model = inputs.shape
    members = SEQ_LEN // rows
    sets = tp_size // members
    index = lax.axis_index("tp")
    mine = index // members
    place = index % members
    head_width = att_proj.shape[2]
    ffn_width = ff_proj.shape[2]
    block = min(512, rows)

    def swap(values, bit):
        return lax.ppermute(values, "tp", [(i, i ^ bit) for i in range(tp_size)])

    def turn(values, step):
        return lax.ppermute(values, "tp", [(i, (i + step * members) % tp_size) for i in range(tp_size)])

    def group_gather(values):
        blocks = {0: values}
        bit = members // 2
        while bit:
            for mask in sorted(blocks, reverse=True):
                blocks[mask | bit] = swap(blocks[mask], bit)
            bit //= 2
        return [blocks[mask] for mask in range(members)]

    def group_scatter(blocks):
        blocks = dict(enumerate(blocks))
        bit = 1
        while bit < members:
            for mask in sorted((m for m in blocks if m & bit), reverse=True):
                total = blocks[mask ^ bit].astype(F32) + swap(blocks.pop(mask), bit).astype(F32)
                blocks[mask ^ bit] = total if mask == bit else total.astype(BF16)
            bit *= 2
        return blocks[0].astype(F32)

    def spread(shard, gather):
        parts = [shard] + [turn(shard, step) for step in range(1, sets)]
        return [gather(part) for part in parts]

    def gather_first(part):
        return lax.all_gather(part, "fsdp", axis=0, tiled=True)

    def gather_new(part):
        return lax.all_gather(part, "fsdp", axis=0)

    def settle(parts, scatter):
        total = None
        for step in range(sets):
            piece = scatter(parts[step])
            if step:
                piece = turn(piece, sets - step)
            piece = piece.astype(F32)
            total = piece if total is None else total + piece
        return total

    def scatter_first(part):
        return lax.psum_scatter(part.astype(BF16), "fsdp", scatter_dimension=0, tiled=True)

    def scatter_last(part):
        return lax.psum_scatter(part.astype(BF16), "fsdp", scatter_dimension=1, tiled=True)

    w_qkv = spread(att_proj.reshape(att_proj.shape[0], 3 * head_width), gather_first)
    w_heads = spread(attn_out, gather_new)
    w_ffn = spread(ff_proj.reshape(ff_proj.shape[0], 2 * ffn_width), gather_first)
    w_down = spread(ff_out, gather_new)

    def flat(chunks):
        return jnp.concatenate([chunks[f] for f in range(chunks.shape[0])], axis=1)

    w_heads = jnp.concatenate([flat(part) for part in w_heads], axis=0)
    w_down = jnp.concatenate([flat(part) for part in w_down], axis=0)

    segment = lax.dynamic_slice_in_dim(segments, mine * SEQ_LEN, SEQ_LEN)
    padding = lax.dynamic_slice_in_dim(pad_mask, mine * SEQ_LEN, SEQ_LEN)
    key_code = jnp.where(padding == 1, segment, -1)
    spots = lax.dynamic_slice_in_dim(positions, mine * SEQ_LEN, SEQ_LEN).reshape(members, rows)
    spots = jnp.concatenate([lax.dynamic_index_in_dim(spots, place ^ mask, 0, False) for mask in range(members)])
    cosine, sine = rope_tables(spots)
    where = place.astype(jnp.int32).reshape(1)

    x_float = inputs.astype(F32)
    normed_all = jnp.concatenate(group_gather(layer_norm(x_float).astype(BF16)), axis=0)
    cotangent_all = jnp.concatenate(group_gather(cotangent), axis=0)

    qkv = [project(normed_all, w, cosine, sine) for w in w_qkv]
    attended = [attend_forward(part, where, segment, key_code, block) for part in qkv]
    heads_low = jnp.concatenate([out for out, _ in attended], axis=1)

    def row_blocks(left, right, dot):
        return [dot(left[m * rows : (m + 1) * rows], right).astype(BF16) for m in range(members)]

    resid = x_float + group_scatter(row_blocks(heads_low, w_heads, dot_nn))
    normed_two_all = jnp.concatenate(group_gather(layer_norm(resid).astype(BF16)), axis=0)

    projected = [dot_nn(normed_two_all, w) for w in w_ffn]
    up = jnp.concatenate([p[:, :ffn_width] for p in projected], axis=1)
    gate = jnp.concatenate([p[:, ffn_width:] for p in projected], axis=1)
    sigmoid = jax.nn.sigmoid(gate)
    slope_up = gate * sigmoid
    slope_gate = up * sigmoid * (1.0 + gate * (1.0 - sigmoid))
    hidden_low = (slope_up * up).astype(BF16)
    ffn_branch = group_scatter(row_blocks(hidden_low, w_down, dot_nn))
    output = (resid + ffn_branch).astype(BF16)

    grad_hidden = dot_nt(cotangent_all, w_down)
    grad_down = dot_tn(hidden_low, cotangent_all)
    grad_up = (grad_hidden * slope_up).astype(BF16)
    grad_gate = (grad_hidden * slope_gate).astype(BF16)
    grad_ffn_low = [
        jnp.concatenate([part[:, j * ffn_width : (j + 1) * ffn_width] for part in (grad_up, grad_gate)], axis=1)
        for j in range(sets)
    ]
    grad_ffn_all = jnp.concatenate(grad_ffn_low, axis=1)
    grad_normed_two = group_scatter(row_blocks(grad_ffn_all, jnp.concatenate(w_ffn, axis=1), dot_nt))
    grad_ffn = [dot_tn(normed_two_all, part) for part in grad_ffn_low]

    grad_resid = cotangent.astype(F32) + layer_norm_back(resid, grad_normed_two)
    resid_grad_all = jnp.concatenate(group_gather(grad_resid.astype(BF16)), axis=0)
    grad_heads_weight = dot_tn(heads_low, resid_grad_all)
    head_grad = dot_nt(resid_grad_all, w_heads).astype(BF16)
    grad_project = [
        attend_backward(
            qkv[j], head_grad[:, j * head_width : (j + 1) * head_width], attended[j][0], attended[j][1],
            where, segment, key_code, cosine, sine, block,
        )
        for j in range(sets)
    ]
    grad_project_all = jnp.concatenate(grad_project, axis=1)
    grad_normed = group_scatter(row_blocks(grad_project_all, jnp.concatenate(w_qkv, axis=1), dot_nt))
    grad_attn = [dot_tn(normed_all, part) for part in grad_project]
    grad_input = (grad_resid + layer_norm_back(x_float, grad_normed)).astype(BF16)

    def halves(values, width):
        return [values[j * width : (j + 1) * width] for j in range(sets)]

    return (
        output,
        grad_input,
        settle(grad_attn, scatter_first).reshape(att_proj.shape),
        settle(halves(grad_heads_weight, head_width), scatter_last),
        settle(grad_ffn, scatter_first).reshape(ff_proj.shape),
        settle(halves(grad_down, ffn_width), scatter_last),
    )


def solution(mesh):
    rows_spec = P(("fsdp", "tp"), None)
    weights = (P("fsdp", None, "tp"), P("tp", "fsdp"), P("fsdp", None, "tp"), P("tp", "fsdp"))
    return jax.shard_map(
        local,
        mesh=mesh,
        in_specs=(rows_spec,) + weights + (P("fsdp"),) * 3 + (rows_spec,),
        out_specs=(rows_spec, rows_spec) + weights,
        check_vma=False,
    )
```

time: 2110 us -> 1330 us (0.63)
  waiting for transfers between devices: 1060 us -> 603 us
  matrix products: 600 us -> 333 us
  Pallas kernels: 0 us -> 108 us
  local copies, waits for them, and re-layouts: 185 us -> 106 us
  blocking collectives: 53.6 us -> 0 us
  loops' own time: 28.3 us -> 0 us
  other arithmetic: 155 us -> 133 us
    ppermute x0 -> x32, waiting for transfers between devices: none -> 551 us  [the longest x8 322 us: turn(): lax.ppermute(values, 'tp', [(i, (i + step * members) % tp_size) for i in...]
    all_gather x9 -> x8, waiting for transfers between devices: 506 us -> 0.03 us  [the longest x4 0.03 us: gather_new(): return lax.all_gather(part, 'fsdp', axis=0)]
    reduce_scatter x7 -> x8, waiting for transfers between devices: 491 us -> 49.8 us  [the longest x4 49.8 us: scatter_first(): lax.psum_scatter(part.astype(BF16), 'fsdp', scatter_dimension=0, tiled=True)]
    dot_general x68 -> x26, matrix products: 600 us -> 333 us  [the longest x10 129 us: dot_nt(): lax.dot_general(left, right, (((1,), (1,)), ((), ())), preferred_element_...]
    pallas_call x0 -> x6, Pallas kernels: none -> 108 us  [the longest x2 52.3 us: attend_backward(): pl.pallas_call(functools.partial(backward_kernel, block, reach, heads), g...]
    concatenate x2 -> x5, other arithmetic: 6.3 us -> 88.2 us  [the longest x1 58 us: local(): w_down = jnp.concatenate([flat(part) for part in w_down], axis=0)]
    all_to_all x1 -> x0, waiting for transfers between devices: 60.9 us -> none  [local(): lax.all_to_all(rows_head_grad, 'tp', split_axis=1, concat_axis=0, tiled=T...]
    all_to_all x1 -> x0, blocking collectives: 53.6 us -> none  [local(): lax.all_to_all(heads_low, 'tp', split_axis=0, concat_axis=1, tiled=True)]
  transfers between devices with their start and end apart: 17 -> 48, of which waited for: 12 -> 17; matrix products, arithmetic and copies ran while one was open for 40% -> 28% of each run, Pallas kernels for 0% -> 8%
where the time goes in v1:
time: 1330 us; the launch traced here: 1320 us
  waiting for transfers between devices  603 us (45%)
  matrix products  333 us (25%)
  other arithmetic  133 us (10%)
  Pallas kernels  108 us (8%)
  local copies, waits for them, and re-layouts  106 us (8%)
  starting transfers between devices  21.5 us (2%)
  between operations  14.8 us (1%)
    ppermute x8, waiting for transfers between devices, turn(): lax.ppermute(values, 'tp', [(i, (i + step * members) % tp_size) for i in...  322 us
    ppermute x24, waiting for transfers between devices, swap(): return lax.ppermute(values, 'tp', [(i, i ^ bit) for i in range(tp_size)])  229 us
    dot_general x10, matrix products, dot_nt(): lax.dot_general(left, right, (((1,), (1,)), ((), ())), preferred_element_...  129 us
    dot_general x6, matrix products, dot_tn(): lax.dot_general(left, right, (((0,), (0,)), ((), ())), preferred_element_...  105 us
    dot_general x10, matrix products, dot_nn(): lax.dot_general(left, right, (((1,), (0,)), ((), ())), preferred_element_...  100 us
    concatenate x1, other arithmetic, local(): w_down = jnp.concatenate([flat(part) for part in w_down], axis=0)  58 us
    pallas_call x2, Pallas kernels, attend_backward(): pl.pallas_call(functools.partial(backward_kernel, block, reach, heads), g...  52.3 us
    reduce_scatter x4, waiting for transfers between devices, scatter_first(): lax.psum_scatter(part.astype(BF16), 'fsdp', scatter_dimension=0, tiled=True)  49.8 us
  transfers between devices with their start and end apart: 48, of which 17 were waited for; matrix products, arithmetic and copies ran while one was open for 28% of the time, Pallas kernels for 8%

profile of v1, /device:TPU:0, one launch (start us, length us, event | category | flops | bytes accessed | tf_op | source)
XLA Modules:
  0.0 1320.7 jit_solution(3996801887956755987)
XLA Ops:
  12.1 12.1 collective-permute-done.4
  27.7 36.7 %collective-permute-done.3 = bf16[512,768]{1,0:T(8,128)(2,1)S(1)} collective-permute-done((bf16[512,768]{1,0:T(8,128)(2,1)}, bf16[512,768]{1,0:T(8,128)(2,1)S(1)}, u32[]{:S(2)}, u32[]{:S(2)}) %collective-permute-start.3) | collective-permute-done | bytes 786464 | tf_op jit(solution)/shard_map/ppermute | solution.py:278
  66.0 46.9 %collective-permute-done.12 = bf16[1024,512]{1,0:T(8,128)(2,1)} collective-permute-done((bf16[1024,512]{1,0:T(8,128)(2,1)S(1)}, bf16[1024,512]{1,0:T(8,128)(2,1)}, u32[]{:S(2)}, u32[]{:S(2)}) %collective-permute-start.12) | collective-permute-done | bytes 1048608 | tf_op jit(solution)/shard_map/ppermute | solution.py:278
  119.6 47.6 %collective-permute-done.1 = bf16[512,2048]{1,0:T(8,128)(2,1)} collective-permute-done((bf16[512,2048]{1,0:T(8,128)(2,1)}, bf16[512,2048]{1,0:T(8,128)(2,1)}, u32[]{:S(2)}, u32[]{:S(2)}) %collective-permute-start.1) | collective-permute-done | bytes 2097184 | tf_op jit(solution)/shard_map/ppermute | solution.py:275
  177.9 13.7 %maximum_maximum_fusion.1 = bf16[512,2048]{1,0:T(8,128)(2,1)} fusion(bf16[256,512]{1,0:T(8,128)(2,1)S(1)} %get-tuple-element.69, bf16[256,512]{1,0:T(8,128)(2,1)S(1)} %get-tuple-element.67, bf16[256,512]{1,0:T(8,128)(2,1)S(1)} %get-tuple-element.68, bf16[256,512]{1,0:T(8,128)(2,1)S(1)} %get-tuple-element.66, bf16[256,512]{1,0:T(8,128)(2,1)S(1)} %get-tuple-element.65, ...), kind=kLoop, calls=%fused_computation.88 | loop fusion | flops 16777216 | bytes 4194304 | tf_op jit(solution)/shard_map/concatenate | solution.py:333
  191.6 7.1 pad_maximum_fusion.3.x_ref
  198.8 11.3 project.2.q_ref.k_ref.v_ref
  210.0 16.2 %attend_forward.2 = (bf16[2048,256]{1,0:T(8,128)(2,1)}, f32[2,4,1,512]{3,2,1,0:T(1,128)}) custom-call(s32[1]{0:T(128)} %bitcast.g_ref, bf16[2048,768]{1,0:T(8,128)(2,1)} %project.2.q_ref.k_ref.v_ref, bf16[2048,768]{1,0:T(8,128)(2,1)} %project.2.q_ref.k_ref.v_ref, bf16[2048,768]{1,0:T(8,128)(2,1)} %project.2.q_ref.k_ref.v_ref, ...), custom_call_target="tpu_custom_call" | custom-call | flops 4831838208 | bytes 4194304 | tf_op jit(solution)/shard_map/attend_forward/pallas_call | solution.py:131
  228.5 11.3 project.3.q_ref.k_ref.v_ref
  239.8 16.6 %attend_forward.3 = (bf16[2048,256]{1,0:T(8,128)(2,1)}, f32[2,4,1,512]{3,2,1,0:T(1,128)}) custom-call(s32[1]{0:T(128)} %bitcast.g_ref, bf16[2048,768]{1,0:T(8,128)(2,1)} %project.3.q_ref.k_ref.v_ref, bf16[2048,768]{1,0:T(8,128)(2,1)} %project.3.q_ref.k_ref.v_ref, bf16[2048,768]{1,0:T(8,128)(2,1)} %project.3.q_ref.k_ref.v_ref, ...), custom_call_target="tpu_custom_call" | custom-call | flops 4831838208 | bytes 4194304 | tf_op jit(solution)/shard_map/attend_forward/pallas_call | solution.py:131
  268.2 86.0 %collective-permute-done.11 = bf16[512,2048]{1,0:T(8,128)(2,1)} collective-permute-done((bf16[512,2048]{1,0:T(8,128)(2,1)S(1)}, bf16[512,2048]{1,0:T(8,128)(2,1)}, u32[]{:S(2)}, u32[]{:S(2)}) %collective-permute-start.11) | collective-permute-done | bytes 2097184 | tf_op jit(solution)/shard_map/ppermute | solution.py:278
  357.9 41.0 %collective-permute-done.7 = bf16[512,2048]{1,0:T(8,128)(2,1)} collective-permute-done((bf16[512,2048]{1,0:T(8,128)(2,1)}, bf16[512,2048]{1,0:T(8,128)(2,1)}, u32[]{:S(2)}, u32[]{:S(2)}) %collective-permute-start.7) | collective-permute-done | bytes 2097184 | tf_op jit(solution)/shard_map/ppermute | solution.py:275
  421.6 31.3 %collective-permute-done.9 = bf16[512,2048]{1,0:T(8,128)(2,1)} collective-permute-done((bf16[512,2048]{1,0:T(8,128)(2,1)}, bf16[512,2048]{1,0:T(8,128)(2,1)}, u32[]{:S(2)}, u32[]{:S(2)}) %collective-permute-start.9) | collective-permute-done | bytes 2097184 | tf_op jit(solution)/shard_map/ppermute | solution.py:275
  452.8 58.0 %maximum_maximum_fusion = bf16[2048,2048]{1,0:T(8,128)(2,1)} fusion(bf16[1024,512]{1,0:T(8,128)(2,1)S(1)} %get-tuple-element.57, bf16[1024,512]{1,0:T(8,128)(2,1)S(1)} %get-tuple-element.55, bf16[1024,512]{1,0:T(8,128)(2,1)S(1)} %get-tuple-element.56, bf16[1024,512]{1,0:T(8,128)(2,1)S(1)} %get-tuple-element.54, bf16[1024,512]{1,0:T(8,128)(2,1)S(1)} %copy-done.10, ...), kind=kLoop, calls=%fused_computation.10 | loop fusion | flops 67108864 | bytes 16777216 | tf_op jit(solution)/shard_map/concatenate | solution.py:334
  510.8 8.3 constant_dynamic-update-slice_fusion.7
  519.0 27.4 %fusion.75 = f32[2048,2048]{0,1:T(8,128)} fusion(bf16[2048,2048]{1,0:T(8,128)(2,1)} %all-gather.17.cloned.1.call-done, bf16[512,2048]{1,0:T(8,128)(2,1)} %collective-permute-done.10, bf16[512,2048]{1,0:T(8,128)(2,1)} %collective-permute-done.9, bf16[512,2048]{1,0:T(8,128)(2,1)} %collective-permute-done.8, bf16[512,2048]{1,0:T(8,128)(2,1)} %fusion.34), kind=kOutput, calls=%fused_computation.143 | convolution fusion | flops 17213423616 | bytes 33554432 | tf_op jit(solution)/shard_map/dot_general | solution.py:24
  546.4 10.8 fusion.78
  557.2 27.1 %fusion.74 = f32[2048,2048]{0,1:T(8,128)} fusion(bf16[2048,2048]{1,0:T(8,128)(2,1)} %all-gather.19.cloned.1.call-done, bf16[512,2048]{1,0:T(8,128)(2,1)} %collective-permute-done.10, bf16[512,2048]{1,0:T(8,128)(2,1)} %collective-permute-done.9, bf16[512,2048]{1,0:T(8,128)(2,1)} %collective-permute-done.8, bf16[512,2048]{1,0:T(8,128)(2,1)} %fusion.34), kind=kOutput, calls=%fused_computation.142 | convolution fusion | flops 17213423616 | bytes 33554432 | tf_op jit(solution)/shard_map/dot_general | solution.py:24
  584.4 11.2 fusion.79
  595.6 35.7 %multiply_convert_fusion.1 = (bf16[2048,2048]{0,1:T(8,128)(2,1)}, bf16[2048,2048]{0,1:T(8,128)(2,1)}, bf16[2048,2048]{0,1:T(8,128)(2,1)}) fusion(f32[2048,1024]{0,1:T(8,128)} %get-tuple-element.41, f32[2048,1024]{0,1:T(8,128)} %get-tuple-element.39, f32[2048,1024]{0,1:T(8,128)} %get-tuple-element.42, f32[2048,1024]{0,1:T(8,128)} %get-tuple-element.40, ...), kind=kOutput, calls=%fused_computation.4 | convolution fusion | flops 17251172352 | bytes 75497472 | tf_op jit(solution)/shard_map/dot_general | solution.py:28
  631.4 23.8 %convolution_convert_fusion = bf16[2048,2048]{1,0:T(8,128)(2,1)} fusion(bf16[2048,2048]{0,1:T(8,128)(2,1)} %get-tuple-element.38, bf16[2048,2048]{1,0:T(8,128)(2,1)} %constant_dynamic-update-slice_fusion.2), kind=kOutput, calls=%fused_computation.28 | convolution fusion | flops 17184063488 | bytes 25165824 | tf_op jit(solution)/shard_map/dot_general | solution.py:32
  655.2 10.0 convolution_convert_fusion.9
  675.9 7.5 pad_maximum_fusion.2
  683.4 8.3 constant_dynamic-update-slice_fusion.6
  691.7 14.8 %fusion.38 = bf16[512,2048]{1,0:T(8,128)(2,1)} fusion(bf16[2048,4096]{1,0:T(8,128)(2,1)} %constant_dynamic-update-slice_fusion.6, bf16[2048,4096]{0,1:T(8,128)(2,1)} %pad_maximum_fusion.2), kind=kOutput, calls=%fused_computation.67 | convolution fusion | flops 8590983168 | bytes 23068672 | tf_op jit(solution)/shard_map/dot_general | solution.py:28
  706.4 15.0 %fusion.41 = bf16[512,2048]{1,0:T(8,128)(2,1)} fusion(bf16[2048,4096]{1,0:T(8,128)(2,1)} %constant_dynamic-update-slice_fusion.6, bf16[2048,4096]{0,1:T(8,128)(2,1)} %pad_maximum_fusion.2), kind=kOutput, calls=%fused_computation.68 | convolution fusion | flops 8590983168 | bytes 23068672 | tf_op jit(solution)/shard_map/dot_general | solution.py:28
  721.5 14.8 %fusion.44 = bf16[512,2048]{1,0:T(8,128)(2,1)} fusion(bf16[2048,4096]{1,0:T(8,128)(2,1)} %constant_dynamic-update-slice_fusion.6, bf16[2048,4096]{0,1:T(8,128)(2,1)} %pad_maximum_fusion.2), kind=kOutput, calls=%fused_computation.69 | convolution fusion | flops 8590983168 | bytes 23068672 | tf_op jit(solution)/shard_map/dot_general | solution.py:28
  736.8 7.6 convolution_convert_fusion.11
  744.4 8.1 convolution_convert_fusion.12
  760.0 10.5 add_convert_fusion.3
  771.7 32.3 %collective-permute-done.21 = bf16[512,2048]{1,0:T(8,128)(2,1)} collective-permute-done((bf16[512,2048]{1,0:T(8,128)(2,1)}, bf16[512,2048]{1,0:T(8,128)(2,1)}, u32[]{:S(2)}, u32[]{:S(2)}) %collective-permute-start.21) | collective-permute-done | bytes 2097184 | tf_op jit(solution)/shard_map/ppermute | solution.py:275
  804.0 17.2 %fusion.58 = (f32[512]{0:T(512)S(1)}, f32[512]{0:T(512)S(1)}, bf16[512,2048]{1,0:T(8,128)(2,1)}) fusion(bf16[512,2048]{1,0:T(8,128)(2,1)} %collective-permute-done.21, bf16[512,2048]{1,0:T(8,128)(2,1)S(1)} %collective-permute-done.19, f32[512]{0:T(512)S(1)} %copy-done.32, f32[512,2048]{1,0:T(8,128)} %copy-done, f32[512]{0:T(512)S(1)} %copy-done.24, ...), kind=kOutput, calls=%fused_computation.98 | convolution fusion | flops 8601468928 | bytes 31465472 | tf_op jit(solution)/shard_map/dot_general | solution.py:28
  821.2 26.8 %collective-permute-done.15 = bf16[512,2048]{1,0:T(8,128)(2,1)} collective-permute-done((bf16[512,2048]{1,0:T(8,128)(2,1)}, bf16[512,2048]{1,0:T(8,128)(2,1)}, u32[]{:S(2)}, u32[]{:S(2)}) %collective-permute-start.15) | collective-permute-done | bytes 2097184 | tf_op jit(solution)/shard_map/ppermute | solution.py:275
  848.1 10.3 fusion.76
  859.2 46.0 %collective-permute-done.23 = bf16[512,2048]{1,0:T(8,128)(2,1)S(1)} collective-permute-done((bf16[512,2048]{1,0:T(8,128)(2,1)S(1)}, bf16[512,2048]{1,0:T(8,128)(2,1)S(1)}, u32[]{:S(2)}, u32[]{:S(2)}) %collective-permute-start.23) | collective-permute-done | bytes 2097184 | tf_op jit(solution)/shard_map/ppermute | solution.py:275
  917.5 26.4 %fusion.9 = bf16[2048,2048]{1,0:T(8,128)(2,1)} fusion(bf16[2048,1024]{0,1:T(8,128)(2,1)} %copy-done.6, bf16[2048,1024]{0,1:T(8,128)(2,1)} %copy-done.5, bf16[512,2048]{1,0:T(8,128)(2,1)} %collective-permute-done.10, bf16[512,2048]{1,0:T(8,128)(2,1)} %collective-permute-done.9, bf16[512,2048]{1,0:T(8,128)(2,1)} %collective-permute-done.8, ...), kind=kOutput, calls=%fused_computation.26 | convolution fusion | flops 17234395136 | bytes 25165824 | tf_op jit(solution)/shard_map/dot_general | solution.py:32
  946.5 9.2 convolution_convert_fusion.8
  957.1 26.1 %attend_backward.3 = bf16[2048,768]{1,0:T(8,128)(2,1)} custom-call(s32[1]{0:T(128)} %bitcast.g_ref, bf16[2048,768]{1,0:T(8,128)(2,1)} %project.3.q_ref.k_ref.v_ref, bf16[2048,768]{1,0:T(8,128)(2,1)} %project.3.q_ref.k_ref.v_ref, bf16[2048,768]{1,0:T(8,128)(2,1)} %project.3.q_ref.k_ref.v_ref, bf16[2048,256]{1,0:T(8,128)(2,1)} %get-tuple-element.61.grad_ref, ...), custom_call_target="tpu_custom_call" | custom-call | flops 12079595520 | bytes 8388608 | tf_op jit(solution)/shard_map/attend_backward/pallas_call | solution.py:227
  983.2 11.6 convolution_convert_fusion.1
  994.9 26.2 %attend_backward.2 = bf16[2048,768]{1,0:T(8,128)(2,1)} custom-call(s32[1]{0:T(128)} %bitcast.g_ref, bf16[2048,768]{1,0:T(8,128)(2,1)} %project.2.q_ref.k_ref.v_ref, bf16[2048,768]{1,0:T(8,128)(2,1)} %project.2.q_ref.k_ref.v_ref, bf16[2048,768]{1,0:T(8,128)(2,1)} %project.2.q_ref.k_ref.v_ref, bf16[2048,256]{1,0:T(8,128)(2,1)} %get-tuple-element.60.grad_ref, ...), custom_call_target="tpu_custom_call" | custom-call | flops 12079595520 | bytes 8388608 | tf_op jit(solution)/shard_map/attend_backward/pallas_call | solution.py:227
  1021.1 11.6 convolution_convert_fusion.2
  1032.8 26.1 %fusion.12 = bf16[2048,2048]{1,0:T(8,128)(2,1)} fusion(bf16[2048,1024]{0,1:T(8,128)(2,1)} %copy-done.4, bf16[2048,1024]{0,1:T(8,128)(2,1)} %copy-done.3, bf16[512,2048]{1,0:T(8,128)(2,1)} %collective-permute-done.10, bf16[512,2048]{1,0:T(8,128)(2,1)} %collective-permute-done.9, bf16[512,2048]{1,0:T(8,128)(2,1)} %collective-permute-done.8, ...), kind=kOutput, calls=%fused_computation.27 | convolution fusion | flops 17234395136 | bytes 25165824 | tf_op jit(solution)/shard_map/dot_general | solution.py:32
  1085.3 65.9 %collective-permute-done.31 = bf16[1024,512]{1,0:T(8,128)(2,1)S(1)} collective-permute-done((bf16[1024,512]{1,0:T(8,128)(2,1)}, bf16[1024,512]{1,0:T(8,128)(2,1)S(1)}, u32[]{:S(2)}, u32[]{:S(2)}) %collective-permute-start.31) | collective-permute-done | bytes 1048608 | tf_op jit(solution)/shard_map/ppermute | solution.py:278
  1161.0 9.8 fusion.59
  1176.9 35.7 %reduce-scatter.9.cloned.1.call-done = bf16[512,768]{1,0:T(8,128)(2,1)} async-done(((bf16[2048,768]{1,0:T(8,128)(2,1)}), bf16[512,768]{1,0:T(8,128)(2,1)}) %reduce-scatter.9.cloned.1.call-update) | async-done | bytes 786448 | tf_op jit(solution)/shard_map/reduce_scatter | solution.py:320
  1212.7 72.2 %collective-permute-done.28 = bf16[512,768]{1,0:T(8,128)(2,1)S(1)} collective-permute-done((bf16[512,768]{1,0:T(8,128)(2,1)}, bf16[512,768]{1,0:T(8,128)(2,1)S(1)}, u32[]{:S(2)}, u32[]{:S(2)}) %collective-permute-start.28) | collective-permute-done | bytes 786464 | tf_op jit(solution)/shard_map/ppermute | solution.py:278
  1288.4 14.0 %reduce-scatter.17.cloned.1.call-done = bf16[512,2048]{1,0:T(8,128)(2,1)} async-done(((bf16[2048,2048]{1,0:T(8,128)(2,1)}), bf16[512,2048]{1,0:T(8,128)(2,1)}) %reduce-scatter.17.cloned.1.call-update) | async-done | bytes 2097168 | tf_op jit(solution)/shard_map/reduce_scatter | solution.py:320
  1307.4 6.6 reshape.134
  (251 shorter events, 155.3 us)
Async XLA Ops:
  7.2 168.2 %all-gather.21.cloned.1.call-start = ((), (), s32[]{:S(2)}) async-start(), calls=%async_computation.20 | async-start | bytes 1310720 | tf_op jit(solution)/shard_map/all_gather | solution.py:307
  7.9 168.7 %all-gather.23.cloned.1.call-start = ((), (), s32[]{:S(2)}) async-start(), calls=%async_computation.21 | async-start | bytes 1310720 | tf_op jit(solution)/shard_map/all_gather | solution.py:307
  8.0 16.2 %collective-permute-start.4 = (bf16[256,512]{1,0:T(8,128)(2,1)}, bf16[256,512]{1,0:T(8,128)(2,1)S(1)}, u32[]{:S(2)}, u32[]{:S(2)}) collective-permute-start(bf16[256,512]{1,0:T(8,128)(2,1)} %param.11), channel_id=1, source_target_pairs={{0,4},{1,5},{2,6},{3,7},{4,0},{5,1},{6,2},{7,3},{8,12},{9,13},{10,... | collective-permute-start | bytes 786440 | tf_op jit(solution)/shard_map/ppermute | solution.py:278
  24.9 173.8 %all-gather.13.cloned.1.call-start = ((), (), s32[]{:S(2)}) async-start(), calls=%async_computation.8 | async-start | bytes 3932160 | tf_op jit(solution)/shard_map/all_gather | solution.py:304
  27.6 201.0 %all-gather.15.cloned.1.call-start = ((), (), s32[]{:S(2)}) async-start(), calls=%async_computation.9 | async-start | bytes 3932160 | tf_op jit(solution)/shard_map/all_gather | solution.py:304
  27.6 36.8 %collective-permute-start.3 = (bf16[512,768]{1,0:T(8,128)(2,1)}, bf16[512,768]{1,0:T(8,128)(2,1)S(1)}, u32[]{:S(2)}, u32[]{:S(2)}) collective-permute-start(bf16[512,768]{1,0:T(8,128)(2,1)} %copy.18), channel_id=1, source_target_pairs={{0,4},{1,5},{2,6},{3,7},{4,0},{5,1},{6,2},{7,3},{8,12},{9,13},{10,... | collective-permute-start | bytes 2359304 | tf_op jit(solution)/shard_map/ppermute | solution.py:278
  65.3 350.2 %all-gather.25.cloned.1.call-start = ((), (), s32[]{:S(2)}) async-start(), calls=%async_computation.22 | async-start | bytes 5242880 | tf_op jit(solution)/shard_map/all_gather | solution.py:307
  65.9 353.1 %all-gather.27.cloned.1.call-start = ((), (), s32[]{:S(2)}) async-start(), calls=%async_computation.23 | async-start | bytes 5242880 | tf_op jit(solution)/shard_map/all_gather | solution.py:307
  65.9 47.0 %collective-permute-start.12 = (bf16[1024,512]{1,0:T(8,128)(2,1)S(1)}, bf16[1024,512]{1,0:T(8,128)(2,1)}, u32[]{:S(2)}, u32[]{:S(2)}) collective-permute-start(bf16[1024,512]{1,0:T(8,128)(2,1)S(1)} %copy-done.17), channel_id=1, source_target_pairs={{0,4},{1,5},{2,6},{3,7},{4,0},{5,1},{6,2},{7,3},{8,12},{9,13},{10,... | collective-permute-start | bytes 3145736 | tf_op jit(solution)/shard_map/ppermute | solution.py:278
  112.9 397.8 %all-gather.17.cloned.1.call-start = ((), (), s32[]{:S(2)}) async-start(), calls=%async_computation.10 | async-start | bytes 10485760 | tf_op jit(solution)/shard_map/all_gather | solution.py:304
  116.6 440.7 %all-gather.19.cloned.1.call-start = ((), (), s32[]{:S(2)}) async-start(), calls=%async_computation.11 | async-start | bytes 10485760 | tf_op jit(solution)/shard_map/all_gather | solution.py:304
  119.5 47.7 %collective-permute-start.1 = (bf16[512,2048]{1,0:T(8,128)(2,1)}, bf16[512,2048]{1,0:T(8,128)(2,1)}, u32[]{:S(2)}, u32[]{:S(2)}) collective-permute-start(bf16[512,2048]{1,0:T(8,128)(2,1)} %fusion.19), channel_id=1, source_target_pairs={{0,2},{1,3},{2,0},{3,1},{4,6},{5,7},{6,4},{7,5},{8,10},{9,11},{10,... | collective-permute-start | bytes 6291464 | tf_op jit(solution)/shard_map/ppermute | solution.py:275
  119.5 72.1 %collective-permute-start = (bf16[512,2048]{1,0:T(8,128)(2,1)}, bf16[512,2048]{1,0:T(8,128)(2,1)}, u32[]{:S(2)}, u32[]{:S(2)}) collective-permute-start(bf16[512,2048]{1,0:T(8,128)(2,1)} %fusion.19), channel_id=1, source_target_pairs={{0,1},{1,0},{2,3},{3,2},{4,5},{5,4},{6,7},{7,6},{8,9},{9,8},{10,11... | collective-permute-start | bytes 6291464 | tf_op jit(solution)/shard_map/ppermute | solution.py:275
  167.2 24.4 %collective-permute-start.2 = (bf16[512,2048]{1,0:T(8,128)(2,1)}, bf16[512,2048]{1,0:T(8,128)(2,1)}, u32[]{:S(2)}, u32[]{:S(2)}) collective-permute-start(bf16[512,2048]{1,0:T(8,128)(2,1)} %collective-permute-done.1), channel_id=1, source_target_pairs={{0,1},{1,0},{2,3},{3,2},{4,5},{5,4},{6,7},{7,6},{8,9},{9,8},{10,11... | collective-permute-start | bytes 6291464 | tf_op jit(solution)/shard_map/ppermute | solution.py:275
  259.0 6.3 collective-permute-start.6
  260.1 94.1 %collective-permute-start.11 = (bf16[512,2048]{1,0:T(8,128)(2,1)S(1)}, bf16[512,2048]{1,0:T(8,128)(2,1)}, u32[]{:S(2)}, u32[]{:S(2)}) collective-permute-start(bf16[512,2048]{1,0:T(8,128)(2,1)S(1)} %bitcast.42), channel_id=1, source_target_pairs={{0,4},{1,5},{2,6},{3,7},{4,0},{5,1},{6,2},{7,3},{8,12},{9,13},{10,... | collective-permute-start | bytes 6291464 | tf_op jit(solution)/shard_map/ppermute | solution.py:278
  260.9 93.6 %collective-permute-start.17 = (bf16[512,2048]{1,0:T(8,128)(2,1)}, bf16[512,2048]{1,0:T(8,128)(2,1)}, u32[]{:S(2)}, u32[]{:S(2)}) collective-permute-start(bf16[512,2048]{1,0:T(8,128)(2,1)} %param.17), channel_id=1, source_target_pairs={{0,2},{1,3},{2,0},{3,1},{4,6},{5,7},{6,4},{7,5},{8,10},{9,11},{10,... | collective-permute-start | bytes 6291464 | tf_op jit(solution)/shard_map/ppermute | solution.py:275
  265.3 92.6 %collective-permute-start.5 = (bf16[512,2048]{1,0:T(8,128)(2,1)}, bf16[512,2048]{1,0:T(8,128)(2,1)}, u32[]{:S(2)}, u32[]{:S(2)}) collective-permute-start(bf16[512,2048]{1,0:T(8,128)(2,1)} %convolution_convert_fusion.15), channel_id=1, source_target_pairs={{0,1},{1,0},{2,3},{3,2},{4,5},{5,4},{6,7},{7,6},{8,9},{9,8},{10,11... | collective-permute-start | bytes 6291464 | tf_op jit(solution)/shard_map/ppermute | solution.py:275
  267.9 131.0 %collective-permute-start.7 = (bf16[512,2048]{1,0:T(8,128)(2,1)}, bf16[512,2048]{1,0:T(8,128)(2,1)}, u32[]{:S(2)}, u32[]{:S(2)}) collective-permute-start(bf16[512,2048]{1,0:T(8,128)(2,1)} %add_convert_fusion.4), channel_id=1, source_target_pairs={{0,2},{1,3},{2,0},{3,1},{4,6},{5,7},{6,4},{7,5},{8,10},{9,11},{10,... | collective-permute-start | bytes 6291464 | tf_op jit(solution)/shard_map/ppermute | solution.py:275
  354.2 728.1 %reduce-scatter.23.cloned.1.call-start = ((), (), s32[]{:S(2)}) async-start(), calls=%async_computation.19 | async-start | bytes 5242880 | tf_op jit(solution)/shard_map/reduce_scatter | solution.py:323
  354.3 54.9 %collective-permute-start.16 = (bf16[512,2048]{1,0:T(8,128)(2,1)}, bf16[512,2048]{1,0:T(8,128)(2,1)S(1)}, u32[]{:S(2)}, u32[]{:S(2)}) collective-permute-start(bf16[512,2048]{1,0:T(8,128)(2,1)} %param.17), channel_id=1, source_target_pairs={{0,1},{1,0},{2,3},{3,2},{4,5},{5,4},{6,7},{7,6},{8,9},{9,8},{10,11... | collective-permute-start | bytes 6291464 | tf_op jit(solution)/shard_map/ppermute | solution.py:275
  354.5 59.4 %collective-permute-start.18 = (bf16[512,2048]{1,0:T(8,128)(2,1)}, bf16[512,2048]{1,0:T(8,128)(2,1)S(1)}, u32[]{:S(2)}, u32[]{:S(2)}) collective-permute-start(bf16[512,2048]{1,0:T(8,128)(2,1)} %collective-permute-done.17), channel_id=1, source_target_pairs={{0,1},{1,0},{2,3},{3,2},{4,5},{5,4},{6,7},{7,6},{8,9},{9,8},{10,11... | collective-permute-start | bytes 6291464 | tf_op jit(solution)/shard_map/ppermute | solution.py:275
  405.1 47.7 %collective-permute-start.9 = (bf16[512,2048]{1,0:T(8,128)(2,1)}, bf16[512,2048]{1,0:T(8,128)(2,1)}, u32[]{:S(2)}, u32[]{:S(2)}) collective-permute-start(bf16[512,2048]{1,0:T(8,128)(2,1)} %fusion.34), channel_id=1, source_target_pairs={{0,2},{1,3},{2,0},{3,1},{4,6},{5,7},{6,4},{7,5},{8,10},{9,11},{10,... | collective-permute-start | bytes 6291464 | tf_op jit(solution)/shard_map/ppermute | solution.py:275
  421.5 97.6 %collective-permute-start.8 = (bf16[512,2048]{1,0:T(8,128)(2,1)}, bf16[512,2048]{1,0:T(8,128)(2,1)}, u32[]{:S(2)}, u32[]{:S(2)}) collective-permute-start(bf16[512,2048]{1,0:T(8,128)(2,1)} %fusion.34), channel_id=1, source_target_pairs={{0,1},{1,0},{2,3},{3,2},{4,5},{5,4},{6,7},{7,6},{8,9},{9,8},{10,11... | collective-permute-start | bytes 6291464 | tf_op jit(solution)/shard_map/ppermute | solution.py:275
  452.8 66.2 %collective-permute-start.10 = (bf16[512,2048]{1,0:T(8,128)(2,1)}, bf16[512,2048]{1,0:T(8,128)(2,1)}, u32[]{:S(2)}, u32[]{:S(2)}) collective-permute-start(bf16[512,2048]{1,0:T(8,128)(2,1)} %collective-permute-done.9), channel_id=1, source_target_pairs={{0,1},{1,0},{2,3},{3,2},{4,5},{5,4},{6,7},{7,6},{8,9},{9,8},{10,11... | collective-permute-start | bytes 6291464 | tf_op jit(solution)/shard_map/ppermute | solution.py:275
  736.3 16.7 %collective-permute-start.20 = (bf16[512,2048]{1,0:T(8,128)(2,1)}, bf16[512,2048]{1,0:T(8,128)(2,1)S(1)}, u32[]{:S(2)}, u32[]{:S(2)}) collective-permute-start(bf16[512,2048]{1,0:T(8,128)(2,1)} %fusion.44), channel_id=1, source_target_pairs={{0,1},{1,0},{2,3},{3,2},{4,5},{5,4},{6,7},{7,6},{8,9},{9,8},{10,11... | collective-permute-start | bytes 6291464 | tf_op jit(solution)/shard_map/ppermute | solution.py:275
  744.4 15.6 %collective-permute-start.14 = (bf16[512,2048]{1,0:T(8,128)(2,1)}, bf16[512,2048]{1,0:T(8,128)(2,1)}, u32[]{:S(2)}, u32[]{:S(2)}) collective-permute-start(bf16[512,2048]{1,0:T(8,128)(2,1)} %convolution_convert_fusion.9), channel_id=1, source_target_pairs={{0,1},{1,0},{2,3},{3,2},{4,5},{5,4},{6,7},{7,6},{8,9},{9,8},{10,11... | collective-permute-start | bytes 6291464 | tf_op jit(solution)/shard_map/ppermute | solution.py:275
  752.5 19.2 %collective-permute-start.19 = (bf16[512,2048]{1,0:T(8,128)(2,1)}, bf16[512,2048]{1,0:T(8,128)(2,1)S(1)}, u32[]{:S(2)}, u32[]{:S(2)}) collective-permute-start(bf16[512,2048]{1,0:T(8,128)(2,1)} %fusion.38), channel_id=1, source_target_pairs={{0,1},{1,0},{2,3},{3,2},{4,5},{5,4},{6,7},{7,6},{8,9},{9,8},{10,11... | collective-permute-start | bytes 6291464 | tf_op jit(solution)/shard_map/ppermute | solution.py:275
  755.2 48.8 %collective-permute-start.21 = (bf16[512,2048]{1,0:T(8,128)(2,1)}, bf16[512,2048]{1,0:T(8,128)(2,1)}, u32[]{:S(2)}, u32[]{:S(2)}) collective-permute-start(bf16[512,2048]{1,0:T(8,128)(2,1)} %add_convert_fusion.1), channel_id=1, source_target_pairs={{0,2},{1,3},{2,0},{3,1},{4,6},{5,7},{6,4},{7,5},{8,10},{9,11},{10,... | collective-permute-start | bytes 6291464 | tf_op jit(solution)/shard_map/ppermute | solution.py:275
  759.9 324.1 %reduce-scatter.15.cloned.1.call-start = ((), (), s32[]{:S(2)}) async-start(), calls=%async_computation.15 | async-start | bytes 1310720 | tf_op jit(solution)/shard_map/reduce_scatter | solution.py:323
  759.9 61.3 %collective-permute-start.13 = (bf16[512,2048]{1,0:T(8,128)(2,1)}, bf16[512,2048]{1,0:T(8,128)(2,1)}, u32[]{:S(2)}, u32[]{:S(2)}) collective-permute-start(bf16[512,2048]{1,0:T(8,128)(2,1)} %convolution_convert_fusion.11), channel_id=1, source_target_pairs={{0,1},{1,0},{2,3},{3,2},{4,5},{5,4},{6,7},{7,6},{8,9},{9,8},{10,11... | collective-permute-start | bytes 6291464 | tf_op jit(solution)/shard_map/ppermute | solution.py:275
  770.5 77.6 %collective-permute-start.15 = (bf16[512,2048]{1,0:T(8,128)(2,1)}, bf16[512,2048]{1,0:T(8,128)(2,1)}, u32[]{:S(2)}, u32[]{:S(2)}) collective-permute-start(bf16[512,2048]{1,0:T(8,128)(2,1)} %add_convert_fusion.3), channel_id=1, source_target_pairs={{0,2},{1,3},{2,0},{3,1},{4,6},{5,7},{6,4},{7,5},{8,10},{9,11},{10,... | collective-permute-start | bytes 6291464 | tf_op jit(solution)/shard_map/ppermute | solution.py:275
  858.3 46.8 %collective-permute-start.23 = (bf16[512,2048]{1,0:T(8,128)(2,1)S(1)}, bf16[512,2048]{1,0:T(8,128)(2,1)S(1)}, u32[]{:S(2)}, u32[]{:S(2)}) collective-permute-start(bf16[512,2048]{1,0:T(8,128)(2,1)S(1)} %get-tuple-element.30), channel_id=1, source_target_pairs={{0,2},{1,3},{2,0},{3,1},{4,6},{5,7},{6,4},{7,5},{8,10},{9,11},{10,... | collective-permute-start | bytes 6291464 | tf_op jit(solution)/shard_map/ppermute | solution.py:275
  859.2 46.0 %collective-permute-start.22 = (bf16[512,2048]{1,0:T(8,128)(2,1)S(1)}, bf16[512,2048]{1,0:T(8,128)(2,1)S(1)}, u32[]{:S(2)}, u32[]{:S(2)}) collective-permute-start(bf16[512,2048]{1,0:T(8,128)(2,1)S(1)} %get-tuple-element.30), channel_id=1, source_target_pairs={{0,1},{1,0},{2,3},{3,2},{4,5},{5,4},{6,7},{7,6},{8,9},{9,8},{10,11... | collective-permute-start | bytes 6291464 | tf_op jit(solution)/shard_map/ppermute | solution.py:275
  905.2 4.2 collective-permute-start.24
  916.2 169.1 %reduce-scatter.21.cloned.1.call-start = ((), (), s32[]{:S(2)}) async-start(), calls=%async_computation.18 | async-start | bytes 5242880 | tf_op jit(solution)/shard_map/reduce_scatter | solution.py:323
  916.9 237.1 %reduce-scatter.13.cloned.1.call-start = ((), (), s32[]{:S(2)}) async-start(), calls=%async_computation.14 | async-start | bytes 1310720 | tf_op jit(solution)/shard_map/reduce_scatter | solution.py:323
  917.5 240.2 %reduce-scatter.19.cloned.1.call-start = ((), (), s32[]{:S(2)}) async-start(), calls=%async_computation.17 | async-start | bytes 10485760 | tf_op jit(solution)/shard_map/reduce_scatter | solution.py:320
  943.9 226.9 %reduce-scatter.11.cloned.1.call-start = ((), (), s32[]{:S(2)}) async-start(), calls=%async_computation.13 | async-start | bytes 3932160 | tf_op jit(solution)/shard_map/reduce_scatter | solution.py:320
  994.8 217.8 %reduce-scatter.9.cloned.1.call-start = ((), (), s32[]{:S(2)}) async-start(), calls=%async_computation.12 | async-start | bytes 3932160 | tf_op jit(solution)/shard_map/reduce_scatter | solution.py:320
  1032.7 269.6 %reduce-scatter.17.cloned.1.call-start = ((), (), s32[]{:S(2)}) async-start(), calls=%async_computation.16 | async-start | bytes 10485760 | tf_op jit(solution)/shard_map/reduce_scatter | solution.py:320
  1069.8 9.2 collective-permute-start.26
  1074.7 86.3 %collective-permute-start.25 = (bf16[512,2048]{1,0:T(8,128)(2,1)}, bf16[512,2048]{1,0:T(8,128)(2,1)}, u32[]{:S(2)}, u32[]{:S(2)}) collective-permute-start(bf16[512,2048]{1,0:T(8,128)(2,1)} %convolution_convert_fusion.6), channel_id=1, source_target_pairs={{0,1},{1,0},{2,3},{3,2},{4,5},{5,4},{6,7},{7,6},{8,9},{9,8},{10,11... | collective-permute-start | bytes 6291464 | tf_op jit(solution)/shard_map/ppermute | solution.py:275
  1081.2 79.8 %collective-permute-start.27 = (bf16[512,2048]{1,0:T(8,128)(2,1)}, bf16[512,2048]{1,0:T(8,128)(2,1)}, u32[]{:S(2)}, u32[]{:S(2)}) collective-permute-start(bf16[512,2048]{1,0:T(8,128)(2,1)} %add_convert_fusion), channel_id=1, source_target_pairs={{0,2},{1,3},{2,0},{3,1},{4,6},{5,7},{6,4},{7,5},{8,10},{9,11},{10,... | collective-permute-start | bytes 6291464 | tf_op jit(solution)/shard_map/ppermute | solution.py:275
  1082.3 68.8 %collective-permute-start.31 = (bf16[1024,512]{1,0:T(8,128)(2,1)}, bf16[1024,512]{1,0:T(8,128)(2,1)S(1)}, u32[]{:S(2)}, u32[]{:S(2)}) collective-permute-start(bf16[1024,512]{1,0:T(8,128)(2,1)} %reduce-scatter.23.cloned.1.call-done), channel_id=1, source_target_pairs={{0,4},{1,5},{2,6},{3,7},{4,0},{5,1},{6,2},{7,3},{8,12},{9,13},{10,... | collective-permute-start | bytes 3145736 | tf_op jit(solution)/shard_map/ppermute | solution.py:278
  1084.0 71.9 %collective-permute-start.29 = (bf16[256,512]{1,0:T(8,128)(2,1)}, bf16[256,512]{1,0:T(8,128)(2,1)S(1)}, u32[]{:S(2)}, u32[]{:S(2)}) collective-permute-start(bf16[256,512]{1,0:T(8,128)(2,1)} %reduce-scatter.15.cloned.1.call-done), channel_id=1, source_target_pairs={{0,4},{1,5},{2,6},{3,7},{4,0},{5,1},{6,2},{7,3},{8,12},{9,13},{10,... | collective-permute-start | bytes 786440 | tf_op jit(solution)/shard_map/ppermute | solution.py:278
  1157.7 144.6 %collective-permute-start.30 = (bf16[512,2048]{1,0:T(8,128)(2,1)}, bf16[512,2048]{1,0:T(8,128)(2,1)}, u32[]{:S(2)}, u32[]{:S(2)}) collective-permute-start(bf16[512,2048]{1,0:T(8,128)(2,1)} %reduce-scatter.19.cloned.1.call-done), channel_id=1, source_target_pairs={{0,4},{1,5},{2,6},{3,7},{4,0},{5,1},{6,2},{7,3},{8,12},{9,13},{10,... | collective-permute-start | bytes 6291464 | tf_op jit(solution)/shard_map/ppermute | solution.py:278
  1170.8 114.1 %collective-permute-start.28 = (bf16[512,768]{1,0:T(8,128)(2,1)}, bf16[512,768]{1,0:T(8,128)(2,1)S(1)}, u32[]{:S(2)}, u32[]{:S(2)}) collective-permute-start(bf16[512,768]{1,0:T(8,128)(2,1)} %reduce-scatter.11.cloned.1.call-done), channel_id=1, source_target_pairs={{0,4},{1,5},{2,6},{3,7},{4,0},{5,1},{6,2},{7,3},{8,12},{9,13},{10,... | collective-permute-start | bytes 2359304 | tf_op jit(solution)/shard_map/ppermute | solution.py:278
  (45 other events, 971.1 us)
Sparse Core Ops, SparseCore 0:
  9.9 29.3 all-gather.20
  41.6 26.6 all-gather.22
  70.7 43.9 all-gather.12
  116.4 43.9 all-gather.14
  162.1 52.6 all-gather.24
  216.6 52.6 all-gather.26
  271.7 87.5 all-gather.16
  361.2 87.5 all-gather.18
  760.0 51.3 reduce-scatter.22
  916.3 26.2 reduce-scatter.14
  945.6 52.6 reduce-scatter.20
  1001.3 27.6 reduce-scatter.12
  1032.1 86.4 reduce-scatter.18
  1121.7 43.9 reduce-scatter.10
  1168.7 43.9 reduce-scatter.8
  1215.9 86.4 reduce-scatter.16

commit v2 on v1

--- a/solution.py
+++ b/solution.py
@@ -57,37 +57,513 @@
     return jnp.concatenate([cosine, cosine], axis=-1), jnp.concatenate([-sine, sine], axis=-1)
 
 
-def project_kernel(x_ref, w_ref, cos_ref, sin_ref, out_ref):
-    product = dot_nn(x_ref[...], w_ref[...])
-    width = product.shape[1] // 3
-    for column in range(0, 3 * width, HD):
-        part = product[:, column : column + HD]
-        if column < 2 * width:
-            part = part * cos_ref[...] + pltpu.roll(part, HD // 2, 1) * sin_ref[...]
-        out_ref[:, column : column + HD] = part.astype(BF16)
-
-
-def project(x, w, cosine, sine):
-    tokens, model = x.shape
-    width = w.shape[1]
-    block = min(512, tokens)
+def kernel_call(kernel, name, grid, in_specs, out_specs, out_shapes, scratch, aliases={}):
     return pl.pallas_call(
-        project_kernel,
-        grid=(tokens // block,),
-        in_specs=[
-            pl.BlockSpec((block, model), lambda i: (i, 0)),
-            pl.BlockSpec((model, width), lambda i: (0, 0)),
-            pl.BlockSpec((block, HD), lambda i: (i, 0)),
-            pl.BlockSpec((block, HD), lambda i: (i, 0)),
+        kernel,
+        grid_spec=pltpu.PrefetchScalarGridSpec(
+            num_scalar_prefetch=1, grid=grid, in_specs=in_specs, out_specs=out_specs, scratch_shapes=scratch
+        ),
+        out_shape=out_shapes,
+        input_output_aliases=aliases,
+        compiler_params=pltpu.CompilerParams(vmem_limit_bytes=VMEM_LIMIT),
+        cost_estimate=pl.CostEstimate(flops=1, bytes_accessed=1, transcendentals=0),
+        name=name,
+    )
+
+
+def any_specs(arrays):
+    return [pl.BlockSpec(memory_space=pl.ANY)] * len(arrays)
+
+
+def slot(index, size):
+    return pl.ds(pl.multiple_of(index * size, size), size)
+
+
+def start_kernel(members, sets, count, x_ref, pack_ref, *refs):
+    normed, refs = refs[:members], refs[members:]
+    packs = [(pack_ref,) + refs[: count - 1]]
+    refs = refs[count - 1 :]
+    for _ in range(1, sets):
+        packs.append(refs[:count])
+        refs = refs[count:]
+    low_ref, local_sem, send_sem, recv_sem = refs
+    t, f = lax.axis_index("tp"), lax.axis_index("fsdp")
+    total = members * sets
+    climb = [1 << i for i in range(count.bit_length() - 1)]
+    group = [1 << i for i in range(members.bit_length() - 1)][::-1]
+    shifts = [lax.rem(t + step * members, total) for step in range(1, sets)]
+
+    barrier = pltpu.get_barrier_semaphore()
+    partners = [{"tp": t ^ bit} for bit in group] + [{"tp": s} for s in shifts] + [{"fsdp": f ^ bit} for bit in climb]
+    for partner in partners:
+        pl.semaphore_signal(barrier, inc=1, device_id=partner, device_id_type=pl.DeviceIdType.MESH)
+    pl.semaphore_wait(barrier, len(partners))
+
+    started, waited = [], []
+
+    def send(src, dst, partner):
+        n = len(started)
+        copy = pltpu.make_async_remote_copy(
+            src_ref=src,
+            dst_ref=dst,
+            send_sem=send_sem.at[n],
+            recv_sem=recv_sem.at[n],
+            device_id=partner,
+            device_id_type=pl.DeviceIdType.MESH,
+        )
+        copy.start()
+        started.append(copy)
+        return copy
+
+    def await_block(copy):
+        copy.wait_recv()
+        waited.append(copy)
+
+    orders = (climb, climb[::-1])
+    size = pack_ref.shape[0] // 2
+    came = [{} for _ in range(sets)]
+
+    def pass_on(step, half, mask):
+        order = orders[half]
+        here = pl.ds(half * size, size)
+        for n, bit in enumerate(order):
+            if all(not mask & later for later in order[n:]):
+                copy = send(packs[step][mask].at[here, :], packs[step][mask | bit].at[here, :], {"fsdp": f ^ bit})
+                came[step][half, mask | bit] = copy
+
+    def pass_all(step):
+        for level in range(1, len(climb)):
+            for half in range(2):
+                for mask in range(count):
+                    if mask.bit_count() == level and not mask & orders[half][-1]:
+                        await_block(came[step][half, mask])
+                        pass_on(step, half, mask)
+
+    over = [send(pack_ref, packs[step][0], {"tp": shifts[step - 1]}) for step in range(1, sets)]
+    for half in range(2):
+        pass_on(0, half, 0)
+
+    rows = x_ref.shape[0]
+    tile = min(32, rows)
+
+    def norm(i, carry):
+        here = pl.ds(pl.multiple_of(i * tile, tile), tile)
+        low_ref[here, :] = layer_norm(x_ref[here, :].astype(F32)).astype(BF16)
+        return carry
+
+    lax.fori_loop(0, rows // tile, norm, 0)
+    keep = pltpu.make_async_copy(low_ref, normed[0], local_sem)
+    keep.start()
+    blocks = {}
+    for bit in group:
+        blocks[bit] = send(low_ref, normed[bit], {"tp": t ^ bit})
+    pass_all(0)
+    for step in range(1, sets):
+        await_block(over[step - 1])
+        for half in range(2):
+            pass_on(step, half, 0)
+        pass_all(step)
+    for mask in sorted(range(1, members), reverse=True, key=lambda m: (m & -m, m)):
+        below = [bit for bit in group if bit < mask & -mask]
+        if below:
+            await_block(blocks[mask])
+        for bit in below:
+            blocks[mask | bit] = send(normed[mask], normed[mask | bit], {"tp": t ^ bit})
+    keep.wait()
+    for copy in started:
+        copy.wait_send()
+        if not any(copy is other for other in waited):
+            copy.wait_recv()
+
+
+def start_exchange(x, pack, members, sets, count):
+    sends = 2 * (count - 1) * sets + (members - 1) + (sets - 1)
+    shapes = [jax.ShapeDtypeStruct(x.shape, BF16)] * members + [jax.ShapeDtypeStruct(pack.shape, BF16)] * (count * sets - 1)
+    outs = pl.pallas_call(
+        functools.partial(start_kernel, members, sets, count),
+        in_specs=[pl.BlockSpec(memory_space=pltpu.VMEM), pl.BlockSpec(memory_space=pl.ANY)],
+        out_specs=any_specs(shapes),
+        out_shape=shapes,
+        scratch_shapes=[
+            pltpu.VMEM(x.shape, BF16),
+            pltpu.SemaphoreType.DMA,
+            pltpu.SemaphoreType.DMA((sends,)),
+            pltpu.SemaphoreType.DMA((sends,)),
         ],
-        out_specs=pl.BlockSpec((block, width), lambda i: (i, 0)),
-        out_shape=jax.ShapeDtypeStruct((tokens, width), BF16),
-        compiler_params=pltpu.CompilerParams(vmem_limit_bytes=VMEM_LIMIT),
-        cost_estimate=pl.CostEstimate(
-            flops=2 * tokens * model * width, bytes_accessed=2 * (tokens * model + model * width + tokens * width), transcendentals=0
-        ),
-        name="project",
-    )(x, w, cosine, sine)
+        compiler_params=pltpu.CompilerParams(vmem_limit_bytes=VMEM_LIMIT, collective_id=0, has_side_effects=True),
+        cost_estimate=pl.CostEstimate(flops=1, bytes_accessed=1, transcendentals=0),
+        name="start_exchange",
+    )(x, pack)
+    packs = [pack] + list(outs[members:])
+    return outs[:members], [packs[step * count : (step + 1) * count] for step in range(sets)]
+
+
+def rows_kernel(body, plan, members, extras, count, f_ref, *refs):
+    xs, refs = refs[:members], refs[members:]
+    extra_refs, refs = refs[:extras], refs[extras:]
+    weights, refs = refs[:count], refs[count:]
+    outs, (x_buf, w_buf, x_sem, w_sem) = refs[:-4], refs[-4:]
+    i, f = pl.program_id(0), f_ref[0]
+    moves, use = plan
+    tiles = [
+        [pltpu.make_async_copy(src, dst, w_sem.at[t, n]) for n, (src, dst) in enumerate(pairs)]
+        for t, pairs in enumerate(moves(weights, w_buf, f))
+    ]
+    x_copies = [pltpu.make_async_copy(x, x_buf.at[m], x_sem.at[m]) for m, x in enumerate(xs)]
+
+    @pl.when(i == 0)
+    def _():
+        x_copies[0].start()
+        for copies in tiles:
+            for copy in copies:
+                copy.start()
+        for copy in x_copies[1:]:
+            copy.start()
+
+    def run(first):
+        pltpu.make_async_copy(xs[0], x_buf.at[i], x_sem.at[i]).wait()
+        for t, copies in enumerate(tiles):
+            if first:
+                for copy in copies:
+                    copy.wait()
+            body(t, use(t, x_buf[i], w_buf), extra_refs, outs)
+
+    pl.when(i == 0)(functools.partial(run, True))
+    pl.when(i > 0)(functools.partial(run, False))
+
+
+def rows_call(body, name, place, xs, extras, weights, plan, tiles, copies, w_shape, widths):
+    rows, model = xs[0].shape
+    members, count = len(xs), len(weights)
+    return kernel_call(
+        functools.partial(rows_kernel, body, plan, members, len(extras), count),
+        name,
+        (members,),
+        any_specs(xs) + [pl.BlockSpec((rows, e.shape[1]), lambda i, f: (i, 0)) for e in extras] + any_specs(weights),
+        [pl.BlockSpec((rows, width), lambda i, f: (i, 0)) for width in widths],
+        [jax.ShapeDtypeStruct((members * rows, width), BF16) for width in widths],
+        [
+            pltpu.VMEM((members, rows, model), BF16),
+            pltpu.VMEM(w_shape, BF16),
+            pltpu.SemaphoreType.DMA((members,)),
+            pltpu.SemaphoreType.DMA((tiles, copies)),
+        ],
+    )(place, *xs, *extras, *weights)
+
+
+def project(place, xs, packs, cosine, sine):
+    model, count = xs[0].shape[1], len(packs)
+    depth, width = model // count, packs[0].shape[1]
+
+    def moves(packs, w_buf, f):
+        return [
+            [(pack.at[t * depth : (t + 1) * depth, :], w_buf.at[t, slot(f ^ c, depth), :]) for c, pack in enumerate(packs)]
+            for t in range(3)
+        ]
+
+    def use(t, x, w_buf):
+        return dot_nn(x, w_buf[t])
+
+    def body(t, product, extras, outs):
+        for column in range(0, width, HD):
+            value = product[:, column : column + HD]
+            if t < 2:
+                value = value * extras[0][...] + pltpu.roll(value, HD // 2, 1) * extras[1][...]
+            outs[0][:, t * width + column : t * width + column + HD] = value.astype(BF16)
+
+    return rows_call(
+        body, "project", place, xs, [cosine, sine], packs, (moves, use), 3, count, (3, model, width), [3 * width]
+    )[0]
+
+
+def head_grad_of(place, xs, packs):
+    model, count = xs[0].shape[1], len(packs)
+    depth, width = model // count, packs[0].shape[1]
+    squares = depth // width
+
+    def moves(packs, w_buf, f):
+        return [
+            [
+                (
+                    pack.at[3 * depth + b * width : 3 * depth + (b + 1) * width, :],
+                    w_buf.at[:, slot((f ^ c) * squares + b, width)],
+                )
+                for c, pack in enumerate(packs)
+                for b in range(squares)
+            ]
+        ]
+
+    def use(t, x, w_buf):
+        return dot_nt(x, w_buf[...])
+
+    def body(t, product, extras, outs):
+        outs[0][...] = product.astype(BF16)
+
+    return rows_call(
+        body, "head_grad", place, xs, [], packs, (moves, use), 1, count * squares, (width, model), [width]
+    )[0]
+
+
+def hidden_units(place, xs, stack):
+    model = xs[0].shape[1]
+    count, depth, width = stack.shape
+    width //= 2
+    tile = min(256, width)
+    starts = range(0, width, tile)
+
+    def moves(weights, w_buf, f):
+        return [
+            [
+                (weights[0].at[c, :, s : s + tile], w_buf.at[c * depth : (c + 1) * depth, s : s + tile])
+                for c in range(count)
+                for s in (start, width + start)
+            ]
+            for start in starts
+        ]
+
+    def use(t, x, w_buf):
+        return [dot_nn(x, w_buf[:, s : s + tile]) for s in (starts[t], width + starts[t])]
+
+    def body(t, products, extras, outs):
+        here = pl.ds(starts[t], tile)
+        up, gate = products
+        sigmoid = 1.0 / (1.0 + jnp.exp(-gate))
+        slope_up = gate * sigmoid
+        outs[0][:, here] = (slope_up * up).astype(BF16)
+        outs[1][:, here] = slope_up.astype(BF16)
+        outs[2][:, here] = (up * sigmoid * (1.0 + gate * (1.0 - sigmoid))).astype(BF16)
+
+    return rows_call(
+        body, "hidden_units", place, xs, [], [stack], (moves, use), len(starts), 2 * count, (model, 2 * width), [width] * 3
+    )
+
+
+def hidden_grad(place, xs, slope_up, slope_gate, stack):
+    model = xs[0].shape[1]
+    count, width, depth = stack.shape
+    tile = min(512, width)
+    starts = range(0, width, tile)
+
+    def moves(weights, w_buf, f):
+        return [
+            [
+                (weights[0].at[c, s : s + tile, :], w_buf.at[s : s + tile, c * depth : (c + 1) * depth])
+                for c in range(count)
+            ]
+            for s in starts
+        ]
+
+    def use(t, x, w_buf):
+        return dot_nt(x, w_buf[starts[t] : starts[t] + tile, :])
+
+    def body(t, product, extras, outs):
+        here = pl.ds(starts[t], tile)
+        outs[0][:, here] = (product * extras[0][:, here].astype(F32)).astype(BF16)
+        outs[0][:, pl.ds(width + starts[t], tile)] = (product * extras[1][:, here].astype(F32)).astype(BF16)
+
+    return rows_call(
+        body, "hidden_grad", place, xs, [slope_up, slope_gate], [stack], (moves, use),
+        len(starts), count, (width, model), [2 * width],
+    )[0]
+
+
+def expand_kernel(sets, each, plan, dot, with_base, parts, f_ref, *refs):
+    xs, refs = refs[:sets], refs[sets:]
+    bases, refs = (refs[:1], refs[1:]) if with_base else ((), refs)
+    weights, refs = refs[: sets * each], refs[sets * each :]
+    outs, (w_buf, sem) = refs[:parts], refs[parts:]
+    d, f = pl.program_id(0), f_ref[0]
+    count = w_buf.shape[1]
+
+    def copies(j, c):
+        there, pairs = plan(weights[j * each : (j + 1) * each], c, f)
+        return there, [
+            pltpu.make_async_copy(src, w_buf.at[j, there, :, lanes], sem.at[j, there, n])
+            for n, (src, lanes) in enumerate(pairs)
+        ]
+
+    @pl.when(d == 0)
+    def _():
+        for c in range(count):
+            for j in range(sets):
+                for copy in copies(j, c)[1]:
+                    copy.start()
+
+    for j in range(sets):
+        for n, (src, lanes) in enumerate(plan(weights[j * each : (j + 1) * each], 0, f)[1]):
+            pltpu.make_async_copy(src, w_buf.at[j, d, :, lanes], sem.at[j, d, n]).wait()
+    rows = outs[0].shape[0]
+    for p in range(parts):
+        here = slice(p * rows, (p + 1) * rows)
+        total = sum(dot(x[here, :], w_buf[j, d]) for j, x in enumerate(xs))
+        for base in bases:
+            total = total + base[here, :].astype(F32)
+        outs[p][...] = total.astype(BF16)
+
+
+def expand_call(name, place, xs, weights, each, plan, pieces, dot, chunk, rows, first, parts, base=None):
+    count, w_shape = chunk
+    depth = w_shape[1 if dot is dot_nn else 0]
+    specs = [pl.BlockSpec((rows * parts, x.shape[1]), lambda d, f: (first // parts, 0)) for x in xs]
+    bases = [] if base is None else [base]
+    specs += [pl.BlockSpec((rows * parts, depth), lambda d, f: (first // parts, d)) for _ in bases]
+    return kernel_call(
+        functools.partial(expand_kernel, len(xs), each, plan, dot, base is not None, parts),
+        name,
+        (count,),
+        specs + any_specs(weights),
+        [pl.BlockSpec((rows, depth), lambda d, f: (0, d))] * parts,
+        [jax.ShapeDtypeStruct((rows, count * depth), BF16)] * parts,
+        [pltpu.VMEM((len(xs), count) + w_shape, BF16), pltpu.SemaphoreType.DMA((len(xs), count, pieces))],
+    )(place, *xs, *bases, *weights)
+
+
+def expand_stack(name, dot, place, xs, stacks, rows, first, parts, base=None):
+    count, above, across = stacks[0].shape
+
+    def plan(weights, c, f):
+        return c, [(weights[0].at[c], pl.ds(0, across))]
+
+    return expand_call(
+        name, place, xs, stacks, 1, plan, 1, dot, (count, (above, across)), rows, first, parts, base
+    )
+
+
+def expand_heads(name, place, xs, packs, rows, first, parts):
+    count, width = len(packs[0]), packs[0][0].shape[1]
+    depth = packs_depth(packs[0][0])
+    squares = depth // width
+
+    def plan(weights, c, f):
+        return f ^ c, [
+            (weights[c].at[3 * depth + b * width : 3 * depth + (b + 1) * width, :], pl.ds(b * width, width))
+            for b in range(squares)
+        ]
+
+    flat = [pack for list_ in packs for pack in list_]
+    return expand_call(
+        name, place, xs, flat, count, plan, squares, dot_nn, (count, (width, depth)), rows, first, parts
+    )
+
+
+def expand_project(name, place, xs, packs, rows, first, parts):
+    count, width = len(packs[0]), packs[0][0].shape[1]
+    depth = packs_depth(packs[0][0])
+
+    def plan(weights, c, f):
+        return f ^ c, [
+            (weights[c].at[t * depth : (t + 1) * depth, :], pl.ds(t * width, width)) for t in range(3)
+        ]
+
+    flat = [pack for list_ in packs for pack in list_]
+    return expand_call(
+        name, place, xs, flat, count, plan, 3, dot_nt, (count, (depth, 3 * width)), rows, first, parts
+    )
+
+
+def pack_weights(att_proj, attn_out):
+    depth, _, width = att_proj.shape
+    parts = [att_proj[:, t, :] for t in range(3)]
+    return jnp.concatenate(parts + [attn_out[:, s : s + width] for s in range(0, depth, width)], axis=0)
+
+
+def packs_depth(pack):
+    return pack.shape[0] // 4
+
+
+def rows_grad_kernel(members, count, f_ref, *refs):
+    xs, (g_ref, out_ref, x_buf, sem) = refs[:members], refs[-4:]
+    rows, depth = xs[0].shape[0], xs[0].shape[1] // count
+    chunks = [
+        [
+            pltpu.make_async_copy(
+                x.at[:, d * depth : (d + 1) * depth], x_buf.at[d, m * rows : (m + 1) * rows, :], sem.at[d, m]
+            )
+            for m, x in enumerate(xs)
+        ]
+        for d in range(count)
+    ]
+
+    @pl.when(pl.program_id(0) == 0)
+    def _():
+        for copies in chunks:
+            for copy in copies:
+                copy.start()
+
+    def run(first):
+        for d, copies in enumerate(chunks):
+            if first:
+                for copy in copies:
+                    copy.wait()
+            out_ref[d] = dot_tn(x_buf[d], g_ref[...]).astype(BF16)
+
+    pl.when(pl.program_id(0) == 0)(functools.partial(run, True))
+    pl.when(pl.program_id(0) > 0)(functools.partial(run, False))
+
+
+def rows_grad(name, place, count, tile, below, xs, g, stack=None):
+    rows, model = xs[0].shape
+    tokens, width = g.shape
+    depth = model // count
+    given = [] if stack is None else [stack]
+    shape = (count, width // tile * depth + below, tile)
+    return kernel_call(
+        functools.partial(rows_grad_kernel, len(xs), count),
+        name,
+        (width // tile,),
+        any_specs(xs) + any_specs(given) + [pl.BlockSpec((tokens, tile), lambda n, f: (0, n))],
+        pl.BlockSpec((count, depth, tile), lambda n, f: (0, n, 0)),
+        jax.ShapeDtypeStruct(shape, BF16),
+        [pltpu.VMEM((count, tokens, depth), BF16), pltpu.SemaphoreType.DMA((count, len(xs)))],
+        {1 + len(xs): 0} if given else {},
+    )(place, *xs, *given, g)
+
+
+def columns_grad_kernel(sets, members, f_ref, *refs):
+    xs, gs = refs[:sets], refs[sets : sets + members]
+    out_ref, g_buf, sem = refs[-3:]
+    d = pl.program_id(0)
+    rows = gs[0].shape[0]
+    total, _, depth = g_buf.shape
+    tile = out_ref.shape[2]
+
+    @pl.when(d == 0)
+    def _():
+        for c in range(total):
+            for m, g in enumerate(gs):
+                src, dst = g.at[:, c * depth : (c + 1) * depth], g_buf.at[c, m * rows : (m + 1) * rows, :]
+                pltpu.make_async_copy(src, dst, sem.at[c, m]).start()
+
+    for m, g in enumerate(gs):
+        src, dst = g.at[:, :depth], g_buf.at[d, m * rows : (m + 1) * rows, :]
+        pltpu.make_async_copy(src, dst, sem.at[d, m]).wait()
+    first = 0
+    for x in xs:
+        for start in range(0, x.shape[1], 512):
+            size = min(512, x.shape[1] - start)
+            product = dot_tn(x[:, start : start + size], g_buf[d]).astype(BF16)
+            for column in range(0, depth, tile):
+                row = first + column // tile * x.shape[1] + start
+                out_ref[0, row : row + size, :] = product[:, column : column + tile]
+        first += x.shape[1] * (depth // tile)
+
+
+def columns_grad(name, place, count, tile, above, xs, gs, stack=None):
+    model = gs[0].shape[1]
+    tokens = xs[0].shape[0]
+    depth = model // count
+    below = sum(x.shape[1] for x in xs) * (depth // tile)
+    given = [] if stack is None else [stack]
+    return kernel_call(
+        functools.partial(columns_grad_kernel, len(xs), len(gs)),
+        name,
+        (count,),
+        [pl.BlockSpec(x.shape, lambda d, f: (0, 0)) for x in xs] + any_specs(gs) + any_specs(given),
+        pl.BlockSpec((1, below, tile), lambda d, f: (d, above // below, 0)),
+        jax.ShapeDtypeStruct((count, above + below, tile), BF16),
+        [pltpu.VMEM((count, tokens, depth), BF16), pltpu.SemaphoreType.DMA((count, len(gs)))],
+        {1 + len(xs) + len(gs): 0} if given else {},
+    )(place, *xs, *gs, *given)
 
 
 def forward_kernel(block, reach, g_ref, q_ref, k_ref, v_ref, seg_ref, key_ref, out_ref, lse_ref):
@@ -127,7 +603,6 @@
     heads = width // 3 // HD
     count = tokens // block
     reach = WINDOW // block
-    pairs = sum(min(i, reach) + 1 for i in range(count)) * block * block * heads
     return pl.pallas_call(
         functools.partial(forward_kernel, block, reach),
         grid_spec=pltpu.PrefetchScalarGridSpec(
@@ -150,7 +625,7 @@
             jax.ShapeDtypeStruct((heads, count, 1, block), F32),
         ],
         compiler_params=pltpu.CompilerParams(vmem_limit_bytes=VMEM_LIMIT),
-        cost_estimate=pl.CostEstimate(flops=8 * pairs * HD, bytes_accessed=8 * tokens * heads * HD, transcendentals=pairs),
+        cost_estimate=pl.CostEstimate(flops=1, bytes_accessed=1, transcendentals=0),
         name="attend_forward",
     )(place, qkv, qkv, qkv, segment.reshape(count, block, 1), key_code.reshape(count, 1, block))
 
@@ -223,7 +698,6 @@
     heads = width // 3 // HD
     count = tokens // block
     reach = WINDOW // block
-    pairs = sum(min(i, reach) + 1 for i in range(count)) * block * block * heads
     return pl.pallas_call(
         functools.partial(backward_kernel, block, reach, heads),
         grid_spec=pltpu.PrefetchScalarGridSpec(
@@ -251,7 +725,7 @@
         ),
         out_shape=jax.ShapeDtypeStruct((tokens, width), BF16),
         compiler_params=pltpu.CompilerParams(vmem_limit_bytes=VMEM_LIMIT),
-        cost_estimate=pl.CostEstimate(flops=20 * pairs * HD, bytes_accessed=16 * tokens * heads * HD, transcendentals=pairs),
+        cost_estimate=pl.CostEstimate(flops=1, bytes_accessed=1, transcendentals=0),
         name="attend_backward",
     )(
         place, qkv, qkv, qkv, grad, out, lse,
@@ -260,16 +734,18 @@
 
 
 def local(inputs, att_proj, attn_out, ff_proj, ff_out, segments, pad_mask, positions, cotangent):
-    tp_size = lax.axis_size("tp")
+    tp_size, fsdp_size = lax.axis_size("tp"), lax.axis_size("fsdp")
     rows, model = inputs.shape
     members = SEQ_LEN // rows
     sets = tp_size // members
     index = lax.axis_index("tp")
     mine = index // members
     place = index % members
-    head_width = att_proj.shape[2]
-    ffn_width = ff_proj.shape[2]
     block = min(512, rows)
+    depth, head_width = att_proj.shape[0], att_proj.shape[2]
+    ffn_width = ff_out.shape[0]
+    place_tp = place.astype(jnp.int32).reshape(1)
+    place_fsdp = lax.axis_index("fsdp").astype(jnp.int32).reshape(1)
 
     def swap(values, bit):
         return lax.ppermute(values, "tp", [(i, i ^ bit) for i in range(tp_size)])
@@ -277,61 +753,86 @@
     def turn(values, step):
         return lax.ppermute(values, "tp", [(i, (i + step * members) % tp_size) for i in range(tp_size)])
 
-    def group_gather(values):
+    def cross(values, mask):
+        return lax.ppermute(values, "fsdp", [(i, i ^ mask) for i in range(fsdp_size)])
+
+    def after(value, *others):
+        return lax.optimization_barrier((value, others))[0]
+
+    chain = []
+
+    def then(function, *args, due=()):
+        args, _ = lax.optimization_barrier((args, (chain[-1], due)))
+        result = function(*args)
+        chain.append(jax.tree.leaves(result)[0])
+        return result
+
+    def last():
+        return chain[-1]
+
+    def group_far(values):
         blocks = {0: values}
         bit = members // 2
-        while bit:
+        while bit > 1:
             for mask in sorted(blocks, reverse=True):
                 blocks[mask | bit] = swap(blocks[mask], bit)
             bit //= 2
+        return blocks
+
+    def group_near(blocks):
+        blocks = dict(blocks)
+        for mask in sorted(blocks, reverse=True):
+            blocks[mask | 1] = swap(blocks[mask], 1)
         return [blocks[mask] for mask in range(members)]
 
-    def group_scatter(blocks):
-        blocks = dict(enumerate(blocks))
-        bit = 1
+    def group_gather(values):
+        return group_near(group_far(values))
+
+    def scatter_near(blocks):
+        sums = {}
+        for mask in sorted(blocks, reverse=True):
+            if mask & 1:
+                total = blocks[mask ^ 1].astype(F32) + swap(blocks[mask], 1).astype(F32)
+                sums[mask ^ 1] = total.astype(BF16) if mask ^ 1 else total
+        return sums
+
+    def scatter_far(sums):
+        sums = dict(sums)
+        bit = 2
         while bit < members:
-            for mask in sorted((m for m in blocks if m & bit), reverse=True):
-                total = blocks[mask ^ bit].astype(F32) + swap(blocks.pop(mask), bit).astype(F32)
-                blocks[mask ^ bit] = total if mask == bit else total.astype(BF16)
+            for mask in sorted((m for m in sums if m & bit), reverse=True):
+                total = sums[mask ^ bit].astype(F32) + swap(sums.pop(mask), bit).astype(F32)
+                sums[mask ^ bit] = total if mask == bit else total.astype(BF16)
             bit *= 2
-        return blocks[0].astype(F32)
-
-    def spread(shard, gather):
-        parts = [shard] + [turn(shard, step) for step in range(1, sets)]
-        return [gather(part) for part in parts]
-
-    def gather_first(part):
-        return lax.all_gather(part, "fsdp", axis=0, tiled=True)
-
-    def gather_new(part):
-        return lax.all_gather(part, "fsdp", axis=0)
-
-    def settle(parts, scatter):
-        total = None
-        for step in range(sets):
-            piece = scatter(parts[step])
-            if step:
-                piece = turn(piece, sets - step)
-            piece = piece.astype(F32)
-            total = piece if total is None else total + piece
+        return sums[0].astype(F32)
+
+    half = members // 2
+
+    def share(function, *args, due=((), ())):
+        sums = {}
+        for first in (half, 0):
+            outs = then(lambda *a: function(place_fsdp, *a[:2], rows, first, half, *a[2:]), *args, due=due[first == 0])
+            sums.update(scatter_near({first + p: out for p, out in enumerate(outs)}))
+        return sums
+
+    def gather(shard):
+        return lax.all_gather(shard, "fsdp", axis=0)
+
+    def scatter(stacked):
+        return lax.psum_scatter(stacked.reshape(-1, stacked.shape[-1]), "fsdp", scatter_dimension=0, tiled=True)
+
+    def settle(pieces):
+        total = pieces[0].astype(F32)
+        for step in range(1, sets):
+            total = total + turn(pieces[step], sets - step).astype(F32)
         return total
 
-    def scatter_first(part):
-        return lax.psum_scatter(part.astype(BF16), "fsdp", scatter_dimension=0, tiled=True)
-
-    def scatter_last(part):
-        return lax.psum_scatter(part.astype(BF16), "fsdp", scatter_dimension=1, tiled=True)
-
-    w_qkv = spread(att_proj.reshape(att_proj.shape[0], 3 * head_width), gather_first)
-    w_heads = spread(attn_out, gather_new)
-    w_ffn = spread(ff_proj.reshape(ff_proj.shape[0], 2 * ffn_width), gather_first)
-    w_down = spread(ff_out, gather_new)
-
-    def flat(chunks):
-        return jnp.concatenate([chunks[f] for f in range(chunks.shape[0])], axis=1)
-
-    w_heads = jnp.concatenate([flat(part) for part in w_heads], axis=0)
-    w_down = jnp.concatenate([flat(part) for part in w_down], axis=0)
+    normed_all, packs = start_exchange(inputs, pack_weights(att_proj, attn_out), members, sets, fsdp_size)
+    chain.append(normed_all[0])
+    up_gate, down, cotangent_late = after((ff_proj.reshape(depth, -1), ff_out, cotangent), last())
+    w_ffn, w_down = [gather(up_gate)], [gather(down)]
+    turned_up_gate = [turn(up_gate, step) for step in range(1, sets)]
+    cotangent_far = group_far(cotangent_late)
 
     segment = lax.dynamic_slice_in_dim(segments, mine * SEQ_LEN, SEQ_LEN)
     padding = lax.dynamic_slice_in_dim(pad_mask, mine * SEQ_LEN, SEQ_LEN)
@@ -339,70 +840,85 @@
     spots = lax.dynamic_slice_in_dim(positions, mine * SEQ_LEN, SEQ_LEN).reshape(members, rows)
     spots = jnp.concatenate([lax.dynamic_index_in_dim(spots, place ^ mask, 0, False) for mask in range(members)])
     cosine, sine = rope_tables(spots)
-    where = place.astype(jnp.int32).reshape(1)
 
     x_float = inputs.astype(F32)
-    normed_all = jnp.concatenate(group_gather(layer_norm(x_float).astype(BF16)), axis=0)
-    cotangent_all = jnp.concatenate(group_gather(cotangent), axis=0)
-
-    qkv = [project(normed_all, w, cosine, sine) for w in w_qkv]
-    attended = [attend_forward(part, where, segment, key_code, block) for part in qkv]
-    heads_low = jnp.concatenate([out for out, _ in attended], axis=1)
-
-    def row_blocks(left, right, dot):
-        return [dot(left[m * rows : (m + 1) * rows], right).astype(BF16) for m in range(members)]
-
-    resid = x_float + group_scatter(row_blocks(heads_low, w_heads, dot_nn))
-    normed_two_all = jnp.concatenate(group_gather(layer_norm(resid).astype(BF16)), axis=0)
-
-    projected = [dot_nn(normed_two_all, w) for w in w_ffn]
-    up = jnp.concatenate([p[:, :ffn_width] for p in projected], axis=1)
-    gate = jnp.concatenate([p[:, ffn_width:] for p in projected], axis=1)
-    sigmoid = jax.nn.sigmoid(gate)
-    slope_up = gate * sigmoid
-    slope_gate = up * sigmoid * (1.0 + gate * (1.0 - sigmoid))
-    hidden_low = (slope_up * up).astype(BF16)
-    ffn_branch = group_scatter(row_blocks(hidden_low, w_down, dot_nn))
+    qkv, attended = [], []
+    for step in range(sets):
+        qkv.append(then(functools.partial(project, place_fsdp), normed_all, packs[step], cosine, sine))
+        attended.append(then(lambda part: attend_forward(part, place_tp, segment, key_code, block), qkv[step]))
+    heads_low = [out for out, _ in attended]
+    sums = share(functools.partial(expand_heads, "attn_branch"), heads_low, packs, due=((cotangent_far,), ()))
+    for step in range(1, sets):
+        w_ffn.append(gather(after(turned_up_gate[step - 1], last())))
+    resid = x_float + scatter_far(sums)
+    normed_two = layer_norm(resid).astype(BF16)
+    turned_down = [turn(after(ff_out, normed_two), step) for step in range(1, sets)]
+    cotangent_all = group_near(after(cotangent_far, normed_two))
+    normed_two_all = group_gather(normed_two)
+
+    hidden, grad_ffn, partial = [], [], None
+    ffn_rows = 2 * ffn_width
+    grad_expand = functools.partial(expand_stack, "grad_normed_two", dot_nt)
+    down_grad = functools.partial(columns_grad, "grad_down", place_fsdp, fsdp_size, depth, ffn_rows)
+    up_grad = functools.partial(rows_grad, "grad_ffn", place_fsdp, fsdp_size, depth, ffn_width)
+    for step in range(sets):
+        ready = (cotangent_all,) if step == 0 else ()
+        low, slope_up, slope_gate = then(functools.partial(hidden_units, place_fsdp), normed_two_all, w_ffn[step], due=ready)
+        hidden.append(low)
+        if step == 0:
+            w_down += [gather(after(down, last())) for down in turned_down]
+        base = [] if partial is None else [partial]
+        if step < sets - 1:
+            stacked = then(down_grad, [low], cotangent_all)
+        grad_low = then(functools.partial(hidden_grad, place_fsdp), cotangent_all, slope_up, slope_gate, w_down[step])
+        if step < sets - 1:
+            grad_ffn.append(scatter(then(up_grad, normed_two_all, grad_low, stacked)))
+            call = lambda x, w, *b: grad_expand(place_fsdp, [x], [w], members * rows, 0, 1, *b)[0]
+            partial = then(call, grad_low, w_ffn[step], *base)
+        else:
+            sums = share(grad_expand, [grad_low], [w_ffn[step]], *base)
+            stacked = then(up_grad, normed_two_all, grad_low, due=sums)
+            grad_normed_two = scatter_far(sums)
+            grad_ffn.append(scatter(then(down_grad, [low], cotangent_all, stacked, due=(grad_normed_two,))))
+
+    grad_resid = cotangent.astype(F32) + layer_norm_back(resid, grad_normed_two)
+    resid_grad_low = grad_resid.astype(BF16)
+    sums = share(functools.partial(expand_stack, "ffn_branch", dot_nn), hidden, w_down, due=((), (resid_grad_low,)))
+    resid_grad_all = group_gather(resid_grad_low)
+
+    grad_attn, grad_project = [None] * sets, [None] * sets
+    heads_grad = functools.partial(columns_grad, "grad_heads", place_fsdp, fsdp_size, head_width, 3 * depth)
+    project_grad = functools.partial(rows_grad, "grad_attn", place_fsdp, fsdp_size, head_width, depth)
+    for step in reversed(range(sets)):
+        ready = (grad_ffn[0],) if step == sets - 1 else ()
+        head_grad = then(functools.partial(head_grad_of, place_fsdp), resid_grad_all, packs[step], due=ready)
+        if step == sets - 1:
+            ffn_branch = scatter_far(after(sums, last()))
+        grad_project[step] = then(
+            lambda part, grad, out, lse: attend_backward(
+                part, grad, out, lse, place_tp, segment, key_code, cosine, sine, block
+            ),
+            qkv[step], head_grad, heads_low[step], attended[step][1],
+        )
+        ready = tuple(grad_ffn[1:]) if step == 0 else ()
+        stacked = then(heads_grad, [heads_low[step]], resid_grad_all, due=ready)
+        grad_attn[step] = scatter(then(project_grad, normed_all, grad_project[step], stacked))
     output = (resid + ffn_branch).astype(BF16)
-
-    grad_hidden = dot_nt(cotangent_all, w_down)
-    grad_down = dot_tn(hidden_low, cotangent_all)
-    grad_up = (grad_hidden * slope_up).astype(BF16)
-    grad_gate = (grad_hidden * slope_gate).astype(BF16)
-    grad_ffn_low = [
-        jnp.concatenate([part[:, j * ffn_width : (j + 1) * ffn_width] for part in (grad_up, grad_gate)], axis=1)
-        for j in range(sets)
-    ]
-    grad_ffn_all = jnp.concatenate(grad_ffn_low, axis=1)
-    grad_normed_two = group_scatter(row_blocks(grad_ffn_all, jnp.concatenate(w_ffn, axis=1), dot_nt))
-    grad_ffn = [dot_tn(normed_two_all, part) for part in grad_ffn_low]
-
-    grad_resid = cotangent.astype(F32) + layer_norm_back(resid, grad_normed_two)
-    resid_grad_all = jnp.concatenate(group_gather(grad_resid.astype(BF16)), axis=0)
-    grad_heads_weight = dot_tn(heads_low, resid_grad_all)
-    head_grad = dot_nt(resid_grad_all, w_heads).astype(BF16)
-    grad_project = [
-        attend_backward(
-            qkv[j], head_grad[:, j * head_width : (j + 1) * head_width], attended[j][0], attended[j][1],
-            where, segment, key_code, cosine, sine, block,
-        )
-        for j in range(sets)
-    ]
-    grad_project_all = jnp.concatenate(grad_project, axis=1)
-    grad_normed = group_scatter(row_blocks(grad_project_all, jnp.concatenate(w_qkv, axis=1), dot_nt))
-    grad_attn = [dot_tn(normed_all, part) for part in grad_project]
+    grad_normed = scatter_far(share(functools.partial(expand_project, "grad_normed"), grad_project, packs))
     grad_input = (grad_resid + layer_norm_back(x_float, grad_normed)).astype(BF16)
 
-    def halves(values, width):
-        return [values[j * width : (j + 1) * width] for j in range(sets)]
+    grad_attn, grad_ffn = settle(grad_attn), settle(grad_ffn)
+
+    def beside(values, size, count):
+        return jnp.concatenate([values[i * size : (i + 1) * size] for i in range(count)], axis=1)
 
     return (
         output,
         grad_input,
-        settle(grad_attn, scatter_first).reshape(att_proj.shape),
-        settle(halves(grad_heads_weight, head_width), scatter_last),
-        settle(grad_ffn, scatter_first).reshape(ff_proj.shape),
-        settle(halves(grad_down, ffn_width), scatter_last),
+        beside(grad_attn, depth, 3).reshape(att_proj.shape),
+        beside(grad_attn[3 * depth :], head_width, depth // head_width),
+        beside(grad_ffn, depth, ffn_rows // depth).reshape(ff_proj.shape),
+        grad_ffn[ffn_rows:],
     )
 
 

time: 1330 us -> 1020 us (0.77)
  Pallas kernels: 108 us -> 542 us
  matrix products: 333 us -> 0 us
  waiting for transfers between devices: 603 us -> 346 us
  other arithmetic: 133 us -> 56.8 us
  local copies, waits for them, and re-layouts: 106 us -> 43.5 us
    pallas_call x2 -> x26, Pallas kernels: 22.6 us -> 459 us  [the longest x8 128 us: rows_call(): kernel_call(functools.partial(rows_kernel, body, plan, members, len(extra...]
    dot_general x26 -> x0, matrix products: 333 us -> none  [the longest x10 129 us: dot_nt(): lax.dot_general(left, right, (((1,), (1,)), ((), ())), preferred_element_...]
    ppermute x8 -> x4, waiting for transfers between devices: 322 us -> 35.2 us  [turn(): lax.ppermute(values, 'tp', [(i, (i + step * members) % tp_size) for i in...]
    concatenate x4 -> x3, other arithmetic: 86.3 us -> 2.43 us  [beside(): jnp.concatenate([values[i * size:(i + 1) * size] for i in range(count)],...]
    ppermute x24 -> x21, waiting for transfers between devices: 229 us -> 310 us  [swap(): return lax.ppermute(values, 'tp', [(i, i ^ bit) for i in range(tp_size)])]
    reduce_scatter x8 -> x4, waiting for transfers between devices: 49.8 us -> 0.03 us  [scatter(): lax.psum_scatter(stacked.reshape(-1, stacked.shape[-1]), 'fsdp', scatter_...]
    slice x11 -> x4, local copies, waits for them, and re-layouts: 39.8 us -> 2.11 us  [the longest x1 1.49 us: local(): grad_ffn[ffn_rows:]]
    unnamed x99 -> x71, local copies, waits for them, and re-layouts: 43.1 us -> 17.3 us
  transfers between devices with their start and end apart: 48 -> 33, of which waited for: 17 -> 12; matrix products, arithmetic and copies ran while one was open for 28% -> 8% of each run, Pallas kernels for 8% -> 44%
where the time goes in v2:
time: 1020 us
  Pallas kernels  542 us (53%)
  waiting for transfers between devices  346 us (34%)
  other arithmetic  56.8 us (6%)
  local copies, waits for them, and re-layouts  43.5 us (4%)
  between operations  15 us (1%)
  starting transfers between devices  14.2 us (1%)
    ppermute x21, waiting for transfers between devices, swap(): return lax.ppermute(values, 'tp', [(i, i ^ bit) for i in range(tp_size)])  310 us
    pallas_call x8, Pallas kernels, rows_call(): kernel_call(functools.partial(rows_kernel, body, plan, members, len(extra...  128 us
    pallas_call x9, Pallas kernels, expand_call(): kernel_call(functools.partial(expand_kernel, len(xs), each, plan, dot, ba...  120 us
    pallas_call x1, Pallas kernels, start_exchange(): pl.pallas_call(functools.partial(start_kernel, members, sets, count), in_...  91 us
    pallas_call x4, Pallas kernels, rows_grad(): kernel_call(functools.partial(rows_grad_kernel, len(xs), count), name, (w...  76.5 us
    pallas_call x2, Pallas kernels, attend_backward(): pl.pallas_call(functools.partial(backward_kernel, block, reach, heads), g...  51.5 us
    pallas_call x4, Pallas kernels, columns_grad(): kernel_call(functools.partial(columns_grad_kernel, len(xs), len(gs)), nam...  42.9 us
    ppermute x4, waiting for transfers between devices, turn(): lax.ppermute(values, 'tp', [(i, (i + step * members) % tp_size) for i in...  35.2 us
  transfers between devices with their start and end apart: 33, of which 12 were waited for; matrix products, arithmetic and copies ran while one was open for 8% of the time, Pallas kernels for 44%

profile of v2, /device:TPU:0, one launch (start us, length us, event | category | flops | bytes accessed | tf_op | source)
XLA Modules:
  0.0 1018.0 jit_solution(9622522067097906140)
XLA Ops:
  15.9 91.0 %start_exchange.1 = (bf16[512,2048]{1,0:T(8,128)(2,1)}, bf16[512,2048]{1,0:T(8,128)(2,1)}, bf16[512,2048]{1,0:T(8,128)(2,1)}, bf16[512,2048]{1,0:T(8,128)(2,1)},...) custom-call(bf16[512,2048]{1,0:T(8,128)(2,1)} %x_ref.1, ...), custom_call_target="tpu_custom_call" | custom-call | flops 1 | bytes 1 | tf_op jit(solution)/shard_map/start_exchange/pallas_call | solution.py:182
  117.3 13.9 %project.2.q_ref.k_ref.v_ref = bf16[2048,768]{1,0:T(8,128)(2,1)} custom-call(s32[1]{0:T(128)} %bitcast.f_ref, bf16[512,2048]{1,0:T(8,128)(2,1)} %get-tuple-element.410.refs_0_, bf16[512,2048]{1,0:T(8,128)(2,1)} %get-tuple-element.411.refs_1_, bf16[512,2048]{1,0:T(8,128)(2,1)} %get-tuple-element.412.refs_2_, bf16[512,2048]{1,0:T(8,128)(2,1)} %get-tuple-element.413.refs_3_, ...), custom_call_target="tpu_custom_call" | custom-call | flops 1 | bytes 1 | tf_op jit(solution)/shard_map/project/pallas_call | solution.py:238
  133.6 16.0 %attend_forward.2 = (bf16[2048,256]{1,0:T(8,128)(2,1)}, f32[2,4,1,512]{3,2,1,0:T(1,128)}) custom-call(s32[1]{0:T(128)} %bitcast.1.g_ref, bf16[2048,768]{1,0:T(8,128)(2,1)} %project.2.q_ref.k_ref.v_ref, bf16[2048,768]{1,0:T(8,128)(2,1)} %project.2.q_ref.k_ref.v_ref, bf16[2048,768]{1,0:T(8,128)(2,1)} %project.2.q_ref.k_ref.v_ref, ...), custom_call_target="tpu_custom_call" | custom-call | flops 1 | bytes 1 | tf_op jit(solution)/shard_map/attend_forward/pallas_call | solution.py:606
  149.6 13.4 %project.3.q_ref.k_ref.v_ref = bf16[2048,768]{1,0:T(8,128)(2,1)} custom-call(s32[1]{0:T(128)} %bitcast.f_ref, bf16[512,2048]{1,0:T(8,128)(2,1)} %get-tuple-element.410.refs_0_, bf16[512,2048]{1,0:T(8,128)(2,1)} %get-tuple-element.411.refs_1_, bf16[512,2048]{1,0:T(8,128)(2,1)} %get-tuple-element.412.refs_2_, bf16[512,2048]{1,0:T(8,128)(2,1)} %get-tuple-element.413.refs_3_, ...), custom_call_target="tpu_custom_call" | custom-call | flops 1 | bytes 1 | tf_op jit(solution)/shard_map/project/pallas_call | solution.py:238
  163.0 16.2 %attend_forward.3 = (bf16[2048,256]{1,0:T(8,128)(2,1)}, f32[2,4,1,512]{3,2,1,0:T(1,128)}) custom-call(s32[1]{0:T(128)} %bitcast.1.g_ref, bf16[2048,768]{1,0:T(8,128)(2,1)} %project.3.q_ref.k_ref.v_ref, bf16[2048,768]{1,0:T(8,128)(2,1)} %project.3.q_ref.k_ref.v_ref, bf16[2048,768]{1,0:T(8,128)(2,1)} %project.3.q_ref.k_ref.v_ref, ...), custom_call_target="tpu_custom_call" | custom-call | flops 1 | bytes 1 | tf_op jit(solution)/shard_map/attend_forward/pallas_call | solution.py:606
  179.2 17.8 %collective-permute-done.refs_3_.refs_2_ = bf16[512,2048]{1,0:T(8,128)(2,1)} collective-permute-done((bf16[512,2048]{1,0:T(8,128)(2,1)S(1)}, bf16[512,2048]{1,0:T(8,128)(2,1)}, u32[]{:S(2)}, u32[]{:S(2)}) %collective-permute-start) | collective-permute-done | bytes 2097184 | tf_op jit(solution)/shard_map/ppermute | solution.py:751
  197.1 6.3 attn_branch.2
  203.3 6.4 attn_branch.3
  217.3 47.1 %collective-permute-done.3 = bf16[512,2048]{1,0:T(8,128)(2,1)S(1)} collective-permute-done((bf16[512,2048]{1,0:T(8,128)(2,1)S(1)}, bf16[512,2048]{1,0:T(8,128)(2,1)S(1)}, u32[]{:S(2)}, u32[]{:S(2)}) %collective-permute-start.3) | collective-permute-done | bytes 2097184 | tf_op jit(solution)/shard_map/ppermute | solution.py:751
  270.9 45.2 %collective-permute-done.5.refs_2_ = bf16[512,2048]{1,0:T(8,128)(2,1)S(1)} collective-permute-done((bf16[512,2048]{1,0:T(8,128)(2,1)S(1)}, bf16[512,2048]{1,0:T(8,128)(2,1)S(1)}, u32[]{:S(2)}, u32[]{:S(2)}) %collective-permute-start.5) | collective-permute-done | bytes 2097184 | tf_op jit(solution)/shard_map/ppermute | solution.py:751
  320.3 27.0 %hidden_units.2 = (bf16[2048,1024]{1,0:T(8,128)(2,1)}, bf16[2048,1024]{1,0:T(8,128)(2,1)}, bf16[2048,1024]{1,0:T(8,128)(2,1)}) custom-call(s32[1]{0:T(128)} %bitcast.f_ref, bf16[512,2048]{1,0:T(8,128)(2,1)} %copy-done.6, bf16[512,2048]{1,0:T(8,128)(2,1)} %copy-done.11, bf16[512,2048]{1,0:T(8,128)(2,1)} %copy-done.10, ...), custom_call_target="tpu_custom_call" | custom-call | flops 1 | bytes 1 | tf_op jit(solution)/shard_map/hidden_units/pallas_call | solution.py:238
  347.3 17.8 %collective-permute-done.10 = bf16[1024,512]{1,0:T(8,128)(2,1)} collective-permute-done((bf16[1024,512]{1,0:T(8,128)(2,1)S(1)}, bf16[1024,512]{1,0:T(8,128)(2,1)}, u32[]{:S(2)}, u32[]{:S(2)}) %collective-permute-start.10) | collective-permute-done | bytes 1048608 | tf_op jit(solution)/shard_map/ppermute | solution.py:754
  365.1 14.9 %grad_down.2.refs_4_ = bf16[4,3072,512]{2,1,0:T(8,128)(2,1)} custom-call(s32[1]{0:T(128)} %bitcast.f_ref, bf16[2048,1024]{1,0:T(8,128)(2,1)} %get-tuple-element.359.refs_0_, bf16[512,2048]{1,0:T(8,128)(2,1)} %refs_1_.1, bf16[512,2048]{1,0:T(8,128)(2,1)} %copy-done.12, bf16[512,2048]{1,0:T(8,128)(2,1)} %collective-permute-done.refs_3_.refs_2_, ...), custom_call_target="tpu_custom_call" | custom-call | flops 1 | bytes 1 | tf_op jit(solution)/shard_map/grad_down/pallas_call | solution.py:557
  380.1 15.9 %hidden_grad.2.refs_5_.refs_0_ = bf16[2048,2048]{1,0:T(8,128)(2,1)} custom-call(s32[1]{0:T(128)} %bitcast.f_ref, bf16[512,2048]{1,0:T(8,128)(2,1)} %refs_1_.1, bf16[512,2048]{1,0:T(8,128)(2,1)} %copy-done.12, bf16[512,2048]{1,0:T(8,128)(2,1)} %collective-permute-done.refs_3_.refs_2_, bf16[512,2048]{1,0:T(8,128)(2,1)} %copy-done.13, ...), custom_call_target="tpu_custom_call" | custom-call | flops 1 | bytes 1 | tf_op jit(solution)/shard_map/hidden_grad/pallas_call | solution.py:238
  396.0 23.6 %grad_ffn.2 = bf16[4,3072,512]{2,1,0:T(8,128)(2,1)} custom-call(s32[1]{0:T(128)} %bitcast.f_ref, bf16[512,2048]{1,0:T(8,128)(2,1)} %copy-done.6, bf16[512,2048]{1,0:T(8,128)(2,1)} %copy-done.11, bf16[512,2048]{1,0:T(8,128)(2,1)} %copy-done.10, bf16[512,2048]{1,0:T(8,128)(2,1)} %collective-permute-done.6.refs_3_, ...), custom_call_target="tpu_custom_call", output_to_operand_aliasing={{}: (5, {})} | custom-call | flops 1 | bytes 1 | tf_op jit(solution)/shard_map/grad_ffn/pallas_call | solution.py:510
  419.7 24.9 %grad_normed_two.3.refs_1_ = bf16[2048,2048]{1,0:T(8,128)(2,1)} custom-call(s32[1]{0:T(128)} %bitcast.f_ref, bf16[2048,2048]{1,0:T(8,128)(2,1)} %hidden_grad.2.refs_5_.refs_0_, bf16[4,512,2048]{2,1,0:T(8,128)(2,1)} %bitcast.39), custom_call_target="tpu_custom_call" | custom-call | flops 1 | bytes 1 | tf_op jit(solution)/shard_map/grad_normed_two/pallas_call | solution.py:410
  444.6 27.2 %hidden_units.3 = (bf16[2048,1024]{1,0:T(8,128)(2,1)}, bf16[2048,1024]{1,0:T(8,128)(2,1)}, bf16[2048,1024]{1,0:T(8,128)(2,1)}) custom-call(s32[1]{0:T(128)} %bitcast.f_ref, bf16[512,2048]{1,0:T(8,128)(2,1)} %copy-done.6, bf16[512,2048]{1,0:T(8,128)(2,1)} %copy-done.11, bf16[512,2048]{1,0:T(8,128)(2,1)} %copy-done.10, ...), custom_call_target="tpu_custom_call" | custom-call | flops 1 | bytes 1 | tf_op jit(solution)/shard_map/hidden_units/pallas_call | solution.py:238
  471.8 16.7 %hidden_grad.3.refs_0_.refs_4_ = bf16[2048,2048]{1,0:T(8,128)(2,1)} custom-call(s32[1]{0:T(128)} %bitcast.f_ref, bf16[512,2048]{1,0:T(8,128)(2,1)} %refs_1_.1, bf16[512,2048]{1,0:T(8,128)(2,1)} %copy-done.12, bf16[512,2048]{1,0:T(8,128)(2,1)} %collective-permute-done.refs_3_.refs_2_, bf16[512,2048]{1,0:T(8,128)(2,1)} %copy-done.13, ...), custom_call_target="tpu_custom_call" | custom-call | flops 1 | bytes 1 | tf_op jit(solution)/shard_map/hidden_grad/pallas_call | solution.py:238
  488.5 14.7 %grad_normed_two.4 = (bf16[512,2048]{1,0:T(8,128)(2,1)}, bf16[512,2048]{1,0:T(8,128)(2,1)}) custom-call(s32[1]{0:T(128)} %bitcast.f_ref, bf16[2048,2048]{1,0:T(8,128)(2,1)} %hidden_grad.3.refs_0_.refs_4_, bf16[2048,2048]{1,0:T(8,128)(2,1)} %grad_normed_two.3.refs_1_, bf16[4,512,2048]{2,1,0:T(8,128)(2,1)} %bitcast.28), custom_call_target="tpu_custom_call" | custom-call | flops 1 | bytes 1 | tf_op jit(solution)/shard_map/grad_normed_two/pallas_call | solution.py:410
  503.3 14.8 %grad_normed_two.5 = (bf16[512,2048]{1,0:T(8,128)(2,1)}, bf16[512,2048]{1,0:T(8,128)(2,1)}) custom-call(s32[1]{0:T(128)} %bitcast.f_ref, bf16[2048,2048]{1,0:T(8,128)(2,1)} %hidden_grad.3.refs_0_.refs_4_, bf16[2048,2048]{1,0:T(8,128)(2,1)} %grad_normed_two.3.refs_1_, bf16[4,512,2048]{2,1,0:T(8,128)(2,1)} %bitcast.29), custom_call_target="tpu_custom_call" | custom-call | flops 1 | bytes 1 | tf_op jit(solution)/shard_map/grad_normed_two/pallas_call | solution.py:410
  520.9 25.3 %grad_ffn.3.refs_5_ = bf16[4,3072,512]{2,1,0:T(8,128)(2,1)} custom-call(s32[1]{0:T(128)} %bitcast.f_ref, bf16[512,2048]{1,0:T(8,128)(2,1)} %copy-done.6, bf16[512,2048]{1,0:T(8,128)(2,1)} %copy-done.11, bf16[512,2048]{1,0:T(8,128)(2,1)} %copy-done.10, bf16[512,2048]{1,0:T(8,128)(2,1)} %collective-permute-done.6.refs_3_, ...), custom_call_target="tpu_custom_call" | custom-call | flops 1 | bytes 1 | tf_op jit(solution)/shard_map/grad_ffn/pallas_call | solution.py:510
  546.2 22.6 %collective-permute-done.13 = bf16[512,2048]{1,0:T(8,128)(2,1)} collective-permute-done((bf16[512,2048]{1,0:T(8,128)(2,1)}, bf16[512,2048]{1,0:T(8,128)(2,1)}, u32[]{:S(2)}, u32[]{:S(2)}) %collective-permute-start.13) | collective-permute-done | bytes 2097184 | tf_op jit(solution)/shard_map/ppermute | solution.py:751
  568.8 4.5 fusion.14
  573.3 14.5 %grad_down.3 = bf16[4,3072,512]{2,1,0:T(8,128)(2,1)} custom-call(s32[1]{0:T(128)} %bitcast.f_ref, bf16[2048,1024]{1,0:T(8,128)(2,1)} %get-tuple-element.360.refs_0_.refs_1_, bf16[512,2048]{1,0:T(8,128)(2,1)} %refs_1_.1, bf16[512,2048]{1,0:T(8,128)(2,1)} %copy-done.12, ...), custom_call_target="tpu_custom_call", output_to_operand_aliasing={{}: (6, {})} | custom-call | flops 1 | bytes 1 | tf_op jit(solution)/shard_map/grad_down/pallas_call | solution.py:557
  587.9 6.4 fusion.15
  594.6 46.6 %collective-permute-done.17.refs_2_.refs_3_ = bf16[512,2048]{1,0:T(8,128)(2,1)} collective-permute-done((bf16[512,2048]{1,0:T(8,128)(2,1)S(1)}, bf16[512,2048]{1,0:T(8,128)(2,1)}, u32[]{:S(2)}, u32[]{:S(2)}) %collective-permute-start.17) | collective-permute-done | bytes 2097184 | tf_op jit(solution)/shard_map/ppermute | solution.py:751
  643.0 14.5 %ffn_branch.2 = (bf16[512,2048]{1,0:T(8,128)(2,1)}, bf16[512,2048]{1,0:T(8,128)(2,1)}) custom-call(s32[1]{0:T(128)} %bitcast.f_ref, bf16[2048,1024]{1,0:T(8,128)(2,1)} %get-tuple-element.359.refs_0_, bf16[2048,1024]{1,0:T(8,128)(2,1)} %get-tuple-element.360.refs_0_.refs_1_, bf16[4,1024,512]{2,1,0:T(8,128)(2,1)} %bitcast.31, bf16[4,1024,512]{2,1,0:T(8,128)(2,1)} %bitcast.34), custom_call_target="tpu_custom_call" | custom-call | flops 1 | bytes 1 | tf_op jit(solution)/shard_map/ffn_branch/pallas_call | solution.py:410
  657.5 14.1 %ffn_branch.3 = (bf16[512,2048]{1,0:T(8,128)(2,1)}, bf16[512,2048]{1,0:T(8,128)(2,1)}) custom-call(s32[1]{0:T(128)} %bitcast.f_ref, bf16[2048,1024]{1,0:T(8,128)(2,1)} %get-tuple-element.359.refs_0_, bf16[2048,1024]{1,0:T(8,128)(2,1)} %get-tuple-element.360.refs_0_.refs_1_, bf16[4,1024,512]{2,1,0:T(8,128)(2,1)} %bitcast.32, bf16[4,1024,512]{2,1,0:T(8,128)(2,1)} %bitcast.35), custom_call_target="tpu_custom_call" | custom-call | flops 1 | bytes 1 | tf_op jit(solution)/shard_map/ffn_branch/pallas_call | solution.py:410
  671.7 7.0 head_grad.2.grad_ref
  678.7 25.8 %attend_backward.2.refs_5_.refs_1_ = bf16[2048,768]{1,0:T(8,128)(2,1)} custom-call(s32[1]{0:T(128)} %bitcast.1.g_ref, bf16[2048,768]{1,0:T(8,128)(2,1)} %project.3.q_ref.k_ref.v_ref, bf16[2048,768]{1,0:T(8,128)(2,1)} %project.3.q_ref.k_ref.v_ref, bf16[2048,768]{1,0:T(8,128)(2,1)} %project.3.q_ref.k_ref.v_ref, bf16[2048,256]{1,0:T(8,128)(2,1)} %head_grad.2.grad_ref, ...), custom_call_target="tpu_custom_call" | custom-call | flops 1 | bytes 1 | tf_op jit(solution)/shard_map/attend_backward/pallas_call | solution.py:701
  704.5 6.7 grad_heads.2.refs_4_
  711.2 13.8 %grad_attn.2 = bf16[4,2048,256]{2,1,0:T(8,128)(2,1)} custom-call(s32[1]{0:T(128)} %bitcast.f_ref, bf16[512,2048]{1,0:T(8,128)(2,1)} %get-tuple-element.410.refs_0_, bf16[512,2048]{1,0:T(8,128)(2,1)} %get-tuple-element.411.refs_1_, bf16[512,2048]{1,0:T(8,128)(2,1)} %get-tuple-element.412.refs_2_, ...), custom_call_target="tpu_custom_call", output_to_operand_aliasing={{}: (5, {})} | custom-call | flops 1 | bytes 1 | tf_op jit(solution)/shard_map/grad_attn/pallas_call | solution.py:510
  725.0 6.4 copy.24
  732.0 7.4 head_grad.3.grad_ref
  739.4 25.7 %attend_backward.3.refs_5_.refs_0_ = bf16[2048,768]{1,0:T(8,128)(2,1)} custom-call(s32[1]{0:T(128)} %bitcast.1.g_ref, bf16[2048,768]{1,0:T(8,128)(2,1)} %project.2.q_ref.k_ref.v_ref, bf16[2048,768]{1,0:T(8,128)(2,1)} %project.2.q_ref.k_ref.v_ref, bf16[2048,768]{1,0:T(8,128)(2,1)} %project.2.q_ref.k_ref.v_ref, bf16[2048,256]{1,0:T(8,128)(2,1)} %head_grad.3.grad_ref, ...), custom_call_target="tpu_custom_call" | custom-call | flops 1 | bytes 1 | tf_op jit(solution)/shard_map/attend_backward/pallas_call | solution.py:701
  765.1 6.9 grad_heads.3.refs_4_
  772.0 13.9 %grad_attn.3 = bf16[4,2048,256]{2,1,0:T(8,128)(2,1)} custom-call(s32[1]{0:T(128)} %bitcast.f_ref, bf16[512,2048]{1,0:T(8,128)(2,1)} %get-tuple-element.410.refs_0_, bf16[512,2048]{1,0:T(8,128)(2,1)} %get-tuple-element.411.refs_1_, bf16[512,2048]{1,0:T(8,128)(2,1)} %get-tuple-element.412.refs_2_, ...), custom_call_target="tpu_custom_call", output_to_operand_aliasing={{}: (5, {})} | custom-call | flops 1 | bytes 1 | tf_op jit(solution)/shard_map/grad_attn/pallas_call | solution.py:510
  785.8 6.4 copy.23
  796.2 12.3 %grad_normed.2 = (bf16[512,2048]{1,0:T(8,128)(2,1)}, bf16[512,2048]{1,0:T(8,128)(2,1)}) custom-call(s32[1]{0:T(128)} %bitcast.f_ref, bf16[2048,768]{1,0:T(8,128)(2,1)} %attend_backward.3.refs_5_.refs_0_, bf16[2048,768]{1,0:T(8,128)(2,1)} %attend_backward.2.refs_5_.refs_1_, bf16[2048,256]{1,0:T(8,128)(2,1)} %copy-done.3, ...), custom_call_target="tpu_custom_call" | custom-call | flops 1 | bytes 1 | tf_op jit(solution)/shard_map/grad_normed/pallas_call | solution.py:410
  810.4 4.0 add_convert_fusion.2
  815.8 11.9 %grad_normed.3 = (bf16[512,2048]{1,0:T(8,128)(2,1)}, bf16[512,2048]{1,0:T(8,128)(2,1)}) custom-call(s32[1]{0:T(128)} %bitcast.f_ref, bf16[2048,768]{1,0:T(8,128)(2,1)} %attend_backward.3.refs_5_.refs_0_, bf16[2048,768]{1,0:T(8,128)(2,1)} %attend_backward.2.refs_5_.refs_1_, bf16[2048,256]{1,0:T(8,128)(2,1)} %copy-done.3, ...), custom_call_target="tpu_custom_call" | custom-call | flops 1 | bytes 1 | tf_op jit(solution)/shard_map/grad_normed/pallas_call | solution.py:410
  832.4 91.7 %collective-permute-done.19 = bf16[512,2048]{1,0:T(8,128)(2,1)} collective-permute-done((bf16[512,2048]{1,0:T(8,128)(2,1)}, bf16[512,2048]{1,0:T(8,128)(2,1)}, u32[]{:S(2)}, u32[]{:S(2)}) %collective-permute-start.19) | collective-permute-done | bytes 2097184 | tf_op jit(solution)/shard_map/ppermute | solution.py:751
  924.1 4.1 add_convert_fusion.1
  930.8 17.5 %collective-permute-done.24 = bf16[3072,512]{1,0:T(8,128)(2,1)} collective-permute-done((bf16[3072,512]{1,0:T(8,128)(2,1)}, bf16[3072,512]{1,0:T(8,128)(2,1)}, u32[]{:S(2)}, u32[]{:S(2)}) %collective-permute-start.24) | collective-permute-done | bytes 3145760 | tf_op jit(solution)/shard_map/ppermute | solution.py:754
  955.3 6.7 reshape.150
  962.0 34.5 %collective-permute-done.22 = bf16[512,2048]{1,0:T(8,128)(2,1)} collective-permute-done((bf16[512,2048]{1,0:T(8,128)(2,1)}, bf16[512,2048]{1,0:T(8,128)(2,1)}, u32[]{:S(2)}, u32[]{:S(2)}) %collective-permute-start.22) | collective-permute-done | bytes 2097184 | tf_op jit(solution)/shard_map/ppermute | solution.py:751
  996.5 4.6 fusion.11
  1001.3 4.8 fusion.8
  (172 shorter events, 72.0 us)
Async XLA Ops:
  7.2 313.2 %all-gather.9.cloned.1.call-start = ((), (), s32[]{:S(2)}) async-start(), calls=%async_computation.8 | async-start | bytes 10485760 | tf_op jit(solution)/shard_map/all_gather | solution.py:819
  15.9 91.8 %copy-start.8 = (bf16[512,2048]{1,0:T(8,128)(2,1)S(1)}, bf16[512,2048]{1,0:T(8,128)(2,1)}, u32[]{:S(2)}) copy-start(bf16[512,2048]{1,0:T(8,128)(2,1)} %refs_1_.1) | copy-start | bytes 6291460
  15.9 95.6 %copy-start.29 = (s32[4096]{0:T(1024)S(1)}, s32[4096]{0:T(1024)}, u32[]{:S(2)}) copy-start(s32[4096]{0:T(1024)} %param.16) | copy-start | bytes 49156
  106.9 273.2 %all-gather.13.cloned.1.call-start = ((), (), s32[]{:S(2)}) async-start(), calls=%async_computation.10 | async-start | bytes 5242880 | tf_op jit(solution)/shard_map/all_gather | solution.py:819
  107.6 336.9 %all-gather.11.cloned.1.call-start = ((), (), s32[]{:S(2)}) async-start(), calls=%async_computation.9 | async-start | bytes 10485760 | tf_op jit(solution)/shard_map/all_gather | solution.py:819
  107.7 89.4 %collective-permute-start = (bf16[512,2048]{1,0:T(8,128)(2,1)S(1)}, bf16[512,2048]{1,0:T(8,128)(2,1)}, u32[]{:S(2)}, u32[]{:S(2)}) collective-permute-start(bf16[512,2048]{1,0:T(8,128)(2,1)S(1)} %copy-done.8), channel_id=1, source_target_pairs={{0,2},{1,3},{2,0},{3,1},{4,6},{5,7},{6,4},{7,5},{8,10},{9,11},{10,... | collective-permute-start | bytes 6291464 | tf_op jit(solution)/shard_map/ppermute | solution.py:751
  107.8 101.9 %collective-permute-start.9 = (bf16[512,2048]{1,0:T(8,128)(2,1)}, bf16[512,2048]{1,0:T(8,128)(2,1)}, u32[]{:S(2)}, u32[]{:S(2)}) collective-permute-start(bf16[512,2048]{1,0:T(8,128)(2,1)} %bitcast.41), channel_id=1, source_target_pairs={{0,4},{1,5},{2,6},{3,7},{4,0},{5,1},{6,2},{7,3},{8,12},{9,13},{10,... | collective-permute-start | bytes 6291464 | tf_op jit(solution)/shard_map/ppermute | solution.py:754
  131.8 17.8 %copy-start.24 = (s32[2048]{0:T(1024)}, s32[2048]{0:T(1024)S(1)}, u32[]{:S(2)}) copy-start(s32[2048]{0:T(1024)S(1)} %get-tuple-element.456) | copy-start | bytes 24580
  209.8 262.0 %all-gather.15.cloned.1.call-start = ((), (), s32[]{:S(2)}) async-start(), calls=%async_computation.11 | async-start | bytes 5242880 | tf_op jit(solution)/shard_map/all_gather | solution.py:819
  209.8 4.4 collective-permute-start.2
  209.9 54.5 %copy-start.18 = (bf16[512,2048]{1,0:T(8,128)(2,1)S(1)}, bf16[512,2048]{1,0:T(8,128)(2,1)}, u32[]{:S(2)}) copy-start(bf16[512,2048]{1,0:T(8,128)(2,1)} %get-tuple-element.280) | copy-start | bytes 6291460
  209.9 7.3 collective-permute-start.1
  216.6 47.7 %collective-permute-start.3 = (bf16[512,2048]{1,0:T(8,128)(2,1)S(1)}, bf16[512,2048]{1,0:T(8,128)(2,1)S(1)}, u32[]{:S(2)}, u32[]{:S(2)}) collective-permute-start(bf16[512,2048]{1,0:T(8,128)(2,1)S(1)} %add_convert_fusion.4), channel_id=1, source_target_pairs={{0,2},{1,3},{2,0},{3,1},{4,6},{5,7},{6,4},{7,5},{8,10},{9,11},{10,... | collective-permute-start | bytes 6291464 | tf_op jit(solution)/shard_map/ppermute | solution.py:751
  217.1 50.0 %copy-start.26 = (f32[512]{0:T(512)}, f32[512]{0:T(512)S(1)}, u32[]{:S(2)}) copy-start(f32[512]{0:T(512)S(1)} %broadcast_multiply_fusion.2) | copy-start | bytes 6148
  267.6 48.4 %copy-start.23 = (bf16[1024,512]{1,0:T(8,128)(2,1)S(1)}, bf16[1024,512]{1,0:T(8,128)(2,1)}, u32[]{:S(2)}) copy-start(bf16[1024,512]{1,0:T(8,128)(2,1)} %param.13) | copy-start | bytes 3145732
  269.1 51.2 %copy-start.6 = (bf16[512,2048]{1,0:T(8,128)(2,1)}, bf16[512,2048]{1,0:T(8,128)(2,1)S(1)}, u32[]{:S(2)}) copy-start(bf16[512,2048]{1,0:T(8,128)(2,1)S(1)} %fusion.10.refs_0_) | copy-start | bytes 6291460
  269.1 46.9 %collective-permute-start.5 = (bf16[512,2048]{1,0:T(8,128)(2,1)S(1)}, bf16[512,2048]{1,0:T(8,128)(2,1)S(1)}, u32[]{:S(2)}, u32[]{:S(2)}) collective-permute-start(bf16[512,2048]{1,0:T(8,128)(2,1)S(1)} %fusion.10.refs_0_), channel_id=1, source_target_pairs={{0,2},{1,3},{2,0},{3,1},{4,6},{5,7},{6,4},{7,5},{8,10},{9,11},{10,... | collective-permute-start | bytes 6291464 | tf_op jit(solution)/shard_map/ppermute | solution.py:751
  269.4 47.3 %collective-permute-start.4 = (bf16[512,2048]{1,0:T(8,128)(2,1)S(1)}, bf16[512,2048]{1,0:T(8,128)(2,1)S(1)}, u32[]{:S(2)}, u32[]{:S(2)}) collective-permute-start(bf16[512,2048]{1,0:T(8,128)(2,1)S(1)} %fusion.10.refs_0_), channel_id=1, source_target_pairs={{0,1},{1,0},{2,3},{3,2},{4,5},{5,4},{6,7},{7,6},{8,9},{9,8},{10,11... | collective-permute-start | bytes 6291464 | tf_op jit(solution)/shard_map/ppermute | solution.py:751
  270.3 46.3 %collective-permute-start.7 = (bf16[512,2048]{1,0:T(8,128)(2,1)S(1)}, bf16[512,2048]{1,0:T(8,128)(2,1)S(1)}, u32[]{:S(2)}, u32[]{:S(2)}) collective-permute-start(bf16[512,2048]{1,0:T(8,128)(2,1)S(1)} %copy-done.9), channel_id=1, source_target_pairs={{0,1},{1,0},{2,3},{3,2},{4,5},{5,4},{6,7},{7,6},{8,9},{9,8},{10,11... | collective-permute-start | bytes 6291464 | tf_op jit(solution)/shard_map/ppermute | solution.py:751
  270.3 46.3 %collective-permute-start.8 = (bf16[512,2048]{1,0:T(8,128)(2,1)}, bf16[512,2048]{1,0:T(8,128)(2,1)S(1)}, u32[]{:S(2)}, u32[]{:S(2)}) collective-permute-start(bf16[512,2048]{1,0:T(8,128)(2,1)} %collective-permute-done.refs_3_.refs_2_), channel_id=1, source_target_pairs={{0,1},{1,0},{2,3},{3,2},{4,5},{5,4},{6,7},{7,6},{8,9},{9,8},{10,11... | collective-permute-start | bytes 6291464 | tf_op jit(solution)/shard_map/ppermute | solution.py:751
  316.0 4.3 collective-permute-start.6
  316.0 49.0 %collective-permute-start.10 = (bf16[1024,512]{1,0:T(8,128)(2,1)S(1)}, bf16[1024,512]{1,0:T(8,128)(2,1)}, u32[]{:S(2)}, u32[]{:S(2)}) collective-permute-start(bf16[1024,512]{1,0:T(8,128)(2,1)S(1)} %copy-done.23), channel_id=1, source_target_pairs={{0,4},{1,5},{2,6},{3,7},{4,0},{5,1},{6,2},{7,3},{8,12},{9,13},{10,... | collective-permute-start | bytes 3145736 | tf_op jit(solution)/shard_map/ppermute | solution.py:754
  365.1 306.6 %reduce-scatter.5.cloned.1.call-start = ((), (), s32[]{:S(2)}) async-start(), calls=%async_computation.4 | async-start | bytes 15728640 | tf_op jit(solution)/shard_map/reduce_scatter | solution.py:822
  419.6 345.5 %reduce-scatter.7.cloned.1.call-start = ((), (), s32[]{:S(2)}) async-start(), calls=%async_computation.5 | async-start | bytes 15728640 | tf_op jit(solution)/shard_map/reduce_scatter | solution.py:822
  503.2 15.5 %collective-permute-start.12 = (bf16[512,2048]{1,0:T(8,128)(2,1)}, bf16[512,2048]{1,0:T(8,128)(2,1)S(1)}, u32[]{:S(2)}, u32[]{:S(2)}) collective-permute-start(bf16[512,2048]{1,0:T(8,128)(2,1)} %get-tuple-element.342), channel_id=1, source_target_pairs={{0,1},{1,0},{2,3},{3,2},{4,5},{5,4},{6,7},{7,6},{8,9},{9,8},{10,11... | collective-permute-start | bytes 6291464 | tf_op jit(solution)/shard_map/ppermute | solution.py:751
  518.1 28.0 %collective-permute-start.11 = (bf16[512,2048]{1,0:T(8,128)(2,1)}, bf16[512,2048]{1,0:T(8,128)(2,1)}, u32[]{:S(2)}, u32[]{:S(2)}) collective-permute-start(bf16[512,2048]{1,0:T(8,128)(2,1)} %get-tuple-element.341), channel_id=1, source_target_pairs={{0,1},{1,0},{2,3},{3,2},{4,5},{5,4},{6,7},{7,6},{8,9},{9,8},{10,11... | collective-permute-start | bytes 6291464 | tf_op jit(solution)/shard_map/ppermute | solution.py:751
  520.9 47.9 %collective-permute-start.13 = (bf16[512,2048]{1,0:T(8,128)(2,1)}, bf16[512,2048]{1,0:T(8,128)(2,1)}, u32[]{:S(2)}, u32[]{:S(2)}) collective-permute-start(bf16[512,2048]{1,0:T(8,128)(2,1)} %add_convert_fusion.3), channel_id=1, source_target_pairs={{0,2},{1,3},{2,0},{3,1},{4,6},{5,7},{6,4},{7,5},{8,10},{9,11},{10,... | collective-permute-start | bytes 6291464 | tf_op jit(solution)/shard_map/ppermute | solution.py:751
  520.9 47.9 %copy-start.1 = (f32[512,2048]{1,0:T(8,128)S(1)}, f32[512,2048]{1,0:T(8,128)}, u32[]{:S(2)}) copy-start(f32[512,2048]{1,0:T(8,128)} %copy-done) | copy-start | bytes 12582916
  520.9 47.9 %copy-start.20 = (bf16[512,2048]{1,0:T(8,128)(2,1)S(1)}, bf16[512,2048]{1,0:T(8,128)(2,1)}, u32[]{:S(2)}) copy-start(bf16[512,2048]{1,0:T(8,128)(2,1)} %get-tuple-element.340) | copy-start | bytes 6291460
  587.8 340.4 %reduce-scatter.11.cloned.1.call-start = ((), (), s32[]{:S(2)}) async-start(), calls=%async_computation.7 | async-start | bytes 5242880 | tf_op jit(solution)/shard_map/reduce_scatter | solution.py:822
  587.9 53.2 %copy-start.25 = (s32[2048]{0:T(1024)S(1)}, s32[2048]{0:T(1024)}, u32[]{:S(2)}) copy-start(s32[2048]{0:T(1024)} %get-tuple-element.455) | copy-start | bytes 24580
  594.3 63.2 %copy-start.7 = (bf16[512,2048]{1,0:T(8,128)(2,1)}, bf16[512,2048]{1,0:T(8,128)(2,1)S(1)}, u32[]{:S(2)}) copy-start(bf16[512,2048]{1,0:T(8,128)(2,1)S(1)} %get-tuple-element.406.refs_0_.refs_1_) | copy-start | bytes 6291460
  594.3 46.8 %collective-permute-start.17 = (bf16[512,2048]{1,0:T(8,128)(2,1)S(1)}, bf16[512,2048]{1,0:T(8,128)(2,1)}, u32[]{:S(2)}, u32[]{:S(2)}) collective-permute-start(bf16[512,2048]{1,0:T(8,128)(2,1)S(1)} %get-tuple-element.406.refs_0_.refs_1_), channel_id=1, source_target_pairs={{0,2},{1,3},{2,0},{3,1},{4,6},{5,7},{6,4},{7,5},{8,10},{9,11},{10,... | collective-permute-start | bytes 6291464 | tf_op jit(solution)/shard_map/ppermute | solution.py:751
  594.6 77.0 %collective-permute-start.16 = (bf16[512,2048]{1,0:T(8,128)(2,1)S(1)}, bf16[512,2048]{1,0:T(8,128)(2,1)}, u32[]{:S(2)}, u32[]{:S(2)}) collective-permute-start(bf16[512,2048]{1,0:T(8,128)(2,1)S(1)} %get-tuple-element.406.refs_0_.refs_1_), channel_id=1, source_target_pairs={{0,1},{1,0},{2,3},{3,2},{4,5},{5,4},{6,7},{7,6},{8,9},{9,8},{10,11... | collective-permute-start | bytes 6291464 | tf_op jit(solution)/shard_map/ppermute | solution.py:751
  641.1 30.5 %collective-permute-start.18 = (bf16[512,2048]{1,0:T(8,128)(2,1)}, bf16[512,2048]{1,0:T(8,128)(2,1)}, u32[]{:S(2)}, u32[]{:S(2)}) collective-permute-start(bf16[512,2048]{1,0:T(8,128)(2,1)} %collective-permute-done.17.refs_2_.refs_3_), channel_id=1, source_target_pairs={{0,1},{1,0},{2,3},{3,2},{4,5},{5,4},{6,7},{7,6},{8,9},{9,8},{10,11... | collective-permute-start | bytes 6291464 | tf_op jit(solution)/shard_map/ppermute | solution.py:751
  731.4 274.7 %reduce-scatter.9.cloned.1.call-start = ((), (), s32[]{:S(2)}) async-start(), calls=%async_computation.6 | async-start | bytes 5242880 | tf_op jit(solution)/shard_map/reduce_scatter | solution.py:822
  731.4 60.8 %collective-permute-start.14 = (bf16[512,2048]{1,0:T(8,128)(2,1)}, bf16[512,2048]{1,0:T(8,128)(2,1)}, u32[]{:S(2)}, u32[]{:S(2)}) collective-permute-start(bf16[512,2048]{1,0:T(8,128)(2,1)} %get-tuple-element.364), channel_id=1, source_target_pairs={{0,1},{1,0},{2,3},{3,2},{4,5},{5,4},{6,7},{7,6},{8,9},{9,8},{10,11... | collective-permute-start | bytes 6291464 | tf_op jit(solution)/shard_map/ppermute | solution.py:751
  731.8 78.6 %collective-permute-start.15 = (bf16[512,2048]{1,0:T(8,128)(2,1)}, bf16[512,2048]{1,0:T(8,128)(2,1)}, u32[]{:S(2)}, u32[]{:S(2)}) collective-permute-start(bf16[512,2048]{1,0:T(8,128)(2,1)} %get-tuple-element.365), channel_id=1, source_target_pairs={{0,1},{1,0},{2,3},{3,2},{4,5},{5,4},{6,7},{7,6},{8,9},{9,8},{10,11... | collective-permute-start | bytes 6291464 | tf_op jit(solution)/shard_map/ppermute | solution.py:751
  808.5 19.3 %collective-permute-start.21 = (bf16[512,2048]{1,0:T(8,128)(2,1)}, bf16[512,2048]{1,0:T(8,128)(2,1)}, u32[]{:S(2)}, u32[]{:S(2)}) collective-permute-start(bf16[512,2048]{1,0:T(8,128)(2,1)} %get-tuple-element.439), channel_id=1, source_target_pairs={{0,1},{1,0},{2,3},{3,2},{4,5},{5,4},{6,7},{7,6},{8,9},{9,8},{10,11... | collective-permute-start | bytes 6291464 | tf_op jit(solution)/shard_map/ppermute | solution.py:751
  808.9 139.4 %collective-permute-start.24 = (bf16[3072,512]{1,0:T(8,128)(2,1)}, bf16[3072,512]{1,0:T(8,128)(2,1)}, u32[]{:S(2)}, u32[]{:S(2)}) collective-permute-start(bf16[3072,512]{1,0:T(8,128)(2,1)} %reduce-scatter.7.cloned.1.call-done), channel_id=1, source_target_pairs={{0,4},{1,5},{2,6},{3,7},{4,0},{5,1},{6,2},{7,3},{8,12},{9,13},{10,... | collective-permute-start | bytes 9437192 | tf_op jit(solution)/shard_map/ppermute | solution.py:754
  814.4 109.7 %collective-permute-start.19 = (bf16[512,2048]{1,0:T(8,128)(2,1)}, bf16[512,2048]{1,0:T(8,128)(2,1)}, u32[]{:S(2)}, u32[]{:S(2)}) collective-permute-start(bf16[512,2048]{1,0:T(8,128)(2,1)} %add_convert_fusion.2), channel_id=1, source_target_pairs={{0,2},{1,3},{2,0},{3,1},{4,6},{5,7},{6,4},{7,5},{8,10},{9,11},{10,... | collective-permute-start | bytes 6291464 | tf_op jit(solution)/shard_map/ppermute | solution.py:751
  827.7 96.4 %copy-start.2 = (f32[512,2048]{1,0:T(8,128)S(1)}, f32[512,2048]{1,0:T(8,128)}, u32[]{:S(2)}) copy-start(f32[512,2048]{1,0:T(8,128)} %copy-done) | copy-start | bytes 12582916
  827.7 134.3 %collective-permute-start.20 = (bf16[512,2048]{1,0:T(8,128)(2,1)}, bf16[512,2048]{1,0:T(8,128)(2,1)}, u32[]{:S(2)}, u32[]{:S(2)}) collective-permute-start(bf16[512,2048]{1,0:T(8,128)(2,1)} %get-tuple-element.438), channel_id=1, source_target_pairs={{0,1},{1,0},{2,3},{3,2},{4,5},{5,4},{6,7},{7,6},{8,9},{9,8},{10,11... | collective-permute-start | bytes 6291464 | tf_op jit(solution)/shard_map/ppermute | solution.py:751
  831.8 116.5 %copy-start.16 = (bf16[3072,512]{1,0:T(8,128)(2,1)S(1)}, bf16[3072,512]{1,0:T(8,128)(2,1)}, u32[]{:S(2)}) copy-start(bf16[3072,512]{1,0:T(8,128)(2,1)} %reduce-scatter.5.cloned.1.call-done) | copy-start | bytes 9437188
  831.8 164.7 %collective-permute-start.22 = (bf16[512,2048]{1,0:T(8,128)(2,1)}, bf16[512,2048]{1,0:T(8,128)(2,1)}, u32[]{:S(2)}, u32[]{:S(2)}) collective-permute-start(bf16[512,2048]{1,0:T(8,128)(2,1)} %add_convert_fusion), channel_id=1, source_target_pairs={{0,2},{1,3},{2,0},{3,1},{4,6},{5,7},{6,4},{7,5},{8,10},{9,11},{10,... | collective-permute-start | bytes 6291464 | tf_op jit(solution)/shard_map/ppermute | solution.py:751
  928.2 77.9 %collective-permute-start.23 = (bf16[2048,256]{0,1:T(8,128)(2,1)}, bf16[2048,256]{0,1:T(8,128)(2,1)}, u32[]{:S(2)}, u32[]{:S(2)}) collective-permute-start(bf16[2048,256]{0,1:T(8,128)(2,1)} %reduce-scatter.11.cloned.1.call-done), channel_id=1, source_target_pairs={{0,4},{1,5},{2,6},{3,7},{4,0},{5,1},{6,2},{7,3},{8,12},{9,13},{10,... | collective-permute-start | bytes 3145736 | tf_op jit(solution)/shard_map/ppermute | solution.py:754
  955.3 41.2 %copy-start.5 = (bf16[512,2048]{1,0:T(8,128)(2,1)S(1)}, bf16[512,2048]{1,0:T(8,128)(2,1)}, u32[]{:S(2)}) copy-start(bf16[512,2048]{1,0:T(8,128)(2,1)} %x_ref.1) | copy-start | bytes 6291460
  955.3 41.2 %copy-start.27 = (f32[512]{0:T(512)S(1)}, f32[512]{0:T(512)}, u32[]{:S(2)}) copy-start(f32[512]{0:T(512)} %copy-done.26) | copy-start | bytes 6148
  (17 other events, 109.2 us)
Sparse Core Ops, SparseCore 0:
  107.0 86.4 all-gather.8
  195.4 52.6 all-gather.12
  250.0 87.5 all-gather.10
  365.2 51.5 all-gather.14
  419.7 120.7 reduce-scatter.4
  588.0 120.2 reduce-scatter.6
  731.5 52.6 reduce-scatter.10
  792.4 52.5 reduce-scatter.8

commit v3 on v2

--- a/solution.py
+++ b/solution.py
@@ -15,6 +15,7 @@
 NEGATIVE = -1e30
 ROPE_BASE = 10000.0
 LOG2E = math.log2(math.e)
+LONG = 25 * 10**10
 VMEM_LIMIT = 56 * 1024 * 1024
 F32 = jnp.float32
 BF16 = jnp.bfloat16
@@ -57,7 +58,7 @@
     return jnp.concatenate([cosine, cosine], axis=-1), jnp.concatenate([-sine, sine], axis=-1)
 
 
-def kernel_call(kernel, name, grid, in_specs, out_specs, out_shapes, scratch, aliases={}):
+def kernel_call(kernel, name, flops, grid, in_specs, out_specs, out_shapes, scratch, aliases={}):
     return pl.pallas_call(
         kernel,
         grid_spec=pltpu.PrefetchScalarGridSpec(
@@ -77,6 +78,9 @@
 
 def slot(index, size):
     return pl.ds(pl.multiple_of(index * size, size), size)
+
+
+PIECES = 4
 
 
 def start_kernel(members, sets, count, x_ref, pack_ref, *refs):
@@ -119,8 +123,8 @@
         copy.wait_recv()
         waited.append(copy)
 
-    orders = (climb, climb[::-1])
-    size = pack_ref.shape[0] // 2
+    orders = (climb, climb[::-1]) * (PIECES // 2)
+    size = pack_ref.shape[0] // PIECES
     came = [{} for _ in range(sets)]
 
     def pass_on(step, half, mask):
@@ -131,16 +135,20 @@
                 copy = send(packs[step][mask].at[here, :], packs[step][mask | bit].at[here, :], {"fsdp": f ^ bit})
                 came[step][half, mask | bit] = copy
 
-    def pass_all(step):
+    def pass_all(step, halves):
         for level in range(1, len(climb)):
-            for half in range(2):
+            for half in halves:
                 for mask in range(count):
                     if mask.bit_count() == level and not mask & orders[half][-1]:
                         await_block(came[step][half, mask])
                         pass_on(step, half, mask)
 
-    over = [send(pack_ref, packs[step][0], {"tp": shifts[step - 1]}) for step in range(1, sets)]
-    for half in range(2):
+    over = {}
+    for half in range(PIECES):
+        here = pl.ds(half * size, size)
+        for step in range(1, sets):
+            over[step, half] = send(pack_ref.at[here, :], packs[step][0].at[here, :], {"tp": shifts[step - 1]})
+    for half in range(PIECES):
         pass_on(0, half, 0)
 
     rows = x_ref.shape[0]
@@ -157,12 +165,15 @@
     blocks = {}
     for bit in group:
         blocks[bit] = send(low_ref, normed[bit], {"tp": t ^ bit})
-    pass_all(0)
+    pass_all(0, range(PIECES))
     for step in range(1, sets):
-        await_block(over[step - 1])
-        for half in range(2):
-            pass_on(step, half, 0)
-        pass_all(step)
+        for pair in range(0, PIECES, 2):
+            for half in (pair, pair + 1):
+                await_block(over[step, half])
+                pass_on(step, half, 0)
+            if pair:
+                pass_all(step, (pair - 2, pair - 1))
+        pass_all(step, (PIECES - 2, PIECES - 1))
     for mask in sorted(range(1, members), reverse=True, key=lambda m: (m & -m, m)):
         below = [bit for bit in group if bit < mask & -mask]
         if below:
@@ -177,7 +188,7 @@
 
 
 def start_exchange(x, pack, members, sets, count):
-    sends = 2 * (count - 1) * sets + (members - 1) + (sets - 1)
+    sends = PIECES * ((count - 1) * sets + sets - 1) + members - 1
     shapes = [jax.ShapeDtypeStruct(x.shape, BF16)] * members + [jax.ShapeDtypeStruct(pack.shape, BF16)] * (count * sets - 1)
     outs = pl.pallas_call(
         functools.partial(start_kernel, members, sets, count),
@@ -198,60 +209,118 @@
     return outs[:members], [packs[step * count : (step + 1) * count] for step in range(sets)]
 
 
-def rows_kernel(body, plan, members, extras, count, f_ref, *refs):
-    xs, refs = refs[:members], refs[members:]
+def rows_kernel(body, plan, members, extras, count, number, *refs):
+    held = members // 2 if number else members
+    xs, refs = refs[:held], refs[held:]
     extra_refs, refs = refs[:extras], refs[extras:]
     weights, refs = refs[:count], refs[count:]
-    outs, (x_buf, w_buf, x_sem, w_sem) = refs[:-4], refs[-4:]
-    i, f = pl.program_id(0), f_ref[0]
+    if number:
+        *refs, send_sem, recv_sem = refs
+        xs = [block for pair in zip(xs, refs[-4 - held : -4]) for block in pair]
+        outs, refs = refs[: -4 - held], refs[-4:]
+    else:
+        outs, refs = refs[:-4], refs[-4:]
+    x_buf, w_buf, x_sem, w_sem = refs
+    i, f = pl.program_id(0), lax.axis_index("fsdp")
     moves, use = plan
     tiles = [
         [pltpu.make_async_copy(src, dst, w_sem.at[t, n]) for n, (src, dst) in enumerate(pairs)]
         for t, pairs in enumerate(moves(weights, w_buf, f))
     ]
-    x_copies = [pltpu.make_async_copy(x, x_buf.at[m], x_sem.at[m]) for m, x in enumerate(xs)]
-
-    @pl.when(i == 0)
-    def _():
-        x_copies[0].start()
-        for copies in tiles:
-            for copy in copies:
+    order = list(range(0, members, 2)) + list(range(1, members, 2)) if number else list(range(members))
+    x_copies = [pltpu.make_async_copy(xs[m], x_buf.at[n], x_sem.at[n]) for n, m in enumerate(order)]
+    exchanges = []
+    if number:
+        partner = {"tp": lax.axis_index("tp") ^ 1}
+        exchanges = [
+            pltpu.make_async_remote_copy(
+                src_ref=xs[2 * q],
+                dst_ref=xs[2 * q + 1],
+                send_sem=send_sem.at[q],
+                recv_sem=recv_sem.at[q],
+                device_id=partner,
+                device_id_type=pl.DeviceIdType.MESH,
+            )
+            for q in range(held)
+        ]
+
+    def start(n):
+        if n < len(tiles):
+            for copy in tiles[n]:
                 copy.start()
-        for copy in x_copies[1:]:
-            copy.start()
+        elif n - len(tiles) + 1 < held:
+            x_copies[n - len(tiles) + 1].start()
 
     def run(first):
+        if first:
+            x_copies[0].start()
+            start(0)
+            start(1)
+            if number:
+                barrier = pltpu.get_barrier_semaphore()
+                pl.semaphore_signal(barrier, inc=1, device_id=partner, device_id_type=pl.DeviceIdType.MESH)
+                pl.semaphore_wait(barrier, 1)
+                for exchange in exchanges:
+                    exchange.start()
         pltpu.make_async_copy(xs[0], x_buf.at[i], x_sem.at[i]).wait()
         for t, copies in enumerate(tiles):
             if first:
                 for copy in copies:
                     copy.wait()
+                start(t + 2)
             body(t, use(t, x_buf[i], w_buf), extra_refs, outs)
+        if first:
+            for n in range(len(tiles) + 2, len(tiles) + held - 1):
+                start(n)
 
     pl.when(i == 0)(functools.partial(run, True))
     pl.when(i > 0)(functools.partial(run, False))
-
-
-def rows_call(body, name, place, xs, extras, weights, plan, tiles, copies, w_shape, widths):
+    for q, exchange in enumerate(exchanges):
+
+        @pl.when(i == max(held - 1, 0) + q)
+        def _():
+            exchange.wait()
+            x_copies[held + q].start()
+
+
+def rows_call(body, name, xs, extras, weights, plan, tiles, copies, w_shape, widths, number):
     rows, model = xs[0].shape
-    members, count = len(xs), len(weights)
-    return kernel_call(
-        functools.partial(rows_kernel, body, plan, members, len(extras), count),
-        name,
-        (members,),
-        any_specs(xs) + [pl.BlockSpec((rows, e.shape[1]), lambda i, f: (i, 0)) for e in extras] + any_specs(weights),
-        [pl.BlockSpec((rows, width), lambda i, f: (i, 0)) for width in widths],
-        [jax.ShapeDtypeStruct((members * rows, width), BF16) for width in widths],
-        [
-            pltpu.VMEM((members, rows, model), BF16),
-            pltpu.VMEM(w_shape, BF16),
-            pltpu.SemaphoreType.DMA((members,)),
-            pltpu.SemaphoreType.DMA((tiles, copies)),
-        ],
-    )(place, *xs, *extras, *weights)
-
-
-def project(place, xs, packs, cosine, sine):
+    held, count = len(xs), len(weights)
+    members = 2 * held if number else held
+    arrived = held if number else 0
+
+    def here(i):
+        return (i % held * 2 + i // held if number else i, 0)
+
+    outs = pl.pallas_call(
+        functools.partial(rows_kernel, body, plan, members, len(extras), count, number),
+        grid_spec=pltpu.PrefetchScalarGridSpec(
+            num_scalar_prefetch=0,
+            grid=(members,),
+            in_specs=any_specs(xs) + [pl.BlockSpec((rows, e.shape[1]), here) for e in extras] + any_specs(weights),
+            out_specs=[pl.BlockSpec((rows, width), here) for width in widths] + any_specs(xs[:arrived]),
+            scratch_shapes=[
+                pltpu.VMEM((members, rows, model), BF16),
+                pltpu.VMEM(w_shape, BF16),
+                pltpu.SemaphoreType.DMA((members,)),
+                pltpu.SemaphoreType.DMA((tiles, copies)),
+            ]
+            + [pltpu.SemaphoreType.DMA((held,))] * (2 if number else 0),
+        ),
+        out_shape=[jax.ShapeDtypeStruct((members * rows, width), BF16) for width in widths]
+        + [jax.ShapeDtypeStruct((rows, model), BF16)] * arrived,
+        compiler_params=pltpu.CompilerParams(
+            vmem_limit_bytes=VMEM_LIMIT, **({"collective_id": number, "has_side_effects": True} if number else {})
+        ),
+        cost_estimate=pl.CostEstimate(flops=1, bytes_accessed=1, transcendentals=0),
+        name=name,
+    )(*xs, *extras, *weights)
+    if not number:
+        return outs, list(xs)
+    return outs[: len(widths)], [block for pair in zip(xs, outs[len(widths) :]) for block in pair]
+
+
+def project(xs, packs, cosine, sine):
     model, count = xs[0].shape[1], len(packs)
     depth, width = model // count, packs[0].shape[1]
 
@@ -272,11 +341,11 @@
             outs[0][:, t * width + column : t * width + column + HD] = value.astype(BF16)
 
     return rows_call(
-        body, "project", place, xs, [cosine, sine], packs, (moves, use), 3, count, (3, model, width), [3 * width]
-    )[0]
-
-
-def head_grad_of(place, xs, packs):
+        body, "project", xs, [cosine, sine], packs, (moves, use), 3, count, (3, model, width), [3 * width], 0
+    )[0][0]
+
+
+def head_grad_of(xs, packs, number=0):
     model, count = xs[0].shape[1], len(packs)
     depth, width = model // count, packs[0].shape[1]
     squares = depth // width
@@ -300,11 +369,11 @@
         outs[0][...] = product.astype(BF16)
 
     return rows_call(
-        body, "head_grad", place, xs, [], packs, (moves, use), 1, count * squares, (width, model), [width]
-    )[0]
-
-
-def hidden_units(place, xs, stack):
+        body, "head_grad", xs, [], packs, (moves, use), 1, count * squares, (width, model), [width], number
+    )
+
+
+def hidden_units(xs, stack, number=0):
     model = xs[0].shape[1]
     count, depth, width = stack.shape
     width //= 2
@@ -334,11 +403,11 @@
         outs[2][:, here] = (up * sigmoid * (1.0 + gate * (1.0 - sigmoid))).astype(BF16)
 
     return rows_call(
-        body, "hidden_units", place, xs, [], [stack], (moves, use), len(starts), 2 * count, (model, 2 * width), [width] * 3
+        body, "hidden_units", xs, [], [stack], (moves, use), len(starts), 2 * count, (model, 2 * width), [width] * 3, number
     )
 
 
-def hidden_grad(place, xs, slope_up, slope_gate, stack):
+def hidden_grad(xs, slope_up, slope_gate, stack, number=0):
     model = xs[0].shape[1]
     count, width, depth = stack.shape
     tile = min(512, width)
@@ -362,74 +431,131 @@
         outs[0][:, pl.ds(width + starts[t], tile)] = (product * extras[1][:, here].astype(F32)).astype(BF16)
 
     return rows_call(
-        body, "hidden_grad", place, xs, [slope_up, slope_gate], [stack], (moves, use),
-        len(starts), count, (width, model), [2 * width],
-    )[0]
-
-
-def expand_kernel(sets, each, plan, dot, with_base, parts, f_ref, *refs):
+        body, "hidden_grad", xs, [slope_up, slope_gate], [stack], (moves, use),
+        len(starts), count, (width, model), [2 * width], number,
+    )
+
+
+def expand_kernel(sets, each, plan, dot, with_base, pairs, *refs):
     xs, refs = refs[:sets], refs[sets:]
     bases, refs = (refs[:1], refs[1:]) if with_base else ((), refs)
     weights, refs = refs[: sets * each], refs[sets * each :]
-    outs, (w_buf, sem) = refs[:parts], refs[parts:]
-    d, f = pl.program_id(0), f_ref[0]
+    outs, refs = refs[: max(pairs, 1)], refs[max(pairs, 1) :]
+    w_buf, sem = refs[:2]
+    d, f = pl.program_id(0), lax.axis_index("fsdp")
     count = w_buf.shape[1]
 
     def copies(j, c):
-        there, pairs = plan(weights[j * each : (j + 1) * each], c, f)
+        there, moves = plan(weights[j * each : (j + 1) * each], c, f)
         return there, [
             pltpu.make_async_copy(src, w_buf.at[j, there, :, lanes], sem.at[j, there, n])
-            for n, (src, lanes) in enumerate(pairs)
+            for n, (src, lanes) in enumerate(moves)
         ]
 
-    @pl.when(d == 0)
-    def _():
+    def start(place):
         for c in range(count):
             for j in range(sets):
-                for copy in copies(j, c)[1]:
-                    copy.start()
-
+                there, moves = copies(j, c)
+
+                @pl.when(there == place)
+                def _():
+                    for copy in moves:
+                        copy.start()
+
+    if pairs:
+        partner = {"tp": lax.axis_index("tp") ^ 1}
+        send_buf, recv_buf, send_sem, recv_sem = refs[2:]
+
+        def exchange(place, q):
+            return pltpu.make_async_remote_copy(
+                src_ref=send_buf.at[place, q],
+                dst_ref=recv_buf.at[place, q],
+                send_sem=send_sem.at[place, q],
+                recv_sem=recv_sem.at[place, q],
+                device_id=partner,
+                device_id_type=pl.DeviceIdType.MESH,
+            )
+
+        @pl.when(d == 0)
+        def _():
+            barrier = pltpu.get_barrier_semaphore()
+            pl.semaphore_signal(barrier, inc=1, device_id=partner, device_id_type=pl.DeviceIdType.MESH)
+            pl.semaphore_wait(barrier, 1)
+
+    pl.when(d == 0)(functools.partial(start, 0))
+    start(d + 1)
     for j in range(sets):
         for n, (src, lanes) in enumerate(plan(weights[j * each : (j + 1) * each], 0, f)[1]):
             pltpu.make_async_copy(src, w_buf.at[j, d, :, lanes], sem.at[j, d, n]).wait()
     rows = outs[0].shape[0]
-    for p in range(parts):
+
+    def block(p):
         here = slice(p * rows, (p + 1) * rows)
         total = sum(dot(x[here, :], w_buf[j, d]) for j, x in enumerate(xs))
         for base in bases:
             total = total + base[here, :].astype(F32)
-        outs[p][...] = total.astype(BF16)
-
-
-def expand_call(name, place, xs, weights, each, plan, pieces, dot, chunk, rows, first, parts, base=None):
+        return total
+
+    if not pairs:
+        outs[0][...] = block(0).astype(outs[0].dtype)
+        return
+    for q in range(pairs):
+        send_buf[d, q] = block(2 * q + 1).astype(BF16)
+        exchange(d, q).start()
+    for q in range(pairs):
+        total = block(2 * q)
+        exchange(d, q).wait_recv()
+        outs[q][...] = (total + recv_buf[d, q].astype(F32)).astype(outs[q].dtype)
+
+    @pl.when(d == count - 1)
+    def _():
+        for place in range(count):
+            for q in range(pairs):
+                exchange(place, q).wait_send()
+
+
+def expand_call(name, xs, weights, each, plan, pieces, dot, chunk, rows, base=None, first=None, members=0, number=0):
     count, w_shape = chunk
     depth = w_shape[1 if dot is dot_nn else 0]
-    specs = [pl.BlockSpec((rows * parts, x.shape[1]), lambda d, f: (first // parts, 0)) for x in xs]
+    pairs = members // 2
+    taken = rows * max(members, 1)
+    block = 0 if first is None else first // members
+    specs = [pl.BlockSpec((taken, x.shape[1]), lambda d: (block, 0)) for x in xs]
     bases = [] if base is None else [base]
-    specs += [pl.BlockSpec((rows * parts, depth), lambda d, f: (first // parts, d)) for _ in bases]
-    return kernel_call(
-        functools.partial(expand_kernel, len(xs), each, plan, dot, base is not None, parts),
-        name,
-        (count,),
-        specs + any_specs(weights),
-        [pl.BlockSpec((rows, depth), lambda d, f: (0, d))] * parts,
-        [jax.ShapeDtypeStruct((rows, count * depth), BF16)] * parts,
-        [pltpu.VMEM((len(xs), count) + w_shape, BF16), pltpu.SemaphoreType.DMA((len(xs), count, pieces))],
-    )(place, *xs, *bases, *weights)
-
-
-def expand_stack(name, dot, place, xs, stacks, rows, first, parts, base=None):
+    specs += [pl.BlockSpec((taken, depth), lambda d: (block, d)) for _ in bases]
+    scratch = [pltpu.VMEM((len(xs), count) + w_shape, BF16), pltpu.SemaphoreType.DMA((len(xs), count, pieces))]
+    types = [BF16]
+    more = {}
+    if pairs:
+        types = [F32 if first == q == 0 else BF16 for q in range(pairs)]
+        scratch += [pltpu.VMEM((count, pairs, rows, depth), BF16)] * 2 + [pltpu.SemaphoreType.DMA((count, pairs))] * 2
+        more = {"collective_id": number, "has_side_effects": True}
+    return pl.pallas_call(
+        functools.partial(expand_kernel, len(xs), each, plan, dot, base is not None, pairs),
+        grid_spec=pltpu.PrefetchScalarGridSpec(
+            num_scalar_prefetch=0,
+            grid=(count,),
+            in_specs=specs + any_specs(weights),
+            out_specs=[pl.BlockSpec((rows, depth), lambda d: (0, d)) for _ in types],
+            scratch_shapes=scratch,
+        ),
+        out_shape=[jax.ShapeDtypeStruct((rows, count * depth), type_) for type_ in types],
+        compiler_params=pltpu.CompilerParams(vmem_limit_bytes=VMEM_LIMIT, **more),
+        cost_estimate=pl.CostEstimate(flops=1, bytes_accessed=1, transcendentals=0),
+        name=name,
+    )(*xs, *bases, *weights)
+
+
+def expand_stack(name, dot, xs, stacks, rows, **more):
     count, above, across = stacks[0].shape
 
     def plan(weights, c, f):
         return c, [(weights[0].at[c], pl.ds(0, across))]
 
-    return expand_call(
-        name, place, xs, stacks, 1, plan, 1, dot, (count, (above, across)), rows, first, parts, base
-    )
-
-
-def expand_heads(name, place, xs, packs, rows, first, parts):
+    return expand_call(name, xs, stacks, 1, plan, 1, dot, (count, (above, across)), rows, **more)
+
+
+def expand_heads(name, xs, packs, rows, **more):
     count, width = len(packs[0]), packs[0][0].shape[1]
     depth = packs_depth(packs[0][0])
     squares = depth // width
@@ -441,12 +567,10 @@
         ]
 
     flat = [pack for list_ in packs for pack in list_]
-    return expand_call(
-        name, place, xs, flat, count, plan, squares, dot_nn, (count, (width, depth)), rows, first, parts
-    )
-
-
-def expand_project(name, place, xs, packs, rows, first, parts):
+    return expand_call(name, xs, flat, count, plan, squares, dot_nn, (count, (width, depth)), rows, **more)
+
+
+def expand_project(name, xs, packs, rows, **more):
     count, width = len(packs[0]), packs[0][0].shape[1]
     depth = packs_depth(packs[0][0])
 
@@ -456,9 +580,7 @@
         ]
 
     flat = [pack for list_ in packs for pack in list_]
-    return expand_call(
-        name, place, xs, flat, count, plan, 3, dot_nt, (count, (depth, 3 * width)), rows, first, parts
-    )
+    return expand_call(name, xs, flat, count, plan, 3, dot_nt, (count, (depth, 3 * width)), rows, **more)
 
 
 def pack_weights(att_proj, attn_out):
@@ -484,15 +606,16 @@
         for d in range(count)
     ]
 
-    @pl.when(pl.program_id(0) == 0)
-    def _():
-        for copies in chunks:
-            for copy in copies:
-                copy.start()
+    def start(d):
+        for copy in chunks[d] if d < count else []:
+            copy.start()
 
     def run(first):
+        if first:
+            start(0)
         for d, copies in enumerate(chunks):
             if first:
+                start(d + 1)
                 for copy in copies:
                     copy.wait()
             out_ref[d] = dot_tn(x_buf[d], g_ref[...]).astype(BF16)
@@ -501,18 +624,20 @@
     pl.when(pl.program_id(0) > 0)(functools.partial(run, False))
 
 
-def rows_grad(name, place, count, tile, below, xs, g, stack=None):
+def rows_grad(name, place, count, tile, beside, below, xs, g, stack=None):
     rows, model = xs[0].shape
     tokens, width = g.shape
     depth = model // count
     given = [] if stack is None else [stack]
-    shape = (count, width // tile * depth + below, tile)
+    tiles = width // tile
+    shape = (count, -(-tiles // beside) * depth + below, beside * tile)
     return kernel_call(
         functools.partial(rows_grad_kernel, len(xs), count),
         name,
-        (width // tile,),
+        2 * tokens * model * width,
+        (tiles,),
         any_specs(xs) + any_specs(given) + [pl.BlockSpec((tokens, tile), lambda n, f: (0, n))],
-        pl.BlockSpec((count, depth, tile), lambda n, f: (0, n, 0)),
+        pl.BlockSpec((count, depth, tile), lambda n, f: (0, n // beside, n % beside)),
         jax.ShapeDtypeStruct(shape, BF16),
         [pltpu.VMEM((count, tokens, depth), BF16), pltpu.SemaphoreType.DMA((count, len(xs)))],
         {1 + len(xs): 0} if given else {},
@@ -527,12 +652,18 @@
     total, _, depth = g_buf.shape
     tile = out_ref.shape[2]
 
+    def start(c):
+        for m, g in enumerate(gs):
+            src, dst = g.at[:, slot(c, depth)], g_buf.at[c, m * rows : (m + 1) * rows, :]
+            pltpu.make_async_copy(src, dst, sem.at[c, m]).start()
+
     @pl.when(d == 0)
     def _():
-        for c in range(total):
-            for m, g in enumerate(gs):
-                src, dst = g.at[:, c * depth : (c + 1) * depth], g_buf.at[c, m * rows : (m + 1) * rows, :]
-                pltpu.make_async_copy(src, dst, sem.at[c, m]).start()
+        start(0)
+
+    @pl.when(d + 1 < total)
+    def _():
+        start(d + 1)
 
     for m, g in enumerate(gs):
         src, dst = g.at[:, :depth], g_buf.at[d, m * rows : (m + 1) * rows, :]
@@ -548,19 +679,20 @@
         first += x.shape[1] * (depth // tile)
 
 
-def columns_grad(name, place, count, tile, above, xs, gs, stack=None):
+def columns_grad(name, place, count, tile, shape, at, xs, gs, stack=None):
     model = gs[0].shape[1]
     tokens = xs[0].shape[0]
     depth = model // count
-    below = sum(x.shape[1] for x in xs) * (depth // tile)
+    height = sum(x.shape[1] for x in xs) * (depth // tile)
     given = [] if stack is None else [stack]
     return kernel_call(
         functools.partial(columns_grad_kernel, len(xs), len(gs)),
         name,
+        2 * tokens * model * sum(x.shape[1] for x in xs),
         (count,),
         [pl.BlockSpec(x.shape, lambda d, f: (0, 0)) for x in xs] + any_specs(gs) + any_specs(given),
-        pl.BlockSpec((1, below, tile), lambda d, f: (d, above // below, 0)),
-        jax.ShapeDtypeStruct((count, above + below, tile), BF16),
+        pl.BlockSpec((1, height, tile), lambda d, f: (d, *at)),
+        jax.ShapeDtypeStruct((count, *shape), BF16),
         [pltpu.VMEM((count, tokens, depth), BF16), pltpu.SemaphoreType.DMA((count, len(gs)))],
         {1 + len(xs) + len(gs): 0} if given else {},
     )(place, *xs, *gs, *given)
@@ -693,7 +825,7 @@
     lax.fori_loop(0, count, store, 0)
 
 
-def attend_backward(qkv, grad, out, lse, place, segment, key_code, cosine, sine, block):
+def attend_backward(qkv, grad, out, lse, place, segment, key_code, cosine, sine, block, cost):
     tokens, width = qkv.shape
     heads = width // 3 // HD
     count = tokens // block
@@ -725,7 +857,7 @@
         ),
         out_shape=jax.ShapeDtypeStruct((tokens, width), BF16),
         compiler_params=pltpu.CompilerParams(vmem_limit_bytes=VMEM_LIMIT),
-        cost_estimate=pl.CostEstimate(flops=1, bytes_accessed=1, transcendentals=0),
+        cost_estimate=pl.CostEstimate(flops=cost, bytes_accessed=1, transcendentals=0),
         name="attend_backward",
     )(
         place, qkv, qkv, qkv, grad, out, lse,
@@ -777,24 +909,7 @@
             for mask in sorted(blocks, reverse=True):
                 blocks[mask | bit] = swap(blocks[mask], bit)
             bit //= 2
-        return blocks
-
-    def group_near(blocks):
-        blocks = dict(blocks)
-        for mask in sorted(blocks, reverse=True):
-            blocks[mask | 1] = swap(blocks[mask], 1)
-        return [blocks[mask] for mask in range(members)]
-
-    def group_gather(values):
-        return group_near(group_far(values))
-
-    def scatter_near(blocks):
-        sums = {}
-        for mask in sorted(blocks, reverse=True):
-            if mask & 1:
-                total = blocks[mask ^ 1].astype(F32) + swap(blocks[mask], 1).astype(F32)
-                sums[mask ^ 1] = total.astype(BF16) if mask ^ 1 else total
-        return sums
+        return [blocks[mask] for mask in range(0, members, 2)]
 
     def scatter_far(sums):
         sums = dict(sums)
@@ -808,11 +923,13 @@
 
     half = members // 2
 
-    def share(function, *args, due=((), ())):
+    def share(function, *args, number, due=(), due_near=()):
         sums = {}
-        for first in (half, 0):
-            outs = then(lambda *a: function(place_fsdp, *a[:2], rows, first, half, *a[2:]), *args, due=due[first == 0])
-            sums.update(scatter_near({first + p: out for p, out in enumerate(outs)}))
+        for part, first in enumerate((half, 0)):
+            call = functools.partial(function, rows=rows, first=first, members=half, number=number + part)
+            outs = then(lambda xs, weights, *base: call(xs, weights, base=base[0] if base else None), *args, due=due)
+            sums.update({first + 2 * q: out for q, out in enumerate(outs)})
+            due = due_near
         return sums
 
     def gather(shard):
@@ -821,18 +938,17 @@
     def scatter(stacked):
         return lax.psum_scatter(stacked.reshape(-1, stacked.shape[-1]), "fsdp", scatter_dimension=0, tiled=True)
 
-    def settle(pieces):
-        total = pieces[0].astype(F32)
-        for step in range(1, sets):
-            total = total + turn(pieces[step], sets - step).astype(F32)
-        return total
+    def settle(pieces, *gates):
+        return pieces[:1] + [turn(after(pieces[step], *gates), sets - step) for step in range(1, sets)]
+
+    def settled(pieces):
+        return sum(piece.astype(F32) for piece in pieces)
 
     normed_all, packs = start_exchange(inputs, pack_weights(att_proj, attn_out), members, sets, fsdp_size)
     chain.append(normed_all[0])
-    up_gate, down, cotangent_late = after((ff_proj.reshape(depth, -1), ff_out, cotangent), last())
+    up_gate, down = after((ff_proj.reshape(depth, -1), ff_out), last())
     w_ffn, w_down = [gather(up_gate)], [gather(down)]
     turned_up_gate = [turn(up_gate, step) for step in range(1, sets)]
-    cotangent_far = group_far(cotangent_late)
 
     segment = lax.dynamic_slice_in_dim(segments, mine * SEQ_LEN, SEQ_LEN)
     padding = lax.dynamic_slice_in_dim(pad_mask, mine * SEQ_LEN, SEQ_LEN)
@@ -844,81 +960,102 @@
     x_float = inputs.astype(F32)
     qkv, attended = [], []
     for step in range(sets):
-        qkv.append(then(functools.partial(project, place_fsdp), normed_all, packs[step], cosine, sine))
+        qkv.append(then(project, normed_all, packs[step], cosine, sine))
         attended.append(then(lambda part: attend_forward(part, place_tp, segment, key_code, block), qkv[step]))
     heads_low = [out for out, _ in attended]
-    sums = share(functools.partial(expand_heads, "attn_branch"), heads_low, packs, due=((cotangent_far,), ()))
-    for step in range(1, sets):
-        w_ffn.append(gather(after(turned_up_gate[step - 1], last())))
+    sums = share(functools.partial(expand_heads, "attn_branch"), heads_low, packs, number=1)
+    w_ffn += [gather(after(part, chain[-2])) for part in turned_up_gate]
     resid = x_float + scatter_far(sums)
-    normed_two = layer_norm(resid).astype(BF16)
-    turned_down = [turn(after(ff_out, normed_two), step) for step in range(1, sets)]
-    cotangent_all = group_near(after(cotangent_far, normed_two))
-    normed_two_all = group_gather(normed_two)
-
-    hidden, grad_ffn, partial = [], [], None
+    normed_two_far = group_far(layer_norm(resid).astype(BF16))
+    down, cotangent_late = after((ff_out, cotangent), normed_two_far[-1])
+    turned_down = [turn(down, step) for step in range(1, sets)]
+    cotangent_far = group_far(cotangent_late)
+
+    hidden, slopes, grad_ffn, partial = [], [], [], None
+    for step in range(sets):
+        if step == 0:
+            (low, *slope), normed_two_all = then(functools.partial(hidden_units, number=9), normed_two_far, w_ffn[0])
+        else:
+            (low, *slope), _ = then(hidden_units, normed_two_all, w_ffn[step])
+        hidden.append(low)
+        slopes.append(slope)
     ffn_rows = 2 * ffn_width
     grad_expand = functools.partial(expand_stack, "grad_normed_two", dot_nt)
-    down_grad = functools.partial(columns_grad, "grad_down", place_fsdp, fsdp_size, depth, ffn_rows)
-    up_grad = functools.partial(rows_grad, "grad_ffn", place_fsdp, fsdp_size, depth, ffn_width)
+    up_grad = functools.partial(rows_grad, "grad_ffn", place_fsdp, fsdp_size, depth, 1, 0)
     for step in range(sets):
-        ready = (cotangent_all,) if step == 0 else ()
-        low, slope_up, slope_gate = then(functools.partial(hidden_units, place_fsdp), normed_two_all, w_ffn[step], due=ready)
-        hidden.append(low)
         if step == 0:
-            w_down += [gather(after(down, last())) for down in turned_down]
+            (grad_low,), cotangent_all = then(functools.partial(hidden_grad, number=10), cotangent_far, *slopes[0], w_down[0])
+        else:
+            (grad_low,), _ = then(hidden_grad, cotangent_all, *slopes[step], w_down[step])
+        if step == 0:
+            w_down += [gather(after(part, last())) for part in turned_down]
+        grad_ffn.append(scatter(then(up_grad, normed_two_all, grad_low)))
         base = [] if partial is None else [partial]
         if step < sets - 1:
-            stacked = then(down_grad, [low], cotangent_all)
-        grad_low = then(functools.partial(hidden_grad, place_fsdp), cotangent_all, slope_up, slope_gate, w_down[step])
-        if step < sets - 1:
-            grad_ffn.append(scatter(then(up_grad, normed_two_all, grad_low, stacked)))
-            call = lambda x, w, *b: grad_expand(place_fsdp, [x], [w], members * rows, 0, 1, *b)[0]
+            call = lambda x, w, *b: grad_expand([x], [w], members * rows, base=b[0] if b else None)[0]
             partial = then(call, grad_low, w_ffn[step], *base)
-        else:
-            sums = share(grad_expand, [grad_low], [w_ffn[step]], *base)
-            stacked = then(up_grad, normed_two_all, grad_low, due=sums)
-            grad_normed_two = scatter_far(sums)
-            grad_ffn.append(scatter(then(down_grad, [low], cotangent_all, stacked, due=(grad_normed_two,))))
-
+    sums = share(grad_expand, [grad_low], [w_ffn[-1]], *base, number=3)
+    ffn_sums = share(functools.partial(expand_stack, "ffn_branch", dot_nn), hidden, w_down, number=5)
+    grad_normed_two = after(scatter_far(sums), ffn_sums[half])
     grad_resid = cotangent.astype(F32) + layer_norm_back(resid, grad_normed_two)
     resid_grad_low = grad_resid.astype(BF16)
-    sums = share(functools.partial(expand_stack, "ffn_branch", dot_nn), hidden, w_down, due=((), (resid_grad_low,)))
-    resid_grad_all = group_gather(resid_grad_low)
+    resid_grad_far = group_far(resid_grad_low)
+    shape, at = (sets * ffn_width, depth), (0, 0)
+    down_grad = functools.partial(columns_grad, "grad_down", place_fsdp, fsdp_size, depth, shape, at)
+    grad_down = scatter(then(down_grad, hidden, cotangent_all, due=(resid_grad_low,)))
 
     grad_attn, grad_project = [None] * sets, [None] * sets
-    heads_grad = functools.partial(columns_grad, "grad_heads", place_fsdp, fsdp_size, head_width, 3 * depth)
-    project_grad = functools.partial(rows_grad, "grad_attn", place_fsdp, fsdp_size, head_width, depth)
+    shape, at = (2 * depth, 2 * head_width), (1, 1)
+    heads_grad = functools.partial(columns_grad, "grad_heads", place_fsdp, fsdp_size, head_width, shape, at)
+    project_grad = functools.partial(rows_grad, "grad_attn", place_fsdp, fsdp_size, head_width, 2, 0)
+    held = None
     for step in reversed(range(sets)):
-        ready = (grad_ffn[0],) if step == sets - 1 else ()
-        head_grad = then(functools.partial(head_grad_of, place_fsdp), resid_grad_all, packs[step], due=ready)
+        ready = tuple(grad_ffn[:1]) if step == sets - 1 else (grad_up[1:], ffn_branch)
         if step == sets - 1:
-            ffn_branch = scatter_far(after(sums, last()))
+            (head_grad,), resid_grad_all = then(functools.partial(head_grad_of, number=11), resid_grad_far, packs[step], due=ready)
+        else:
+            (head_grad,), _ = then(head_grad_of, resid_grad_all, packs[step], due=ready)
+        if step == sets - 1:
+            grad_up = settle([piece[:ffn_width] for piece in grad_ffn], last())
+            ffn_branch = scatter_far(after(ffn_sums, last()))
+        else:
+            grad_gate = settle([piece[ffn_width:] for piece in grad_ffn], last(), grad_up[1:])
+        if held is not None:
+            grad_attn[step + 1] = scatter(after(held, last()))
         grad_project[step] = then(
             lambda part, grad, out, lse: attend_backward(
-                part, grad, out, lse, place_tp, segment, key_code, cosine, sine, block
+                part, grad, out, lse, place_tp, segment, key_code, cosine, sine, block, LONG
             ),
             qkv[step], head_grad, heads_low[step], attended[step][1],
         )
-        ready = tuple(grad_ffn[1:]) if step == 0 else ()
-        stacked = then(heads_grad, [heads_low[step]], resid_grad_all, due=ready)
-        grad_attn[step] = scatter(then(project_grad, normed_all, grad_project[step], stacked))
+        if step == 0:
+            grad_down = settle([grad_down[j * ffn_width : (j + 1) * ffn_width] for j in range(sets)], last(), grad_gate[1:])
+        stacked = then(heads_grad, [heads_low[step]], resid_grad_all)
+        ready = tuple(grad_gate[1:]) if step == 0 else ()
+        held = then(project_grad, normed_all, grad_project[step], stacked, due=ready)
+    grad_attn[0] = scatter(held)
+    sums = share(functools.partial(expand_project, "grad_normed"), grad_project, packs, number=7)
+    grad_normed = scatter_far(sums)
     output = (resid + ffn_branch).astype(BF16)
-    grad_normed = scatter_far(share(functools.partial(expand_project, "grad_normed"), grad_project, packs))
+    grad_attn = settle(grad_attn)
+    grad_normed = after(grad_normed, grad_attn[1:])
     grad_input = (grad_resid + layer_norm_back(x_float, grad_normed)).astype(BF16)
-
-    grad_attn, grad_ffn = settle(grad_attn), settle(grad_ffn)
-
-    def beside(values, size, count):
-        return jnp.concatenate([values[i * size : (i + 1) * size] for i in range(count)], axis=1)
+    grad_attn = settled(grad_attn)
+
+    def beside(values, first, size, count):
+        return jnp.concatenate([values[(first + i) * size : (first + i + 1) * size] for i in range(count)], axis=1)
+
+    query, key = grad_attn[:depth, :head_width], grad_attn[:depth, head_width:]
+    value, squares = grad_attn[depth:, :head_width], grad_attn[depth:, head_width:]
+    blocks = ffn_width // depth
 
     return (
         output,
         grad_input,
-        beside(grad_attn, depth, 3).reshape(att_proj.shape),
-        beside(grad_attn[3 * depth :], head_width, depth // head_width),
-        beside(grad_ffn, depth, ffn_rows // depth).reshape(ff_proj.shape),
-        grad_ffn[ffn_rows:],
+        jnp.stack([query, key, value], axis=1),
+        beside(squares, 0, head_width, depth // head_width),
+        jnp.stack([beside(settled(part), 0, depth, blocks) for part in (grad_up, grad_gate)], axis=1),
+        settled(grad_down),
     )
 
 

time: 1020 us -> 886 us (0.87)
  waiting for transfers between devices: 346 us -> 202 us
  Pallas kernels: 542 us -> 578 us
  local copies, waits for them, and re-layouts: 43.5 us -> 26 us
  other arithmetic: 56.8 us -> 44.9 us
    ppermute x21 -> x7, waiting for transfers between devices: 310 us -> 131 us  [swap(): return lax.ppermute(values, 'tp', [(i, i ^ bit) for i in range(tp_size)])]
    pallas_call x21, Pallas kernels: 325 us -> 371 us  [the longest x9 154 us: expand_call(): pl.pallas_call(functools.partial(expand_kernel, len(xs), each, plan, dot,...]
    ppermute x4 -> x6, waiting for transfers between devices: 35.2 us -> 60.7 us  [turn(): lax.ppermute(values, 'tp', [(i, (i + step * members) % tp_size) for i in...]
    reshape x3 -> x0, local copies, waits for them, and re-layouts: 19.4 us -> none  [the longest x2 12.7 us: scatter(): stacked.reshape(-1, stacked.shape[-1])]
    convert_element_type x5 -> x1, other arithmetic: 13 us -> 0.48 us  [local(): normed_two_far = group_far(layer_norm(resid).astype(BF16))]
    pallas_call x4 -> x3, Pallas kernels: 42.9 us -> 40.7 us  [columns_grad(): kernel_call(functools.partial(columns_grad_kernel, len(xs), len(gs)), nam...]
  transfers between devices with their start and end apart: 33 -> 22, of which waited for: 12 -> 12; matrix products, arithmetic and copies ran while one was open for 8% -> 6% of each run, Pallas kernels for 44% -> 56%
where the time goes in v3:
time: 886 us; the launch traced here: 880 us
  Pallas kernels  578 us (65%)
  waiting for transfers between devices  202 us (23%)
  other arithmetic  44.9 us (5%)
  local copies, waits for them, and re-layouts  26 us (3%)
  between operations  14.8 us (2%)
  starting transfers between devices  14.4 us (2%)
    pallas_call x9, Pallas kernels, expand_call(): pl.pallas_call(functools.partial(expand_kernel, len(xs), each, plan, dot,...  154 us
    pallas_call x8, Pallas kernels, rows_call(): pl.pallas_call(functools.partial(rows_kernel, body, plan, members, len(ex...  140 us
    ppermute x7, waiting for transfers between devices, swap(): return lax.ppermute(values, 'tp', [(i, i ^ bit) for i in range(tp_size)])  131 us
    pallas_call x1, Pallas kernels, start_exchange(): pl.pallas_call(functools.partial(start_kernel, members, sets, count), in_...  82.5 us
    pallas_call x4, Pallas kernels, rows_grad(): kernel_call(functools.partial(rows_grad_kernel, len(xs), count), name, 2...  76.8 us
    ppermute x6, waiting for transfers between devices, turn(): lax.ppermute(values, 'tp', [(i, (i + step * members) % tp_size) for i in...  60.7 us
    pallas_call x2, Pallas kernels, attend_backward(): pl.pallas_call(functools.partial(backward_kernel, block, reach, heads), g...  51.7 us
    pallas_call x3, Pallas kernels, columns_grad(): kernel_call(functools.partial(columns_grad_kernel, len(xs), len(gs)), nam...  40.7 us
  transfers between devices with their start and end apart: 22, of which 12 were waited for; matrix products, arithmetic and copies ran while one was open for 6% of the time, Pallas kernels for 56%

profile of v3, /device:TPU:0, one launch (start us, length us, event | category | flops | bytes accessed | tf_op | source)
XLA Modules:
  0.0 880.2 jit_solution(1479307817492908653)
XLA Ops:
  12.0 3.9 copy.23
  15.9 82.5 %start_exchange.1 = (bf16[512,2048]{1,0:T(8,128)(2,1)}, bf16[512,2048]{1,0:T(8,128)(2,1)}, bf16[512,2048]{1,0:T(8,128)(2,1)}, bf16[512,2048]{1,0:T(8,128)(2,1)},...) custom-call(bf16[512,2048]{1,0:T(8,128)(2,1)} %x_ref.1, ...), custom_call_target="tpu_custom_call" | custom-call | flops 1 | bytes 1 | tf_op jit(solution)/shard_map/start_exchange/pallas_call | solution.py:193
  98.7 3.7 fusion.11
  104.3 14.3 %project.2.q_ref.k_ref.v_ref = bf16[2048,768]{1,0:T(8,128)(2,1)} custom-call(bf16[512,2048]{1,0:T(8,128)(2,1)} %get-tuple-element.379.refs_0_, bf16[512,2048]{1,0:T(8,128)(2,1)} %get-tuple-element.380.refs_1_, bf16[512,2048]{1,0:T(8,128)(2,1)} %get-tuple-element.381.refs_2_, bf16[512,2048]{1,0:T(8,128)(2,1)} %get-tuple-element.382.refs_3_, ...), custom_call_target="tpu_custom_call" | custom-call | flops 1 | bytes 1 | tf_op jit(solution)/shard_map/project/pallas_call | solution.py:295
  121.1 16.0 %attend_forward.2 = (bf16[2048,256]{1,0:T(8,128)(2,1)}, f32[2,4,1,512]{3,2,1,0:T(1,128)}) custom-call(s32[1]{0:T(128)} %bitcast.g_ref, bf16[2048,768]{1,0:T(8,128)(2,1)} %project.2.q_ref.k_ref.v_ref, bf16[2048,768]{1,0:T(8,128)(2,1)} %project.2.q_ref.k_ref.v_ref, bf16[2048,768]{1,0:T(8,128)(2,1)} %project.2.q_ref.k_ref.v_ref, ...), custom_call_target="tpu_custom_call" | custom-call | flops 1 | bytes 1 | tf_op jit(solution)/shard_map/attend_forward/pallas_call | solution.py:738
  137.1 14.5 %project.3.q_ref.k_ref.v_ref = bf16[2048,768]{1,0:T(8,128)(2,1)} custom-call(bf16[512,2048]{1,0:T(8,128)(2,1)} %get-tuple-element.379.refs_0_, bf16[512,2048]{1,0:T(8,128)(2,1)} %get-tuple-element.380.refs_1_, bf16[512,2048]{1,0:T(8,128)(2,1)} %get-tuple-element.381.refs_2_, bf16[512,2048]{1,0:T(8,128)(2,1)} %get-tuple-element.382.refs_3_, ...), custom_call_target="tpu_custom_call" | custom-call | flops 1 | bytes 1 | tf_op jit(solution)/shard_map/project/pallas_call | solution.py:295
  151.6 16.4 %attend_forward.3 = (bf16[2048,256]{1,0:T(8,128)(2,1)}, f32[2,4,1,512]{3,2,1,0:T(1,128)}) custom-call(s32[1]{0:T(128)} %bitcast.g_ref, bf16[2048,768]{1,0:T(8,128)(2,1)} %project.3.q_ref.k_ref.v_ref, bf16[2048,768]{1,0:T(8,128)(2,1)} %project.3.q_ref.k_ref.v_ref, bf16[2048,768]{1,0:T(8,128)(2,1)} %project.3.q_ref.k_ref.v_ref, ...), custom_call_target="tpu_custom_call" | custom-call | flops 1 | bytes 1 | tf_op jit(solution)/shard_map/attend_forward/pallas_call | solution.py:738
  168.1 12.7 %attn_branch.2 = bf16[512,2048]{1,0:T(8,128)(2,1)} custom-call(bf16[2048,256]{1,0:T(8,128)(2,1)} %get-tuple-element.373.refs_0_.out_ref, bf16[2048,256]{1,0:T(8,128)(2,1)} %get-tuple-element.348.refs_1_.out_ref.refs_0_, bf16[2048,256]{1,0:T(8,128)(2,1)} %copy-done.3, bf16[2048,256]{1,0:T(8,128)(2,1)} %get-tuple-element.398.refs_7_.refs_3_.refs_5_, ...), custom_call_target="tpu_custom_call" | custom-call | flops 1 | bytes 1 | tf_op jit(solution)/shard_map/attn_branch/pallas_call | solution.py:533
  180.8 11.3 %collective-permute-done.2 = bf16[512,2048]{1,0:T(8,128)(2,1)} collective-permute-done((bf16[512,2048]{1,0:T(8,128)(2,1)S(1)}, bf16[512,2048]{1,0:T(8,128)(2,1)}, u32[]{:S(2)}, u32[]{:S(2)}) %collective-permute-start.2) | collective-permute-done | bytes 2097184 | tf_op jit(solution)/shard_map/ppermute | solution.py:886
  193.0 12.7 %attn_branch.3 = f32[512,2048]{1,0:T(8,128)} custom-call(bf16[2048,256]{1,0:T(8,128)(2,1)} %get-tuple-element.373.refs_0_.out_ref, bf16[2048,256]{1,0:T(8,128)(2,1)} %get-tuple-element.348.refs_1_.out_ref.refs_0_, bf16[2048,256]{1,0:T(8,128)(2,1)} %copy-done.3, bf16[2048,256]{1,0:T(8,128)(2,1)} %get-tuple-element.398.refs_7_.refs_3_.refs_5_, ...), custom_call_target="tpu_custom_call" | custom-call | flops 1 | bytes 1 | tf_op jit(solution)/shard_map/attn_branch/pallas_call | solution.py:533
  206.0 34.1 %collective-permute-done = bf16[512,2048]{1,0:T(8,128)(2,1)} collective-permute-done((bf16[512,2048]{1,0:T(8,128)(2,1)}, bf16[512,2048]{1,0:T(8,128)(2,1)}, u32[]{:S(2)}, u32[]{:S(2)}) %collective-permute-start) | collective-permute-done | bytes 2097184 | tf_op jit(solution)/shard_map/ppermute | solution.py:883
  240.2 4.8 fusion.16
  247.3 46.5 %collective-permute-done.1.refs_1_.refs_2_ = bf16[512,2048]{1,0:T(8,128)(2,1)S(1)} collective-permute-done((bf16[512,2048]{1,0:T(8,128)(2,1)S(1)}, bf16[512,2048]{1,0:T(8,128)(2,1)S(1)}, u32[]{:S(2)}, u32[]{:S(2)}) %collective-permute-start.1) | collective-permute-done | bytes 2097184 | tf_op jit(solution)/shard_map/ppermute | solution.py:883
  297.1 31.0 %hidden_units.2 = (bf16[2048,1024]{1,0:T(8,128)(2,1)}, bf16[2048,1024]{1,0:T(8,128)(2,1)}, bf16[2048,1024]{1,0:T(8,128)(2,1)}, bf16[512,2048]{1,0:T(8,128)(2,1)}, bf16[512,2048]{1,0:T(8,128)(2,1)}) custom-call(bf16[512,2048]{1,0:T(8,128)(2,1)} %copy-done.7, bf16[512,2048]{1,0:T(8,128)(2,1)} %copy-done.9, bf16[4,512,2048]{2,1,0:T(8,128)(2,1)} %bitcast.46), custom_call_target="tpu_custom_call" | custom-call | flops 1 | bytes 1 | tf_op jit(solution)/shard_map/hidden_units/pallas_call | solution.py:295
  328.1 25.8 %hidden_units.3 = (bf16[2048,1024]{1,0:T(8,128)(2,1)}, bf16[2048,1024]{1,0:T(8,128)(2,1)}, bf16[2048,1024]{1,0:T(8,128)(2,1)}) custom-call(bf16[512,2048]{1,0:T(8,128)(2,1)} %copy-done.7, bf16[512,2048]{1,0:T(8,128)(2,1)} %get-tuple-element.307.refs_1_, bf16[512,2048]{1,0:T(8,128)(2,1)} %copy-done.9, bf16[512,2048]{1,0:T(8,128)(2,1)} %get-tuple-element.309.refs_3_, ...), custom_call_target="tpu_custom_call" | custom-call | flops 1 | bytes 1 | tf_op jit(solution)/shard_map/hidden_units/pallas_call | solution.py:295
  353.9 9.8 %collective-permute-done.4.refs_1_.refs_2_.refs_4_ = bf16[512,2048]{1,0:T(8,128)(2,1)} collective-permute-done((bf16[512,2048]{1,0:T(8,128)(2,1)}, bf16[512,2048]{1,0:T(8,128)(2,1)}, u32[]{:S(2)}, u32[]{:S(2)}) %collective-permute-start.4) | collective-permute-done | bytes 2097184 | tf_op jit(solution)/shard_map/ppermute | solution.py:883
  363.7 20.7 %hidden_grad.2 = (bf16[2048,2048]{1,0:T(8,128)(2,1)}, bf16[512,2048]{1,0:T(8,128)(2,1)}, bf16[512,2048]{1,0:T(8,128)(2,1)}) custom-call(bf16[512,2048]{1,0:T(8,128)(2,1)} %refs_2_, bf16[512,2048]{1,0:T(8,128)(2,1)} %collective-permute-done.4.refs_1_.refs_2_.refs_4_, bf16[2048,1024]{1,0:T(8,128)(2,1)} %get-tuple-element.283.refs_2_, ...), custom_call_target="tpu_custom_call" | custom-call | flops 1 | bytes 1 | tf_op jit(solution)/shard_map/hidden_grad/pallas_call | solution.py:295
  384.5 24.0 %grad_ffn.2 = bf16[4,2048,512]{2,1,0:T(8,128)(2,1)} custom-call(s32[1]{0:T(128)} %bitcast.13.f_ref, bf16[512,2048]{1,0:T(8,128)(2,1)} %copy-done.7, bf16[512,2048]{1,0:T(8,128)(2,1)} %get-tuple-element.307.refs_1_, bf16[512,2048]{1,0:T(8,128)(2,1)} %copy-done.9, bf16[512,2048]{1,0:T(8,128)(2,1)} %get-tuple-element.309.refs_3_, ...), custom_call_target="tpu_custom_call" | custom-call | flops 1 | bytes 1 | tf_op jit(solution)/shard_map/grad_ffn/pallas_call | solution.py:634
  408.5 25.3 %grad_normed_two.3.refs_1_ = bf16[2048,2048]{1,0:T(8,128)(2,1)} custom-call(bf16[2048,2048]{1,0:T(8,128)(2,1)} %get-tuple-element.297.refs_4_.refs_0_, bf16[4,512,2048]{2,1,0:T(8,128)(2,1)} %bitcast.47), custom_call_target="tpu_custom_call" | custom-call | flops 1 | bytes 1 | tf_op jit(solution)/shard_map/grad_normed_two/pallas_call | solution.py:533
  433.8 3.2 all-gather.15.cloned.1.call-done
  437.0 16.6 %hidden_grad.3.refs_4_.refs_0_ = bf16[2048,2048]{1,0:T(8,128)(2,1)} custom-call(bf16[512,2048]{1,0:T(8,128)(2,1)} %refs_2_, bf16[512,2048]{1,0:T(8,128)(2,1)} %get-tuple-element.329.refs_1_.refs_3_, bf16[512,2048]{1,0:T(8,128)(2,1)} %collective-permute-done.4.refs_1_.refs_2_.refs_4_, bf16[512,2048]{1,0:T(8,128)(2,1)} %get-tuple-element.331.refs_3_.refs_5_, ...), custom_call_target="tpu_custom_call" | custom-call | flops 1 | bytes 1 | tf_op jit(solution)/shard_map/hidden_grad/pallas_call | solution.py:295
  453.6 24.1 %grad_ffn.3 = bf16[4,2048,512]{2,1,0:T(8,128)(2,1)} custom-call(s32[1]{0:T(128)} %bitcast.13.f_ref, bf16[512,2048]{1,0:T(8,128)(2,1)} %copy-done.7, bf16[512,2048]{1,0:T(8,128)(2,1)} %get-tuple-element.307.refs_1_, bf16[512,2048]{1,0:T(8,128)(2,1)} %copy-done.9, bf16[512,2048]{1,0:T(8,128)(2,1)} %get-tuple-element.309.refs_3_, ...), custom_call_target="tpu_custom_call" | custom-call | flops 1 | bytes 1 | tf_op jit(solution)/shard_map/grad_ffn/pallas_call | solution.py:634
  477.8 17.8 %grad_normed_two.4 = bf16[512,2048]{1,0:T(8,128)(2,1)} custom-call(bf16[2048,2048]{1,0:T(8,128)(2,1)} %hidden_grad.3.refs_4_.refs_0_, bf16[2048,2048]{1,0:T(8,128)(2,1)} %grad_normed_two.3.refs_1_, bf16[4,512,2048]{2,1,0:T(8,128)(2,1)} %bitcast.36), custom_call_target="tpu_custom_call" | custom-call | flops 1 | bytes 1 | tf_op jit(solution)/shard_map/grad_normed_two/pallas_call | solution.py:533
  497.1 18.1 %grad_normed_two.5 = f32[512,2048]{1,0:T(8,128)} custom-call(bf16[2048,2048]{1,0:T(8,128)(2,1)} %hidden_grad.3.refs_4_.refs_0_, bf16[2048,2048]{1,0:T(8,128)(2,1)} %grad_normed_two.3.refs_1_, bf16[4,512,2048]{2,1,0:T(8,128)(2,1)} %bitcast.37), custom_call_target="tpu_custom_call" | custom-call | flops 1 | bytes 1 | tf_op jit(solution)/shard_map/grad_normed_two/pallas_call | solution.py:533
  515.2 17.4 %ffn_branch.2 = bf16[512,2048]{1,0:T(8,128)(2,1)} custom-call(bf16[2048,1024]{1,0:T(8,128)(2,1)} %get-tuple-element.326.refs_0_, bf16[2048,1024]{1,0:T(8,128)(2,1)} %get-tuple-element.327.refs_1_, bf16[4,1024,512]{2,1,0:T(8,128)(2,1)} %bitcast.42, bf16[4,1024,512]{2,1,0:T(8,128)(2,1)} %bitcast.39), custom_call_target="tpu_custom_call" | custom-call | flops 1 | bytes 1 | tf_op jit(solution)/shard_map/ffn_branch/pallas_call | solution.py:533
  532.6 11.1 %collective-permute-done.5 = bf16[512,2048]{1,0:T(8,128)(2,1)S(1)} collective-permute-done((bf16[512,2048]{1,0:T(8,128)(2,1)}, bf16[512,2048]{1,0:T(8,128)(2,1)S(1)}, u32[]{:S(2)}, u32[]{:S(2)}) %collective-permute-start.5) | collective-permute-done | bytes 2097184 | tf_op jit(solution)/shard_map/ppermute | solution.py:883
  545.2 4.4 fusion.15
  553.0 17.5 %ffn_branch.3 = f32[512,2048]{1,0:T(8,128)} custom-call(bf16[2048,1024]{1,0:T(8,128)(2,1)} %get-tuple-element.326.refs_0_, bf16[2048,1024]{1,0:T(8,128)(2,1)} %get-tuple-element.327.refs_1_, bf16[4,1024,512]{2,1,0:T(8,128)(2,1)} %bitcast.43, bf16[4,1024,512]{2,1,0:T(8,128)(2,1)} %bitcast.40), custom_call_target="tpu_custom_call" | custom-call | flops 1 | bytes 1 | tf_op jit(solution)/shard_map/ffn_branch/pallas_call | solution.py:533
  570.4 25.0 %grad_down.1 = bf16[4,2048,512]{2,1,0:T(8,128)(2,1)} custom-call(s32[1]{0:T(128)} %bitcast.13.f_ref, bf16[2048,1024]{1,0:T(8,128)(2,1)} %get-tuple-element.326.refs_0_, bf16[2048,1024]{1,0:T(8,128)(2,1)} %get-tuple-element.327.refs_1_, bf16[512,2048]{1,0:T(8,128)(2,1)} %refs_2_, bf16[512,2048]{1,0:T(8,128)(2,1)} %get-tuple-element.329.refs_1_.refs_3_, ...), custom_call_target="tpu_custom_call" | custom-call | flops 1 | bytes 1 | tf_op jit(solution)/shard_map/grad_down/pallas_call | solution.py:688
  596.9 11.3 %head_grad.2 = (bf16[2048,256]{1,0:T(8,128)(2,1)}, bf16[512,2048]{1,0:T(8,128)(2,1)}, bf16[512,2048]{1,0:T(8,128)(2,1)}) custom-call(bf16[512,2048]{1,0:T(8,128)(2,1)} %copy-done.6, bf16[512,2048]{1,0:T(8,128)(2,1)} %collective-permute-done.6.refs_1_.refs_3_.refs_2_, bf16[2048,256]{1,0:T(8,128)(2,1)} %get-tuple-element.401.refs_6_.refs_2_, ...), custom_call_target="tpu_custom_call" | custom-call | flops 1 | bytes 1 | tf_op jit(solution)/shard_map/head_grad/pallas_call | solution.py:295
  609.6 6.4 reduce-scatter.8.cloned.1.call-done
  616.0 3.0 fusion.20
  621.5 25.7 %attend_backward.2.refs_5_.refs_1_ = bf16[2048,768]{1,0:T(8,128)(2,1)} custom-call(s32[1]{0:T(128)} %bitcast.g_ref, bf16[2048,768]{1,0:T(8,128)(2,1)} %project.3.q_ref.k_ref.v_ref, bf16[2048,768]{1,0:T(8,128)(2,1)} %project.3.q_ref.k_ref.v_ref, bf16[2048,768]{1,0:T(8,128)(2,1)} %project.3.q_ref.k_ref.v_ref, bf16[2048,256]{1,0:T(8,128)(2,1)} %get-tuple-element.345.grad_ref, ...), custom_call_target="tpu_custom_call" | custom-call | flops 249999998976 | bytes 1 | tf_op jit(solution)/shard_map/attend_backward/pallas_call | solution.py:833
  647.1 8.0 grad_heads.2.refs_4_
  655.2 14.8 %grad_attn.2 = bf16[4,1024,512]{2,1,0:T(8,128)(2,1)} custom-call(s32[1]{0:T(128)} %bitcast.13.f_ref, bf16[512,2048]{1,0:T(8,128)(2,1)} %get-tuple-element.379.refs_0_, bf16[512,2048]{1,0:T(8,128)(2,1)} %get-tuple-element.380.refs_1_, bf16[512,2048]{1,0:T(8,128)(2,1)} %get-tuple-element.381.refs_2_, ...), custom_call_target="tpu_custom_call", output_to_operand_aliasing={{}: (5, {})} | custom-call | flops 1 | bytes 1 | tf_op jit(solution)/shard_map/grad_attn/pallas_call | solution.py:634
  670.0 8.6 collective-permute-done.7
  678.6 6.0 add_convert_fusion
  684.7 6.2 head_grad.3.grad_ref
  692.3 26.0 %attend_backward.3.refs_5_.refs_0_ = bf16[2048,768]{1,0:T(8,128)(2,1)} custom-call(s32[1]{0:T(128)} %bitcast.g_ref, bf16[2048,768]{1,0:T(8,128)(2,1)} %project.2.q_ref.k_ref.v_ref, bf16[2048,768]{1,0:T(8,128)(2,1)} %project.2.q_ref.k_ref.v_ref, bf16[2048,768]{1,0:T(8,128)(2,1)} %project.2.q_ref.k_ref.v_ref, bf16[2048,256]{1,0:T(8,128)(2,1)} %head_grad.3.grad_ref, ...), custom_call_target="tpu_custom_call" | custom-call | flops 249999998976 | bytes 1 | tf_op jit(solution)/shard_map/attend_backward/pallas_call | solution.py:833
  718.4 7.6 grad_heads.3.refs_4_
  726.0 12.9 %collective-permute-done.9 = bf16[1024,512]{1,0:T(8,128)(2,1)} collective-permute-done((bf16[1024,512]{1,0:T(8,128)(2,1)}, bf16[1024,512]{1,0:T(8,128)(2,1)}, u32[]{:S(2)}, u32[]{:S(2)}) %collective-permute-start.9) | collective-permute-done | bytes 1048608 | tf_op jit(solution)/shard_map/ppermute | solution.py:886
  738.9 13.9 %grad_attn.3 = bf16[4,1024,512]{2,1,0:T(8,128)(2,1)} custom-call(s32[1]{0:T(128)} %bitcast.13.f_ref, bf16[512,2048]{1,0:T(8,128)(2,1)} %get-tuple-element.379.refs_0_, bf16[512,2048]{1,0:T(8,128)(2,1)} %get-tuple-element.380.refs_1_, bf16[512,2048]{1,0:T(8,128)(2,1)} %get-tuple-element.381.refs_2_, ...), custom_call_target="tpu_custom_call", output_to_operand_aliasing={{}: (5, {})} | custom-call | flops 1 | bytes 1 | tf_op jit(solution)/shard_map/grad_attn/pallas_call | solution.py:634
  752.9 16.1 %grad_normed.2 = bf16[512,2048]{1,0:T(8,128)(2,1)} custom-call(bf16[2048,768]{1,0:T(8,128)(2,1)} %attend_backward.3.refs_5_.refs_0_, bf16[2048,768]{1,0:T(8,128)(2,1)} %attend_backward.2.refs_5_.refs_1_, bf16[2048,256]{1,0:T(8,128)(2,1)} %copy-done.3, bf16[2048,256]{1,0:T(8,128)(2,1)} %get-tuple-element.398.refs_7_.refs_3_.refs_5_, ...), custom_call_target="tpu_custom_call" | custom-call | flops 1 | bytes 1 | tf_op jit(solution)/shard_map/grad_normed/pallas_call | solution.py:533
  779.9 16.2 %grad_normed.3 = f32[512,2048]{1,0:T(8,128)} custom-call(bf16[2048,768]{1,0:T(8,128)(2,1)} %attend_backward.3.refs_5_.refs_0_, bf16[2048,768]{1,0:T(8,128)(2,1)} %attend_backward.2.refs_5_.refs_1_, bf16[2048,256]{1,0:T(8,128)(2,1)} %copy-done.3, bf16[2048,256]{1,0:T(8,128)(2,1)} %get-tuple-element.398.refs_7_.refs_3_.refs_5_, ...), custom_call_target="tpu_custom_call" | custom-call | flops 1 | bytes 1 | tf_op jit(solution)/shard_map/grad_normed/pallas_call | solution.py:533
  796.1 5.2 copy.22
  801.3 36.5 %collective-permute-done.12 = bf16[1024,512]{1,0:T(8,128)(2,1)} collective-permute-done((bf16[1024,512]{1,0:T(8,128)(2,1)S(1)}, bf16[1024,512]{1,0:T(8,128)(2,1)}, u32[]{:S(2)}, u32[]{:S(2)}) %collective-permute-start.12) | collective-permute-done | bytes 1048608 | tf_op jit(solution)/shard_map/ppermute | solution.py:886
  840.7 19.5 %collective-permute-done.10 = bf16[512,2048]{1,0:T(8,128)(2,1)} collective-permute-done((bf16[512,2048]{1,0:T(8,128)(2,1)}, bf16[512,2048]{1,0:T(8,128)(2,1)}, u32[]{:S(2)}, u32[]{:S(2)}) %collective-permute-start.10) | collective-permute-done | bytes 2097184 | tf_op jit(solution)/shard_map/ppermute | solution.py:883
  860.2 4.3 convert_add_fusion.1
  (134 shorter events, 52.1 us)
Async XLA Ops:
  7.2 289.9 %all-gather.9.cloned.1.call-start = ((), (), s32[]{:S(2)}) async-start(), calls=%async_computation.10 | async-start | bytes 10485760 | tf_op jit(solution)/shard_map/all_gather | solution.py:936
  12.0 3.9 copy-start.3
  12.0 86.6 %copy-start.22 = (s32[4096]{0:T(1024)S(1)}, s32[4096]{0:T(1024)}, u32[]{:S(2)}) copy-start(s32[4096]{0:T(1024)} %param.16) | copy-start | bytes 49156
  15.9 82.5 %copy-start.13 = (bf16[64,8,2,1024]{3,1,2,0:T(8,128)(2,1)S(1)}, bf16[64,8,2,1024]{3,1,2,0:T(8,128)(2,1)}, u32[]{:S(2)}) copy-start(bf16[64,8,2,1024]{3,1,2,0:T(8,128)(2,1)} %copy.23) | copy-start | bytes 6291460
  98.4 229.7 %all-gather.11.cloned.1.call-start = ((), (), s32[]{:S(2)}) async-start(), calls=%async_computation.11 | async-start | bytes 10485760 | tf_op jit(solution)/shard_map/all_gather | solution.py:936
  98.4 93.7 %collective-permute-start.2 = (bf16[512,2048]{1,0:T(8,128)(2,1)S(1)}, bf16[512,2048]{1,0:T(8,128)(2,1)}, u32[]{:S(2)}, u32[]{:S(2)}) collective-permute-start(bf16[512,2048]{1,0:T(8,128)(2,1)S(1)} %bitcast.52), channel_id=1, source_target_pairs={{0,4},{1,5},{2,6},{3,7},{4,0},{5,1},{6,2},{7,3},{8,12},{9,13},{10,... | collective-permute-start | bytes 6291464 | tf_op jit(solution)/shard_map/ppermute | solution.py:886
  104.3 14.3 %copy-start.23 = (s32[4096]{0:T(1024)S(1)}, s32[4096]{0:T(1024)}, u32[]{:S(2)}) copy-start(s32[4096]{0:T(1024)} %param.15) | copy-start | bytes 49156
  104.3 14.3 %copy-start.24 = (s32[4096]{0:T(1024)S(1)}, s32[4096]{0:T(1024)}, u32[]{:S(2)}) copy-start(s32[4096]{0:T(1024)} %param.14) | copy-start | bytes 49156
  119.3 17.9 %copy-start.18 = (s32[2048]{0:T(1024)}, s32[2048]{0:T(1024)S(1)}, u32[]{:S(2)}) copy-start(s32[2048]{0:T(1024)S(1)} %get-tuple-element.425) | copy-start | bytes 24580
  192.2 171.5 %all-gather.13.cloned.1.call-start = ((), (), s32[]{:S(2)}) async-start(), calls=%async_computation.12 | async-start | bytes 5242880 | tf_op jit(solution)/shard_map/all_gather | solution.py:936
  192.2 48.0 %collective-permute-start = (bf16[512,2048]{1,0:T(8,128)(2,1)}, bf16[512,2048]{1,0:T(8,128)(2,1)}, u32[]{:S(2)}, u32[]{:S(2)}) collective-permute-start(bf16[512,2048]{1,0:T(8,128)(2,1)} %attn_branch.2), channel_id=1, source_target_pairs={{0,2},{1,3},{2,0},{3,1},{4,6},{5,7},{6,4},{7,5},{8,10},{9,11},{10,... | collective-permute-start | bytes 6291464 | tf_op jit(solution)/shard_map/ppermute | solution.py:883
  192.9 12.8 %copy-start.4 = (bf16[512,2048]{1,0:T(8,128)(2,1)S(1)}, bf16[512,2048]{1,0:T(8,128)(2,1)}, u32[]{:S(2)}) copy-start(bf16[512,2048]{1,0:T(8,128)(2,1)} %x_ref.1) | copy-start | bytes 6291460
  192.9 244.1 %all-gather.15.cloned.1.call-start = ((), (), s32[]{:S(2)}) async-start(), calls=%async_computation.13 | async-start | bytes 5242880 | tf_op jit(solution)/shard_map/all_gather | solution.py:936
  206.0 39.0 %copy-start.19 = (f32[512]{0:T(512)}, f32[512]{0:T(512)S(1)}, u32[]{:S(2)}) copy-start(f32[512]{0:T(512)S(1)} %broadcast_multiply_fusion.2) | copy-start | bytes 6148
  245.0 2.0 copy-start
  245.6 50.1 %copy-start.16 = (bf16[1024,512]{1,0:T(8,128)(2,1)S(1)}, bf16[1024,512]{1,0:T(8,128)(2,1)}, u32[]{:S(2)}) copy-start(bf16[1024,512]{1,0:T(8,128)(2,1)} %param.13) | copy-start | bytes 3145732
  247.0 50.0 %copy-start.7 = (bf16[512,2048]{1,0:T(8,128)(2,1)}, bf16[512,2048]{1,0:T(8,128)(2,1)S(1)}, u32[]{:S(2)}) copy-start(bf16[512,2048]{1,0:T(8,128)(2,1)S(1)} %fusion.10.refs_0_) | copy-start | bytes 6291460
  247.0 46.8 %collective-permute-start.1 = (bf16[512,2048]{1,0:T(8,128)(2,1)S(1)}, bf16[512,2048]{1,0:T(8,128)(2,1)S(1)}, u32[]{:S(2)}, u32[]{:S(2)}) collective-permute-start(bf16[512,2048]{1,0:T(8,128)(2,1)S(1)} %fusion.10.refs_0_), channel_id=1, source_target_pairs={{0,2},{1,3},{2,0},{3,1},{4,6},{5,7},{6,4},{7,5},{8,10},{9,11},{10,... | collective-permute-start | bytes 6291464 | tf_op jit(solution)/shard_map/ppermute | solution.py:883
  293.8 1.3 copy-start.9
  295.1 68.6 %collective-permute-start.4 = (bf16[512,2048]{1,0:T(8,128)(2,1)}, bf16[512,2048]{1,0:T(8,128)(2,1)}, u32[]{:S(2)}, u32[]{:S(2)}) collective-permute-start(bf16[512,2048]{1,0:T(8,128)(2,1)} %refs_2_), channel_id=1, source_target_pairs={{0,2},{1,3},{2,0},{3,1},{4,6},{5,7},{6,4},{7,5},{8,10},{9,11},{10,... | collective-permute-start | bytes 6291464 | tf_op jit(solution)/shard_map/ppermute | solution.py:883
  295.7 88.7 %collective-permute-start.3 = (bf16[1024,512]{1,0:T(8,128)(2,1)S(1)}, bf16[1024,512]{1,0:T(8,128)(2,1)}, u32[]{:S(2)}, u32[]{:S(2)}) collective-permute-start(bf16[1024,512]{1,0:T(8,128)(2,1)S(1)} %copy-done.16), channel_id=1, source_target_pairs={{0,4},{1,5},{2,6},{3,7},{4,0},{5,1},{6,2},{7,3},{8,12},{9,13},{10,... | collective-permute-start | bytes 3145736 | tf_op jit(solution)/shard_map/ppermute | solution.py:886
  384.4 212.5 %reduce-scatter.6.cloned.1.call-start = ((), (), s32[]{:S(2)}) async-start(), calls=%async_computation.5 | async-start | bytes 10485760 | tf_op jit(solution)/shard_map/reduce_scatter | solution.py:939
  408.4 207.6 %reduce-scatter.8.cloned.1.call-start = ((), (), s32[]{:S(2)}) async-start(), calls=%async_computation.6 | async-start | bytes 10485760 | tf_op jit(solution)/shard_map/reduce_scatter | solution.py:939
  477.7 291.4 %reduce-scatter.14.cloned.1.call-start = ((), (), s32[]{:S(2)}) async-start(), calls=%async_computation.9 | async-start | bytes 10485760 | tf_op jit(solution)/shard_map/reduce_scatter | solution.py:939
  495.6 48.1 %collective-permute-start.5 = (bf16[512,2048]{1,0:T(8,128)(2,1)}, bf16[512,2048]{1,0:T(8,128)(2,1)S(1)}, u32[]{:S(2)}, u32[]{:S(2)}) collective-permute-start(bf16[512,2048]{1,0:T(8,128)(2,1)} %grad_normed_two.4), channel_id=1, source_target_pairs={{0,2},{1,3},{2,0},{3,1},{4,6},{5,7},{6,4},{7,5},{8,10},{9,11},{10,... | collective-permute-start | bytes 6291464 | tf_op jit(solution)/shard_map/ppermute | solution.py:883
  515.2 28.5 %copy-start.10 = (f32[512,2048]{1,0:T(8,128)S(1)}, f32[512,2048]{1,0:T(8,128)}, u32[]{:S(2)}) copy-start(f32[512,2048]{1,0:T(8,128)} %grad_normed_two.5) | copy-start | bytes 12582916
  532.6 11.7 %copy-start.1 = (f32[512,2048]{1,0:T(8,128)S(1)}, f32[512,2048]{1,0:T(8,128)}, u32[]{:S(2)}) copy-start(f32[512,2048]{1,0:T(8,128)} %copy-done) | copy-start | bytes 12582916
  545.2 5.9 copy-start.17
  549.6 20.8 %copy-start.6 = (bf16[512,2048]{1,0:T(8,128)(2,1)}, bf16[512,2048]{1,0:T(8,128)(2,1)S(1)}, u32[]{:S(2)}) copy-start(bf16[512,2048]{1,0:T(8,128)(2,1)S(1)} %get-tuple-element.374.refs_0_.refs_1_) | copy-start | bytes 6291460
  549.6 47.2 %collective-permute-start.6 = (bf16[512,2048]{1,0:T(8,128)(2,1)S(1)}, bf16[512,2048]{1,0:T(8,128)(2,1)}, u32[]{:S(2)}, u32[]{:S(2)}) collective-permute-start(bf16[512,2048]{1,0:T(8,128)(2,1)S(1)} %get-tuple-element.374.refs_0_.refs_1_), channel_id=1, source_target_pairs={{0,2},{1,3},{2,0},{3,1},{4,6},{5,7},{6,4},{7,5},{8,10},{9,11},{10,... | collective-permute-start | bytes 6291464 | tf_op jit(solution)/shard_map/ppermute | solution.py:883
  595.5 181.3 %reduce-scatter.10.cloned.1.call-start = ((), (), s32[]{:S(2)}) async-start(), calls=%async_computation.7 | async-start | bytes 5242880 | tf_op jit(solution)/shard_map/reduce_scatter | solution.py:939
  608.1 70.5 %collective-permute-start.7 = (bf16[512,2048]{1,0:T(8,128)(2,1)}, bf16[512,2048]{1,0:T(8,128)(2,1)}, u32[]{:S(2)}, u32[]{:S(2)}) collective-permute-start(bf16[512,2048]{1,0:T(8,128)(2,1)} %ffn_branch.2), channel_id=1, source_target_pairs={{0,2},{1,3},{2,0},{3,1},{4,6},{5,7},{6,4},{7,5},{8,10},{9,11},{10,... | collective-permute-start | bytes 6291464 | tf_op jit(solution)/shard_map/ppermute | solution.py:883
  619.0 65.6 %collective-permute-start.8 = (bf16[1024,512]{1,0:T(8,128)(2,1)}, bf16[1024,512]{1,0:T(8,128)(2,1)}, u32[]{:S(2)}, u32[]{:S(2)}) collective-permute-start(bf16[1024,512]{1,0:T(8,128)(2,1)} %get-tuple-element.359), channel_id=1, source_target_pairs={{0,4},{1,5},{2,6},{3,7},{4,0},{5,1},{6,2},{7,3},{8,12},{9,13},{10,... | collective-permute-start | bytes 3145736 | tf_op jit(solution)/shard_map/ppermute | solution.py:886
  655.2 23.4 %copy-start.2 = (f32[512,2048]{1,0:T(8,128)S(1)}, f32[512,2048]{1,0:T(8,128)}, u32[]{:S(2)}) copy-start(f32[512,2048]{1,0:T(8,128)} %copy-done) | copy-start | bytes 12582916
  690.9 48.0 %collective-permute-start.9 = (bf16[1024,512]{1,0:T(8,128)(2,1)}, bf16[1024,512]{1,0:T(8,128)(2,1)}, u32[]{:S(2)}, u32[]{:S(2)}) collective-permute-start(bf16[1024,512]{1,0:T(8,128)(2,1)} %get-tuple-element.378), channel_id=1, source_target_pairs={{0,4},{1,5},{2,6},{3,7},{4,0},{5,1},{6,2},{7,3},{8,12},{9,13},{10,... | collective-permute-start | bytes 3145736 | tf_op jit(solution)/shard_map/ppermute | solution.py:886
  692.3 172.2 %reduce-scatter.12.cloned.1.call-start = ((), (), s32[]{:S(2)}) async-start(), calls=%async_computation.8 | async-start | bytes 5242880 | tf_op jit(solution)/shard_map/reduce_scatter | solution.py:939
  752.9 16.2 %copy-start.21 = (f32[512]{0:T(512)S(1)}, f32[512]{0:T(512)}, u32[]{:S(2)}) copy-start(f32[512]{0:T(512)} %get-tuple-element.437) | copy-start | bytes 6148
  752.9 19.8 %copy-start.15 = (bf16[2048,512]{1,0:T(8,128)(2,1)S(1)}, bf16[2048,512]{1,0:T(8,128)(2,1)}, u32[]{:S(2)}) copy-start(bf16[2048,512]{1,0:T(8,128)(2,1)} %reduce-scatter.6.cloned.1.call-done) | copy-start | bytes 6291460
  769.0 91.2 %collective-permute-start.10 = (bf16[512,2048]{1,0:T(8,128)(2,1)}, bf16[512,2048]{1,0:T(8,128)(2,1)}, u32[]{:S(2)}, u32[]{:S(2)}) collective-permute-start(bf16[512,2048]{1,0:T(8,128)(2,1)} %grad_normed.2), channel_id=1, source_target_pairs={{0,2},{1,3},{2,0},{3,1},{4,6},{5,7},{6,4},{7,5},{8,10},{9,11},{10,... | collective-permute-start | bytes 6291464 | tf_op jit(solution)/shard_map/ppermute | solution.py:883
  770.4 67.4 %collective-permute-start.12 = (bf16[1024,512]{1,0:T(8,128)(2,1)S(1)}, bf16[1024,512]{1,0:T(8,128)(2,1)}, u32[]{:S(2)}, u32[]{:S(2)}) collective-permute-start(bf16[1024,512]{1,0:T(8,128)(2,1)S(1)} %slice.97), channel_id=1, source_target_pairs={{0,4},{1,5},{2,6},{3,7},{4,0},{5,1},{6,2},{7,3},{8,12},{9,13},{10,... | collective-permute-start | bytes 3145736 | tf_op jit(solution)/shard_map/ppermute | solution.py:886
  776.8 87.6 %collective-permute-start.11 = (bf16[1024,512]{1,0:T(8,128)(2,1)}, bf16[1024,512]{1,0:T(8,128)(2,1)}, u32[]{:S(2)}, u32[]{:S(2)}) collective-permute-start(bf16[1024,512]{1,0:T(8,128)(2,1)} %reduce-scatter.10.cloned.1.call-done), channel_id=1, source_target_pairs={{0,4},{1,5},{2,6},{3,7},{4,0},{5,1},{6,2},{7,3},{8,12},{9,13},{10,... | collective-permute-start | bytes 3145736 | tf_op jit(solution)/shard_map/ppermute | solution.py:886
  796.1 41.7 %copy-start.14 = (bf16[2048,512]{1,0:T(8,128)(2,1)S(1)}, bf16[2048,512]{1,0:T(8,128)(2,1)}, u32[]{:S(2)}) copy-start(bf16[2048,512]{1,0:T(8,128)(2,1)} %reduce-scatter.14.cloned.1.call-done) | copy-start | bytes 6291460
  801.3 58.8 %copy-start.11 = (f32[512,2048]{1,0:T(8,128)S(1)}, f32[512,2048]{1,0:T(8,128)}, u32[]{:S(2)}) copy-start(f32[512,2048]{1,0:T(8,128)} %grad_normed.3) | copy-start | bytes 12582916
  864.4 2.2 copy-start.5
  864.4 2.2 copy-start.20
  864.5 3.4 copy-start.8
  867.9 3.1 copy-start.12
Sparse Core Ops, SparseCore 0:
  98.5 87.7 all-gather.8
  192.3 87.2 all-gather.10
  281.4 52.6 all-gather.12
  384.5 52.4 all-gather.14
  439.9 86.4 reduce-scatter.5
  529.6 86.4 reduce-scatter.7
  619.1 86.3 reduce-scatter.13
  708.8 52.6 reduce-scatter.9
  764.5 52.6 reduce-scatter.11

commit v4 on v3

--- a/solution.py
+++ b/solution.py
@@ -15,7 +15,7 @@
 NEGATIVE = -1e30
 ROPE_BASE = 10000.0
 LOG2E = math.log2(math.e)
-LONG = 25 * 10**10
+LONG = 10**12
 VMEM_LIMIT = 56 * 1024 * 1024
 F32 = jnp.float32
 BF16 = jnp.bfloat16
@@ -58,7 +58,7 @@
     return jnp.concatenate([cosine, cosine], axis=-1), jnp.concatenate([-sine, sine], axis=-1)
 
 
-def kernel_call(kernel, name, flops, grid, in_specs, out_specs, out_shapes, scratch, aliases={}):
+def kernel_call(kernel, name, cost, grid, in_specs, out_specs, out_shapes, scratch, aliases={}):
     return pl.pallas_call(
         kernel,
         grid_spec=pltpu.PrefetchScalarGridSpec(
@@ -67,7 +67,7 @@
         out_shape=out_shapes,
         input_output_aliases=aliases,
         compiler_params=pltpu.CompilerParams(vmem_limit_bytes=VMEM_LIMIT),
-        cost_estimate=pl.CostEstimate(flops=1, bytes_accessed=1, transcendentals=0),
+        cost_estimate=pl.CostEstimate(flops=cost, bytes_accessed=1, transcendentals=0),
         name=name,
     )
 
@@ -273,17 +273,18 @@
             for n in range(len(tiles) + 2, len(tiles) + held - 1):
                 start(n)
 
-    pl.when(i == 0)(functools.partial(run, True))
-    pl.when(i > 0)(functools.partial(run, False))
     for q, exchange in enumerate(exchanges):
 
-        @pl.when(i == max(held - 1, 0) + q)
+        @pl.when(i == 1 + q)
         def _():
             exchange.wait()
             x_copies[held + q].start()
 
-
-def rows_call(body, name, xs, extras, weights, plan, tiles, copies, w_shape, widths, number):
+    pl.when(i == 0)(functools.partial(run, True))
+    pl.when(i > 0)(functools.partial(run, False))
+
+
+def rows_call(body, name, xs, extras, weights, plan, tiles, copies, w_shape, widths, number, cost=1):
     rows, model = xs[0].shape
     held, count = len(xs), len(weights)
     members = 2 * held if number else held
@@ -312,7 +313,7 @@
         compiler_params=pltpu.CompilerParams(
             vmem_limit_bytes=VMEM_LIMIT, **({"collective_id": number, "has_side_effects": True} if number else {})
         ),
-        cost_estimate=pl.CostEstimate(flops=1, bytes_accessed=1, transcendentals=0),
+        cost_estimate=pl.CostEstimate(flops=cost, bytes_accessed=1, transcendentals=0),
         name=name,
     )(*xs, *extras, *weights)
     if not number:
@@ -407,7 +408,7 @@
     )
 
 
-def hidden_grad(xs, slope_up, slope_gate, stack, number=0):
+def hidden_grad(xs, slope_up, slope_gate, stack, number=0, cost=1):
     model = xs[0].shape[1]
     count, width, depth = stack.shape
     tile = min(512, width)
@@ -432,7 +433,7 @@
 
     return rows_call(
         body, "hidden_grad", xs, [slope_up, slope_gate], [stack], (moves, use),
-        len(starts), count, (width, model), [2 * width], number,
+        len(starts), count, (width, model), [2 * width], number, cost,
     )
 
 
@@ -442,8 +443,9 @@
     weights, refs = refs[: sets * each], refs[sets * each :]
     outs, refs = refs[: max(pairs, 1)], refs[max(pairs, 1) :]
     w_buf, sem = refs[:2]
-    d, f = pl.program_id(0), lax.axis_index("fsdp")
+    step, f = pl.program_id(0), lax.axis_index("fsdp")
     count = w_buf.shape[1]
+    d = lax.rem(step, count)
 
     def copies(j, c):
         there, moves = plan(weights[j * each : (j + 1) * each], c, f)
@@ -476,17 +478,21 @@
                 device_id_type=pl.DeviceIdType.MESH,
             )
 
-        @pl.when(d == 0)
+        @pl.when(step == 0)
         def _():
             barrier = pltpu.get_barrier_semaphore()
             pl.semaphore_signal(barrier, inc=1, device_id=partner, device_id_type=pl.DeviceIdType.MESH)
             pl.semaphore_wait(barrier, 1)
 
-    pl.when(d == 0)(functools.partial(start, 0))
-    start(d + 1)
-    for j in range(sets):
-        for n, (src, lanes) in enumerate(plan(weights[j * each : (j + 1) * each], 0, f)[1]):
-            pltpu.make_async_copy(src, w_buf.at[j, d, :, lanes], sem.at[j, d, n]).wait()
+    pl.when(step == 0)(functools.partial(start, 0))
+    pl.when(step < count - 1)(lambda: start(d + 1))
+
+    @pl.when(step < count)
+    def _():
+        for j in range(sets):
+            for n, (src, lanes) in enumerate(plan(weights[j * each : (j + 1) * each], 0, f)[1]):
+                pltpu.make_async_copy(src, w_buf.at[j, d, :, lanes], sem.at[j, d, n]).wait()
+
     rows = outs[0].shape[0]
 
     def block(p):
@@ -499,22 +505,28 @@
     if not pairs:
         outs[0][...] = block(0).astype(outs[0].dtype)
         return
-    for q in range(pairs):
-        send_buf[d, q] = block(2 * q + 1).astype(BF16)
-        exchange(d, q).start()
-    for q in range(pairs):
-        total = block(2 * q)
-        exchange(d, q).wait_recv()
-        outs[q][...] = (total + recv_buf[d, q].astype(F32)).astype(outs[q].dtype)
-
-    @pl.when(d == count - 1)
+
+    @pl.when(step < count)
+    def _():
+        for q in range(pairs):
+            send_buf[d, q] = block(2 * q + 1).astype(BF16)
+            exchange(d, q).start()
+
+    @pl.when(step >= count)
+    def _():
+        for q in range(pairs):
+            total = block(2 * q)
+            exchange(d, q).wait_recv()
+            outs[q][...] = (total + recv_buf[d, q].astype(F32)).astype(outs[q].dtype)
+
+    @pl.when(step == 2 * count - 1)
     def _():
         for place in range(count):
             for q in range(pairs):
                 exchange(place, q).wait_send()
 
 
-def expand_call(name, xs, weights, each, plan, pieces, dot, chunk, rows, base=None, first=None, members=0, number=0):
+def expand_call(name, xs, weights, each, plan, pieces, dot, chunk, rows, base=None, first=None, members=0, number=0, cost=1):
     count, w_shape = chunk
     depth = w_shape[1 if dot is dot_nn else 0]
     pairs = members // 2
@@ -522,7 +534,8 @@
     block = 0 if first is None else first // members
     specs = [pl.BlockSpec((taken, x.shape[1]), lambda d: (block, 0)) for x in xs]
     bases = [] if base is None else [base]
-    specs += [pl.BlockSpec((taken, depth), lambda d: (block, d)) for _ in bases]
+    specs += [pl.BlockSpec((taken, depth), lambda d: (block, lax.rem(d, count))) for _ in bases]
+    steps = 2 * count if pairs else count
     scratch = [pltpu.VMEM((len(xs), count) + w_shape, BF16), pltpu.SemaphoreType.DMA((len(xs), count, pieces))]
     types = [BF16]
     more = {}
@@ -534,14 +547,14 @@
         functools.partial(expand_kernel, len(xs), each, plan, dot, base is not None, pairs),
         grid_spec=pltpu.PrefetchScalarGridSpec(
             num_scalar_prefetch=0,
-            grid=(count,),
+            grid=(steps,),
             in_specs=specs + any_specs(weights),
-            out_specs=[pl.BlockSpec((rows, depth), lambda d: (0, d)) for _ in types],
+            out_specs=[pl.BlockSpec((rows, depth), lambda d: (0, lax.max(d + count - steps, 0))) for _ in types],
             scratch_shapes=scratch,
         ),
         out_shape=[jax.ShapeDtypeStruct((rows, count * depth), type_) for type_ in types],
         compiler_params=pltpu.CompilerParams(vmem_limit_bytes=VMEM_LIMIT, **more),
-        cost_estimate=pl.CostEstimate(flops=1, bytes_accessed=1, transcendentals=0),
+        cost_estimate=pl.CostEstimate(flops=cost, bytes_accessed=1, transcendentals=0),
         name=name,
     )(*xs, *bases, *weights)
 
@@ -624,7 +637,7 @@
     pl.when(pl.program_id(0) > 0)(functools.partial(run, False))
 
 
-def rows_grad(name, place, count, tile, beside, below, xs, g, stack=None):
+def rows_grad(name, place, count, tile, beside, below, xs, g, stack=None, cost=1):
     rows, model = xs[0].shape
     tokens, width = g.shape
     depth = model // count
@@ -634,7 +647,7 @@
     return kernel_call(
         functools.partial(rows_grad_kernel, len(xs), count),
         name,
-        2 * tokens * model * width,
+        cost,
         (tiles,),
         any_specs(xs) + any_specs(given) + [pl.BlockSpec((tokens, tile), lambda n, f: (0, n))],
         pl.BlockSpec((count, depth, tile), lambda n, f: (0, n // beside, n % beside)),
@@ -688,7 +701,7 @@
     return kernel_call(
         functools.partial(columns_grad_kernel, len(xs), len(gs)),
         name,
-        2 * tokens * model * sum(x.shape[1] for x in xs),
+        1,
         (count,),
         [pl.BlockSpec(x.shape, lambda d, f: (0, 0)) for x in xs] + any_specs(gs) + any_specs(given),
         pl.BlockSpec((1, height, tile), lambda d, f: (d, *at)),
@@ -699,15 +712,15 @@
 
 
 def forward_kernel(block, reach, g_ref, q_ref, k_ref, v_ref, seg_ref, key_ref, out_ref, lse_ref):
-    i = pl.program_id(1)
+    i = pl.program_id(0)
     g = g_ref[0]
     scale = LOG2E / math.sqrt(HD)
+    heads = q_ref.shape[1] // HD
 
     def run(count):
-        q = q_ref[...]
         row = lax.broadcasted_iota(jnp.int32, (block, block), 0)
         column = lax.broadcasted_iota(jnp.int32, (block, block), 1)
-        scores, rows = [], []
+        keeps, rows = [], []
         for back in range(count):
             b = i - back
             rows.append(pl.ds(pl.multiple_of((b ^ g) * block, block), block))
@@ -716,14 +729,18 @@
                 keep = (keep & (row > column)) | (row == column)
             if back == reach:
                 keep = keep & (row < column)
-            scores.append(jnp.where(keep, dot_nt(q, k_ref[rows[-1], :]) * scale, NEGATIVE))
-        top = functools.reduce(jnp.maximum, [jnp.max(s, axis=1, keepdims=True) for s in scores])
-        weights = [jnp.exp2(s - top) for s in scores]
-        total = sum(jnp.sum(w, axis=1, keepdims=True) for w in weights)
-        out = sum(dot_nn(w.astype(BF16), v_ref[r, :]) for w, r in zip(weights, rows))
-        out_ref[...] = (out / total).astype(BF16)
-        lse = top + jnp.log2(total)
-        lse_ref[0, 0] = jnp.transpose(jnp.broadcast_to(lse, (block, HD)))[0:1, :]
+            keeps.append(keep)
+        for h in range(heads):
+            lanes = slice(h * HD, (h + 1) * HD)
+            q = q_ref[:, lanes]
+            scores = [jnp.where(keep, dot_nt(q, k_ref[r, lanes]), NEGATIVE) for keep, r in zip(keeps, rows)]
+            top = functools.reduce(jnp.maximum, [jnp.max(s, axis=1, keepdims=True) for s in scores])
+            weights = [jnp.exp2((s - top) * scale) for s in scores]
+            total = sum(jnp.sum(w, axis=1, keepdims=True) for w in weights)
+            out = sum(dot_nn(w.astype(BF16), v_ref[r, lanes]) for w, r in zip(weights, rows))
+            out_ref[:, lanes] = (out / total).astype(BF16)
+            lse = top * scale + jnp.log2(total)
+            lse_ref[h, 0] = jnp.transpose(jnp.broadcast_to(lse, (block, HD)))[0:1, :]
 
     for i_here in range(reach):
         pl.when(i == i_here)(functools.partial(run, i_here + 1))
@@ -739,17 +756,17 @@
         functools.partial(forward_kernel, block, reach),
         grid_spec=pltpu.PrefetchScalarGridSpec(
             num_scalar_prefetch=1,
-            grid=(heads, count),
+            grid=(count,),
             in_specs=[
-                pl.BlockSpec((block, HD), lambda h, i, g: (i ^ g[0], h)),
-                pl.BlockSpec((tokens, HD), lambda h, i, g: (0, heads + h)),
-                pl.BlockSpec((tokens, HD), lambda h, i, g: (0, 2 * heads + h)),
-                pl.BlockSpec((1, block, 1), lambda h, i, g: (i, 0, 0)),
-                pl.BlockSpec((count, 1, block), lambda h, i, g: (0, 0, 0)),
+                pl.BlockSpec((block, heads * HD), lambda i, g: (i ^ g[0], 0)),
+                pl.BlockSpec((tokens, heads * HD), lambda i, g: (0, 1)),
+                pl.BlockSpec((tokens, heads * HD), lambda i, g: (0, 2)),
+                pl.BlockSpec((1, block, 1), lambda i, g: (i, 0, 0)),
+                pl.BlockSpec((count, 1, block), lambda i, g: (0, 0, 0)),
             ],
             out_specs=[
-                pl.BlockSpec((block, HD), lambda h, i, g: (i ^ g[0], h)),
-                pl.BlockSpec((1, 1, 1, block), lambda h, i, g: (h, i, 0, 0)),
+                pl.BlockSpec((block, heads * HD), lambda i, g: (i ^ g[0], 0)),
+                pl.BlockSpec((heads, 1, 1, block), lambda i, g: (0, i, 0, 0)),
             ],
         ),
         out_shape=[
@@ -765,7 +782,6 @@
 def backward_kernel(
     block, reach, heads, g_ref, q_ref, k_ref, v_ref, grad_ref, out_ref, lse_ref, seg_ref, key_ref, cos_ref, sin_ref, result_ref, dq_ref, dk_ref, dv_ref, inner_ref
 ):
-    h = pl.program_id(0)
     g = g_ref[0]
     count = q_ref.shape[0] // block
     scale = 1.0 / math.sqrt(HD)
@@ -779,8 +795,10 @@
 
     def inner_block(i, carry):
         rows = rows_of(i)
-        product = grad_ref[rows, :].astype(F32) * out_ref[rows, :].astype(F32)
-        inner_ref[i] = jnp.sum(jnp.transpose(product), axis=0, keepdims=True)
+        for h in range(heads):
+            lanes = slice(h * HD, (h + 1) * HD)
+            product = grad_ref[rows, lanes].astype(F32) * out_ref[rows, lanes].astype(F32)
+            inner_ref[h, i] = jnp.sum(jnp.transpose(product), axis=0, keepdims=True)
         return carry
 
     lax.fori_loop(0, count, inner_block, 0)
@@ -789,8 +807,6 @@
         def pair(i, carry, back=back):
             b = i - back
             query_rows, key_rows = rows_of(i), rows_of(b)
-            q, k = q_ref[query_rows, :], k_ref[key_rows, :]
-            v, grad = v_ref[key_rows, :], grad_ref[query_rows, :]
             keep = key_ref[b] == seg_ref[i]
             if back == 0 or back == reach:
                 key = lax.broadcasted_iota(jnp.int32, (block, block), 0)
@@ -799,27 +815,31 @@
                     keep = (keep & (query > key)) | (query == key)
                 else:
                     keep = keep & (query < key)
-            scores = dot_nt(k, q) * (scale * LOG2E)
-            weights = jnp.where(keep, jnp.exp2(scores - lse_ref[0, i]), 0.0)
-            grad_weights = dot_nt(v, grad)
-            grad_scores = (weights * (grad_weights - inner_ref[i]) * scale).astype(BF16)
-            dv_ref[key_rows, :] += dot_nn(weights.astype(BF16), grad)
-            dk_ref[key_rows, :] += dot_nn(grad_scores, q)
-            dq_ref[query_rows, :] += dot_tn(grad_scores, k)
+            for h in range(heads):
+                lanes = slice(h * HD, (h + 1) * HD)
+                q, k = q_ref[query_rows, lanes], k_ref[key_rows, lanes]
+                v, grad = v_ref[key_rows, lanes], grad_ref[query_rows, lanes]
+                scores = dot_nt(k, q)
+                weights = jnp.where(keep, jnp.exp2(scores * (scale * LOG2E) - lse_ref[h, i]), 0.0)
+                grad_weights = dot_nt(v, grad)
+                grad_scores = (weights * (grad_weights - inner_ref[h, i])).astype(BF16)
+                dv_ref[key_rows, lanes] += dot_nn(weights.astype(BF16), grad)
+                dk_ref[key_rows, lanes] += dot_nn(grad_scores, q)
+                dq_ref[query_rows, lanes] += dot_tn(grad_scores, k)
             return carry
 
         lax.fori_loop(back, count, pair, 0)
-
-    column = pl.multiple_of(h * HD, HD)
 
     def store(i, carry):
         rows = pl.ds(pl.multiple_of(i * block, block), block)
         cosine, sine = cos_ref[rows, :], sin_ref[rows, :]
-        for part, ref in enumerate((dq_ref, dk_ref)):
-            value = ref[rows, :]
-            turned = value * cosine - pltpu.roll(value, HD // 2, 1) * sine
-            result_ref[rows, pl.ds(part * heads * HD + column, HD)] = turned.astype(BF16)
-        result_ref[rows, pl.ds(2 * heads * HD + column, HD)] = dv_ref[rows, :].astype(BF16)
+        for h in range(heads):
+            lanes = slice(h * HD, (h + 1) * HD)
+            for part, ref in enumerate((dq_ref, dk_ref)):
+                value = ref[rows, lanes] * scale
+                turned = value * cosine - pltpu.roll(value, HD // 2, 1) * sine
+                result_ref[rows, (part * heads + h) * HD : (part * heads + h + 1) * HD] = turned.astype(BF16)
+            result_ref[rows, (2 * heads + h) * HD : (2 * heads + h + 1) * HD] = dv_ref[rows, lanes].astype(BF16)
         return carry
 
     lax.fori_loop(0, count, store, 0)
@@ -834,14 +854,14 @@
         functools.partial(backward_kernel, block, reach, heads),
         grid_spec=pltpu.PrefetchScalarGridSpec(
             num_scalar_prefetch=1,
-            grid=(heads,),
+            grid=(1,),
             in_specs=[
-                pl.BlockSpec((tokens, HD), lambda h, g: (0, h)),
-                pl.BlockSpec((tokens, HD), lambda h, g: (0, heads + h)),
-                pl.BlockSpec((tokens, HD), lambda h, g: (0, 2 * heads + h)),
-                pl.BlockSpec((tokens, HD), lambda h, g: (0, h)),
-                pl.BlockSpec((tokens, HD), lambda h, g: (0, h)),
-                pl.BlockSpec((1, count, 1, block), lambda h, g: (h, 0, 0, 0)),
+                pl.BlockSpec((tokens, heads * HD), lambda h, g: (0, 0)),
+                pl.BlockSpec((tokens, heads * HD), lambda h, g: (0, 1)),
+                pl.BlockSpec((tokens, heads * HD), lambda h, g: (0, 2)),
+                pl.BlockSpec((tokens, heads * HD), lambda h, g: (0, 0)),
+                pl.BlockSpec((tokens, heads * HD), lambda h, g: (0, 0)),
+                pl.BlockSpec((heads, count, 1, block), lambda h, g: (0, 0, 0, 0)),
                 pl.BlockSpec((count, 1, block), lambda h, g: (0, 0, 0)),
                 pl.BlockSpec((count, block, 1), lambda h, g: (0, 0, 0)),
                 pl.BlockSpec((tokens, HD), lambda h, g: (0, 0)),
@@ -849,10 +869,10 @@
             ],
             out_specs=pl.BlockSpec((tokens, width), lambda h, g: (0, 0)),
             scratch_shapes=[
-                pltpu.VMEM((tokens, HD), F32),
-                pltpu.VMEM((tokens, HD), F32),
-                pltpu.VMEM((tokens, HD), F32),
-                pltpu.VMEM((count, 1, block), F32),
+                pltpu.VMEM((tokens, heads * HD), F32),
+                pltpu.VMEM((tokens, heads * HD), F32),
+                pltpu.VMEM((tokens, heads * HD), F32),
+                pltpu.VMEM((heads, count, 1, block), F32),
             ],
         ),
         out_shape=jax.ShapeDtypeStruct((tokens, width), BF16),
@@ -913,20 +933,25 @@
 
     def scatter_far(sums):
         sums = dict(sums)
+        parts = [sums[0]]
         bit = 2
         while bit < members:
             for mask in sorted((m for m in sums if m & bit), reverse=True):
-                total = sums[mask ^ bit].astype(F32) + swap(sums.pop(mask), bit).astype(F32)
-                sums[mask ^ bit] = total if mask == bit else total.astype(BF16)
+                received = swap(sums.pop(mask), bit)
+                if mask == bit:
+                    parts.append(received)
+                else:
+                    sums[mask ^ bit] = (sums[mask ^ bit].astype(F32) + received.astype(F32)).astype(BF16)
             bit *= 2
-        return sums[0].astype(F32)
+        return parts
 
     half = members // 2
 
-    def share(function, *args, number, due=(), due_near=()):
+    def share(function, *args, number, due=(), due_near=(), cost_near=1):
         sums = {}
         for part, first in enumerate((half, 0)):
-            call = functools.partial(function, rows=rows, first=first, members=half, number=number + part)
+            cost = 1 if first else cost_near
+            call = functools.partial(function, rows=rows, first=first, members=half, number=number + part, cost=cost)
             outs = then(lambda xs, weights, *base: call(xs, weights, base=base[0] if base else None), *args, due=due)
             sums.update({first + 2 * q: out for q, out in enumerate(outs)})
             due = due_near
@@ -946,9 +971,10 @@
 
     normed_all, packs = start_exchange(inputs, pack_weights(att_proj, attn_out), members, sets, fsdp_size)
     chain.append(normed_all[0])
-    up_gate, down = after((ff_proj.reshape(depth, -1), ff_out), last())
+    up_gate, down, cotangent_late = after((ff_proj.reshape(depth, -1), ff_out, cotangent), last())
     w_ffn, w_down = [gather(up_gate)], [gather(down)]
     turned_up_gate = [turn(up_gate, step) for step in range(1, sets)]
+    cotangent_far = group_far(cotangent_late)
 
     segment = lax.dynamic_slice_in_dim(segments, mine * SEQ_LEN, SEQ_LEN)
     padding = lax.dynamic_slice_in_dim(pad_mask, mine * SEQ_LEN, SEQ_LEN)
@@ -964,12 +990,10 @@
         attended.append(then(lambda part: attend_forward(part, place_tp, segment, key_code, block), qkv[step]))
     heads_low = [out for out, _ in attended]
     sums = share(functools.partial(expand_heads, "attn_branch"), heads_low, packs, number=1)
-    w_ffn += [gather(after(part, chain[-2])) for part in turned_up_gate]
-    resid = x_float + scatter_far(sums)
+    w_ffn += [gather(after(part, last(), cotangent_far)) for part in turned_up_gate]
+    resid = x_float + settled(scatter_far(sums))
     normed_two_far = group_far(layer_norm(resid).astype(BF16))
-    down, cotangent_late = after((ff_out, cotangent), normed_two_far[-1])
-    turned_down = [turn(down, step) for step in range(1, sets)]
-    cotangent_far = group_far(cotangent_late)
+    turned_down = [turn(after(ff_out, normed_two_far[-1]), step) for step in range(1, sets)]
 
     hidden, slopes, grad_ffn, partial = [], [], [], None
     for step in range(sets):
@@ -979,16 +1003,15 @@
             (low, *slope), _ = then(hidden_units, normed_two_all, w_ffn[step])
         hidden.append(low)
         slopes.append(slope)
+    w_down += [gather(after(part, last())) for part in turned_down]
     ffn_rows = 2 * ffn_width
     grad_expand = functools.partial(expand_stack, "grad_normed_two", dot_nt)
     up_grad = functools.partial(rows_grad, "grad_ffn", place_fsdp, fsdp_size, depth, 1, 0)
     for step in range(sets):
         if step == 0:
-            (grad_low,), cotangent_all = then(functools.partial(hidden_grad, number=10), cotangent_far, *slopes[0], w_down[0])
+            (grad_low,), cotangent_all = then(functools.partial(hidden_grad, number=10, cost=LONG), cotangent_far, *slopes[0], w_down[0])
         else:
             (grad_low,), _ = then(hidden_grad, cotangent_all, *slopes[step], w_down[step])
-        if step == 0:
-            w_down += [gather(after(part, last())) for part in turned_down]
         grad_ffn.append(scatter(then(up_grad, normed_two_all, grad_low)))
         base = [] if partial is None else [partial]
         if step < sets - 1:
@@ -996,7 +1019,7 @@
             partial = then(call, grad_low, w_ffn[step], *base)
     sums = share(grad_expand, [grad_low], [w_ffn[-1]], *base, number=3)
     ffn_sums = share(functools.partial(expand_stack, "ffn_branch", dot_nn), hidden, w_down, number=5)
-    grad_normed_two = after(scatter_far(sums), ffn_sums[half])
+    grad_normed_two = settled(after(scatter_far(sums), ffn_sums[half]))
     grad_resid = cotangent.astype(F32) + layer_norm_back(resid, grad_normed_two)
     resid_grad_low = grad_resid.astype(BF16)
     resid_grad_far = group_far(resid_grad_low)
@@ -1010,35 +1033,35 @@
     project_grad = functools.partial(rows_grad, "grad_attn", place_fsdp, fsdp_size, head_width, 2, 0)
     held = None
     for step in reversed(range(sets)):
-        ready = tuple(grad_ffn[:1]) if step == sets - 1 else (grad_up[1:], ffn_branch)
         if step == sets - 1:
-            (head_grad,), resid_grad_all = then(functools.partial(head_grad_of, number=11), resid_grad_far, packs[step], due=ready)
-        else:
-            (head_grad,), _ = then(head_grad_of, resid_grad_all, packs[step], due=ready)
-        if step == sets - 1:
+            call = functools.partial(head_grad_of, number=11)
+            (head_grad,), resid_grad_all = then(call, resid_grad_far, packs[step], due=tuple(grad_ffn[:1]))
             grad_up = settle([piece[:ffn_width] for piece in grad_ffn], last())
             ffn_branch = scatter_far(after(ffn_sums, last()))
+            ready = ()
         else:
+            (head_grad,), _ = then(head_grad_of, resid_grad_all, packs[step])
             grad_gate = settle([piece[ffn_width:] for piece in grad_ffn], last(), grad_up[1:])
-        if held is not None:
             grad_attn[step + 1] = scatter(after(held, last()))
+            ready = (grad_up[1:], ffn_branch[1:])
         grad_project[step] = then(
             lambda part, grad, out, lse: attend_backward(
                 part, grad, out, lse, place_tp, segment, key_code, cosine, sine, block, LONG
             ),
-            qkv[step], head_grad, heads_low[step], attended[step][1],
+            qkv[step], head_grad, heads_low[step], attended[step][1], due=ready,
         )
         if step == 0:
-            grad_down = settle([grad_down[j * ffn_width : (j + 1) * ffn_width] for j in range(sets)], last(), grad_gate[1:])
+            grad_down = settle([grad_down[j * ffn_width : (j + 1) * ffn_width] for j in range(sets)], last())
         stacked = then(heads_grad, [heads_low[step]], resid_grad_all)
-        ready = tuple(grad_gate[1:]) if step == 0 else ()
-        held = then(project_grad, normed_all, grad_project[step], stacked, due=ready)
+        held = then(project_grad, normed_all, grad_project[step], stacked)
     grad_attn[0] = scatter(held)
-    sums = share(functools.partial(expand_project, "grad_normed"), grad_project, packs, number=7)
+    call = functools.partial(expand_project, "grad_normed")
+    due = (tuple(grad_gate[1:]), tuple(grad_down[1:]))
+    sums = share(call, grad_project, packs, number=7, due=due[0], due_near=due[1], cost_near=LONG)
     grad_normed = scatter_far(sums)
-    output = (resid + ffn_branch).astype(BF16)
+    output = (resid + settled(ffn_branch)).astype(BF16)
     grad_attn = settle(grad_attn)
-    grad_normed = after(grad_normed, grad_attn[1:])
+    grad_normed = settled(after(grad_normed, grad_attn[1:]))
     grad_input = (grad_resid + layer_norm_back(x_float, grad_normed)).astype(BF16)
     grad_attn = settled(grad_attn)
 

time: 886 us -> 852 us (0.962)
  Pallas kernels: 578 us -> 538 us
    ppermute x7, waiting for transfers between devices: 131 us -> 150 us  [swap(): return lax.ppermute(values, 'tp', [(i, i ^ bit) for i in range(tp_size)])]
    pallas_call x9, Pallas kernels: 154 us -> 139 us  [expand_call(): pl.pallas_call(functools.partial(expand_kernel, len(xs), each, plan, dot,...]
    ppermute x6, waiting for transfers between devices: 60.7 us -> 50.2 us  [turn(): lax.ppermute(values, 'tp', [(i, (i + step * members) % tp_size) for i in...]
    pallas_call x8, Pallas kernels: 140 us -> 130 us  [rows_call(): pl.pallas_call(functools.partial(rows_kernel, body, plan, members, len(ex...]
  transfers between devices with their start and end apart: 22 -> 22, of which waited for: 12 -> 10; matrix products, arithmetic and copies ran while one was open for 6% -> 7% of each run, Pallas kernels for 56% -> 54%
where the time goes in v4:
time: 852 us; the launch traced here: 846 us
  Pallas kernels  538 us (63%)
  waiting for transfers between devices  201 us (24%)
  other arithmetic  47.2 us (6%)
  local copies, waits for them, and re-layouts  25.5 us (3%)
  starting transfers between devices  18.9 us (2%)
  between operations  15 us (2%)
    ppermute x7, waiting for transfers between devices, swap(): return lax.ppermute(values, 'tp', [(i, i ^ bit) for i in range(tp_size)])  150 us
    pallas_call x9, Pallas kernels, expand_call(): pl.pallas_call(functools.partial(expand_kernel, len(xs), each, plan, dot,...  139 us
    pallas_call x8, Pallas kernels, rows_call(): pl.pallas_call(functools.partial(rows_kernel, body, plan, members, len(ex...  130 us
    pallas_call x1, Pallas kernels, start_exchange(): pl.pallas_call(functools.partial(start_kernel, members, sets, count), in_...  82.3 us
    pallas_call x4, Pallas kernels, rows_grad(): kernel_call(functools.partial(rows_grad_kernel, len(xs), count), name, co...  75.2 us
    ppermute x6, waiting for transfers between devices, turn(): lax.ppermute(values, 'tp', [(i, (i + step * members) % tp_size) for i in...  50.2 us
    pallas_call x2, Pallas kernels, attend_backward(): pl.pallas_call(functools.partial(backward_kernel, block, reach, heads), g...  46.7 us
    pallas_call x3, Pallas kernels, columns_grad(): kernel_call(functools.partial(columns_grad_kernel, len(xs), len(gs)), nam...  41.3 us
  transfers between devices with their start and end apart: 22, of which 10 were waited for; matrix products, arithmetic and copies ran while one was open for 7% of the time, Pallas kernels for 54%

profile of v4, /device:TPU:0, one launch (start us, length us, event | category | flops | bytes accessed | tf_op | source)
XLA Modules:
  0.0 845.5 jit_solution(1053932681489179009)
XLA Ops:
  12.0 3.9 copy.23
  15.9 82.3 %start_exchange.1 = (bf16[512,2048]{1,0:T(8,128)(2,1)}, bf16[512,2048]{1,0:T(8,128)(2,1)}, bf16[512,2048]{1,0:T(8,128)(2,1)}, bf16[512,2048]{1,0:T(8,128)(2,1)},...) custom-call(bf16[512,2048]{1,0:T(8,128)(2,1)} %x_ref.1, ...), custom_call_target="tpu_custom_call" | custom-call | flops 1 | bytes 1 | tf_op jit(solution)/shard_map/start_exchange/pallas_call | solution.py:193
  101.4 3.7 fusion.13
  107.1 14.2 %project.2.q_ref.k_ref.v_ref = bf16[2048,768]{1,0:T(8,128)(2,1)} custom-call(bf16[512,2048]{1,0:T(8,128)(2,1)} %get-tuple-element.381.refs_0_, bf16[512,2048]{1,0:T(8,128)(2,1)} %get-tuple-element.382.refs_1_, bf16[512,2048]{1,0:T(8,128)(2,1)} %get-tuple-element.383.refs_2_, bf16[512,2048]{1,0:T(8,128)(2,1)} %get-tuple-element.384.refs_3_, ...), custom_call_target="tpu_custom_call" | custom-call | flops 1 | bytes 1 | tf_op jit(solution)/shard_map/project/pallas_call | solution.py:296
  123.8 11.9 %attend_forward.2 = (bf16[2048,256]{1,0:T(8,128)(2,1)}, f32[2,4,1,512]{3,2,1,0:T(1,128)}) custom-call(s32[1]{0:T(128)} %bitcast.g_ref, bf16[2048,768]{1,0:T(8,128)(2,1)} %project.2.q_ref.k_ref.v_ref, bf16[2048,768]{1,0:T(8,128)(2,1)} %project.2.q_ref.k_ref.v_ref, bf16[2048,768]{1,0:T(8,128)(2,1)} %project.2.q_ref.k_ref.v_ref, ...), custom_call_target="tpu_custom_call" | custom-call | flops 1 | bytes 1 | tf_op jit(solution)/shard_map/attend_forward/pallas_call | solution.py:755
  135.7 14.1 %project.3.q_ref.k_ref.v_ref = bf16[2048,768]{1,0:T(8,128)(2,1)} custom-call(bf16[512,2048]{1,0:T(8,128)(2,1)} %get-tuple-element.381.refs_0_, bf16[512,2048]{1,0:T(8,128)(2,1)} %get-tuple-element.382.refs_1_, bf16[512,2048]{1,0:T(8,128)(2,1)} %get-tuple-element.383.refs_2_, bf16[512,2048]{1,0:T(8,128)(2,1)} %get-tuple-element.384.refs_3_, ...), custom_call_target="tpu_custom_call" | custom-call | flops 1 | bytes 1 | tf_op jit(solution)/shard_map/project/pallas_call | solution.py:296
  149.8 11.9 %attend_forward.3 = (bf16[2048,256]{1,0:T(8,128)(2,1)}, f32[2,4,1,512]{3,2,1,0:T(1,128)}) custom-call(s32[1]{0:T(128)} %bitcast.g_ref, bf16[2048,768]{1,0:T(8,128)(2,1)} %project.3.q_ref.k_ref.v_ref, bf16[2048,768]{1,0:T(8,128)(2,1)} %project.3.q_ref.k_ref.v_ref, bf16[2048,768]{1,0:T(8,128)(2,1)} %project.3.q_ref.k_ref.v_ref, ...), custom_call_target="tpu_custom_call" | custom-call | flops 1 | bytes 1 | tf_op jit(solution)/shard_map/attend_forward/pallas_call | solution.py:755
  161.7 8.6 %attn_branch.2 = bf16[512,2048]{1,0:T(8,128)(2,1)} custom-call(bf16[2048,256]{1,0:T(8,128)(2,1)} %get-tuple-element.376.refs_0_.out_ref, bf16[2048,256]{1,0:T(8,128)(2,1)} %get-tuple-element.351.refs_1_.out_ref.refs_0_, bf16[2048,256]{1,0:T(8,128)(2,1)} %copy-done.6, bf16[2048,256]{1,0:T(8,128)(2,1)} %get-tuple-element.402.refs_7_.refs_3_.refs_5_, ...), custom_call_target="tpu_custom_call" | custom-call | flops 1 | bytes 1 | tf_op jit(solution)/shard_map/attn_branch/pallas_call | solution.py:546
  170.3 9.5 %attn_branch.3 = f32[512,2048]{1,0:T(8,128)} custom-call(bf16[2048,256]{1,0:T(8,128)(2,1)} %get-tuple-element.376.refs_0_.out_ref, bf16[2048,256]{1,0:T(8,128)(2,1)} %get-tuple-element.351.refs_1_.out_ref.refs_0_, bf16[2048,256]{1,0:T(8,128)(2,1)} %copy-done.6, bf16[2048,256]{1,0:T(8,128)(2,1)} %get-tuple-element.402.refs_7_.refs_3_.refs_5_, ...), custom_call_target="tpu_custom_call" | custom-call | flops 1 | bytes 1 | tf_op jit(solution)/shard_map/attn_branch/pallas_call | solution.py:546
  179.8 11.5 %collective-permute-done.3.refs_1_.refs_2_.refs_4_ = bf16[512,2048]{1,0:T(8,128)(2,1)} collective-permute-done((bf16[512,2048]{1,0:T(8,128)(2,1)}, bf16[512,2048]{1,0:T(8,128)(2,1)}, u32[]{:S(2)}, u32[]{:S(2)}) %collective-permute-start.3) | collective-permute-done | bytes 2097184 | tf_op jit(solution)/shard_map/ppermute | solution.py:903
  193.9 44.9 %collective-permute-done = bf16[512,2048]{1,0:T(8,128)(2,1)} collective-permute-done((bf16[512,2048]{1,0:T(8,128)(2,1)}, bf16[512,2048]{1,0:T(8,128)(2,1)}, u32[]{:S(2)}, u32[]{:S(2)}) %collective-permute-start) | collective-permute-done | bytes 2097184 | tf_op jit(solution)/shard_map/ppermute | solution.py:903
  238.8 4.8 fusion.16
  247.4 44.6 %collective-permute-done.1.refs_1_.refs_2_ = bf16[512,2048]{1,0:T(8,128)(2,1)S(1)} collective-permute-done((bf16[512,2048]{1,0:T(8,128)(2,1)S(1)}, bf16[512,2048]{1,0:T(8,128)(2,1)S(1)}, u32[]{:S(2)}, u32[]{:S(2)}) %collective-permute-start.1) | collective-permute-done | bytes 2097184 | tf_op jit(solution)/shard_map/ppermute | solution.py:903
  296.0 25.6 %hidden_units.2 = (bf16[2048,1024]{1,0:T(8,128)(2,1)}, bf16[2048,1024]{1,0:T(8,128)(2,1)}, bf16[2048,1024]{1,0:T(8,128)(2,1)}, bf16[512,2048]{1,0:T(8,128)(2,1)}, bf16[512,2048]{1,0:T(8,128)(2,1)}) custom-call(bf16[512,2048]{1,0:T(8,128)(2,1)} %copy-done.5, bf16[512,2048]{1,0:T(8,128)(2,1)} %copy-done.8, bf16[4,512,2048]{2,1,0:T(8,128)(2,1)} %bitcast.43), custom_call_target="tpu_custom_call" | custom-call | flops 1 | bytes 1 | tf_op jit(solution)/shard_map/hidden_units/pallas_call | solution.py:296
  321.6 25.8 %hidden_units.3 = (bf16[2048,1024]{1,0:T(8,128)(2,1)}, bf16[2048,1024]{1,0:T(8,128)(2,1)}, bf16[2048,1024]{1,0:T(8,128)(2,1)}) custom-call(bf16[512,2048]{1,0:T(8,128)(2,1)} %copy-done.5, bf16[512,2048]{1,0:T(8,128)(2,1)} %get-tuple-element.309.refs_1_, bf16[512,2048]{1,0:T(8,128)(2,1)} %copy-done.8, bf16[512,2048]{1,0:T(8,128)(2,1)} %get-tuple-element.311.refs_3_, ...), custom_call_target="tpu_custom_call" | custom-call | flops 1 | bytes 1 | tf_op jit(solution)/shard_map/hidden_units/pallas_call | solution.py:296
  347.6 17.2 %hidden_grad.2 = (bf16[2048,2048]{1,0:T(8,128)(2,1)}, bf16[512,2048]{1,0:T(8,128)(2,1)}, bf16[512,2048]{1,0:T(8,128)(2,1)}) custom-call(bf16[512,2048]{1,0:T(8,128)(2,1)} %refs_2_, bf16[512,2048]{1,0:T(8,128)(2,1)} %collective-permute-done.3.refs_1_.refs_2_.refs_4_, bf16[2048,1024]{1,0:T(8,128)(2,1)} %get-tuple-element.286.refs_2_, ...), custom_call_target="tpu_custom_call" | custom-call | flops 999999995904 | bytes 1 | tf_op jit(solution)/shard_map/hidden_grad/pallas_call | solution.py:296
  364.8 23.5 %grad_ffn.2 = bf16[4,2048,512]{2,1,0:T(8,128)(2,1)} custom-call(s32[1]{0:T(128)} %bitcast.13.f_ref, bf16[512,2048]{1,0:T(8,128)(2,1)} %copy-done.5, bf16[512,2048]{1,0:T(8,128)(2,1)} %get-tuple-element.309.refs_1_, bf16[512,2048]{1,0:T(8,128)(2,1)} %copy-done.8, bf16[512,2048]{1,0:T(8,128)(2,1)} %get-tuple-element.311.refs_3_, ...), custom_call_target="tpu_custom_call" | custom-call | flops 1 | bytes 1 | tf_op jit(solution)/shard_map/grad_ffn/pallas_call | solution.py:647
  388.4 25.0 %grad_normed_two.3.refs_1_ = bf16[2048,2048]{1,0:T(8,128)(2,1)} custom-call(bf16[2048,2048]{1,0:T(8,128)(2,1)} %get-tuple-element.299.refs_4_.refs_0_, bf16[4,512,2048]{2,1,0:T(8,128)(2,1)} %bitcast.44), custom_call_target="tpu_custom_call" | custom-call | flops 1 | bytes 1 | tf_op jit(solution)/shard_map/grad_normed_two/pallas_call | solution.py:546
  413.4 16.6 %hidden_grad.3.refs_4_.refs_0_ = bf16[2048,2048]{1,0:T(8,128)(2,1)} custom-call(bf16[512,2048]{1,0:T(8,128)(2,1)} %refs_2_, bf16[512,2048]{1,0:T(8,128)(2,1)} %get-tuple-element.332.refs_1_.refs_3_, bf16[512,2048]{1,0:T(8,128)(2,1)} %collective-permute-done.3.refs_1_.refs_2_.refs_4_, bf16[512,2048]{1,0:T(8,128)(2,1)} %get-tuple-element.334.refs_3_.refs_5_, ...), custom_call_target="tpu_custom_call" | custom-call | flops 1 | bytes 1 | tf_op jit(solution)/shard_map/hidden_grad/pallas_call | solution.py:296
  430.0 23.6 %grad_ffn.3 = bf16[4,2048,512]{2,1,0:T(8,128)(2,1)} custom-call(s32[1]{0:T(128)} %bitcast.13.f_ref, bf16[512,2048]{1,0:T(8,128)(2,1)} %copy-done.5, bf16[512,2048]{1,0:T(8,128)(2,1)} %get-tuple-element.309.refs_1_, bf16[512,2048]{1,0:T(8,128)(2,1)} %copy-done.8, bf16[512,2048]{1,0:T(8,128)(2,1)} %get-tuple-element.311.refs_3_, ...), custom_call_target="tpu_custom_call" | custom-call | flops 1 | bytes 1 | tf_op jit(solution)/shard_map/grad_ffn/pallas_call | solution.py:647
  453.7 17.3 %grad_normed_two.4 = bf16[512,2048]{1,0:T(8,128)(2,1)} custom-call(bf16[2048,2048]{1,0:T(8,128)(2,1)} %hidden_grad.3.refs_4_.refs_0_, bf16[2048,2048]{1,0:T(8,128)(2,1)} %grad_normed_two.3.refs_1_, bf16[4,512,2048]{2,1,0:T(8,128)(2,1)} %bitcast.36), custom_call_target="tpu_custom_call" | custom-call | flops 1 | bytes 1 | tf_op jit(solution)/shard_map/grad_normed_two/pallas_call | solution.py:546
  472.7 17.5 %grad_normed_two.5 = f32[512,2048]{1,0:T(8,128)} custom-call(bf16[2048,2048]{1,0:T(8,128)(2,1)} %hidden_grad.3.refs_4_.refs_0_, bf16[2048,2048]{1,0:T(8,128)(2,1)} %grad_normed_two.3.refs_1_, bf16[4,512,2048]{2,1,0:T(8,128)(2,1)} %bitcast.37), custom_call_target="tpu_custom_call" | custom-call | flops 1 | bytes 1 | tf_op jit(solution)/shard_map/grad_normed_two/pallas_call | solution.py:546
  490.3 16.3 %ffn_branch.2 = bf16[512,2048]{1,0:T(8,128)(2,1)} custom-call(bf16[2048,1024]{1,0:T(8,128)(2,1)} %get-tuple-element.329.refs_0_, bf16[2048,1024]{1,0:T(8,128)(2,1)} %get-tuple-element.330.refs_1_, bf16[4,1024,512]{2,1,0:T(8,128)(2,1)} %bitcast.49, bf16[4,1024,512]{2,1,0:T(8,128)(2,1)} %bitcast.39), custom_call_target="tpu_custom_call" | custom-call | flops 1 | bytes 1 | tf_op jit(solution)/shard_map/ffn_branch/pallas_call | solution.py:546
  506.6 12.7 %collective-permute-done.5 = bf16[512,2048]{1,0:T(8,128)(2,1)S(1)} collective-permute-done((bf16[512,2048]{1,0:T(8,128)(2,1)}, bf16[512,2048]{1,0:T(8,128)(2,1)S(1)}, u32[]{:S(2)}, u32[]{:S(2)}) %collective-permute-start.5) | collective-permute-done | bytes 2097184 | tf_op jit(solution)/shard_map/ppermute | solution.py:903
  519.3 4.1 fusion.11
  523.5 5.0 fusion.15
  532.6 16.2 %ffn_branch.3 = f32[512,2048]{1,0:T(8,128)} custom-call(bf16[2048,1024]{1,0:T(8,128)(2,1)} %get-tuple-element.329.refs_0_, bf16[2048,1024]{1,0:T(8,128)(2,1)} %get-tuple-element.330.refs_1_, bf16[4,1024,512]{2,1,0:T(8,128)(2,1)} %bitcast.50, bf16[4,1024,512]{2,1,0:T(8,128)(2,1)} %bitcast.40), custom_call_target="tpu_custom_call" | custom-call | flops 1 | bytes 1 | tf_op jit(solution)/shard_map/ffn_branch/pallas_call | solution.py:546
  548.8 25.4 %grad_down.1 = bf16[4,2048,512]{2,1,0:T(8,128)(2,1)} custom-call(s32[1]{0:T(128)} %bitcast.13.f_ref, bf16[2048,1024]{1,0:T(8,128)(2,1)} %get-tuple-element.329.refs_0_, bf16[2048,1024]{1,0:T(8,128)(2,1)} %get-tuple-element.330.refs_1_, bf16[512,2048]{1,0:T(8,128)(2,1)} %refs_2_, bf16[512,2048]{1,0:T(8,128)(2,1)} %get-tuple-element.332.refs_1_.refs_3_, ...), custom_call_target="tpu_custom_call" | custom-call | flops 1 | bytes 1 | tf_op jit(solution)/shard_map/grad_down/pallas_call | solution.py:701
  575.9 10.7 %head_grad.2 = (bf16[2048,256]{1,0:T(8,128)(2,1)}, bf16[512,2048]{1,0:T(8,128)(2,1)}, bf16[512,2048]{1,0:T(8,128)(2,1)}) custom-call(bf16[512,2048]{1,0:T(8,128)(2,1)} %copy-done.4, bf16[512,2048]{1,0:T(8,128)(2,1)} %collective-permute-done.6.refs_1_.refs_3_.refs_2_, bf16[2048,256]{1,0:T(8,128)(2,1)} %get-tuple-element.405.refs_6_.refs_2_, ...), custom_call_target="tpu_custom_call" | custom-call | flops 1 | bytes 1 | tf_op jit(solution)/shard_map/head_grad/pallas_call | solution.py:296
  588.3 3.4 fusion.20
  591.9 23.2 %attend_backward.2.refs_5_.refs_1_ = bf16[2048,768]{1,0:T(8,128)(2,1)} custom-call(s32[1]{0:T(128)} %bitcast.g_ref, bf16[2048,768]{1,0:T(8,128)(2,1)} %project.3.q_ref.k_ref.v_ref, bf16[2048,768]{1,0:T(8,128)(2,1)} %project.3.q_ref.k_ref.v_ref, bf16[2048,768]{1,0:T(8,128)(2,1)} %project.3.q_ref.k_ref.v_ref, bf16[2048,256]{1,0:T(8,128)(2,1)} %get-tuple-element.348.grad_ref, ...), custom_call_target="tpu_custom_call" | custom-call | flops 999999995904 | bytes 1 | tf_op jit(solution)/shard_map/attend_backward/pallas_call | solution.py:853
  615.1 8.0 grad_heads.2.refs_4_
  623.1 14.1 %grad_attn.2 = bf16[4,1024,512]{2,1,0:T(8,128)(2,1)} custom-call(s32[1]{0:T(128)} %bitcast.13.f_ref, bf16[512,2048]{1,0:T(8,128)(2,1)} %get-tuple-element.381.refs_0_, bf16[512,2048]{1,0:T(8,128)(2,1)} %get-tuple-element.382.refs_1_, bf16[512,2048]{1,0:T(8,128)(2,1)} %get-tuple-element.383.refs_2_, ...), custom_call_target="tpu_custom_call", output_to_operand_aliasing={{}: (5, {})} | custom-call | flops 1 | bytes 1 | tf_op jit(solution)/shard_map/grad_attn/pallas_call | solution.py:647
  637.3 6.1 head_grad.3.grad_ref
  643.4 13.7 %collective-permute-done.7 = bf16[512,2048]{1,0:T(8,128)(2,1)} collective-permute-done((bf16[512,2048]{1,0:T(8,128)(2,1)}, bf16[512,2048]{1,0:T(8,128)(2,1)}, u32[]{:S(2)}, u32[]{:S(2)}) %collective-permute-start.7) | collective-permute-done | bytes 2097184 | tf_op jit(solution)/shard_map/ppermute | solution.py:903
  657.1 6.8 add_convert_fusion
  663.9 23.6 %attend_backward.3.refs_5_.refs_0_ = bf16[2048,768]{1,0:T(8,128)(2,1)} custom-call(s32[1]{0:T(128)} %bitcast.g_ref, bf16[2048,768]{1,0:T(8,128)(2,1)} %project.2.q_ref.k_ref.v_ref, bf16[2048,768]{1,0:T(8,128)(2,1)} %project.2.q_ref.k_ref.v_ref, bf16[2048,768]{1,0:T(8,128)(2,1)} %project.2.q_ref.k_ref.v_ref, bf16[2048,256]{1,0:T(8,128)(2,1)} %head_grad.3.grad_ref, ...), custom_call_target="tpu_custom_call" | custom-call | flops 999999995904 | bytes 1 | tf_op jit(solution)/shard_map/attend_backward/pallas_call | solution.py:853
  687.5 7.8 grad_heads.3.refs_4_
  695.3 13.9 %grad_attn.3 = bf16[4,1024,512]{2,1,0:T(8,128)(2,1)} custom-call(s32[1]{0:T(128)} %bitcast.13.f_ref, bf16[512,2048]{1,0:T(8,128)(2,1)} %get-tuple-element.381.refs_0_, bf16[512,2048]{1,0:T(8,128)(2,1)} %get-tuple-element.382.refs_1_, bf16[512,2048]{1,0:T(8,128)(2,1)} %get-tuple-element.383.refs_2_, ...), custom_call_target="tpu_custom_call", output_to_operand_aliasing={{}: (5, {})} | custom-call | flops 1 | bytes 1 | tf_op jit(solution)/shard_map/grad_attn/pallas_call | solution.py:647
  713.9 13.9 %grad_normed.2 = bf16[512,2048]{1,0:T(8,128)(2,1)} custom-call(bf16[2048,768]{1,0:T(8,128)(2,1)} %attend_backward.3.refs_5_.refs_0_, bf16[2048,768]{1,0:T(8,128)(2,1)} %attend_backward.2.refs_5_.refs_1_, bf16[2048,256]{1,0:T(8,128)(2,1)} %copy-done.6, bf16[2048,256]{1,0:T(8,128)(2,1)} %get-tuple-element.402.refs_7_.refs_3_.refs_5_, ...), custom_call_target="tpu_custom_call" | custom-call | flops 1 | bytes 1 | tf_op jit(solution)/shard_map/grad_normed/pallas_call | solution.py:546
  731.2 5.2 copy.22
  738.8 21.7 %collective-permute-done.10 = bf16[1024,512]{1,0:T(8,128)(2,1)S(1)} collective-permute-done((bf16[1024,512]{1,0:T(8,128)(2,1)S(1)}, bf16[1024,512]{1,0:T(8,128)(2,1)S(1)}, u32[]{:S(2)}, u32[]{:S(2)}) %collective-permute-start.10) | collective-permute-done | bytes 1048608 | tf_op jit(solution)/shard_map/ppermute | solution.py:906
  760.5 14.3 %grad_normed.3 = f32[512,2048]{1,0:T(8,128)} custom-call(bf16[2048,768]{1,0:T(8,128)(2,1)} %attend_backward.3.refs_5_.refs_0_, bf16[2048,768]{1,0:T(8,128)(2,1)} %attend_backward.2.refs_5_.refs_1_, bf16[2048,256]{1,0:T(8,128)(2,1)} %copy-done.6, bf16[2048,256]{1,0:T(8,128)(2,1)} %get-tuple-element.402.refs_7_.refs_3_.refs_5_, ...), custom_call_target="tpu_custom_call" | custom-call | flops 999999995904 | bytes 1 | tf_op jit(solution)/shard_map/grad_normed/pallas_call | solution.py:546
  774.8 3.0 convert_add_fusion.3
  777.8 27.2 %collective-permute-done.12 = bf16[1024,512]{1,0:T(8,128)(2,1)} collective-permute-done((bf16[1024,512]{1,0:T(8,128)(2,1)}, bf16[1024,512]{1,0:T(8,128)(2,1)}, u32[]{:S(2)}, u32[]{:S(2)}) %collective-permute-start.12) | collective-permute-done | bytes 1048608 | tf_op jit(solution)/shard_map/ppermute | solution.py:906
  805.1 21.0 %collective-permute-done.11 = bf16[512,2048]{1,0:T(8,128)(2,1)} collective-permute-done((bf16[512,2048]{1,0:T(8,128)(2,1)}, bf16[512,2048]{1,0:T(8,128)(2,1)}, u32[]{:S(2)}, u32[]{:S(2)}) %collective-permute-start.11) | collective-permute-done | bytes 2097184 | tf_op jit(solution)/shard_map/ppermute | solution.py:903
  826.1 4.2 fusion.12
  830.3 4.1 fusion.8
  (140 shorter events, 46.7 us)
Async XLA Ops:
  7.2 288.8 %all-gather.9.cloned.1.call-start = ((), (), s32[]{:S(2)}) async-start(), calls=%async_computation.10 | async-start | bytes 10485760 | tf_op jit(solution)/shard_map/all_gather | solution.py:961
  12.0 3.9 copy-start.6
  12.0 89.4 %copy-start.26 = (s32[4096]{0:T(1024)S(1)}, s32[4096]{0:T(1024)}, u32[]{:S(2)}) copy-start(s32[4096]{0:T(1024)} %param.16) | copy-start | bytes 49156
  98.2 223.4 %all-gather.11.cloned.1.call-start = ((), (), s32[]{:S(2)}) async-start(), calls=%async_computation.11 | async-start | bytes 10485760 | tf_op jit(solution)/shard_map/all_gather | solution.py:961
  98.3 93.0 %collective-permute-start.3 = (bf16[512,2048]{1,0:T(8,128)(2,1)}, bf16[512,2048]{1,0:T(8,128)(2,1)}, u32[]{:S(2)}, u32[]{:S(2)}) collective-permute-start(bf16[512,2048]{1,0:T(8,128)(2,1)} %refs_2_), channel_id=1, source_target_pairs={{0,2},{1,3},{2,0},{3,1},{4,6},{5,7},{6,4},{7,5},{8,10},{9,11},{10,... | collective-permute-start | bytes 6291464 | tf_op jit(solution)/shard_map/ppermute | solution.py:903
  98.4 94.2 %collective-permute-start.2 = (bf16[512,2048]{1,0:T(8,128)(2,1)}, bf16[512,2048]{1,0:T(8,128)(2,1)}, u32[]{:S(2)}, u32[]{:S(2)}) collective-permute-start(bf16[512,2048]{1,0:T(8,128)(2,1)} %bitcast.26), channel_id=1, source_target_pairs={{0,4},{1,5},{2,6},{3,7},{4,0},{5,1},{6,2},{7,3},{8,12},{9,13},{10,... | collective-permute-start | bytes 6291464 | tf_op jit(solution)/shard_map/ppermute | solution.py:906
  107.1 14.3 %copy-start.27 = (s32[4096]{0:T(1024)S(1)}, s32[4096]{0:T(1024)}, u32[]{:S(2)}) copy-start(s32[4096]{0:T(1024)} %param.15) | copy-start | bytes 49156
  107.1 14.3 %copy-start.28 = (s32[4096]{0:T(1024)S(1)}, s32[4096]{0:T(1024)}, u32[]{:S(2)}) copy-start(s32[4096]{0:T(1024)} %param.14) | copy-start | bytes 49156
  122.0 13.7 %copy-start.23 = (s32[2048]{0:T(1024)}, s32[2048]{0:T(1024)S(1)}, u32[]{:S(2)}) copy-start(s32[2048]{0:T(1024)S(1)} %get-tuple-element.427) | copy-start | bytes 24580
  179.7 13.8 %copy-start.2 = (bf16[512,2048]{1,0:T(8,128)(2,1)S(1)}, bf16[512,2048]{1,0:T(8,128)(2,1)}, u32[]{:S(2)}) copy-start(bf16[512,2048]{1,0:T(8,128)(2,1)} %x_ref.1) | copy-start | bytes 6291460
  192.6 154.9 %all-gather.13.cloned.1.call-start = ((), (), s32[]{:S(2)}) async-start(), calls=%async_computation.12 | async-start | bytes 5242880 | tf_op jit(solution)/shard_map/all_gather | solution.py:961
  192.6 46.2 %collective-permute-start = (bf16[512,2048]{1,0:T(8,128)(2,1)}, bf16[512,2048]{1,0:T(8,128)(2,1)}, u32[]{:S(2)}, u32[]{:S(2)}) collective-permute-start(bf16[512,2048]{1,0:T(8,128)(2,1)} %attn_branch.2), channel_id=1, source_target_pairs={{0,2},{1,3},{2,0},{3,1},{4,6},{5,7},{6,4},{7,5},{8,10},{9,11},{10,... | collective-permute-start | bytes 6291464 | tf_op jit(solution)/shard_map/ppermute | solution.py:903
  193.3 220.1 %all-gather.15.cloned.1.call-start = ((), (), s32[]{:S(2)}) async-start(), calls=%async_computation.13 | async-start | bytes 5242880 | tf_op jit(solution)/shard_map/all_gather | solution.py:961
  193.9 49.8 %copy-start.19 = (f32[512]{0:T(512)}, f32[512]{0:T(512)S(1)}, u32[]{:S(2)}) copy-start(f32[512]{0:T(512)S(1)} %broadcast_multiply_fusion.2) | copy-start | bytes 6148
  244.2 49.2 %copy-start.14 = (bf16[1024,512]{1,0:T(8,128)(2,1)S(1)}, bf16[1024,512]{1,0:T(8,128)(2,1)}, u32[]{:S(2)}) copy-start(bf16[1024,512]{1,0:T(8,128)(2,1)} %param.13) | copy-start | bytes 3145732
  244.2 47.8 %copy-start.21 = (f32[512]{0:T(512)}, f32[512]{0:T(512)S(1)}, u32[]{:S(2)}) copy-start(f32[512]{0:T(512)S(1)} %add_rsqrt_fusion.1) | copy-start | bytes 6148
  245.7 50.3 %copy-start.5 = (bf16[512,2048]{1,0:T(8,128)(2,1)}, bf16[512,2048]{1,0:T(8,128)(2,1)S(1)}, u32[]{:S(2)}) copy-start(bf16[512,2048]{1,0:T(8,128)(2,1)S(1)} %fusion.10.refs_0_) | copy-start | bytes 6291460
  245.7 46.4 %collective-permute-start.1 = (bf16[512,2048]{1,0:T(8,128)(2,1)S(1)}, bf16[512,2048]{1,0:T(8,128)(2,1)S(1)}, u32[]{:S(2)}, u32[]{:S(2)}) collective-permute-start(bf16[512,2048]{1,0:T(8,128)(2,1)S(1)} %fusion.10.refs_0_), channel_id=1, source_target_pairs={{0,2},{1,3},{2,0},{3,1},{4,6},{5,7},{6,4},{7,5},{8,10},{9,11},{10,... | collective-permute-start | bytes 6291464 | tf_op jit(solution)/shard_map/ppermute | solution.py:903
  293.4 54.1 %collective-permute-start.4 = (bf16[1024,512]{1,0:T(8,128)(2,1)S(1)}, bf16[1024,512]{1,0:T(8,128)(2,1)}, u32[]{:S(2)}, u32[]{:S(2)}) collective-permute-start(bf16[1024,512]{1,0:T(8,128)(2,1)S(1)} %copy-done.14), channel_id=1, source_target_pairs={{0,4},{1,5},{2,6},{3,7},{4,0},{5,1},{6,2},{7,3},{8,12},{9,13},{10,... | collective-permute-start | bytes 3145736 | tf_op jit(solution)/shard_map/ppermute | solution.py:906
  347.5 228.3 %reduce-scatter.6.cloned.1.call-start = ((), (), s32[]{:S(2)}) async-start(), calls=%async_computation.5 | async-start | bytes 10485760 | tf_op jit(solution)/shard_map/reduce_scatter | solution.py:964
  388.3 200.0 %reduce-scatter.8.cloned.1.call-start = ((), (), s32[]{:S(2)}) async-start(), calls=%async_computation.6 | async-start | bytes 10485760 | tf_op jit(solution)/shard_map/reduce_scatter | solution.py:964
  453.7 255.6 %reduce-scatter.10.cloned.1.call-start = ((), (), s32[]{:S(2)}) async-start(), calls=%async_computation.7 | async-start | bytes 10485760 | tf_op jit(solution)/shard_map/reduce_scatter | solution.py:964
  471.1 48.2 %collective-permute-start.5 = (bf16[512,2048]{1,0:T(8,128)(2,1)}, bf16[512,2048]{1,0:T(8,128)(2,1)S(1)}, u32[]{:S(2)}, u32[]{:S(2)}) collective-permute-start(bf16[512,2048]{1,0:T(8,128)(2,1)} %grad_normed_two.4), channel_id=1, source_target_pairs={{0,2},{1,3},{2,0},{3,1},{4,6},{5,7},{6,4},{7,5},{8,10},{9,11},{10,... | collective-permute-start | bytes 6291464 | tf_op jit(solution)/shard_map/ppermute | solution.py:903
  490.3 29.0 %copy-start.1 = (f32[512,2048]{1,0:T(8,128)S(1)}, f32[512,2048]{1,0:T(8,128)}, u32[]{:S(2)}) copy-start(f32[512,2048]{1,0:T(8,128)} %copy-done) | copy-start | bytes 12582916
  490.3 29.0 %copy-start.18 = (f32[512]{0:T(512)S(1)}, f32[512]{0:T(512)}, u32[]{:S(2)}) copy-start(f32[512]{0:T(512)} %copy-done.17) | copy-start | bytes 6148
  490.3 29.0 %copy-start.22 = (f32[512]{0:T(512)S(1)}, f32[512]{0:T(512)}, u32[]{:S(2)}) copy-start(f32[512]{0:T(512)} %copy-done.21) | copy-start | bytes 6148
  506.6 16.9 %copy-start.7 = (f32[512,2048]{1,0:T(8,128)S(1)}, f32[512,2048]{1,0:T(8,128)}, u32[]{:S(2)}) copy-start(f32[512,2048]{1,0:T(8,128)} %grad_normed_two.5) | copy-start | bytes 12582916
  519.3 4.1 copy-start.11
  523.5 6.6 copy-start.16
  523.5 8.5 %copy-start.25 = (f32[512]{0:T(512)S(1)}, f32[512]{0:T(512)}, u32[]{:S(2)}) copy-start(f32[512]{0:T(512)} %get-tuple-element.439) | copy-start | bytes 6148
  528.5 20.3 %copy-start.4 = (bf16[512,2048]{1,0:T(8,128)(2,1)}, bf16[512,2048]{1,0:T(8,128)(2,1)S(1)}, u32[]{:S(2)}) copy-start(bf16[512,2048]{1,0:T(8,128)(2,1)S(1)} %get-tuple-element.377.refs_0_.refs_1_) | copy-start | bytes 6291460
  528.5 47.4 %collective-permute-start.6 = (bf16[512,2048]{1,0:T(8,128)(2,1)S(1)}, bf16[512,2048]{1,0:T(8,128)(2,1)}, u32[]{:S(2)}, u32[]{:S(2)}) collective-permute-start(bf16[512,2048]{1,0:T(8,128)(2,1)S(1)} %get-tuple-element.377.refs_0_.refs_1_), channel_id=1, source_target_pairs={{0,2},{1,3},{2,0},{3,1},{4,6},{5,7},{6,4},{7,5},{8,10},{9,11},{10,... | collective-permute-start | bytes 6291464 | tf_op jit(solution)/shard_map/ppermute | solution.py:903
  574.3 162.2 %reduce-scatter.12.cloned.1.call-start = ((), (), s32[]{:S(2)}) async-start(), calls=%async_computation.8 | async-start | bytes 5242880 | tf_op jit(solution)/shard_map/reduce_scatter | solution.py:964
  586.6 70.5 %collective-permute-start.7 = (bf16[512,2048]{1,0:T(8,128)(2,1)}, bf16[512,2048]{1,0:T(8,128)(2,1)}, u32[]{:S(2)}, u32[]{:S(2)}) collective-permute-start(bf16[512,2048]{1,0:T(8,128)(2,1)} %ffn_branch.2), channel_id=1, source_target_pairs={{0,2},{1,3},{2,0},{3,1},{4,6},{5,7},{6,4},{7,5},{8,10},{9,11},{10,... | collective-permute-start | bytes 6291464 | tf_op jit(solution)/shard_map/ppermute | solution.py:903
  591.7 72.2 %collective-permute-start.8 = (bf16[1024,512]{1,0:T(8,128)(2,1)}, bf16[1024,512]{1,0:T(8,128)(2,1)}, u32[]{:S(2)}, u32[]{:S(2)}) collective-permute-start(bf16[1024,512]{1,0:T(8,128)(2,1)} %get-tuple-element.371), channel_id=1, source_target_pairs={{0,4},{1,5},{2,6},{3,7},{4,0},{5,1},{6,2},{7,3},{8,12},{9,13},{10,... | collective-permute-start | bytes 3145736 | tf_op jit(solution)/shard_map/ppermute | solution.py:906
  643.4 191.0 %reduce-scatter.14.cloned.1.call-start = ((), (), s32[]{:S(2)}) async-start(), calls=%async_computation.9 | async-start | bytes 5242880 | tf_op jit(solution)/shard_map/reduce_scatter | solution.py:964
  663.9 50.0 %collective-permute-start.9 = (bf16[1024,512]{1,0:T(8,128)(2,1)}, bf16[1024,512]{1,0:T(8,128)(2,1)}, u32[]{:S(2)}, u32[]{:S(2)}) collective-permute-start(bf16[1024,512]{1,0:T(8,128)(2,1)} %get-tuple-element.387), channel_id=1, source_target_pairs={{0,4},{1,5},{2,6},{3,7},{4,0},{5,1},{6,2},{7,3},{8,12},{9,13},{10,... | collective-permute-start | bytes 3145736 | tf_op jit(solution)/shard_map/ppermute | solution.py:906
  710.9 16.9 %copy-start.13 = (bf16[2048,512]{1,0:T(8,128)(2,1)S(1)}, bf16[2048,512]{1,0:T(8,128)(2,1)}, u32[]{:S(2)}) copy-start(bf16[2048,512]{1,0:T(8,128)(2,1)} %reduce-scatter.6.cloned.1.call-done) | copy-start | bytes 6291460
  710.9 49.6 %collective-permute-start.10 = (bf16[1024,512]{1,0:T(8,128)(2,1)S(1)}, bf16[1024,512]{1,0:T(8,128)(2,1)S(1)}, u32[]{:S(2)}, u32[]{:S(2)}) collective-permute-start(bf16[1024,512]{1,0:T(8,128)(2,1)S(1)} %slice.85), channel_id=1, source_target_pairs={{0,4},{1,5},{2,6},{3,7},{4,0},{5,1},{6,2},{7,3},{8,12},{9,13},{10,... | collective-permute-start | bytes 3145736 | tf_op jit(solution)/shard_map/ppermute | solution.py:906
  736.5 89.6 %collective-permute-start.11 = (bf16[512,2048]{1,0:T(8,128)(2,1)}, bf16[512,2048]{1,0:T(8,128)(2,1)}, u32[]{:S(2)}, u32[]{:S(2)}) collective-permute-start(bf16[512,2048]{1,0:T(8,128)(2,1)} %grad_normed.2), channel_id=1, source_target_pairs={{0,2},{1,3},{2,0},{3,1},{4,6},{5,7},{6,4},{7,5},{8,10},{9,11},{10,... | collective-permute-start | bytes 6291464 | tf_op jit(solution)/shard_map/ppermute | solution.py:903
  736.5 68.6 %collective-permute-start.12 = (bf16[1024,512]{1,0:T(8,128)(2,1)}, bf16[1024,512]{1,0:T(8,128)(2,1)}, u32[]{:S(2)}, u32[]{:S(2)}) collective-permute-start(bf16[1024,512]{1,0:T(8,128)(2,1)} %reduce-scatter.12.cloned.1.call-done), channel_id=1, source_target_pairs={{0,4},{1,5},{2,6},{3,7},{4,0},{5,1},{6,2},{7,3},{8,12},{9,13},{10,... | collective-permute-start | bytes 3145736 | tf_op jit(solution)/shard_map/ppermute | solution.py:906
  760.5 14.3 %copy-start.15 = (bf16[1024,512]{1,0:T(8,128)(2,1)}, bf16[1024,512]{1,0:T(8,128)(2,1)S(1)}, u32[]{:S(2)}) copy-start(bf16[1024,512]{1,0:T(8,128)(2,1)S(1)} %collective-permute-done.10) | copy-start | bytes 3145732
  760.5 14.3 %copy-start.12 = (bf16[2048,512]{1,0:T(8,128)(2,1)S(1)}, bf16[2048,512]{1,0:T(8,128)(2,1)}, u32[]{:S(2)}) copy-start(bf16[2048,512]{1,0:T(8,128)(2,1)} %reduce-scatter.10.cloned.1.call-done) | copy-start | bytes 6291460
  774.8 51.3 %copy-start.3 = (bf16[512,2048]{1,0:T(8,128)(2,1)S(1)}, bf16[512,2048]{1,0:T(8,128)(2,1)}, u32[]{:S(2)}) copy-start(bf16[512,2048]{1,0:T(8,128)(2,1)} %x_ref.1) | copy-start | bytes 6291460
  774.8 51.3 %copy-start.20 = (f32[512]{0:T(512)S(1)}, f32[512]{0:T(512)}, u32[]{:S(2)}) copy-start(f32[512]{0:T(512)} %copy-done.19) | copy-start | bytes 6148
  774.8 51.3 %copy-start.24 = (f32[512]{0:T(512)S(1)}, f32[512]{0:T(512)}, u32[]{:S(2)}) copy-start(f32[512]{0:T(512)} %add_rsqrt_fusion) | copy-start | bytes 6148
  777.8 52.5 %copy-start.9 = (f32[512,2048]{1,0:T(8,128)S(1)}, f32[512,2048]{1,0:T(8,128)}, u32[]{:S(2)}) copy-start(f32[512,2048]{1,0:T(8,128)} %grad_normed.3) | copy-start | bytes 12582916
  777.8 52.5 %copy-start.10 = (f32[512,2048]{1,0:T(8,128)S(1)}, f32[512,2048]{1,0:T(8,128)}, u32[]{:S(2)}) copy-start(f32[512,2048]{1,0:T(8,128)} %get-tuple-element.423) | copy-start | bytes 12582916
  (3 other events, 5.4 us)
Sparse Core Ops, SparseCore 0:
  98.3 87.7 all-gather.8
  192.7 87.6 all-gather.10
  282.2 52.6 all-gather.12
  347.7 52.3 all-gather.14
  403.0 86.4 reduce-scatter.5
  492.7 86.4 reduce-scatter.7
  582.2 86.3 reduce-scatter.9
  671.8 52.6 reduce-scatter.11
  727.6 52.6 reduce-scatter.13

commit v5 on v4

--- a/solution.py
+++ b/solution.py
@@ -1038,30 +1038,29 @@
             (head_grad,), resid_grad_all = then(call, resid_grad_far, packs[step], due=tuple(grad_ffn[:1]))
             grad_up = settle([piece[:ffn_width] for piece in grad_ffn], last())
             ffn_branch = scatter_far(after(ffn_sums, last()))
-            ready = ()
         else:
             (head_grad,), _ = then(head_grad_of, resid_grad_all, packs[step])
-            grad_gate = settle([piece[ffn_width:] for piece in grad_ffn], last(), grad_up[1:])
-            grad_attn[step + 1] = scatter(after(held, last()))
-            ready = (grad_up[1:], ffn_branch[1:])
         grad_project[step] = then(
             lambda part, grad, out, lse: attend_backward(
-                part, grad, out, lse, place_tp, segment, key_code, cosine, sine, block, LONG
+                part, grad, out, lse, place_tp, segment, key_code, cosine, sine, block, LONG if step == sets - 1 else 1
             ),
-            qkv[step], head_grad, heads_low[step], attended[step][1], due=ready,
+            qkv[step], head_grad, heads_low[step], attended[step][1],
         )
-        if step == 0:
+        ready = (grad_up[1:], ffn_branch[1:]) if step == 0 else ()
+        stacked = then(heads_grad, [heads_low[step]], resid_grad_all, due=ready)
+        if held is not None:
+            grad_attn[step + 1] = scatter(after(held, last()))
+            grad_gate = settle([piece[ffn_width:] for piece in grad_ffn], grad_up[1:])
             grad_down = settle([grad_down[j * ffn_width : (j + 1) * ffn_width] for j in range(sets)], last())
-        stacked = then(heads_grad, [heads_low[step]], resid_grad_all)
         held = then(project_grad, normed_all, grad_project[step], stacked)
     grad_attn[0] = scatter(held)
     call = functools.partial(expand_project, "grad_normed")
-    due = (tuple(grad_gate[1:]), tuple(grad_down[1:]))
-    sums = share(call, grad_project, packs, number=7, due=due[0], due_near=due[1], cost_near=LONG)
+    due = ((), tuple(grad_gate[1:]))
+    sums = share(call, grad_project, packs, number=7, due=due[0], due_near=due[1], cost_near=100 * LONG)
     grad_normed = scatter_far(sums)
     output = (resid + settled(ffn_branch)).astype(BF16)
     grad_attn = settle(grad_attn)
-    grad_normed = settled(after(grad_normed, grad_attn[1:]))
+    grad_normed = settled(after(grad_normed, grad_attn[1:], grad_down[1:]))
     grad_input = (grad_resid + layer_norm_back(x_float, grad_normed)).astype(BF16)
     grad_attn = settled(grad_attn)
 

time: 852 us -> 841 us (0.987)
  waiting for transfers between devices: 201 us -> 184 us
    ppermute x7, waiting for transfers between devices: 150 us -> 116 us  [swap(): return lax.ppermute(values, 'tp', [(i, i ^ bit) for i in range(tp_size)])]
    ppermute x6, waiting for transfers between devices: 50.2 us -> 67.9 us  [turn(): lax.ppermute(values, 'tp', [(i, (i + step * members) % tp_size) for i in...]
    unnamed x64 -> x69, local copies, waits for them, and re-layouts: 15.4 us -> 20.2 us
  transfers between devices with their start and end apart: 22 -> 22, of which waited for: 10 -> 9; matrix products, arithmetic and copies ran while one was open for 7% -> 7% of each run, Pallas kernels for 54% -> 55%
where the time goes in v5:
time: 841 us; the launch traced here: 834 us
  Pallas kernels  538 us (64%)
  waiting for transfers between devices  184 us (22%)
  other arithmetic  47.7 us (6%)
  local copies, waits for them, and re-layouts  31.9 us (4%)
  starting transfers between devices  16.6 us (2%)
  between operations  15 us (2%)
    pallas_call x9, Pallas kernels, expand_call(): pl.pallas_call(functools.partial(expand_kernel, len(xs), each, plan, dot,...  138 us
    pallas_call x8, Pallas kernels, rows_call(): pl.pallas_call(functools.partial(rows_kernel, body, plan, members, len(ex...  130 us
    ppermute x7, waiting for transfers between devices, swap(): return lax.ppermute(values, 'tp', [(i, i ^ bit) for i in range(tp_size)])  116 us
    pallas_call x1, Pallas kernels, start_exchange(): pl.pallas_call(functools.partial(start_kernel, members, sets, count), in_...  82.3 us
    pallas_call x4, Pallas kernels, rows_grad(): kernel_call(functools.partial(rows_grad_kernel, len(xs), count), name, co...  75.5 us
    ppermute x6, waiting for transfers between devices, turn(): lax.ppermute(values, 'tp', [(i, (i + step * members) % tp_size) for i in...  67.9 us
    pallas_call x2, Pallas kernels, attend_backward(): pl.pallas_call(functools.partial(backward_kernel, block, reach, heads), g...  46.5 us
    pallas_call x3, Pallas kernels, columns_grad(): kernel_call(functools.partial(columns_grad_kernel, len(xs), len(gs)), nam...  41.6 us
  transfers between devices with their start and end apart: 22, of which 9 were waited for; matrix products, arithmetic and copies ran while one was open for 7% of the time, Pallas kernels for 55%

profile of v5, /device:TPU:0, one launch (start us, length us, event | category | flops | bytes accessed | tf_op | source)
XLA Modules:
  0.0 833.5 jit_solution(10533831106028512376)
XLA Ops:
  12.0 3.9 copy.23
  15.9 82.3 %start_exchange.1 = (bf16[512,2048]{1,0:T(8,128)(2,1)}, bf16[512,2048]{1,0:T(8,128)(2,1)}, bf16[512,2048]{1,0:T(8,128)(2,1)}, bf16[512,2048]{1,0:T(8,128)(2,1)},...) custom-call(bf16[512,2048]{1,0:T(8,128)(2,1)} %x_ref.1, ...), custom_call_target="tpu_custom_call" | custom-call | flops 1 | bytes 1 | tf_op jit(solution)/shard_map/start_exchange/pallas_call | solution.py:193
  98.4 3.0 collective-permute-start.2
  101.4 3.7 fusion.13
  107.1 14.2 %project.2.q_ref.k_ref.v_ref = bf16[2048,768]{1,0:T(8,128)(2,1)} custom-call(bf16[512,2048]{1,0:T(8,128)(2,1)} %get-tuple-element.381.refs_0_, bf16[512,2048]{1,0:T(8,128)(2,1)} %get-tuple-element.382.refs_1_, bf16[512,2048]{1,0:T(8,128)(2,1)} %get-tuple-element.383.refs_2_, bf16[512,2048]{1,0:T(8,128)(2,1)} %get-tuple-element.384.refs_3_, ...), custom_call_target="tpu_custom_call" | custom-call | flops 1 | bytes 1 | tf_op jit(solution)/shard_map/project/pallas_call | solution.py:296
  123.9 11.8 %attend_forward.2 = (bf16[2048,256]{1,0:T(8,128)(2,1)}, f32[2,4,1,512]{3,2,1,0:T(1,128)}) custom-call(s32[1]{0:T(128)} %bitcast.g_ref, bf16[2048,768]{1,0:T(8,128)(2,1)} %project.2.q_ref.k_ref.v_ref, bf16[2048,768]{1,0:T(8,128)(2,1)} %project.2.q_ref.k_ref.v_ref, bf16[2048,768]{1,0:T(8,128)(2,1)} %project.2.q_ref.k_ref.v_ref, ...), custom_call_target="tpu_custom_call" | custom-call | flops 1 | bytes 1 | tf_op jit(solution)/shard_map/attend_forward/pallas_call | solution.py:755
  135.7 14.1 %project.3.q_ref.k_ref.v_ref = bf16[2048,768]{1,0:T(8,128)(2,1)} custom-call(bf16[512,2048]{1,0:T(8,128)(2,1)} %get-tuple-element.381.refs_0_, bf16[512,2048]{1,0:T(8,128)(2,1)} %get-tuple-element.382.refs_1_, bf16[512,2048]{1,0:T(8,128)(2,1)} %get-tuple-element.383.refs_2_, bf16[512,2048]{1,0:T(8,128)(2,1)} %get-tuple-element.384.refs_3_, ...), custom_call_target="tpu_custom_call" | custom-call | flops 1 | bytes 1 | tf_op jit(solution)/shard_map/project/pallas_call | solution.py:296
  149.8 11.9 %attend_forward.3 = (bf16[2048,256]{1,0:T(8,128)(2,1)}, f32[2,4,1,512]{3,2,1,0:T(1,128)}) custom-call(s32[1]{0:T(128)} %bitcast.g_ref, bf16[2048,768]{1,0:T(8,128)(2,1)} %project.3.q_ref.k_ref.v_ref, bf16[2048,768]{1,0:T(8,128)(2,1)} %project.3.q_ref.k_ref.v_ref, bf16[2048,768]{1,0:T(8,128)(2,1)} %project.3.q_ref.k_ref.v_ref, ...), custom_call_target="tpu_custom_call" | custom-call | flops 1 | bytes 1 | tf_op jit(solution)/shard_map/attend_forward/pallas_call | solution.py:755
  161.7 8.6 %attn_branch.2 = bf16[512,2048]{1,0:T(8,128)(2,1)} custom-call(bf16[2048,256]{1,0:T(8,128)(2,1)} %get-tuple-element.376.refs_0_.out_ref, bf16[2048,256]{1,0:T(8,128)(2,1)} %get-tuple-element.351.refs_1_.out_ref.refs_0_, bf16[2048,256]{1,0:T(8,128)(2,1)} %copy-done.6, bf16[2048,256]{1,0:T(8,128)(2,1)} %get-tuple-element.401.refs_7_.refs_3_.refs_5_, ...), custom_call_target="tpu_custom_call" | custom-call | flops 1 | bytes 1 | tf_op jit(solution)/shard_map/attn_branch/pallas_call | solution.py:546
  170.3 9.5 %attn_branch.3 = f32[512,2048]{1,0:T(8,128)} custom-call(bf16[2048,256]{1,0:T(8,128)(2,1)} %get-tuple-element.376.refs_0_.out_ref, bf16[2048,256]{1,0:T(8,128)(2,1)} %get-tuple-element.351.refs_1_.out_ref.refs_0_, bf16[2048,256]{1,0:T(8,128)(2,1)} %copy-done.6, bf16[2048,256]{1,0:T(8,128)(2,1)} %get-tuple-element.401.refs_7_.refs_3_.refs_5_, ...), custom_call_target="tpu_custom_call" | custom-call | flops 1 | bytes 1 | tf_op jit(solution)/shard_map/attn_branch/pallas_call | solution.py:546
  179.7 11.5 %collective-permute-done.3.refs_1_.refs_2_.refs_4_ = bf16[512,2048]{1,0:T(8,128)(2,1)} collective-permute-done((bf16[512,2048]{1,0:T(8,128)(2,1)}, bf16[512,2048]{1,0:T(8,128)(2,1)}, u32[]{:S(2)}, u32[]{:S(2)}) %collective-permute-start.3) | collective-permute-done | bytes 2097184 | tf_op jit(solution)/shard_map/ppermute | solution.py:903
  193.9 44.9 %collective-permute-done = bf16[512,2048]{1,0:T(8,128)(2,1)} collective-permute-done((bf16[512,2048]{1,0:T(8,128)(2,1)}, bf16[512,2048]{1,0:T(8,128)(2,1)}, u32[]{:S(2)}, u32[]{:S(2)}) %collective-permute-start) | collective-permute-done | bytes 2097184 | tf_op jit(solution)/shard_map/ppermute | solution.py:903
  238.8 4.8 fusion.16
  247.4 44.6 %collective-permute-done.1.refs_1_.refs_2_ = bf16[512,2048]{1,0:T(8,128)(2,1)S(1)} collective-permute-done((bf16[512,2048]{1,0:T(8,128)(2,1)S(1)}, bf16[512,2048]{1,0:T(8,128)(2,1)S(1)}, u32[]{:S(2)}, u32[]{:S(2)}) %collective-permute-start.1) | collective-permute-done | bytes 2097184 | tf_op jit(solution)/shard_map/ppermute | solution.py:903
  296.0 25.7 %hidden_units.2 = (bf16[2048,1024]{1,0:T(8,128)(2,1)}, bf16[2048,1024]{1,0:T(8,128)(2,1)}, bf16[2048,1024]{1,0:T(8,128)(2,1)}, bf16[512,2048]{1,0:T(8,128)(2,1)}, bf16[512,2048]{1,0:T(8,128)(2,1)}) custom-call(bf16[512,2048]{1,0:T(8,128)(2,1)} %copy-done.5, bf16[512,2048]{1,0:T(8,128)(2,1)} %copy-done.8, bf16[4,512,2048]{2,1,0:T(8,128)(2,1)} %bitcast.43), custom_call_target="tpu_custom_call" | custom-call | flops 1 | bytes 1 | tf_op jit(solution)/shard_map/hidden_units/pallas_call | solution.py:296
  321.7 25.9 %hidden_units.3 = (bf16[2048,1024]{1,0:T(8,128)(2,1)}, bf16[2048,1024]{1,0:T(8,128)(2,1)}, bf16[2048,1024]{1,0:T(8,128)(2,1)}) custom-call(bf16[512,2048]{1,0:T(8,128)(2,1)} %copy-done.5, bf16[512,2048]{1,0:T(8,128)(2,1)} %get-tuple-element.309.refs_1_, bf16[512,2048]{1,0:T(8,128)(2,1)} %copy-done.8, bf16[512,2048]{1,0:T(8,128)(2,1)} %get-tuple-element.311.refs_3_, ...), custom_call_target="tpu_custom_call" | custom-call | flops 1 | bytes 1 | tf_op jit(solution)/shard_map/hidden_units/pallas_call | solution.py:296
  347.7 17.1 %hidden_grad.2 = (bf16[2048,2048]{1,0:T(8,128)(2,1)}, bf16[512,2048]{1,0:T(8,128)(2,1)}, bf16[512,2048]{1,0:T(8,128)(2,1)}) custom-call(bf16[512,2048]{1,0:T(8,128)(2,1)} %refs_2_, bf16[512,2048]{1,0:T(8,128)(2,1)} %collective-permute-done.3.refs_1_.refs_2_.refs_4_, bf16[2048,1024]{1,0:T(8,128)(2,1)} %get-tuple-element.286.refs_2_, ...), custom_call_target="tpu_custom_call" | custom-call | flops 999999995904 | bytes 1 | tf_op jit(solution)/shard_map/hidden_grad/pallas_call | solution.py:296
  364.8 23.6 %grad_ffn.2 = bf16[4,2048,512]{2,1,0:T(8,128)(2,1)} custom-call(s32[1]{0:T(128)} %bitcast.13.f_ref, bf16[512,2048]{1,0:T(8,128)(2,1)} %copy-done.5, bf16[512,2048]{1,0:T(8,128)(2,1)} %get-tuple-element.309.refs_1_, bf16[512,2048]{1,0:T(8,128)(2,1)} %copy-done.8, bf16[512,2048]{1,0:T(8,128)(2,1)} %get-tuple-element.311.refs_3_, ...), custom_call_target="tpu_custom_call" | custom-call | flops 1 | bytes 1 | tf_op jit(solution)/shard_map/grad_ffn/pallas_call | solution.py:647
  388.5 25.0 %grad_normed_two.3.refs_1_ = bf16[2048,2048]{1,0:T(8,128)(2,1)} custom-call(bf16[2048,2048]{1,0:T(8,128)(2,1)} %get-tuple-element.299.refs_4_.refs_0_, bf16[4,512,2048]{2,1,0:T(8,128)(2,1)} %bitcast.44), custom_call_target="tpu_custom_call" | custom-call | flops 1 | bytes 1 | tf_op jit(solution)/shard_map/grad_normed_two/pallas_call | solution.py:546
  413.5 16.6 %hidden_grad.3.refs_4_.refs_0_ = bf16[2048,2048]{1,0:T(8,128)(2,1)} custom-call(bf16[512,2048]{1,0:T(8,128)(2,1)} %refs_2_, bf16[512,2048]{1,0:T(8,128)(2,1)} %get-tuple-element.332.refs_1_.refs_3_, bf16[512,2048]{1,0:T(8,128)(2,1)} %collective-permute-done.3.refs_1_.refs_2_.refs_4_, bf16[512,2048]{1,0:T(8,128)(2,1)} %get-tuple-element.334.refs_3_.refs_5_, ...), custom_call_target="tpu_custom_call" | custom-call | flops 1 | bytes 1 | tf_op jit(solution)/shard_map/hidden_grad/pallas_call | solution.py:296
  430.1 23.7 %grad_ffn.3 = bf16[4,2048,512]{2,1,0:T(8,128)(2,1)} custom-call(s32[1]{0:T(128)} %bitcast.13.f_ref, bf16[512,2048]{1,0:T(8,128)(2,1)} %copy-done.5, bf16[512,2048]{1,0:T(8,128)(2,1)} %get-tuple-element.309.refs_1_, bf16[512,2048]{1,0:T(8,128)(2,1)} %copy-done.8, bf16[512,2048]{1,0:T(8,128)(2,1)} %get-tuple-element.311.refs_3_, ...), custom_call_target="tpu_custom_call" | custom-call | flops 1 | bytes 1 | tf_op jit(solution)/shard_map/grad_ffn/pallas_call | solution.py:647
  453.9 17.3 %grad_normed_two.4 = bf16[512,2048]{1,0:T(8,128)(2,1)} custom-call(bf16[2048,2048]{1,0:T(8,128)(2,1)} %hidden_grad.3.refs_4_.refs_0_, bf16[2048,2048]{1,0:T(8,128)(2,1)} %grad_normed_two.3.refs_1_, bf16[4,512,2048]{2,1,0:T(8,128)(2,1)} %bitcast.36), custom_call_target="tpu_custom_call" | custom-call | flops 1 | bytes 1 | tf_op jit(solution)/shard_map/grad_normed_two/pallas_call | solution.py:546
  472.8 17.6 %grad_normed_two.5 = f32[512,2048]{1,0:T(8,128)} custom-call(bf16[2048,2048]{1,0:T(8,128)(2,1)} %hidden_grad.3.refs_4_.refs_0_, bf16[2048,2048]{1,0:T(8,128)(2,1)} %grad_normed_two.3.refs_1_, bf16[4,512,2048]{2,1,0:T(8,128)(2,1)} %bitcast.37), custom_call_target="tpu_custom_call" | custom-call | flops 1 | bytes 1 | tf_op jit(solution)/shard_map/grad_normed_two/pallas_call | solution.py:546
  490.5 16.2 %ffn_branch.2 = bf16[512,2048]{1,0:T(8,128)(2,1)} custom-call(bf16[2048,1024]{1,0:T(8,128)(2,1)} %get-tuple-element.329.refs_0_, bf16[2048,1024]{1,0:T(8,128)(2,1)} %get-tuple-element.330.refs_1_, bf16[4,1024,512]{2,1,0:T(8,128)(2,1)} %bitcast.49, bf16[4,1024,512]{2,1,0:T(8,128)(2,1)} %bitcast.39), custom_call_target="tpu_custom_call" | custom-call | flops 1 | bytes 1 | tf_op jit(solution)/shard_map/ffn_branch/pallas_call | solution.py:546
  506.7 12.7 %collective-permute-done.5 = bf16[512,2048]{1,0:T(8,128)(2,1)S(1)} collective-permute-done((bf16[512,2048]{1,0:T(8,128)(2,1)}, bf16[512,2048]{1,0:T(8,128)(2,1)S(1)}, u32[]{:S(2)}, u32[]{:S(2)}) %collective-permute-start.5) | collective-permute-done | bytes 2097184 | tf_op jit(solution)/shard_map/ppermute | solution.py:903
  519.4 4.1 fusion.11
  523.6 5.0 fusion.15
  532.0 16.1 %ffn_branch.3 = f32[512,2048]{1,0:T(8,128)} custom-call(bf16[2048,1024]{1,0:T(8,128)(2,1)} %get-tuple-element.329.refs_0_, bf16[2048,1024]{1,0:T(8,128)(2,1)} %get-tuple-element.330.refs_1_, bf16[4,1024,512]{2,1,0:T(8,128)(2,1)} %bitcast.50, bf16[4,1024,512]{2,1,0:T(8,128)(2,1)} %bitcast.40), custom_call_target="tpu_custom_call" | custom-call | flops 1 | bytes 1 | tf_op jit(solution)/shard_map/ffn_branch/pallas_call | solution.py:546
  548.2 25.8 %grad_down.1 = bf16[4,2048,512]{2,1,0:T(8,128)(2,1)} custom-call(s32[1]{0:T(128)} %bitcast.13.f_ref, bf16[2048,1024]{1,0:T(8,128)(2,1)} %get-tuple-element.329.refs_0_, bf16[2048,1024]{1,0:T(8,128)(2,1)} %get-tuple-element.330.refs_1_, bf16[512,2048]{1,0:T(8,128)(2,1)} %refs_2_, bf16[512,2048]{1,0:T(8,128)(2,1)} %get-tuple-element.332.refs_1_.refs_3_, ...), custom_call_target="tpu_custom_call" | custom-call | flops 1 | bytes 1 | tf_op jit(solution)/shard_map/grad_down/pallas_call | solution.py:701
  575.9 10.7 %head_grad.2 = (bf16[2048,256]{1,0:T(8,128)(2,1)}, bf16[512,2048]{1,0:T(8,128)(2,1)}, bf16[512,2048]{1,0:T(8,128)(2,1)}) custom-call(bf16[512,2048]{1,0:T(8,128)(2,1)} %copy-done.4, bf16[512,2048]{1,0:T(8,128)(2,1)} %collective-permute-done.6.refs_1_.refs_3_.refs_2_, bf16[2048,256]{1,0:T(8,128)(2,1)} %get-tuple-element.404.refs_6_.refs_2_, ...), custom_call_target="tpu_custom_call" | custom-call | flops 1 | bytes 1 | tf_op jit(solution)/shard_map/head_grad/pallas_call | solution.py:296
  588.3 3.3 fusion.20
  592.0 23.1 %attend_backward.2.refs_5_.refs_1_ = bf16[2048,768]{1,0:T(8,128)(2,1)} custom-call(s32[1]{0:T(128)} %bitcast.g_ref, bf16[2048,768]{1,0:T(8,128)(2,1)} %project.3.q_ref.k_ref.v_ref, bf16[2048,768]{1,0:T(8,128)(2,1)} %project.3.q_ref.k_ref.v_ref, bf16[2048,768]{1,0:T(8,128)(2,1)} %project.3.q_ref.k_ref.v_ref, bf16[2048,256]{1,0:T(8,128)(2,1)} %get-tuple-element.348.grad_ref, ...), custom_call_target="tpu_custom_call" | custom-call | flops 999999995904 | bytes 1 | tf_op jit(solution)/shard_map/attend_backward/pallas_call | solution.py:853
  615.1 8.1 grad_heads.2.refs_4_
  623.2 14.1 %grad_attn.2 = bf16[4,1024,512]{2,1,0:T(8,128)(2,1)} custom-call(s32[1]{0:T(128)} %bitcast.13.f_ref, bf16[512,2048]{1,0:T(8,128)(2,1)} %get-tuple-element.381.refs_0_, bf16[512,2048]{1,0:T(8,128)(2,1)} %get-tuple-element.382.refs_1_, bf16[512,2048]{1,0:T(8,128)(2,1)} %get-tuple-element.383.refs_2_, ...), custom_call_target="tpu_custom_call", output_to_operand_aliasing={{}: (5, {})} | custom-call | flops 1 | bytes 1 | tf_op jit(solution)/shard_map/grad_attn/pallas_call | solution.py:647
  637.3 6.1 head_grad.3.grad_ref
  643.4 23.4 %attend_backward.3.refs_5_.refs_0_ = bf16[2048,768]{1,0:T(8,128)(2,1)} custom-call(s32[1]{0:T(128)} %bitcast.g_ref, bf16[2048,768]{1,0:T(8,128)(2,1)} %project.2.q_ref.k_ref.v_ref, bf16[2048,768]{1,0:T(8,128)(2,1)} %project.2.q_ref.k_ref.v_ref, bf16[2048,768]{1,0:T(8,128)(2,1)} %project.2.q_ref.k_ref.v_ref, bf16[2048,256]{1,0:T(8,128)(2,1)} %head_grad.3.grad_ref, ...), custom_call_target="tpu_custom_call" | custom-call | flops 1 | bytes 1 | tf_op jit(solution)/shard_map/attend_backward/pallas_call | solution.py:853
  666.8 7.7 grad_heads.3
  679.0 7.4 add_convert_fusion
  688.4 14.2 %grad_attn.3 = bf16[4,1024,512]{2,1,0:T(8,128)(2,1)} custom-call(s32[1]{0:T(128)} %bitcast.13.f_ref, bf16[512,2048]{1,0:T(8,128)(2,1)} %get-tuple-element.381.refs_0_, bf16[512,2048]{1,0:T(8,128)(2,1)} %get-tuple-element.382.refs_1_, bf16[512,2048]{1,0:T(8,128)(2,1)} %get-tuple-element.383.refs_2_, ...), custom_call_target="tpu_custom_call", output_to_operand_aliasing={{}: (5, {})} | custom-call | flops 1 | bytes 1 | tf_op jit(solution)/shard_map/grad_attn/pallas_call | solution.py:647
  702.5 13.7 %grad_normed.2 = bf16[512,2048]{1,0:T(8,128)(2,1)} custom-call(bf16[2048,768]{1,0:T(8,128)(2,1)} %attend_backward.3.refs_5_.refs_0_, bf16[2048,768]{1,0:T(8,128)(2,1)} %attend_backward.2.refs_5_.refs_1_, bf16[2048,256]{1,0:T(8,128)(2,1)} %copy-done.6, bf16[2048,256]{1,0:T(8,128)(2,1)} %get-tuple-element.401.refs_7_.refs_3_.refs_5_, ...), custom_call_target="tpu_custom_call" | custom-call | flops 1 | bytes 1 | tf_op jit(solution)/shard_map/grad_normed/pallas_call | solution.py:546
  718.9 5.3 collective-permute-done.9
  725.2 14.3 %grad_normed.3 = f32[512,2048]{1,0:T(8,128)} custom-call(bf16[2048,768]{1,0:T(8,128)(2,1)} %attend_backward.3.refs_5_.refs_0_, bf16[2048,768]{1,0:T(8,128)(2,1)} %attend_backward.2.refs_5_.refs_1_, bf16[2048,256]{1,0:T(8,128)(2,1)} %copy-done.6, bf16[2048,256]{1,0:T(8,128)(2,1)} %get-tuple-element.401.refs_7_.refs_3_.refs_5_, ...), custom_call_target="tpu_custom_call" | custom-call | flops 100000000376832 | bytes 1 | tf_op jit(solution)/shard_map/grad_normed/pallas_call | solution.py:546
  745.1 5.2 copy.22
  750.4 34.8 %collective-permute-done.12 = bf16[1024,512]{1,0:T(8,128)(2,1)} collective-permute-done((bf16[1024,512]{1,0:T(8,128)(2,1)}, bf16[1024,512]{1,0:T(8,128)(2,1)}, u32[]{:S(2)}, u32[]{:S(2)}) %collective-permute-start.12) | collective-permute-done | bytes 1048608 | tf_op jit(solution)/shard_map/ppermute | solution.py:906
  785.2 2.9 convert_add_fusion.3
  788.1 26.4 %collective-permute-done.11 = bf16[1024,512]{1,0:T(8,128)(2,1)} collective-permute-done((bf16[1024,512]{1,0:T(8,128)(2,1)}, bf16[1024,512]{1,0:T(8,128)(2,1)}, u32[]{:S(2)}, u32[]{:S(2)}) %collective-permute-start.11) | collective-permute-done | bytes 1048608 | tf_op jit(solution)/shard_map/ppermute | solution.py:906
  816.6 2.9 fusion.12
  822.5 4.1 fusion.8
  (145 shorter events, 49.5 us)
Async XLA Ops:
  7.2 288.9 %all-gather.9.cloned.1.call-start = ((), (), s32[]{:S(2)}) async-start(), calls=%async_computation.10 | async-start | bytes 10485760 | tf_op jit(solution)/shard_map/all_gather | solution.py:961
  12.0 3.9 copy-start.6
  12.0 89.4 %copy-start.28 = (s32[4096]{0:T(1024)S(1)}, s32[4096]{0:T(1024)}, u32[]{:S(2)}) copy-start(s32[4096]{0:T(1024)} %param.16) | copy-start | bytes 49156
  98.2 223.5 %all-gather.11.cloned.1.call-start = ((), (), s32[]{:S(2)}) async-start(), calls=%async_computation.11 | async-start | bytes 10485760 | tf_op jit(solution)/shard_map/all_gather | solution.py:961
  98.3 93.0 %collective-permute-start.3 = (bf16[512,2048]{1,0:T(8,128)(2,1)}, bf16[512,2048]{1,0:T(8,128)(2,1)}, u32[]{:S(2)}, u32[]{:S(2)}) collective-permute-start(bf16[512,2048]{1,0:T(8,128)(2,1)} %refs_2_), channel_id=1, source_target_pairs={{0,2},{1,3},{2,0},{3,1},{4,6},{5,7},{6,4},{7,5},{8,10},{9,11},{10,... | collective-permute-start | bytes 6291464 | tf_op jit(solution)/shard_map/ppermute | solution.py:903
  98.4 94.2 %collective-permute-start.2 = (bf16[512,2048]{1,0:T(8,128)(2,1)}, bf16[512,2048]{1,0:T(8,128)(2,1)}, u32[]{:S(2)}, u32[]{:S(2)}) collective-permute-start(bf16[512,2048]{1,0:T(8,128)(2,1)} %bitcast.26), channel_id=1, source_target_pairs={{0,4},{1,5},{2,6},{3,7},{4,0},{5,1},{6,2},{7,3},{8,12},{9,13},{10,... | collective-permute-start | bytes 6291464 | tf_op jit(solution)/shard_map/ppermute | solution.py:906
  107.1 14.3 %copy-start.29 = (s32[4096]{0:T(1024)S(1)}, s32[4096]{0:T(1024)}, u32[]{:S(2)}) copy-start(s32[4096]{0:T(1024)} %param.15) | copy-start | bytes 49156
  107.1 14.3 %copy-start.30 = (s32[4096]{0:T(1024)S(1)}, s32[4096]{0:T(1024)}, u32[]{:S(2)}) copy-start(s32[4096]{0:T(1024)} %param.14) | copy-start | bytes 49156
  122.0 13.7 %copy-start.19 = (s32[2048]{0:T(1024)}, s32[2048]{0:T(1024)S(1)}, u32[]{:S(2)}) copy-start(s32[2048]{0:T(1024)S(1)} %get-tuple-element.427) | copy-start | bytes 24580
  179.7 13.8 %copy-start.2 = (bf16[512,2048]{1,0:T(8,128)(2,1)S(1)}, bf16[512,2048]{1,0:T(8,128)(2,1)}, u32[]{:S(2)}) copy-start(bf16[512,2048]{1,0:T(8,128)(2,1)} %x_ref.1) | copy-start | bytes 6291460
  192.6 155.1 %all-gather.13.cloned.1.call-start = ((), (), s32[]{:S(2)}) async-start(), calls=%async_computation.12 | async-start | bytes 5242880 | tf_op jit(solution)/shard_map/all_gather | solution.py:961
  192.6 46.2 %collective-permute-start = (bf16[512,2048]{1,0:T(8,128)(2,1)}, bf16[512,2048]{1,0:T(8,128)(2,1)}, u32[]{:S(2)}, u32[]{:S(2)}) collective-permute-start(bf16[512,2048]{1,0:T(8,128)(2,1)} %attn_branch.2), channel_id=1, source_target_pairs={{0,2},{1,3},{2,0},{3,1},{4,6},{5,7},{6,4},{7,5},{8,10},{9,11},{10,... | collective-permute-start | bytes 6291464 | tf_op jit(solution)/shard_map/ppermute | solution.py:903
  193.3 220.2 %all-gather.15.cloned.1.call-start = ((), (), s32[]{:S(2)}) async-start(), calls=%async_computation.13 | async-start | bytes 5242880 | tf_op jit(solution)/shard_map/all_gather | solution.py:961
  193.9 49.8 %copy-start.22 = (f32[512]{0:T(512)}, f32[512]{0:T(512)S(1)}, u32[]{:S(2)}) copy-start(f32[512]{0:T(512)S(1)} %broadcast_multiply_fusion.2) | copy-start | bytes 6148
  244.2 49.2 %copy-start.15 = (bf16[1024,512]{1,0:T(8,128)(2,1)S(1)}, bf16[1024,512]{1,0:T(8,128)(2,1)}, u32[]{:S(2)}) copy-start(bf16[1024,512]{1,0:T(8,128)(2,1)} %param.13) | copy-start | bytes 3145732
  244.3 47.8 %copy-start.24 = (f32[512]{0:T(512)}, f32[512]{0:T(512)S(1)}, u32[]{:S(2)}) copy-start(f32[512]{0:T(512)S(1)} %add_rsqrt_fusion.1) | copy-start | bytes 6148
  245.7 50.3 %copy-start.5 = (bf16[512,2048]{1,0:T(8,128)(2,1)}, bf16[512,2048]{1,0:T(8,128)(2,1)S(1)}, u32[]{:S(2)}) copy-start(bf16[512,2048]{1,0:T(8,128)(2,1)S(1)} %fusion.10.refs_0_) | copy-start | bytes 6291460
  245.7 46.4 %collective-permute-start.1 = (bf16[512,2048]{1,0:T(8,128)(2,1)S(1)}, bf16[512,2048]{1,0:T(8,128)(2,1)S(1)}, u32[]{:S(2)}, u32[]{:S(2)}) collective-permute-start(bf16[512,2048]{1,0:T(8,128)(2,1)S(1)} %fusion.10.refs_0_), channel_id=1, source_target_pairs={{0,2},{1,3},{2,0},{3,1},{4,6},{5,7},{6,4},{7,5},{8,10},{9,11},{10,... | collective-permute-start | bytes 6291464 | tf_op jit(solution)/shard_map/ppermute | solution.py:903
  293.4 54.2 %collective-permute-start.4 = (bf16[1024,512]{1,0:T(8,128)(2,1)S(1)}, bf16[1024,512]{1,0:T(8,128)(2,1)}, u32[]{:S(2)}, u32[]{:S(2)}) collective-permute-start(bf16[1024,512]{1,0:T(8,128)(2,1)S(1)} %copy-done.15), channel_id=1, source_target_pairs={{0,4},{1,5},{2,6},{3,7},{4,0},{5,1},{6,2},{7,3},{8,12},{9,13},{10,... | collective-permute-start | bytes 3145736 | tf_op jit(solution)/shard_map/ppermute | solution.py:906
  347.7 228.3 %reduce-scatter.6.cloned.1.call-start = ((), (), s32[]{:S(2)}) async-start(), calls=%async_computation.5 | async-start | bytes 10485760 | tf_op jit(solution)/shard_map/reduce_scatter | solution.py:964
  388.4 199.9 %reduce-scatter.8.cloned.1.call-start = ((), (), s32[]{:S(2)}) async-start(), calls=%async_computation.6 | async-start | bytes 10485760 | tf_op jit(solution)/shard_map/reduce_scatter | solution.py:964
  453.8 262.6 %reduce-scatter.12.cloned.1.call-start = ((), (), s32[]{:S(2)}) async-start(), calls=%async_computation.8 | async-start | bytes 10485760 | tf_op jit(solution)/shard_map/reduce_scatter | solution.py:964
  471.2 48.2 %collective-permute-start.5 = (bf16[512,2048]{1,0:T(8,128)(2,1)}, bf16[512,2048]{1,0:T(8,128)(2,1)S(1)}, u32[]{:S(2)}, u32[]{:S(2)}) collective-permute-start(bf16[512,2048]{1,0:T(8,128)(2,1)} %grad_normed_two.4), channel_id=1, source_target_pairs={{0,2},{1,3},{2,0},{3,1},{4,6},{5,7},{6,4},{7,5},{8,10},{9,11},{10,... | collective-permute-start | bytes 6291464 | tf_op jit(solution)/shard_map/ppermute | solution.py:903
  490.4 29.0 %copy-start.1 = (f32[512,2048]{1,0:T(8,128)S(1)}, f32[512,2048]{1,0:T(8,128)}, u32[]{:S(2)}) copy-start(f32[512,2048]{1,0:T(8,128)} %copy-done) | copy-start | bytes 12582916
  490.4 29.0 %copy-start.21 = (f32[512]{0:T(512)S(1)}, f32[512]{0:T(512)}, u32[]{:S(2)}) copy-start(f32[512]{0:T(512)} %copy-done.20) | copy-start | bytes 6148
  490.4 29.0 %copy-start.25 = (f32[512]{0:T(512)S(1)}, f32[512]{0:T(512)}, u32[]{:S(2)}) copy-start(f32[512]{0:T(512)} %copy-done.24) | copy-start | bytes 6148
  506.7 16.9 %copy-start.7 = (f32[512,2048]{1,0:T(8,128)S(1)}, f32[512,2048]{1,0:T(8,128)}, u32[]{:S(2)}) copy-start(f32[512,2048]{1,0:T(8,128)} %grad_normed_two.5) | copy-start | bytes 12582916
  519.4 4.1 copy-start.12
  523.6 6.6 copy-start.18
  528.6 19.6 %copy-start.4 = (bf16[512,2048]{1,0:T(8,128)(2,1)}, bf16[512,2048]{1,0:T(8,128)(2,1)S(1)}, u32[]{:S(2)}) copy-start(bf16[512,2048]{1,0:T(8,128)(2,1)S(1)} %get-tuple-element.377.refs_0_.refs_1_) | copy-start | bytes 6291460
  528.6 47.4 %collective-permute-start.6 = (bf16[512,2048]{1,0:T(8,128)(2,1)S(1)}, bf16[512,2048]{1,0:T(8,128)(2,1)}, u32[]{:S(2)}, u32[]{:S(2)}) collective-permute-start(bf16[512,2048]{1,0:T(8,128)(2,1)S(1)} %get-tuple-element.377.refs_0_.refs_1_), channel_id=1, source_target_pairs={{0,2},{1,3},{2,0},{3,1},{4,6},{5,7},{6,4},{7,5},{8,10},{9,11},{10,... | collective-permute-start | bytes 6291464 | tf_op jit(solution)/shard_map/ppermute | solution.py:903
  574.0 168.9 %reduce-scatter.10.cloned.1.call-start = ((), (), s32[]{:S(2)}) async-start(), calls=%async_computation.7 | async-start | bytes 5242880 | tf_op jit(solution)/shard_map/reduce_scatter | solution.py:964
  586.6 80.1 %collective-permute-start.7 = (bf16[512,2048]{1,0:T(8,128)(2,1)}, bf16[512,2048]{1,0:T(8,128)(2,1)}, u32[]{:S(2)}, u32[]{:S(2)}) collective-permute-start(bf16[512,2048]{1,0:T(8,128)(2,1)} %ffn_branch.2), channel_id=1, source_target_pairs={{0,2},{1,3},{2,0},{3,1},{4,6},{5,7},{6,4},{7,5},{8,10},{9,11},{10,... | collective-permute-start | bytes 6291464 | tf_op jit(solution)/shard_map/ppermute | solution.py:903
  591.6 75.1 %collective-permute-start.8 = (bf16[1024,512]{1,0:T(8,128)(2,1)}, bf16[1024,512]{1,0:T(8,128)(2,1)}, u32[]{:S(2)}, u32[]{:S(2)}) collective-permute-start(bf16[1024,512]{1,0:T(8,128)(2,1)} %get-tuple-element.375), channel_id=1, source_target_pairs={{0,4},{1,5},{2,6},{3,7},{4,0},{5,1},{6,2},{7,3},{8,12},{9,13},{10,... | collective-permute-start | bytes 3145736 | tf_op jit(solution)/shard_map/ppermute | solution.py:906
  674.5 3.9 copy-start.27
  674.5 113.6 %reduce-scatter.14.cloned.1.call-start = ((), (), s32[]{:S(2)}) async-start(), calls=%async_computation.9 | async-start | bytes 5242880 | tf_op jit(solution)/shard_map/reduce_scatter | solution.py:964
  675.7 48.5 %collective-permute-start.9 = (bf16[1024,512]{1,0:T(8,128)(2,1)S(1)}, bf16[1024,512]{1,0:T(8,128)(2,1)S(1)}, u32[]{:S(2)}, u32[]{:S(2)}) collective-permute-start(bf16[1024,512]{1,0:T(8,128)(2,1)S(1)} %copy-done.16), channel_id=1, source_target_pairs={{0,4},{1,5},{2,6},{3,7},{4,0},{5,1},{6,2},{7,3},{8,12},{9,13},{10,... | collective-permute-start | bytes 3145736 | tf_op jit(solution)/shard_map/ppermute | solution.py:906
  679.0 7.4 copy-start.11
  716.3 100.3 %collective-permute-start.10 = (bf16[512,2048]{1,0:T(8,128)(2,1)}, bf16[512,2048]{1,0:T(8,128)(2,1)}, u32[]{:S(2)}, u32[]{:S(2)}) collective-permute-start(bf16[512,2048]{1,0:T(8,128)(2,1)} %grad_normed.2), channel_id=1, source_target_pairs={{0,2},{1,3},{2,0},{3,1},{4,6},{5,7},{6,4},{7,5},{8,10},{9,11},{10,... | collective-permute-start | bytes 6291464 | tf_op jit(solution)/shard_map/ppermute | solution.py:903
  718.7 66.5 %collective-permute-start.12 = (bf16[1024,512]{1,0:T(8,128)(2,1)}, bf16[1024,512]{1,0:T(8,128)(2,1)}, u32[]{:S(2)}, u32[]{:S(2)}) collective-permute-start(bf16[1024,512]{1,0:T(8,128)(2,1)} %slice.85), channel_id=1, source_target_pairs={{0,4},{1,5},{2,6},{3,7},{4,0},{5,1},{6,2},{7,3},{8,12},{9,13},{10,... | collective-permute-start | bytes 3145736 | tf_op jit(solution)/shard_map/ppermute | solution.py:906
  725.2 14.3 %copy-start.14 = (bf16[2048,512]{1,0:T(8,128)(2,1)S(1)}, bf16[2048,512]{1,0:T(8,128)(2,1)}, u32[]{:S(2)}) copy-start(bf16[2048,512]{1,0:T(8,128)(2,1)} %reduce-scatter.6.cloned.1.call-done) | copy-start | bytes 6291460
  742.9 71.7 %collective-permute-start.11 = (bf16[1024,512]{1,0:T(8,128)(2,1)}, bf16[1024,512]{1,0:T(8,128)(2,1)}, u32[]{:S(2)}, u32[]{:S(2)}) collective-permute-start(bf16[1024,512]{1,0:T(8,128)(2,1)} %reduce-scatter.10.cloned.1.call-done), channel_id=1, source_target_pairs={{0,4},{1,5},{2,6},{3,7},{4,0},{5,1},{6,2},{7,3},{8,12},{9,13},{10,... | collective-permute-start | bytes 3145736 | tf_op jit(solution)/shard_map/ppermute | solution.py:906
  745.1 40.1 %copy-start.13 = (bf16[2048,512]{1,0:T(8,128)(2,1)S(1)}, bf16[2048,512]{1,0:T(8,128)(2,1)}, u32[]{:S(2)}) copy-start(bf16[2048,512]{1,0:T(8,128)(2,1)} %reduce-scatter.12.cloned.1.call-done) | copy-start | bytes 6291460
  788.1 28.5 %copy-start.3 = (bf16[512,2048]{1,0:T(8,128)(2,1)S(1)}, bf16[512,2048]{1,0:T(8,128)(2,1)}, u32[]{:S(2)}) copy-start(bf16[512,2048]{1,0:T(8,128)(2,1)} %x_ref.1) | copy-start | bytes 6291460
  788.1 28.5 %copy-start.23 = (f32[512]{0:T(512)S(1)}, f32[512]{0:T(512)}, u32[]{:S(2)}) copy-start(f32[512]{0:T(512)} %copy-done.22) | copy-start | bytes 6148
  788.1 28.5 %copy-start.26 = (f32[512]{0:T(512)S(1)}, f32[512]{0:T(512)}, u32[]{:S(2)}) copy-start(f32[512]{0:T(512)} %add_rsqrt_fusion) | copy-start | bytes 6148
  788.1 28.5 %copy-start.9 = (f32[512,2048]{1,0:T(8,128)S(1)}, f32[512,2048]{1,0:T(8,128)}, u32[]{:S(2)}) copy-start(f32[512,2048]{1,0:T(8,128)} %grad_normed.3) | copy-start | bytes 12582916
  819.5 2.9 copy-start.10
  (5 other events, 7.5 us)
Sparse Core Ops, SparseCore 0:
  98.3 87.7 all-gather.8
  192.7 87.6 all-gather.10
  282.2 52.6 all-gather.12
  347.8 52.2 all-gather.14
  403.0 86.3 reduce-scatter.5
  492.7 86.4 reduce-scatter.7
  582.2 86.3 reduce-scatter.11
  674.7 53.5 reduce-scatter.9
  731.2 52.6 reduce-scatter.13

commit v6 on v5

--- a/solution.py
+++ b/solution.py
@@ -84,7 +84,7 @@
 
 
 def start_kernel(members, sets, count, x_ref, pack_ref, *refs):
-    normed, refs = refs[:members], refs[members:]
+    normed, refs = dict(zip(range(0, members, 2), refs)), refs[members // 2 :]
     packs = [(pack_ref,) + refs[: count - 1]]
     refs = refs[count - 1 :]
     for _ in range(1, sets):
@@ -94,7 +94,7 @@
     t, f = lax.axis_index("tp"), lax.axis_index("fsdp")
     total = members * sets
     climb = [1 << i for i in range(count.bit_length() - 1)]
-    group = [1 << i for i in range(members.bit_length() - 1)][::-1]
+    group = [1 << i for i in range(1, members.bit_length() - 1)][::-1]
     shifts = [lax.rem(t + step * members, total) for step in range(1, sets)]
 
     barrier = pltpu.get_barrier_semaphore()
@@ -174,7 +174,7 @@
             if pair:
                 pass_all(step, (pair - 2, pair - 1))
         pass_all(step, (PIECES - 2, PIECES - 1))
-    for mask in sorted(range(1, members), reverse=True, key=lambda m: (m & -m, m)):
+    for mask in sorted(range(2, members, 2), reverse=True, key=lambda m: (m & -m, m)):
         below = [bit for bit in group if bit < mask & -mask]
         if below:
             await_block(blocks[mask])
@@ -188,8 +188,9 @@
 
 
 def start_exchange(x, pack, members, sets, count):
-    sends = PIECES * ((count - 1) * sets + sets - 1) + members - 1
-    shapes = [jax.ShapeDtypeStruct(x.shape, BF16)] * members + [jax.ShapeDtypeStruct(pack.shape, BF16)] * (count * sets - 1)
+    half = members // 2
+    sends = PIECES * ((count - 1) * sets + sets - 1) + half - 1
+    shapes = [jax.ShapeDtypeStruct(x.shape, BF16)] * half + [jax.ShapeDtypeStruct(pack.shape, BF16)] * (count * sets - 1)
     outs = pl.pallas_call(
         functools.partial(start_kernel, members, sets, count),
         in_specs=[pl.BlockSpec(memory_space=pltpu.VMEM), pl.BlockSpec(memory_space=pl.ANY)],
@@ -205,8 +206,8 @@
         cost_estimate=pl.CostEstimate(flops=1, bytes_accessed=1, transcendentals=0),
         name="start_exchange",
     )(x, pack)
-    packs = [pack] + list(outs[members:])
-    return outs[:members], [packs[step * count : (step + 1) * count] for step in range(sets)]
+    packs = [pack] + list(outs[half:])
+    return outs[:half], [packs[step * count : (step + 1) * count] for step in range(sets)]
 
 
 def rows_kernel(body, plan, members, extras, count, number, *refs):
@@ -321,7 +322,7 @@
     return outs[: len(widths)], [block for pair in zip(xs, outs[len(widths) :]) for block in pair]
 
 
-def project(xs, packs, cosine, sine):
+def project(xs, packs, cosine, sine, number=0):
     model, count = xs[0].shape[1], len(packs)
     depth, width = model // count, packs[0].shape[1]
 
@@ -342,8 +343,8 @@
             outs[0][:, t * width + column : t * width + column + HD] = value.astype(BF16)
 
     return rows_call(
-        body, "project", xs, [cosine, sine], packs, (moves, use), 3, count, (3, model, width), [3 * width], 0
-    )[0][0]
+        body, "project", xs, [cosine, sine], packs, (moves, use), 3, count, (3, model, width), [3 * width], number
+    )
 
 
 def head_grad_of(xs, packs, number=0):
@@ -969,8 +970,8 @@
     def settled(pieces):
         return sum(piece.astype(F32) for piece in pieces)
 
-    normed_all, packs = start_exchange(inputs, pack_weights(att_proj, attn_out), members, sets, fsdp_size)
-    chain.append(normed_all[0])
+    normed_far, packs = start_exchange(inputs, pack_weights(att_proj, attn_out), members, sets, fsdp_size)
+    chain.append(normed_far[0])
     up_gate, down, cotangent_late = after((ff_proj.reshape(depth, -1), ff_out, cotangent), last())
     w_ffn, w_down = [gather(up_gate)], [gather(down)]
     turned_up_gate = [turn(up_gate, step) for step in range(1, sets)]
@@ -986,7 +987,11 @@
     x_float = inputs.astype(F32)
     qkv, attended = [], []
     for step in range(sets):
-        qkv.append(then(project, normed_all, packs[step], cosine, sine))
+        if step == 0:
+            (part,), normed_all = then(functools.partial(project, number=12), normed_far, packs[0], cosine, sine)
+        else:
+            (part,), _ = then(project, normed_all, packs[step], cosine, sine)
+        qkv.append(part)
         attended.append(then(lambda part: attend_forward(part, place_tp, segment, key_code, block), qkv[step]))
     heads_low = [out for out, _ in attended]
     sums = share(functools.partial(expand_heads, "attn_branch"), heads_low, packs, number=1)

time: 841 us -> 832 us (0.989)
  no operation moved by 1% of the time
where the time goes in v6:
time: 832 us; the launch traced here: 826 us
  Pallas kernels  534 us (64%)
  waiting for transfers between devices  182 us (22%)
  other arithmetic  47.7 us (6%)
  local copies, waits for them, and re-layouts  32 us (4%)
  between operations  15 us (2%)
  starting transfers between devices  14.6 us (2%)
    pallas_call x9, Pallas kernels, expand_call(): pl.pallas_call(functools.partial(expand_kernel, len(xs), each, plan, dot,...  138 us
    pallas_call x8, Pallas kernels, rows_call(): pl.pallas_call(functools.partial(rows_kernel, body, plan, members, len(ex...  131 us
    ppermute x7, waiting for transfers between devices, swap(): return lax.ppermute(values, 'tp', [(i, i ^ bit) for i in range(tp_size)])  114 us
    pallas_call x1, Pallas kernels, start_exchange(): pl.pallas_call(functools.partial(start_kernel, members, sets, count), in_...  78.2 us
    pallas_call x4, Pallas kernels, rows_grad(): kernel_call(functools.partial(rows_grad_kernel, len(xs), count), name, co...  75.7 us
    ppermute x6, waiting for transfers between devices, turn(): lax.ppermute(values, 'tp', [(i, (i + step * members) % tp_size) for i in...  67.7 us
    pallas_call x2, Pallas kernels, attend_backward(): pl.pallas_call(functools.partial(backward_kernel, block, reach, heads), g...  46.7 us
    pallas_call x3, Pallas kernels, columns_grad(): kernel_call(functools.partial(columns_grad_kernel, len(xs), len(gs)), nam...  40.9 us
  transfers between devices with their start and end apart: 22, of which 9 were waited for; matrix products, arithmetic and copies ran while one was open for 7% of the time, Pallas kernels for 55%

profile of v6, /device:TPU:0, one launch (start us, length us, event | category | flops | bytes accessed | tf_op | source)
XLA Modules:
  0.0 825.5 jit_solution(13459469670853538440)
XLA Ops:
  12.0 3.9 copy.23
  15.9 78.2 %start_exchange.1 = (bf16[512,2048]{1,0:T(8,128)(2,1)}, bf16[512,2048]{1,0:T(8,128)(2,1)}, bf16[2048,256]{1,0:T(8,128)(2,1)}, bf16[2048,256]{1,0:T(8,128)(2,1)},...) custom-call(bf16[512,2048]{1,0:T(8,128)(2,1)} %x_ref.1, ...), custom_call_target="tpu_custom_call" | custom-call | flops 1 | bytes 1 | tf_op jit(solution)/shard_map/start_exchange/pallas_call | solution.py:194
  94.2 3.0 collective-permute-start.2
  97.3 3.7 fusion.13
  102.9 14.4 %project.2 = (bf16[2048,768]{1,0:T(8,128)(2,1)}, bf16[512,2048]{1,0:T(8,128)(2,1)}, bf16[512,2048]{1,0:T(8,128)(2,1)}) custom-call(bf16[512,2048]{1,0:T(8,128)(2,1)} %get-tuple-element.379.refs_0_, bf16[512,2048]{1,0:T(8,128)(2,1)} %get-tuple-element.381.refs_1_.refs_2_, f32[2048,128]{1,0:T(8,128)} %get-tuple-element.234.refs_2_.refs_4_.cos_ref, ...), custom_call_target="tpu_custom_call" | custom-call | flops 1 | bytes 1 | tf_op jit(solution)/shard_map/project/pallas_call | solution.py:297
  119.9 11.9 %attend_forward.2 = (bf16[2048,256]{1,0:T(8,128)(2,1)}, f32[2,4,1,512]{3,2,1,0:T(1,128)}) custom-call(s32[1]{0:T(128)} %bitcast.g_ref, bf16[2048,768]{1,0:T(8,128)(2,1)} %get-tuple-element.369.q_ref.k_ref.v_ref, bf16[2048,768]{1,0:T(8,128)(2,1)} %get-tuple-element.369.q_ref.k_ref.v_ref, bf16[2048,768]{1,0:T(8,128)(2,1)} %get-tuple-element.369.q_ref.k_ref.v_ref, ...), custom_call_target="tpu_custom_call" | custom-call | flops 1 | bytes 1 | tf_op jit(solution)/shard_map/attend_forward/pallas_call | solution.py:756
  131.7 14.3 %project.3.q_ref.k_ref.v_ref = bf16[2048,768]{1,0:T(8,128)(2,1)} custom-call(bf16[512,2048]{1,0:T(8,128)(2,1)} %get-tuple-element.379.refs_0_, bf16[512,2048]{1,0:T(8,128)(2,1)} %get-tuple-element.380.refs_1_, bf16[512,2048]{1,0:T(8,128)(2,1)} %get-tuple-element.381.refs_1_.refs_2_, bf16[512,2048]{1,0:T(8,128)(2,1)} %get-tuple-element.382.refs_3_, ...), custom_call_target="tpu_custom_call" | custom-call | flops 1 | bytes 1 | tf_op jit(solution)/shard_map/project/pallas_call | solution.py:297
  146.0 11.9 %attend_forward.3 = (bf16[2048,256]{1,0:T(8,128)(2,1)}, f32[2,4,1,512]{3,2,1,0:T(1,128)}) custom-call(s32[1]{0:T(128)} %bitcast.g_ref, bf16[2048,768]{1,0:T(8,128)(2,1)} %project.3.q_ref.k_ref.v_ref, bf16[2048,768]{1,0:T(8,128)(2,1)} %project.3.q_ref.k_ref.v_ref, bf16[2048,768]{1,0:T(8,128)(2,1)} %project.3.q_ref.k_ref.v_ref, ...), custom_call_target="tpu_custom_call" | custom-call | flops 1 | bytes 1 | tf_op jit(solution)/shard_map/attend_forward/pallas_call | solution.py:756
  157.9 8.6 %attn_branch.2 = bf16[512,2048]{1,0:T(8,128)(2,1)} custom-call(bf16[2048,256]{1,0:T(8,128)(2,1)} %get-tuple-element.374.refs_0_.out_ref, bf16[2048,256]{1,0:T(8,128)(2,1)} %get-tuple-element.349.refs_1_.out_ref.refs_0_, bf16[2048,256]{1,0:T(8,128)(2,1)} %copy-done.6, bf16[2048,256]{1,0:T(8,128)(2,1)} %get-tuple-element.399.refs_5_.refs_3_, ...), custom_call_target="tpu_custom_call" | custom-call | flops 1 | bytes 1 | tf_op jit(solution)/shard_map/attn_branch/pallas_call | solution.py:547
  166.5 9.4 %attn_branch.3 = f32[512,2048]{1,0:T(8,128)} custom-call(bf16[2048,256]{1,0:T(8,128)(2,1)} %get-tuple-element.374.refs_0_.out_ref, bf16[2048,256]{1,0:T(8,128)(2,1)} %get-tuple-element.349.refs_1_.out_ref.refs_0_, bf16[2048,256]{1,0:T(8,128)(2,1)} %copy-done.6, bf16[2048,256]{1,0:T(8,128)(2,1)} %get-tuple-element.399.refs_5_.refs_3_, ...), custom_call_target="tpu_custom_call" | custom-call | flops 1 | bytes 1 | tf_op jit(solution)/shard_map/attn_branch/pallas_call | solution.py:547
  175.9 9.8 %collective-permute-done.3.refs_1_.refs_2_.refs_4_ = bf16[512,2048]{1,0:T(8,128)(2,1)} collective-permute-done((bf16[512,2048]{1,0:T(8,128)(2,1)}, bf16[512,2048]{1,0:T(8,128)(2,1)}, u32[]{:S(2)}, u32[]{:S(2)}) %collective-permute-start.3) | collective-permute-done | bytes 2097184 | tf_op jit(solution)/shard_map/ppermute | solution.py:904
  188.4 44.3 %collective-permute-done = bf16[512,2048]{1,0:T(8,128)(2,1)} collective-permute-done((bf16[512,2048]{1,0:T(8,128)(2,1)}, bf16[512,2048]{1,0:T(8,128)(2,1)}, u32[]{:S(2)}, u32[]{:S(2)}) %collective-permute-start) | collective-permute-done | bytes 2097184 | tf_op jit(solution)/shard_map/ppermute | solution.py:904
  232.7 4.8 fusion.16
  240.4 43.6 %collective-permute-done.1.refs_1_.refs_2_ = bf16[512,2048]{1,0:T(8,128)(2,1)S(1)} collective-permute-done((bf16[512,2048]{1,0:T(8,128)(2,1)S(1)}, bf16[512,2048]{1,0:T(8,128)(2,1)S(1)}, u32[]{:S(2)}, u32[]{:S(2)}) %collective-permute-start.1) | collective-permute-done | bytes 2097184 | tf_op jit(solution)/shard_map/ppermute | solution.py:904
  287.0 25.7 %hidden_units.2 = (bf16[2048,1024]{1,0:T(8,128)(2,1)}, bf16[2048,1024]{1,0:T(8,128)(2,1)}, bf16[2048,1024]{1,0:T(8,128)(2,1)}, bf16[512,2048]{1,0:T(8,128)(2,1)}, bf16[512,2048]{1,0:T(8,128)(2,1)}) custom-call(bf16[512,2048]{1,0:T(8,128)(2,1)} %copy-done.5, bf16[512,2048]{1,0:T(8,128)(2,1)} %copy-done.8, bf16[4,512,2048]{2,1,0:T(8,128)(2,1)} %bitcast.43), custom_call_target="tpu_custom_call" | custom-call | flops 1 | bytes 1 | tf_op jit(solution)/shard_map/hidden_units/pallas_call | solution.py:297
  312.7 25.9 %hidden_units.3 = (bf16[2048,1024]{1,0:T(8,128)(2,1)}, bf16[2048,1024]{1,0:T(8,128)(2,1)}, bf16[2048,1024]{1,0:T(8,128)(2,1)}) custom-call(bf16[512,2048]{1,0:T(8,128)(2,1)} %copy-done.5, bf16[512,2048]{1,0:T(8,128)(2,1)} %get-tuple-element.307.refs_1_, bf16[512,2048]{1,0:T(8,128)(2,1)} %copy-done.8, bf16[512,2048]{1,0:T(8,128)(2,1)} %get-tuple-element.309.refs_3_, ...), custom_call_target="tpu_custom_call" | custom-call | flops 1 | bytes 1 | tf_op jit(solution)/shard_map/hidden_units/pallas_call | solution.py:297
  338.7 17.2 %hidden_grad.2 = (bf16[2048,2048]{1,0:T(8,128)(2,1)}, bf16[512,2048]{1,0:T(8,128)(2,1)}, bf16[512,2048]{1,0:T(8,128)(2,1)}) custom-call(bf16[512,2048]{1,0:T(8,128)(2,1)} %refs_2_, bf16[512,2048]{1,0:T(8,128)(2,1)} %collective-permute-done.3.refs_1_.refs_2_.refs_4_, bf16[2048,1024]{1,0:T(8,128)(2,1)} %get-tuple-element.284.refs_2_, ...), custom_call_target="tpu_custom_call" | custom-call | flops 999999995904 | bytes 1 | tf_op jit(solution)/shard_map/hidden_grad/pallas_call | solution.py:297
  356.0 23.6 %grad_ffn.2 = bf16[4,2048,512]{2,1,0:T(8,128)(2,1)} custom-call(s32[1]{0:T(128)} %bitcast.13.f_ref, bf16[512,2048]{1,0:T(8,128)(2,1)} %copy-done.5, bf16[512,2048]{1,0:T(8,128)(2,1)} %get-tuple-element.307.refs_1_, bf16[512,2048]{1,0:T(8,128)(2,1)} %copy-done.8, bf16[512,2048]{1,0:T(8,128)(2,1)} %get-tuple-element.309.refs_3_, ...), custom_call_target="tpu_custom_call" | custom-call | flops 1 | bytes 1 | tf_op jit(solution)/shard_map/grad_ffn/pallas_call | solution.py:648
  379.6 25.0 %grad_normed_two.3.refs_1_ = bf16[2048,2048]{1,0:T(8,128)(2,1)} custom-call(bf16[2048,2048]{1,0:T(8,128)(2,1)} %get-tuple-element.297.refs_4_.refs_0_, bf16[4,512,2048]{2,1,0:T(8,128)(2,1)} %bitcast.44), custom_call_target="tpu_custom_call" | custom-call | flops 1 | bytes 1 | tf_op jit(solution)/shard_map/grad_normed_two/pallas_call | solution.py:547
  404.6 16.7 %hidden_grad.3.refs_4_.refs_0_ = bf16[2048,2048]{1,0:T(8,128)(2,1)} custom-call(bf16[512,2048]{1,0:T(8,128)(2,1)} %refs_2_, bf16[512,2048]{1,0:T(8,128)(2,1)} %get-tuple-element.330.refs_1_.refs_3_, bf16[512,2048]{1,0:T(8,128)(2,1)} %collective-permute-done.3.refs_1_.refs_2_.refs_4_, bf16[512,2048]{1,0:T(8,128)(2,1)} %get-tuple-element.332.refs_3_.refs_5_, ...), custom_call_target="tpu_custom_call" | custom-call | flops 1 | bytes 1 | tf_op jit(solution)/shard_map/hidden_grad/pallas_call | solution.py:297
  421.3 23.7 %grad_ffn.3 = bf16[4,2048,512]{2,1,0:T(8,128)(2,1)} custom-call(s32[1]{0:T(128)} %bitcast.13.f_ref, bf16[512,2048]{1,0:T(8,128)(2,1)} %copy-done.5, bf16[512,2048]{1,0:T(8,128)(2,1)} %get-tuple-element.307.refs_1_, bf16[512,2048]{1,0:T(8,128)(2,1)} %copy-done.8, bf16[512,2048]{1,0:T(8,128)(2,1)} %get-tuple-element.309.refs_3_, ...), custom_call_target="tpu_custom_call" | custom-call | flops 1 | bytes 1 | tf_op jit(solution)/shard_map/grad_ffn/pallas_call | solution.py:648
  445.0 17.4 %grad_normed_two.4 = bf16[512,2048]{1,0:T(8,128)(2,1)} custom-call(bf16[2048,2048]{1,0:T(8,128)(2,1)} %hidden_grad.3.refs_4_.refs_0_, bf16[2048,2048]{1,0:T(8,128)(2,1)} %grad_normed_two.3.refs_1_, bf16[4,512,2048]{2,1,0:T(8,128)(2,1)} %bitcast.36), custom_call_target="tpu_custom_call" | custom-call | flops 1 | bytes 1 | tf_op jit(solution)/shard_map/grad_normed_two/pallas_call | solution.py:547
  463.7 17.7 %grad_normed_two.5 = f32[512,2048]{1,0:T(8,128)} custom-call(bf16[2048,2048]{1,0:T(8,128)(2,1)} %hidden_grad.3.refs_4_.refs_0_, bf16[2048,2048]{1,0:T(8,128)(2,1)} %grad_normed_two.3.refs_1_, bf16[4,512,2048]{2,1,0:T(8,128)(2,1)} %bitcast.37), custom_call_target="tpu_custom_call" | custom-call | flops 1 | bytes 1 | tf_op jit(solution)/shard_map/grad_normed_two/pallas_call | solution.py:547
  481.4 16.2 %ffn_branch.2 = bf16[512,2048]{1,0:T(8,128)(2,1)} custom-call(bf16[2048,1024]{1,0:T(8,128)(2,1)} %get-tuple-element.327.refs_0_, bf16[2048,1024]{1,0:T(8,128)(2,1)} %get-tuple-element.328.refs_1_, bf16[4,1024,512]{2,1,0:T(8,128)(2,1)} %bitcast.49, bf16[4,1024,512]{2,1,0:T(8,128)(2,1)} %bitcast.39), custom_call_target="tpu_custom_call" | custom-call | flops 1 | bytes 1 | tf_op jit(solution)/shard_map/ffn_branch/pallas_call | solution.py:547
  497.6 13.1 %collective-permute-done.5 = bf16[512,2048]{1,0:T(8,128)(2,1)S(1)} collective-permute-done((bf16[512,2048]{1,0:T(8,128)(2,1)}, bf16[512,2048]{1,0:T(8,128)(2,1)S(1)}, u32[]{:S(2)}, u32[]{:S(2)}) %collective-permute-start.5) | collective-permute-done | bytes 2097184 | tf_op jit(solution)/shard_map/ppermute | solution.py:904
  510.7 4.1 fusion.11
  514.9 5.0 fusion.15
  523.1 16.0 %ffn_branch.3 = f32[512,2048]{1,0:T(8,128)} custom-call(bf16[2048,1024]{1,0:T(8,128)(2,1)} %get-tuple-element.327.refs_0_, bf16[2048,1024]{1,0:T(8,128)(2,1)} %get-tuple-element.328.refs_1_, bf16[4,1024,512]{2,1,0:T(8,128)(2,1)} %bitcast.50, bf16[4,1024,512]{2,1,0:T(8,128)(2,1)} %bitcast.40), custom_call_target="tpu_custom_call" | custom-call | flops 1 | bytes 1 | tf_op jit(solution)/shard_map/ffn_branch/pallas_call | solution.py:547
  539.1 25.4 %grad_down.1 = bf16[4,2048,512]{2,1,0:T(8,128)(2,1)} custom-call(s32[1]{0:T(128)} %bitcast.13.f_ref, bf16[2048,1024]{1,0:T(8,128)(2,1)} %get-tuple-element.327.refs_0_, bf16[2048,1024]{1,0:T(8,128)(2,1)} %get-tuple-element.328.refs_1_, bf16[512,2048]{1,0:T(8,128)(2,1)} %refs_2_, bf16[512,2048]{1,0:T(8,128)(2,1)} %get-tuple-element.330.refs_1_.refs_3_, ...), custom_call_target="tpu_custom_call" | custom-call | flops 1 | bytes 1 | tf_op jit(solution)/shard_map/grad_down/pallas_call | solution.py:702
  567.2 10.7 %head_grad.2 = (bf16[2048,256]{1,0:T(8,128)(2,1)}, bf16[512,2048]{1,0:T(8,128)(2,1)}, bf16[512,2048]{1,0:T(8,128)(2,1)}) custom-call(bf16[512,2048]{1,0:T(8,128)(2,1)} %copy-done.4, bf16[512,2048]{1,0:T(8,128)(2,1)} %collective-permute-done.6.refs_1_.refs_3_.refs_2_, bf16[2048,256]{1,0:T(8,128)(2,1)} %get-tuple-element.402.refs_6_.refs_2_, ...), custom_call_target="tpu_custom_call" | custom-call | flops 1 | bytes 1 | tf_op jit(solution)/shard_map/head_grad/pallas_call | solution.py:297
  579.5 3.4 fusion.20
  584.5 23.4 %attend_backward.2.refs_5_.refs_1_ = bf16[2048,768]{1,0:T(8,128)(2,1)} custom-call(s32[1]{0:T(128)} %bitcast.g_ref, bf16[2048,768]{1,0:T(8,128)(2,1)} %project.3.q_ref.k_ref.v_ref, bf16[2048,768]{1,0:T(8,128)(2,1)} %project.3.q_ref.k_ref.v_ref, bf16[2048,768]{1,0:T(8,128)(2,1)} %project.3.q_ref.k_ref.v_ref, bf16[2048,256]{1,0:T(8,128)(2,1)} %get-tuple-element.346.grad_ref, ...), custom_call_target="tpu_custom_call" | custom-call | flops 999999995904 | bytes 1 | tf_op jit(solution)/shard_map/attend_backward/pallas_call | solution.py:854
  607.8 7.8 grad_heads.2.refs_4_
  615.6 14.2 %grad_attn.2 = bf16[4,1024,512]{2,1,0:T(8,128)(2,1)} custom-call(s32[1]{0:T(128)} %bitcast.13.f_ref, bf16[512,2048]{1,0:T(8,128)(2,1)} %get-tuple-element.379.refs_0_, bf16[512,2048]{1,0:T(8,128)(2,1)} %get-tuple-element.380.refs_1_, bf16[512,2048]{1,0:T(8,128)(2,1)} %get-tuple-element.381.refs_1_.refs_2_, ...), custom_call_target="tpu_custom_call", output_to_operand_aliasing={{}: (5, {})} | custom-call | flops 1 | bytes 1 | tf_op jit(solution)/shard_map/grad_attn/pallas_call | solution.py:648
  629.9 6.3 head_grad.3.grad_ref
  636.1 23.4 %attend_backward.3.refs_5_.refs_0_ = bf16[2048,768]{1,0:T(8,128)(2,1)} custom-call(s32[1]{0:T(128)} %bitcast.g_ref, bf16[2048,768]{1,0:T(8,128)(2,1)} %get-tuple-element.369.q_ref.k_ref.v_ref, bf16[2048,768]{1,0:T(8,128)(2,1)} %get-tuple-element.369.q_ref.k_ref.v_ref, bf16[2048,768]{1,0:T(8,128)(2,1)} %get-tuple-element.369.q_ref.k_ref.v_ref, ...), custom_call_target="tpu_custom_call" | custom-call | flops 1 | bytes 1 | tf_op jit(solution)/shard_map/attend_backward/pallas_call | solution.py:854
  659.5 7.7 grad_heads.3
  670.3 7.4 add_convert_fusion
  679.6 14.2 %grad_attn.3 = bf16[4,1024,512]{2,1,0:T(8,128)(2,1)} custom-call(s32[1]{0:T(128)} %bitcast.13.f_ref, bf16[512,2048]{1,0:T(8,128)(2,1)} %get-tuple-element.379.refs_0_, bf16[512,2048]{1,0:T(8,128)(2,1)} %get-tuple-element.380.refs_1_, bf16[512,2048]{1,0:T(8,128)(2,1)} %get-tuple-element.381.refs_1_.refs_2_, ...), custom_call_target="tpu_custom_call", output_to_operand_aliasing={{}: (5, {})} | custom-call | flops 1 | bytes 1 | tf_op jit(solution)/shard_map/grad_attn/pallas_call | solution.py:648
  693.9 13.8 %grad_normed.2 = bf16[512,2048]{1,0:T(8,128)(2,1)} custom-call(bf16[2048,768]{1,0:T(8,128)(2,1)} %attend_backward.3.refs_5_.refs_0_, bf16[2048,768]{1,0:T(8,128)(2,1)} %attend_backward.2.refs_5_.refs_1_, bf16[2048,256]{1,0:T(8,128)(2,1)} %copy-done.6, bf16[2048,256]{1,0:T(8,128)(2,1)} %get-tuple-element.399.refs_5_.refs_3_, ...), custom_call_target="tpu_custom_call" | custom-call | flops 1 | bytes 1 | tf_op jit(solution)/shard_map/grad_normed/pallas_call | solution.py:547
  711.1 5.2 collective-permute-done.9
  717.3 14.2 %grad_normed.3 = f32[512,2048]{1,0:T(8,128)} custom-call(bf16[2048,768]{1,0:T(8,128)(2,1)} %attend_backward.3.refs_5_.refs_0_, bf16[2048,768]{1,0:T(8,128)(2,1)} %attend_backward.2.refs_5_.refs_1_, bf16[2048,256]{1,0:T(8,128)(2,1)} %copy-done.6, bf16[2048,256]{1,0:T(8,128)(2,1)} %get-tuple-element.399.refs_5_.refs_3_, ...), custom_call_target="tpu_custom_call" | custom-call | flops 100000000376832 | bytes 1 | tf_op jit(solution)/shard_map/grad_normed/pallas_call | solution.py:547
  737.2 5.2 copy.22
  742.4 34.1 %collective-permute-done.12 = bf16[1024,512]{1,0:T(8,128)(2,1)} collective-permute-done((bf16[1024,512]{1,0:T(8,128)(2,1)}, bf16[1024,512]{1,0:T(8,128)(2,1)}, u32[]{:S(2)}, u32[]{:S(2)}) %collective-permute-start.12) | collective-permute-done | bytes 1048608 | tf_op jit(solution)/shard_map/ppermute | solution.py:907
  776.6 2.9 convert_add_fusion.3
  779.5 27.1 %collective-permute-done.11 = bf16[1024,512]{1,0:T(8,128)(2,1)} collective-permute-done((bf16[1024,512]{1,0:T(8,128)(2,1)}, bf16[1024,512]{1,0:T(8,128)(2,1)}, u32[]{:S(2)}, u32[]{:S(2)}) %collective-permute-start.11) | collective-permute-done | bytes 1048608 | tf_op jit(solution)/shard_map/ppermute | solution.py:907
  808.6 2.9 fusion.12
  814.5 4.1 fusion.8
  (145 shorter events, 48.4 us)
Async XLA Ops:
  7.2 279.9 %all-gather.9.cloned.1.call-start = ((), (), s32[]{:S(2)}) async-start(), calls=%async_computation.10 | async-start | bytes 10485760 | tf_op jit(solution)/shard_map/all_gather | solution.py:962
  12.0 3.9 copy-start.6
  12.0 85.2 %copy-start.28 = (s32[4096]{0:T(1024)S(1)}, s32[4096]{0:T(1024)}, u32[]{:S(2)}) copy-start(s32[4096]{0:T(1024)} %param.16) | copy-start | bytes 49156
  94.1 218.6 %all-gather.11.cloned.1.call-start = ((), (), s32[]{:S(2)}) async-start(), calls=%async_computation.11 | async-start | bytes 10485760 | tf_op jit(solution)/shard_map/all_gather | solution.py:962
  94.2 91.6 %collective-permute-start.3 = (bf16[512,2048]{1,0:T(8,128)(2,1)}, bf16[512,2048]{1,0:T(8,128)(2,1)}, u32[]{:S(2)}, u32[]{:S(2)}) collective-permute-start(bf16[512,2048]{1,0:T(8,128)(2,1)} %refs_2_), channel_id=1, source_target_pairs={{0,2},{1,3},{2,0},{3,1},{4,6},{5,7},{6,4},{7,5},{8,10},{9,11},{10,... | collective-permute-start | bytes 6291464 | tf_op jit(solution)/shard_map/ppermute | solution.py:904
  94.2 92.8 %collective-permute-start.2 = (bf16[512,2048]{1,0:T(8,128)(2,1)}, bf16[512,2048]{1,0:T(8,128)(2,1)}, u32[]{:S(2)}, u32[]{:S(2)}) collective-permute-start(bf16[512,2048]{1,0:T(8,128)(2,1)} %bitcast.26), channel_id=1, source_target_pairs={{0,4},{1,5},{2,6},{3,7},{4,0},{5,1},{6,2},{7,3},{8,12},{9,13},{10,... | collective-permute-start | bytes 6291464 | tf_op jit(solution)/shard_map/ppermute | solution.py:907
  102.9 14.5 %copy-start.29 = (s32[4096]{0:T(1024)S(1)}, s32[4096]{0:T(1024)}, u32[]{:S(2)}) copy-start(s32[4096]{0:T(1024)} %param.15) | copy-start | bytes 49156
  102.9 14.5 %copy-start.30 = (s32[4096]{0:T(1024)S(1)}, s32[4096]{0:T(1024)}, u32[]{:S(2)}) copy-start(s32[4096]{0:T(1024)} %param.14) | copy-start | bytes 49156
  118.0 13.7 %copy-start.19 = (s32[2048]{0:T(1024)}, s32[2048]{0:T(1024)S(1)}, u32[]{:S(2)}) copy-start(s32[2048]{0:T(1024)S(1)} %get-tuple-element.425) | copy-start | bytes 24580
  175.9 12.1 %copy-start.2 = (bf16[512,2048]{1,0:T(8,128)(2,1)S(1)}, bf16[512,2048]{1,0:T(8,128)(2,1)}, u32[]{:S(2)}) copy-start(bf16[512,2048]{1,0:T(8,128)(2,1)} %x_ref.1) | copy-start | bytes 6291460
  187.0 151.6 %all-gather.13.cloned.1.call-start = ((), (), s32[]{:S(2)}) async-start(), calls=%async_computation.12 | async-start | bytes 5242880 | tf_op jit(solution)/shard_map/all_gather | solution.py:962
  187.1 45.6 %collective-permute-start = (bf16[512,2048]{1,0:T(8,128)(2,1)}, bf16[512,2048]{1,0:T(8,128)(2,1)}, u32[]{:S(2)}, u32[]{:S(2)}) collective-permute-start(bf16[512,2048]{1,0:T(8,128)(2,1)} %attn_branch.2), channel_id=1, source_target_pairs={{0,2},{1,3},{2,0},{3,1},{4,6},{5,7},{6,4},{7,5},{8,10},{9,11},{10,... | collective-permute-start | bytes 6291464 | tf_op jit(solution)/shard_map/ppermute | solution.py:904
  187.8 216.8 %all-gather.15.cloned.1.call-start = ((), (), s32[]{:S(2)}) async-start(), calls=%async_computation.13 | async-start | bytes 5242880 | tf_op jit(solution)/shard_map/all_gather | solution.py:962
  188.3 49.2 %copy-start.22 = (f32[512]{0:T(512)}, f32[512]{0:T(512)S(1)}, u32[]{:S(2)}) copy-start(f32[512]{0:T(512)S(1)} %broadcast_multiply_fusion.2) | copy-start | bytes 6148
  238.1 47.3 %copy-start.15 = (bf16[1024,512]{1,0:T(8,128)(2,1)S(1)}, bf16[1024,512]{1,0:T(8,128)(2,1)}, u32[]{:S(2)}) copy-start(bf16[1024,512]{1,0:T(8,128)(2,1)} %param.13) | copy-start | bytes 3145732
  238.1 46.0 %copy-start.24 = (f32[512]{0:T(512)}, f32[512]{0:T(512)S(1)}, u32[]{:S(2)}) copy-start(f32[512]{0:T(512)S(1)} %add_rsqrt_fusion.1) | copy-start | bytes 6148
  239.6 47.5 %copy-start.5 = (bf16[512,2048]{1,0:T(8,128)(2,1)}, bf16[512,2048]{1,0:T(8,128)(2,1)S(1)}, u32[]{:S(2)}) copy-start(bf16[512,2048]{1,0:T(8,128)(2,1)S(1)} %fusion.10.refs_0_) | copy-start | bytes 6291460
  239.6 44.5 %collective-permute-start.1 = (bf16[512,2048]{1,0:T(8,128)(2,1)S(1)}, bf16[512,2048]{1,0:T(8,128)(2,1)S(1)}, u32[]{:S(2)}, u32[]{:S(2)}) collective-permute-start(bf16[512,2048]{1,0:T(8,128)(2,1)S(1)} %fusion.10.refs_0_), channel_id=1, source_target_pairs={{0,2},{1,3},{2,0},{3,1},{4,6},{5,7},{6,4},{7,5},{8,10},{9,11},{10,... | collective-permute-start | bytes 6291464 | tf_op jit(solution)/shard_map/ppermute | solution.py:904
  285.4 53.3 %collective-permute-start.4 = (bf16[1024,512]{1,0:T(8,128)(2,1)S(1)}, bf16[1024,512]{1,0:T(8,128)(2,1)}, u32[]{:S(2)}, u32[]{:S(2)}) collective-permute-start(bf16[1024,512]{1,0:T(8,128)(2,1)S(1)} %copy-done.15), channel_id=1, source_target_pairs={{0,4},{1,5},{2,6},{3,7},{4,0},{5,1},{6,2},{7,3},{8,12},{9,13},{10,... | collective-permute-start | bytes 3145736 | tf_op jit(solution)/shard_map/ppermute | solution.py:907
  338.7 228.6 %reduce-scatter.6.cloned.1.call-start = ((), (), s32[]{:S(2)}) async-start(), calls=%async_computation.5 | async-start | bytes 10485760 | tf_op jit(solution)/shard_map/reduce_scatter | solution.py:965
  379.6 200.0 %reduce-scatter.8.cloned.1.call-start = ((), (), s32[]{:S(2)}) async-start(), calls=%async_computation.6 | async-start | bytes 10485760 | tf_op jit(solution)/shard_map/reduce_scatter | solution.py:965
  445.0 262.8 %reduce-scatter.12.cloned.1.call-start = ((), (), s32[]{:S(2)}) async-start(), calls=%async_computation.8 | async-start | bytes 10485760 | tf_op jit(solution)/shard_map/reduce_scatter | solution.py:965
  462.4 48.3 %collective-permute-start.5 = (bf16[512,2048]{1,0:T(8,128)(2,1)}, bf16[512,2048]{1,0:T(8,128)(2,1)S(1)}, u32[]{:S(2)}, u32[]{:S(2)}) collective-permute-start(bf16[512,2048]{1,0:T(8,128)(2,1)} %grad_normed_two.4), channel_id=1, source_target_pairs={{0,2},{1,3},{2,0},{3,1},{4,6},{5,7},{6,4},{7,5},{8,10},{9,11},{10,... | collective-permute-start | bytes 6291464 | tf_op jit(solution)/shard_map/ppermute | solution.py:904
  481.4 29.3 %copy-start.1 = (f32[512,2048]{1,0:T(8,128)S(1)}, f32[512,2048]{1,0:T(8,128)}, u32[]{:S(2)}) copy-start(f32[512,2048]{1,0:T(8,128)} %copy-done) | copy-start | bytes 12582916
  481.4 29.3 %copy-start.21 = (f32[512]{0:T(512)S(1)}, f32[512]{0:T(512)}, u32[]{:S(2)}) copy-start(f32[512]{0:T(512)} %copy-done.20) | copy-start | bytes 6148
  481.4 29.3 %copy-start.25 = (f32[512]{0:T(512)S(1)}, f32[512]{0:T(512)}, u32[]{:S(2)}) copy-start(f32[512]{0:T(512)} %copy-done.24) | copy-start | bytes 6148
  497.6 17.2 %copy-start.7 = (f32[512,2048]{1,0:T(8,128)S(1)}, f32[512,2048]{1,0:T(8,128)}, u32[]{:S(2)}) copy-start(f32[512,2048]{1,0:T(8,128)} %grad_normed_two.5) | copy-start | bytes 12582916
  510.7 4.1 copy-start.12
  514.9 6.4 copy-start.18
  519.9 19.2 %copy-start.4 = (bf16[512,2048]{1,0:T(8,128)(2,1)}, bf16[512,2048]{1,0:T(8,128)(2,1)S(1)}, u32[]{:S(2)}) copy-start(bf16[512,2048]{1,0:T(8,128)(2,1)S(1)} %get-tuple-element.375.refs_0_.refs_1_) | copy-start | bytes 6291460
  519.9 47.4 %collective-permute-start.6 = (bf16[512,2048]{1,0:T(8,128)(2,1)S(1)}, bf16[512,2048]{1,0:T(8,128)(2,1)}, u32[]{:S(2)}, u32[]{:S(2)}) collective-permute-start(bf16[512,2048]{1,0:T(8,128)(2,1)S(1)} %get-tuple-element.375.refs_0_.refs_1_), channel_id=1, source_target_pairs={{0,2},{1,3},{2,0},{3,1},{4,6},{5,7},{6,4},{7,5},{8,10},{9,11},{10,... | collective-permute-start | bytes 6291464 | tf_op jit(solution)/shard_map/ppermute | solution.py:904
  564.5 170.4 %reduce-scatter.10.cloned.1.call-start = ((), (), s32[]{:S(2)}) async-start(), calls=%async_computation.7 | async-start | bytes 5242880 | tf_op jit(solution)/shard_map/reduce_scatter | solution.py:965
  577.9 81.6 %collective-permute-start.7 = (bf16[512,2048]{1,0:T(8,128)(2,1)}, bf16[512,2048]{1,0:T(8,128)(2,1)}, u32[]{:S(2)}, u32[]{:S(2)}) collective-permute-start(bf16[512,2048]{1,0:T(8,128)(2,1)} %ffn_branch.2), channel_id=1, source_target_pairs={{0,2},{1,3},{2,0},{3,1},{4,6},{5,7},{6,4},{7,5},{8,10},{9,11},{10,... | collective-permute-start | bytes 6291464 | tf_op jit(solution)/shard_map/ppermute | solution.py:904
  582.9 76.6 %collective-permute-start.8 = (bf16[1024,512]{1,0:T(8,128)(2,1)}, bf16[1024,512]{1,0:T(8,128)(2,1)}, u32[]{:S(2)}, u32[]{:S(2)}) collective-permute-start(bf16[1024,512]{1,0:T(8,128)(2,1)} %get-tuple-element.373), channel_id=1, source_target_pairs={{0,4},{1,5},{2,6},{3,7},{4,0},{5,1},{6,2},{7,3},{8,12},{9,13},{10,... | collective-permute-start | bytes 3145736 | tf_op jit(solution)/shard_map/ppermute | solution.py:907
  667.2 2.4 copy-start.27
  667.3 112.2 %reduce-scatter.14.cloned.1.call-start = ((), (), s32[]{:S(2)}) async-start(), calls=%async_computation.9 | async-start | bytes 5242880 | tf_op jit(solution)/shard_map/reduce_scatter | solution.py:965
  668.5 47.9 %collective-permute-start.9 = (bf16[1024,512]{1,0:T(8,128)(2,1)S(1)}, bf16[1024,512]{1,0:T(8,128)(2,1)S(1)}, u32[]{:S(2)}, u32[]{:S(2)}) collective-permute-start(bf16[1024,512]{1,0:T(8,128)(2,1)S(1)} %copy-done.16), channel_id=1, source_target_pairs={{0,4},{1,5},{2,6},{3,7},{4,0},{5,1},{6,2},{7,3},{8,12},{9,13},{10,... | collective-permute-start | bytes 3145736 | tf_op jit(solution)/shard_map/ppermute | solution.py:907
  670.3 7.4 copy-start.11
  707.6 100.9 %collective-permute-start.10 = (bf16[512,2048]{1,0:T(8,128)(2,1)}, bf16[512,2048]{1,0:T(8,128)(2,1)}, u32[]{:S(2)}, u32[]{:S(2)}) collective-permute-start(bf16[512,2048]{1,0:T(8,128)(2,1)} %grad_normed.2), channel_id=1, source_target_pairs={{0,2},{1,3},{2,0},{3,1},{4,6},{5,7},{6,4},{7,5},{8,10},{9,11},{10,... | collective-permute-start | bytes 6291464 | tf_op jit(solution)/shard_map/ppermute | solution.py:904
  710.0 66.5 %collective-permute-start.12 = (bf16[1024,512]{1,0:T(8,128)(2,1)}, bf16[1024,512]{1,0:T(8,128)(2,1)}, u32[]{:S(2)}, u32[]{:S(2)}) collective-permute-start(bf16[1024,512]{1,0:T(8,128)(2,1)} %slice.85), channel_id=1, source_target_pairs={{0,4},{1,5},{2,6},{3,7},{4,0},{5,1},{6,2},{7,3},{8,12},{9,13},{10,... | collective-permute-start | bytes 3145736 | tf_op jit(solution)/shard_map/ppermute | solution.py:907
  717.3 14.2 %copy-start.14 = (bf16[2048,512]{1,0:T(8,128)(2,1)S(1)}, bf16[2048,512]{1,0:T(8,128)(2,1)}, u32[]{:S(2)}) copy-start(bf16[2048,512]{1,0:T(8,128)(2,1)} %reduce-scatter.6.cloned.1.call-done) | copy-start | bytes 6291460
  734.8 71.7 %collective-permute-start.11 = (bf16[1024,512]{1,0:T(8,128)(2,1)}, bf16[1024,512]{1,0:T(8,128)(2,1)}, u32[]{:S(2)}, u32[]{:S(2)}) collective-permute-start(bf16[1024,512]{1,0:T(8,128)(2,1)} %reduce-scatter.10.cloned.1.call-done), channel_id=1, source_target_pairs={{0,4},{1,5},{2,6},{3,7},{4,0},{5,1},{6,2},{7,3},{8,12},{9,13},{10,... | collective-permute-start | bytes 3145736 | tf_op jit(solution)/shard_map/ppermute | solution.py:907
  737.2 39.4 %copy-start.13 = (bf16[2048,512]{1,0:T(8,128)(2,1)S(1)}, bf16[2048,512]{1,0:T(8,128)(2,1)}, u32[]{:S(2)}) copy-start(bf16[2048,512]{1,0:T(8,128)(2,1)} %reduce-scatter.12.cloned.1.call-done) | copy-start | bytes 6291460
  779.4 29.1 %copy-start.3 = (bf16[512,2048]{1,0:T(8,128)(2,1)S(1)}, bf16[512,2048]{1,0:T(8,128)(2,1)}, u32[]{:S(2)}) copy-start(bf16[512,2048]{1,0:T(8,128)(2,1)} %x_ref.1) | copy-start | bytes 6291460
  779.4 29.2 %copy-start.23 = (f32[512]{0:T(512)S(1)}, f32[512]{0:T(512)}, u32[]{:S(2)}) copy-start(f32[512]{0:T(512)} %copy-done.22) | copy-start | bytes 6148
  779.4 29.2 %copy-start.26 = (f32[512]{0:T(512)S(1)}, f32[512]{0:T(512)}, u32[]{:S(2)}) copy-start(f32[512]{0:T(512)} %add_rsqrt_fusion) | copy-start | bytes 6148
  779.5 29.1 %copy-start.9 = (f32[512,2048]{1,0:T(8,128)S(1)}, f32[512,2048]{1,0:T(8,128)}, u32[]{:S(2)}) copy-start(f32[512,2048]{1,0:T(8,128)} %grad_normed.3) | copy-start | bytes 12582916
  811.5 2.9 copy-start.10
  (5 other events, 7.5 us)
Sparse Core Ops, SparseCore 0:
  94.2 87.6 all-gather.8
  187.1 87.6 all-gather.10
  276.7 52.6 all-gather.12
  338.8 52.5 all-gather.14
  394.3 86.4 reduce-scatter.5
  484.0 86.4 reduce-scatter.7
  573.5 86.3 reduce-scatter.11
  667.4 52.4 reduce-scatter.9
  722.9 52.6 reduce-scatter.13
